TPU v7x, 128 devices: a whole 4x4x4 slice. The times are simulated.
128 devices in a mesh: dp: 8 (over x, core), group: 16 (over z, y).
Axes of the slice: x: 4, y: 4, z: 4, core: 2. Of those that a mesh axis runs over, the one named last changes fastest.
Arguments:
- gradients: bfloat16 [8, 16, 512, 512], P('dp', 'group'), may hold values from -1 to 1
- block_order: int32 [16], replicated, may hold values from 0 to 15, each once
- owner_count: int32 [16], replicated, may hold values from 0 to 3, as said below
- stat_left: float32 [16, 3, 512, 512], P('group', None, 'dp'), may hold values from -24 to 24
- stat_right: float32 [16, 3, 512, 512], P('group', None, 'dp'), may hold values from -24 to 24
- root_left: float32 [16, 3, 512, 512], P('group', None, 'dp')
- root_right: float32 [16, 3, 512, 512], P('group', None, 'dp')
- momentum: float32 [16, 3, 512, 512], P('group', None, 'dp'), may hold values from -3 to 3
Outputs:
- update_blocks: bfloat16 [16, 512, 512], replicated
- left_stats: float32 [16, 3, 512, 512], P('group', None, 'dp')
- right_stats: float32 [16, 3, 512, 512], P('group', None, 'dp')
- new_momentum: float32 [16, 3, 512, 512], P('group', None, 'dp')
Inputs may be any that keep to these rules, and one draw needn't show every extreme that they name: `block_order`: each block index appears once. `owner_count`: the counts sum to 16; some owner holds exactly 3 blocks.
All inputs are finite; a program needn't handle non-finite values.
Results may differ from a plain program's by a relative error of at most 0.018.
Values may be sent and summed in bfloat16 or wider, within the bound.
No kernel may reach another device: no remote copies, remote signals or barrier semaphores. Data moves between devices by JAX's collectives and lax.ppermute only.
A program may use at most 64 MiB of HBM per device.

v0:
```python
import jax
import jax.numpy as jnp
from jax import lax
from jax.sharding import PartitionSpec as P

decay_stats = 0.95
decay_moment = 0.9
epsilon = 1e-06


def assignment(block_order, owner_count, slot_count, block_count):
    range_ends = jnp.cumsum(owner_count, dtype=jnp.int32)
    range_starts = range_ends - owner_count
    slot_range = jnp.arange(slot_count, dtype=jnp.int32)
    position = range_starts[:, None] + slot_range[None, :]
    slot_valid = slot_range[None, :] < owner_count[:, None]
    slot_blocks = block_order[jnp.minimum(position, block_count - 1)]
    places = jnp.arange(block_count, dtype=jnp.int32)
    block_place = jnp.sum(
        jnp.where(block_order[None, :] == places[:, None], places[None, :], 0),
        axis=1,
        dtype=jnp.int32,
    )
    block_owner = jnp.sum(
        (range_ends[None, :] <= block_place[:, None]).astype(jnp.int32), axis=1, dtype=jnp.int32
    )
    block_slot = block_owner * slot_count + block_place - range_starts[block_owner]
    return (slot_blocks, slot_valid, block_owner, block_slot)


def local(
    gradients, block_order, owner_count, stat_left, stat_right, root_left, root_right, momentum
):
    owner_here = lax.axis_index("group")
    replica_here = lax.axis_index("dp")
    slot_count = stat_left.shape[1]
    row_count = stat_left.shape[2]
    block_size = stat_left.shape[3]
    block_count = block_order.shape[0]
    slot_blocks, slot_valid, block_owner, block_slot = assignment(
        block_order, owner_count, slot_count, block_count
    )
    my_blocks = lax.dynamic_index_in_dim(slot_blocks, owner_here, 0, keepdims=False)
    my_valid = lax.dynamic_index_in_dim(slot_valid, owner_here, 0, keepdims=False)
    live_mask = my_valid[:, None, None]
    zero_half = jnp.zeros((), jnp.bfloat16)
    own_term = gradients[0, 0].astype(jnp.float32)
    summed = lax.psum(own_term.astype(jnp.bfloat16), "dp")
    every_block = lax.all_gather(summed[None], "group", axis=0, tiled=True)
    gradient = jnp.where(live_mask, jnp.take(every_block, my_blocks, axis=0), zero_half)
    grad_rows = lax.dynamic_slice_in_dim(gradient, replica_here * row_count, row_count, 1)
    grad_cols = lax.dynamic_slice_in_dim(gradient, replica_here * row_count, row_count, 2)
    left_term = jnp.einsum("srk,sck->src", grad_rows, gradient, preferred_element_type=jnp.float32)
    right_term = jnp.einsum("skr,skc->src", grad_cols, gradient, preferred_element_type=jnp.float32)
    left_stats = jnp.where(
        live_mask, decay_stats * stat_left[0] + (1.0 - decay_stats) * left_term, stat_left[0]
    )
    right_stats = jnp.where(
        live_mask, decay_stats * stat_right[0] + (1.0 - decay_stats) * right_term, stat_right[0]
    )
    precond = jnp.einsum(
        "srk,skc->src",
        root_left[0].astype(jnp.bfloat16),
        gradient,
        preferred_element_type=jnp.float32,
    ).astype(jnp.bfloat16)
    direction = jnp.einsum(
        "srk,skc->src",
        precond,
        lax.all_gather(root_right[0].astype(jnp.bfloat16), "dp", axis=1, tiled=True),
        preferred_element_type=jnp.float32,
    )
    grad_wide = grad_rows.astype(jnp.float32)
    dir_square, grad_square = lax.psum(
        (jnp.sum(direction * direction, axis=(1, 2)), jnp.sum(grad_wide * grad_wide, axis=(1, 2))),
        "dp",
    )
    entries = float(block_size * block_size)
    graft = jnp.sqrt(grad_square / entries) / jnp.sqrt(dir_square / entries + epsilon)
    new_momentum = jnp.where(
        live_mask, decay_moment * momentum[0] + graft[:, None, None] * direction, momentum[0]
    )
    fresh_rows = new_momentum.astype(jnp.bfloat16)
    every_slot = lax.all_gather(fresh_rows, "group", axis=0, tiled=True)
    picked = jnp.take(every_slot, block_slot, axis=0)
    update_blocks = lax.all_gather(picked, "dp", axis=1, tiled=True)
    return (update_blocks, left_stats[None], right_stats[None], new_momentum[None])


def solution(mesh):
    placed = (
        P("dp", "group", None, None),
        P(),
        P(),
        P("group", None, "dp", None),
        P("group", None, "dp", None),
        P("group", None, "dp", None),
        P("group", None, "dp", None),
        P("group", None, "dp", None),
    )
    return jax.shard_map(
        local,
        mesh=mesh,
        in_specs=placed,
        out_specs=(
            P(),
            P("group", None, "dp", None),
            P("group", None, "dp", None),
            P("group", None, "dp", None),
        ),
        check_vma=False,
    )
```

profile of v0, /device:TPU:1, one launch (start us, length us, event | category | flops | bytes accessed | tf_op | source)
XLA Modules:
  0.0 303.6 jit_solution(18281464938662477551)
XLA Ops:
  7.2 0.0 copy-start.5
  7.2 0.0 copy-start
  7.2 0.0 all-reduce.3.cloned.1.call-start
  7.2 0.7 all-reduce.3.cloned.1.call-update
  7.9 0.0 all-gather.6.cloned.1.call-start
  8.0 64.2 %all-reduce.3.cloned.1.call-done = bf16[1,512,512]{2,1,0:T(8,128)(2,1)} async-done(((bf16[1,512,512]{2,1,0:T(8,128)(2,1)}), bf16[1,512,512]{2,1,0:T(8,128)(2,1)}) %all-reduce.3.cloned.1.call-update) | async-done | bytes 524304 | tf_op jit(solution)/shard_map/psum | solution.py:48
  72.1 0.0 all-gather.6.cloned.1.call-update
  72.1 0.0 all-gather.12.cloned.1.call-start
  72.2 1.7 convert_element_type.32
  73.9 0.0 all-gather.12.cloned.1.call-update
  73.9 0.0 all-gather.8.cloned.1.call-start
  74.0 0.0 copy-done.5
  74.0 0.6 dynamic-slice
  74.6 0.1 copy.18
  74.7 0.1 reduce
  74.8 0.0 copy-start.6
  74.8 0.5 copy-done.6
  75.3 0.1 compare_select_fusion
  75.4 0.1 reshape.179
  75.5 0.0 copy-done
  75.5 0.8 gather_fusion.1
  76.3 0.1 reshape.178
  76.4 0.7 compare_bitcast_fusion
  77.1 69.6 %all-gather.6.cloned.1.call-done = bf16[16,512,512]{2,1,0:T(8,128)(2,1)} async-done(((bf16[1,512,512]{2,1,0:T(8,128)(2,1)}), bf16[16,512,512]{2,1,0:T(8,128)(2,1)}) %all-gather.6.cloned.1.call-update) | async-done | bytes 8388624 | tf_op jit(solution)/shard_map/all_gather | solution.py:49
  146.6 4.0 %gather_fusion.2 = bf16[3,512,512]{2,1,0:T(8,128)(2,1)S(1)} fusion(bf16[16,512,512]{2,1,0:T(8,128)(2,1)} %all-gather.6.cloned.1.call-done, s32[1024]{0:T(1024)S(1)} %pad_clamp_fusion.1), kind=kCustom, calls=%fused_computation.2 | custom fusion | bytes 3145740 | tf_op jit(solution)/shard_map/jit(_take)/gather | solution.py:50
  150.7 0.0 copy-start.1
  150.7 0.2 select_select_fusion
  150.9 0.2 multiply_reduce_fusion.1
  151.1 0.0 copy-start.2
  151.1 22.4 %all-gather.12.cloned.1.call-done = bf16[1,3,512,512]{3,2,1,0:T(8,128)(2,1)} async-done(((bf16[1,3,64,512]{3,2,1,0:T(8,128)(2,1)}), bf16[1,3,512,512]{3,2,1,0:T(8,128)(2,1)}) %all-gather.12.cloned.1.call-update) | async-done | bytes 1572880 | tf_op jit(solution)/shard_map/all_gather | solution.py:70
  173.5 0.0 copy-done.1
  173.5 2.2 multiply_reduce_fusion
  175.7 0.0 copy-start.7
  175.7 12.1 %all-reduce = (f32[3]{0:T(128)S(1)}, f32[3]{0:T(128)S(1)}) all-reduce(f32[3]{0:T(128)S(1)} %get-tuple-element.8, f32[3]{0:T(128)S(1)} %multiply_reduce_fusion.1), channel_id=1, replica_groups=mesh['dp'=8,'group'=16] {'dp'}, use_global_device_ids=true, to_apply=%region_7.8 | all-reduce | flops 6 | bytes 48 | tf_op jit(solution)/shard_map/psum | solution.py:74
  187.9 0.0 copy-done.2
  187.9 1.0 fusion.20
  188.8 0.0 all-gather.8.cloned.1.call-update
  188.8 0.0 all-gather.10.cloned.1.call-start
  188.9 0.1 select_reduce_fusion
  189.0 0.0 copy-done.7
  189.0 0.2 convert_reduce_fusion
  189.2 0.7 gather_fusion
  189.9 46.6 %all-gather.8.cloned.1.call-done = bf16[48,64,512]{2,1,0:T(8,128)(2,1)} async-done(((bf16[3,64,512]{2,1,0:T(8,128)(2,1)}), bf16[48,64,512]{2,1,0:T(8,128)(2,1)}) %all-gather.8.cloned.1.call-update) | async-done | bytes 3145744 | tf_op jit(solution)/shard_map/all_gather | solution.py:84
  236.5 2.5 gather_fusion.3
  239.0 0.0 copy-start.3
  239.1 1.1 broadcast_select_fusion
  240.2 0.0 copy-start.4
  240.2 0.0 all-gather.10.cloned.1.call-update
  240.2 0.0 copy-done.3
  240.2 1.3 fusion.7
  241.6 0.0 copy-done.4
  241.6 1.4 fusion.5
  242.9 46.6 %all-gather.10.cloned.1.call-done = bf16[16,512,512]{2,1,0:T(8,128)(2,1)} async-done(((bf16[16,64,512]{2,1,0:T(8,128)(2,1)}), bf16[16,512,512]{2,1,0:T(8,128)(2,1)}) %all-gather.10.cloned.1.call-update) | async-done | bytes 8388624 | tf_op jit(solution)/shard_map/all_gather | solution.py:86
  289.5 7.5 %copy.24 = bf16[16,512,512]{2,1,0:T(8,128)(2,1)} copy(bf16[16,512,512]{2,1,0:T(8,128)(2,1)} %all-gather.10.cloned.1.call-done) | data formatting | bytes 16777216
  (12 shorter events, 0.1 us)
Async XLA Ops:
  7.2 66.8 %copy-start.5 = (s32[16]{0:T(128)S(1)}, s32[16]{0:T(128)}, u32[]{:S(2)}) copy-start(s32[16]{0:T(128)} %param.10) | copy-start | bytes 196
  7.2 68.3 %copy-start = (s32[16]{0:T(128)S(1)}, s32[16]{0:T(128)}, u32[]{:S(2)}) copy-start(s32[16]{0:T(128)} %param.9) | copy-start | bytes 196
  7.2 64.9 %all-reduce.3.cloned.1.call-start = ((), (), s32[]{:S(2)}) async-start(), calls=%async_computation | async-start | bytes 1048576 | tf_op jit(solution)/shard_map/psum | solution.py:48
  7.9 138.7 %all-gather.6.cloned.1.call-start = ((), (), s32[]{:S(2)}) async-start(), calls=%async_computation.1 | async-start | bytes 8912896 | tf_op jit(solution)/shard_map/all_gather | solution.py:49
  72.1 101.4 %all-gather.12.cloned.1.call-start = ((), (), s32[]{:S(2)}) async-start(), calls=%async_computation.4 | async-start | bytes 1769472 | tf_op jit(solution)/shard_map/all_gather | solution.py:70
  73.9 162.6 %all-gather.8.cloned.1.call-start = ((), (), s32[]{:S(2)}) async-start(), calls=%async_computation.2 | async-start | bytes 3342336 | tf_op jit(solution)/shard_map/all_gather | solution.py:84
  74.8 0.5 copy-start.6
  150.7 22.8 %copy-start.1 = (f32[1,3,64,512]{3,2,1,0:T(8,128)S(1)}, f32[1,3,64,512]{3,2,1,0:T(8,128)}, u32[]{:S(2)}) copy-start(f32[1,3,64,512]{3,2,1,0:T(8,128)} %param.13) | copy-start | bytes 1179652
  151.1 36.8 %copy-start.2 = (f32[1,3,64,512]{3,2,1,0:T(8,128)S(1)}, f32[1,3,64,512]{3,2,1,0:T(8,128)}, u32[]{:S(2)}) copy-start(f32[1,3,64,512]{3,2,1,0:T(8,128)} %param.15) | copy-start | bytes 1179652
  175.7 13.3 %copy-start.7 = (s32[16]{0:T(128)S(1)}, s32[16]{0:T(128)}, u32[]{:S(2)}) copy-start(s32[16]{0:T(128)} %copy-done.6) | copy-start | bytes 196
  188.8 100.7 %all-gather.10.cloned.1.call-start = ((), (), s32[]{:S(2)}) async-start(), calls=%async_computation.3 | async-start | bytes 9437184 | tf_op jit(solution)/shard_map/all_gather | solution.py:86
  239.0 1.2 copy-start.3
  240.2 1.4 copy-start.4
Sparse Core Ops, SparseCore 0:
  10.3 61.7 all-reduce.2
  74.5 72.1 all-gather.5
  149.0 24.4 all-gather.11
  189.0 47.5 all-gather.7
  240.3 49.1 all-gather.9
where the time goes:
time: 304 us
  waiting for transfers between devices  250 us (82%)
  local copies, waits for them, and re-layouts  16.8 us (6%)
  between operations  13.9 us (5%)
  blocking collectives  12.1 us (4%)
  other arithmetic  5.46 us (2%)
  matrix products  4.86 us (2%)
    all_gather x1, waiting for transfers between devices, local(): every_block = lax.all_gather(summed[None], 'group', axis=0, tiled=True)  69.6 us
    psum x1, waiting for transfers between devices, local(): summed = lax.psum(own_term.astype(jnp.bfloat16), 'dp')  64.2 us
    all_gather x1, waiting for transfers between devices, local(): update_blocks = lax.all_gather(picked, 'dp', axis=1, tiled=True)  46.6 us
    all_gather x1, waiting for transfers between devices, local(): every_slot = lax.all_gather(fresh_rows, 'group', axis=0, tiled=True)  46.6 us
    all_gather x1, waiting for transfers between devices, local(): lax.all_gather(root_right[0].astype(jnp.bfloat16), 'dp', axis=1, tiled=True)  22.4 us
    psum x1, blocking collectives, local(): lax.psum((jnp.sum(direction * direction, axis=(1, 2)), jnp.sum(grad_wide...  12.1 us
    unnamed x17, local copies, waits for them, and re-layouts  8.05 us
  transfers between devices with their start and end apart: 5, of which 5 were waited for; matrix products, arithmetic and copies ran while one was open for 4% of the time, Pallas kernels for 0%

commit v1 on v0

v1 whole, which is shorter than its diff:
```python
import jax
import jax.numpy as jnp
from jax import lax
from jax.experimental import pallas as pl
from jax.experimental.pallas import tpu as pltpu
from jax.sharding import PartitionSpec as P

decay_stats = 0.95
decay_moment = 0.9
epsilon = 1e-06

AXES = ("dp", "group")
X, CORES, SIDE, SLOTS = 4, 2, 4, 3
BLOCKS = SIDE * SIDE
BS = 512
ROWS = BS // (X * CORES)
HALF = BS // CORES


def permute(value, target):
    pairs = []
    for x in range(X):
        for c in range(CORES):
            for z in range(SIDE):
                for y in range(SIDE):
                    tx, tc, tz, ty = target(x, c, z, y)
                    pairs.append(
                        ((x * 2 + c) * 16 + z * 4 + y, ((tx % 4) * 2 + tc) * 16 + (tz % 4) * 4 + ty % 4)
                    )
    return lax.ppermute(value, AXES, pairs)


def to_core(value):
    return permute(value, lambda x, c, z, y: (x, 1 - c, z, y))


def to_x(value, k):
    return permute(value, lambda x, c, z, y: (x + k, c, z, y))


def to_u(value, k):
    return permute(value, lambda x, c, z, y: (x, c, z, y + k) if c == 0 else (x, c, z + k, y))


def to_v(value, k):
    return permute(value, lambda x, c, z, y: (x, c, z + k, y) if c == 0 else (x, c, z, y + k))


def pick(options, index):
    out = options[0]
    for n in range(1, len(options)):
        out = jnp.where(index == n, options[n], out)
    return out


def look_up(table, index):
    slots = jnp.arange(table.shape[0], dtype=jnp.int32)
    hit = slots == index[..., None]
    return jnp.sum(jnp.where(hit, table, 0), axis=-1, dtype=jnp.int32)


def fill_grad(c_ref, g_own, g_other, grad):
    c = c_ref[0]
    grad[pl.ds(pl.multiple_of(c * HALF, HALF), HALF), :] = g_own[...]
    grad[pl.ds(pl.multiple_of((1 - c) * HALF, HALF), HALF), :] = g_other[...]


def step_kernel(c_ref, g_own, g_other, a_own, a_other, out, grad, full):
    c = c_ref[0]
    fill_grad(c_ref, g_own, g_other, grad)
    for n in range(3):
        for x in range(X):
            full[n, pl.ds(pl.multiple_of((2 * x + c) * ROWS, ROWS), ROWS), :] = a_own[n, x]
            full[n, pl.ds(pl.multiple_of((2 * x + 1 - c) * ROWS, ROWS), ROWS), :] = a_other[n, x]
    g = grad[...]
    wide = g.astype(jnp.float32)
    grad_square = jnp.sum(wide * wide)
    precond = jnp.dot(full[0], g, preferred_element_type=jnp.float32).astype(jnp.bfloat16)
    direction = jnp.dot(precond, full[1], preferred_element_type=jnp.float32)
    dir_square = jnp.sum(direction * direction)
    entries = float(BS * BS)
    top = jnp.sqrt(jnp.full((1, BS), grad_square / entries, jnp.float32))
    graft = top / jnp.sqrt(jnp.full((1, BS), dir_square / entries + epsilon, jnp.float32))
    out[...] = (decay_moment * full[2].astype(jnp.float32) + graft * direction).astype(jnp.bfloat16)


def term_kernel(c_ref, g_own, g_other, out, grad, held):
    fill_grad(c_ref, g_own, g_other, grad)
    c, x = c_ref[0], c_ref[1]
    g = grad[...]
    rows = grad[pl.ds(pl.multiple_of((2 * x + c) * ROWS, ROWS), ROWS), :]
    out[0] = lax.dot_general(
        rows, g, (((1,), (1,)), ((), ())), preferred_element_type=jnp.float32
    ).astype(jnp.bfloat16)
    columns = grad[:, pl.ds(pl.multiple_of(x * 2 * ROWS, 2 * ROWS), 2 * ROWS)]
    held[...] = lax.dot_general(
        columns, g, (((0,), (0,)), ((), ())), preferred_element_type=jnp.float32
    )
    out[1] = held[pl.ds(pl.multiple_of(c * ROWS, ROWS), ROWS), :].astype(jnp.bfloat16)


def place_kernel(where_ref, *refs):
    sources, out, sems = refs[:8], refs[8], refs[9]
    copies = []
    for n in range(8):
        for j in range(4):
            block = where_ref[n * 4 + j]
            half = where_ref[32] if n < 4 else 1 - where_ref[32]
            copies.append(
                pltpu.make_async_copy(
                    sources[n].at[j],
                    out.at[block, pl.ds(pl.multiple_of(half * HALF, HALF), HALF), :],
                    sems.at[n * 4 + j],
                )
            )
    for copy in copies:
        copy.start()
    for copy in copies:
        copy.wait()


SMEM = pl.BlockSpec(memory_space=pltpu.SMEM)
VMEM = pl.BlockSpec(memory_space=pltpu.VMEM)
ANY = pl.BlockSpec(memory_space=pl.ANY)


def local(
    gradients, block_order, owner_count, stat_left, stat_right, root_left, root_right, momentum
):
    dp = lax.axis_index("dp")
    me = lax.axis_index("group")
    x, c = dp // 2, dp % 2
    y, z = me % 4, me // 4
    first = c == 0
    u, v = jnp.where(first, y, z), jnp.where(first, z, y)

    def place_at(uu, vv):
        yy, zz = jnp.where(first, uu, vv), jnp.where(first, vv, uu)
        return 4 * ((zz - yy) % 4) + yy

    def uv_of_member(g):
        yy, zz = g % 4, g // 4
        return jnp.where(first, yy, zz), jnp.where(first, zz, yy)

    def uv_of_place(q):
        yy, zz = q % 4, (q % 4 + q // 4) % 4
        return jnp.where(first, yy, zz), jnp.where(first, zz, yy)

    four = jnp.arange(4, dtype=jnp.int32)
    three = jnp.arange(SLOTS, dtype=jnp.int32)
    ends = jnp.cumsum(owner_count, dtype=jnp.int32)
    starts = ends - owner_count
    places = jnp.arange(BLOCKS, dtype=jnp.int32)
    place_owner = jnp.sum((ends[None, :] <= places[:, None]).astype(jnp.int32), axis=1, dtype=jnp.int32)

    v_places = place_at(u, (v + four) % 4)
    v_blocks = look_up(block_order, v_places)
    v_owners = look_up(place_owner, v_places)
    block_u, block_v = uv_of_member(v_blocks)
    grad_pick = (u - block_u) % 4
    grad_last = (v - block_v[0]) % 4
    owner_u, owner_v = uv_of_member(v_owners)
    root_pick = (u - owner_u) % 4
    root_last = (v - owner_v[0]) % 4

    my_start, my_count = look_up(starts, me[None])[0], look_up(owner_count, me[None])[0]
    live = three < my_count
    slot_place = jnp.minimum(my_start + three, BLOCKS - 1)
    slot_block = look_up(block_order, slot_place)
    slot_u, _ = uv_of_place(slot_place)
    slot_pick = jnp.sum(
        jnp.where((slot_u[None, :] == ((u + four) % 4)[:, None]) & live[None, :], three[None, :], 0),
        axis=1,
    )
    term_last = (u - slot_u) % 4
    u_far = (u + four) % 4
    u_members = jnp.where(first, 4 * v + u_far, 4 * u_far + v)
    far_place = look_up(starts, u_members)[:, None] + three[None, :]
    far_live = three[None, :] < look_up(owner_count, u_members)[:, None]
    far_u, far_v = uv_of_place(far_place)
    term_pick = jnp.sum(jnp.where(far_live & (far_u == u), (v - far_v) % 4, 0), axis=1)

    own_places = place_at((u - four[None, :]) % 4, (v - four[:, None]) % 4)
    other_places = place_at((u - four[:, None]) % 4, (v - four[None, :]) % 4)
    landing = look_up(block_order, jnp.concatenate([own_places, other_places]).reshape(-1))
    landing = jnp.concatenate([landing, c[None]])
    spot = jnp.stack([c, x])

    halves = gradients[0, 0].reshape(2, HALF, BS)
    mine = lax.dynamic_index_in_dim(halves, c, 0, keepdims=False)
    theirs = lax.dynamic_index_in_dim(halves, 1 - c, 0, keepdims=False)
    pair = mine.astype(jnp.float32) + to_core(theirs).astype(jnp.float32)
    pair = pair.astype(jnp.bfloat16).reshape(X, ROWS, BS)
    total = lax.dynamic_index_in_dim(pair, x, 0, keepdims=False).astype(jnp.float32)
    for k in (1, 3, 2):
        part = lax.dynamic_index_in_dim(pair, (x + k) % 4, 0, keepdims=False)
        total = total + to_x(part, k).astype(jnp.float32)
    chunk = total.astype(jnp.bfloat16)

    def along(send, values):
        got = [values[0], None, None, None]
        for k in (2, 1, 3):
            got[k] = send(values[k], k)
        return got

    row = along(to_u, [chunk] * 4)
    column = along(to_v, [pick(row, grad_pick[k]) for k in range(4)])
    chunk = pick(column, grad_last)

    slots = jnp.stack([root_left[0], root_right[0], momentum[0]], axis=1).astype(jnp.bfloat16)
    packs = [lax.dynamic_index_in_dim(slots, slot_pick[k], 0, keepdims=False) for k in range(4)]
    row = along(to_u, packs)
    column = along(to_v, [pick(row, root_pick[k]) for k in range(4)])
    pack = pick(column, root_last)

    def over_x(value):
        got = along(to_x, [value] * 4)
        return jnp.stack([pick(got, (x - n) % 4) for n in range(4)], axis=-3)

    pack = over_x(pack)
    pack_other = to_core(pack)
    grad_own = over_x(chunk).reshape(HALF, BS)
    grad_other = to_core(grad_own)

    update = pl.pallas_call(
        step_kernel,
        out_shape=jax.ShapeDtypeStruct((BS, BS), jnp.bfloat16),
        in_specs=[SMEM, VMEM, VMEM, VMEM, VMEM],
        out_specs=VMEM,
        scratch_shapes=[
            pltpu.VMEM((BS, BS), jnp.bfloat16),
            pltpu.VMEM((3, BS, BS), jnp.bfloat16),
        ],
        compiler_params=pltpu.CompilerParams(vmem_limit_bytes=32 << 20),
        cost_estimate=pl.CostEstimate(flops=4 * BS**3, bytes_accessed=5 * BS * BS * 2, transcendentals=0),
        name="step",
    )(spot, grad_own, grad_other, pack, pack_other)

    terms = pl.pallas_call(
        term_kernel,
        out_shape=jax.ShapeDtypeStruct((2, ROWS, BS), jnp.bfloat16),
        in_specs=[SMEM, VMEM, VMEM],
        out_specs=VMEM,
        scratch_shapes=[
            pltpu.VMEM((BS, BS), jnp.bfloat16),
            pltpu.VMEM((2 * ROWS, BS), jnp.float32),
        ],
        compiler_params=pltpu.CompilerParams(vmem_limit_bytes=32 << 20),
        cost_estimate=pl.CostEstimate(
            flops=6 * ROWS * BS * BS, bytes_accessed=BS * BS * 2, transcendentals=0
        ),
        name="terms",
    )(spot, grad_own, grad_other)

    half = lax.dynamic_slice_in_dim(update, c * HALF, HALF, 0)
    near = jnp.stack(along(to_u, [half] * 4))
    held = along(to_v, [near] * 4)
    across = [to_core(value) for value in held]
    update_blocks = pl.pallas_call(
        place_kernel,
        out_shape=jax.ShapeDtypeStruct((BLOCKS, BS, BS), jnp.bfloat16),
        in_specs=[SMEM] + [ANY] * 8,
        out_specs=ANY,
        scratch_shapes=[pltpu.SemaphoreType.DMA((32,))],
        name="place",
    )(landing, *held, *across)

    column = along(to_v, [terms] * 4)
    row = along(to_u, [pick(column, term_pick[k]) for k in range(4)])
    back = jnp.stack([pick(row, term_last[s]) for s in range(SLOTS)]).astype(jnp.float32)

    alive = live[:, None, None]
    left_stats = jnp.where(
        alive, decay_stats * stat_left[0] + (1.0 - decay_stats) * back[:, 0], stat_left[0]
    )
    right_stats = jnp.where(
        alive, decay_stats * stat_right[0] + (1.0 - decay_stats) * back[:, 1], stat_right[0]
    )
    fresh = jnp.stack(
        [
            lax.dynamic_slice(update_blocks, (slot_block[s], dp * ROWS, 0), (1, ROWS, BS))[0]
            for s in range(SLOTS)
        ]
    )
    new_momentum = jnp.where(alive, fresh.astype(jnp.float32), momentum[0])
    return (update_blocks, left_stats[None], right_stats[None], new_momentum[None])


def solution(mesh):
    placed = (
        P("dp", "group", None, None),
        P(),
        P(),
        P("group", None, "dp", None),
        P("group", None, "dp", None),
        P("group", None, "dp", None),
        P("group", None, "dp", None),
        P("group", None, "dp", None),
    )
    return jax.shard_map(
        local,
        mesh=mesh,
        in_specs=placed,
        out_specs=(
            P(),
            P("group", None, "dp", None),
            P("group", None, "dp", None),
            P("group", None, "dp", None),
        ),
        check_vma=False,
    )
```

time: 304 us -> 420 us (1.38)
  Pallas kernels: 0 us -> 259 us
  waiting for transfers between devices: 250 us -> 43.1 us
  starting transfers between devices: 0.2 us -> 54.2 us
  between operations: 13.9 us -> 42.4 us
  blocking collectives: 12.1 us -> 0 us
  local copies, waits for them, and re-layouts: 16.8 us -> 6.63 us
  other arithmetic: 5.46 us -> 12.5 us
  matrix products: 4.86 us -> 0 us
    pallas_call x0 -> x3, Pallas kernels: none -> 259 us  [the longest x1 256 us: local(): pl.pallas_call(place_kernel, out_shape=jax.ShapeDtypeStruct((BLOCKS, BS,...]
    all_gather x4 -> x0, waiting for transfers between devices: 185 us -> none  [the longest x1 69.6 us: local(): every_block = lax.all_gather(summed[None], 'group', axis=0, tiled=True)]
    psum x1 -> x0, waiting for transfers between devices: 64.2 us -> none  [local(): summed = lax.psum(own_term.astype(jnp.bfloat16), 'dp')]
    ppermute x0 -> x40, starting transfers between devices: none -> 54.2 us  [permute(): return lax.ppermute(value, AXES, pairs)]
    ppermute x0 -> x40, waiting for transfers between devices: none -> 43.1 us  [permute(): return lax.ppermute(value, AXES, pairs)]
    psum x1 -> x0, blocking collectives: 12.1 us -> none  [local(): lax.psum((jnp.sum(direction * direction, axis=(1, 2)), jnp.sum(grad_wide...]
    gather x5 -> x0, local copies, waits for them, and re-layouts: 8.04 us -> none  [the longest x1 4.03 us: local(): jnp.take(every_block, my_blocks, axis=0)]
    unnamed x17 -> x10, local copies, waits for them, and re-layouts: 8.05 us -> 0.03 us
  transfers between devices with their start and end apart: 5 -> 40, of which waited for: 5 -> 14; matrix products, arithmetic and copies ran while one was open for 4% -> 4% of each run, Pallas kernels for 0% -> 0%
where the time goes in v1:
time: 420 us; the launch traced here: 418 us
  Pallas kernels  259 us (62%)
  starting transfers between devices  54.2 us (13%)
  waiting for transfers between devices  43.1 us (10%)
  between operations  42.4 us (10%)
  other arithmetic  12.5 us (3%)
  local copies, waits for them, and re-layouts  6.63 us (2%)
    pallas_call x1, Pallas kernels, local(): pl.pallas_call(place_kernel, out_shape=jax.ShapeDtypeStruct((BLOCKS, BS,...  256 us
    ppermute x40, starting transfers between devices, permute(): return lax.ppermute(value, AXES, pairs)  54.2 us
    ppermute x40, waiting for transfers between devices, permute(): return lax.ppermute(value, AXES, pairs)  43.1 us
  transfers between devices with their start and end apart: 40, of which 14 were waited for; matrix products, arithmetic and copies ran while one was open for 4% of the time, Pallas kernels for 0%

profile of v1, /device:TPU:1, one launch (start us, length us, event | category | flops | bytes accessed | tf_op | source)
XLA Modules:
  0.0 418.1 jit_solution(12018186281222221880)
XLA Ops:
  0.6 1.0 dynamic-slice_bitcast_fusion
  1.6 1.5 collective-permute-start
  3.1 0.7 copy.24
  4.0 1.3 fusion.37
  5.4 0.7 and_select_fusion
  6.0 0.7 iota_compare_fusion.6
  6.9 0.6 fusion.54
  11.4 1.0 convert_bitcast_fusion.2
  12.4 1.2 convert_bitcast_fusion
  15.6 3.9 collective-permute-start.14
  19.6 0.7 collective-permute-start.16
  20.4 0.9 select_reduce_fusion.5
  21.3 0.6 fusion.55
  29.8 0.7 fusion.53
  39.8 1.0 fusion
  40.9 2.8 collective-permute-start.3
  43.7 0.9 collective-permute-start.2
  44.6 0.6 collective-permute-start.1
  45.3 2.8 collective-permute-start.17
  48.4 0.7 collective-permute-start.19
  49.2 2.0 collective-permute-start.4
  51.2 1.8 collective-permute-start.5
  53.0 1.8 collective-permute-start.6
  54.7 1.8 collective-permute-done.19
  56.6 2.1 collective-permute-start.20
  58.7 0.6 collective-permute-start.22
  59.5 2.3 collective-permute-start.7
  61.8 1.2 collective-permute-start.8
  63.0 0.5 collective-permute-done.20
  63.4 1.4 collective-permute-done.21
  64.8 1.7 collective-permute-done.22
  66.8 6.1 %collective-permute-start.23 = (bf16[3,4,64,512]{3,2,1,0:T(8,128)(2,1)S(1)}, bf16[3,4,64,512]{3,2,1,0:T(8,128)(2,1)S(1)}, u32[]{:S(2)}, u32[]{:S(2)}) collective-permute-start(bf16[3,4,64,512]{3,2,1,0:T(8,128)(2,1)S(1)} %pad_maximum_fusion.1.a_own), channel_id=1, source_target_pairs={{0,16},{1,17},{2,18},{3,19},{4,20},{5,21},{6,22},{7,23},{8,24},{9,... | collective-permute-start | bytes 2359304 | tf_op jit(solution)/shard_map/ppermute | solution.py:30
  72.9 0.9 collective-permute-start.10
  73.8 0.7 collective-permute-start.12
  74.5 1.6 collective-permute-done.10
  76.1 2.4 collective-permute-done.11
  78.5 0.6 collective-permute-done.12
  79.2 5.0 %collective-permute-start.13 = (bf16[256,512]{1,0:T(8,128)(2,1)S(1)}, bf16[256,512]{1,0:T(8,128)(2,1)S(1)}, u32[]{:S(2)}, u32[]{:S(2)}) collective-permute-start(bf16[256,512]{1,0:T(8,128)(2,1)S(1)} %bitcast.178), channel_id=1, source_target_pairs={{0,16},{1,17},{2,18},{3,19},{4,20},{5,21},{6,22},{7,23},{8,24},{9,... | collective-permute-start | bytes 786440 | tf_op jit(solution)/shard_map/ppermute | solution.py:30
  84.3 1.1 collective-permute-done.13.g_other
  85.4 1.9 step.1
  87.3 0.5 collective-permute-start.26
  87.8 1.3 collective-permute-start.25
  89.2 3.7 collective-permute-done.26
  92.9 1.9 collective-permute-done.25
  94.8 2.8 collective-permute-done.24
  97.7 1.1 collective-permute-start.27
  98.8 1.9 collective-permute-start.28
  100.7 0.6 collective-permute-start.29
  101.3 1.0 terms.1
  102.3 0.8 collective-permute-start.34
  103.5 1.9 collective-permute-start.35
  105.5 20.9 %collective-permute-done.34 = bf16[2,64,512]{2,1,0:T(8,128)(2,1)S(1)} collective-permute-done((bf16[2,64,512]{2,1,0:T(8,128)(2,1)S(1)}, bf16[2,64,512]{2,1,0:T(8,128)(2,1)S(1)}, u32[]{:S(2)}, u32[]{:S(2)}) %collective-permute-start.34) | collective-permute-done | bytes 131104 | tf_op jit(solution)/shard_map/ppermute | solution.py:30
  126.3 0.8 collective-permute-start.36
  127.1 0.6 fusion.52
  133.5 0.6 fusion.51
  134.2 0.9 collective-permute-start.37
  135.5 2.6 collective-permute-done.37
  138.1 4.5 %collective-permute-start.30 = (bf16[4,256,512]{2,1,0:T(8,128)(2,1)S(1)}, bf16[4,256,512]{2,1,0:T(8,128)(2,1)}, u32[]{:S(2)}, u32[]{:S(2)}) collective-permute-start(bf16[4,256,512]{2,1,0:T(8,128)(2,1)S(1)} %pad_maximum_fusion.refs_0_), channel_id=1, source_target_pairs={{0,16},{1,17},{2,18},{3,19},{4,20},{5,21},{6,22},{7,23},{8,24},{9,... | collective-permute-start | bytes 3145736 | tf_op jit(solution)/shard_map/ppermute | solution.py:30
  143.2 0.6 add_minimum_fusion
  144.4 0.6 fusion.50
  157.7 0.6 pad_add_fusion.1.where_ref
  158.5 256.3 %place.1 = bf16[16,512,512]{2,1,0:T(8,128)(2,1)} custom-call(s32[33]{0:T(128)} %pad_add_fusion.1.where_ref, bf16[4,256,512]{2,1,0:T(8,128)(2,1)} %copy-done, bf16[4,256,512]{2,1,0:T(8,128)(2,1)} %copy-done.2, bf16[4,256,512]{2,1,0:T(8,128)(2,1)} %collective-permute-done.28.refs_2_, bf16[4,256,512]{2,1,0:T(8,128)(2,1)} %collective-permute-done.29.refs_3_, ...), custom_call_target="tpu_custom_call" | custom-call | tf_op jit(solution)/shard_map/place/pallas_call | solution.py:259
  414.8 0.9 dynamic-slice_bitcast_fusion.6
  415.8 2.3 fusion.3
  (87 shorter events, 4.3 us)
Async XLA Ops:
  1.6 38.2 %collective-permute-start = (bf16[256,512]{1,0:T(8,128)(2,1)S(1)}, bf16[256,512]{1,0:T(8,128)(2,1)S(1)}, u32[]{:S(2)}, u32[]{:S(2)}) collective-permute-start(bf16[256,512]{1,0:T(8,128)(2,1)S(1)} %dynamic-slice_bitcast_fusion), channel_id=1, source_target_pairs={{0,16},{1,17},{2,18},{3,19},{4,20},{5,21},{6,22},{7,23},{8,24},{9,... | collective-permute-start | bytes 786440 | tf_op jit(solution)/shard_map/ppermute | solution.py:30
  15.6 87.5 %copy-start.3 = (s32[16]{0:T(128)S(1)}, s32[16]{0:T(128)}, u32[]{:S(2)}) copy-start(s32[16]{0:T(128)} %param.10) | copy-start | bytes 196
  15.6 28.9 %collective-permute-start.14 = (bf16[3,64,512]{2,1,0:T(8,128)(2,1)S(1)}, bf16[3,64,512]{2,1,0:T(8,128)(2,1)S(1)}, u32[]{:S(2)}, u32[]{:S(2)}) collective-permute-start(bf16[3,64,512]{2,1,0:T(8,128)(2,1)S(1)} %get-tuple-element.32), channel_id=1, source_target_pairs={{0,3},{1,0},{2,1},{3,2},{4,7},{5,4},{6,5},{7,6},{8,11},{9,8},{10,9... | collective-permute-start | bytes 589832 | tf_op jit(solution)/shard_map/ppermute | solution.py:30
  19.5 25.6 %collective-permute-start.15 = (bf16[3,64,512]{2,1,0:T(8,128)(2,1)S(1)}, bf16[3,64,512]{2,1,0:T(8,128)(2,1)S(1)}, u32[]{:S(2)}, u32[]{:S(2)}) collective-permute-start(bf16[3,64,512]{2,1,0:T(8,128)(2,1)S(1)} %get-tuple-element.31), channel_id=1, source_target_pairs={{0,2},{1,3},{2,0},{3,1},{4,6},{5,7},{6,4},{7,5},{8,10},{9,11},{10,... | collective-permute-start | bytes 589832 | tf_op jit(solution)/shard_map/ppermute | solution.py:30
  19.6 25.6 %collective-permute-start.16 = (bf16[3,64,512]{2,1,0:T(8,128)(2,1)S(1)}, bf16[3,64,512]{2,1,0:T(8,128)(2,1)S(1)}, u32[]{:S(2)}, u32[]{:S(2)}) collective-permute-start(bf16[3,64,512]{2,1,0:T(8,128)(2,1)S(1)} %get-tuple-element.30), channel_id=1, source_target_pairs={{0,1},{1,2},{2,3},{3,0},{4,5},{5,6},{6,7},{7,4},{8,9},{9,10},{10,1... | collective-permute-start | bytes 589832 | tf_op jit(solution)/shard_map/ppermute | solution.py:30
  40.9 94.3 %copy-start.4 = (s32[16]{0:T(128)S(1)}, s32[16]{0:T(128)}, u32[]{:S(2)}) copy-start(s32[16]{0:T(128)} %param.9) | copy-start | bytes 196
  40.9 7.5 %collective-permute-start.3 = (bf16[64,512]{1,0:T(8,128)(2,1)S(1)}, bf16[64,512]{1,0:T(8,128)(2,1)S(1)}, u32[]{:S(2)}, u32[]{:S(2)}) collective-permute-start(bf16[64,512]{1,0:T(8,128)(2,1)S(1)} %get-tuple-element.46), channel_id=1, source_target_pairs={{0,64},{1,65},{2,66},{3,67},{4,68},{5,69},{6,70},{7,71},{8,72},{9,... | collective-permute-start | bytes 196616 | tf_op jit(solution)/shard_map/ppermute | solution.py:30
  43.7 5.4 %collective-permute-start.2 = (bf16[64,512]{1,0:T(8,128)(2,1)S(1)}, bf16[64,512]{1,0:T(8,128)(2,1)S(1)}, u32[]{:S(2)}, u32[]{:S(2)}) collective-permute-start(bf16[64,512]{1,0:T(8,128)(2,1)S(1)} %get-tuple-element.47), channel_id=1, source_target_pairs={{0,96},{1,97},{2,98},{3,99},{4,100},{5,101},{6,102},{7,103},{8,104... | collective-permute-start | bytes 196616 | tf_op jit(solution)/shard_map/ppermute | solution.py:30
  44.6 4.5 %collective-permute-start.1 = (bf16[64,512]{1,0:T(8,128)(2,1)S(1)}, bf16[64,512]{1,0:T(8,128)(2,1)S(1)}, u32[]{:S(2)}, u32[]{:S(2)}) collective-permute-start(bf16[64,512]{1,0:T(8,128)(2,1)S(1)} %get-tuple-element.45), channel_id=1, source_target_pairs={{0,32},{1,33},{2,34},{3,35},{4,36},{5,37},{6,38},{7,39},{8,40},{9,... | collective-permute-start | bytes 196616 | tf_op jit(solution)/shard_map/ppermute | solution.py:30
  45.3 7.7 %collective-permute-start.17 = (bf16[3,64,512]{2,1,0:T(8,128)(2,1)S(1)}, bf16[3,64,512]{2,1,0:T(8,128)(2,1)S(1)}, u32[]{:S(2)}, u32[]{:S(2)}) collective-permute-start(bf16[3,64,512]{2,1,0:T(8,128)(2,1)S(1)} %get-tuple-element.23), channel_id=1, source_target_pairs={{0,12},{1,13},{2,14},{3,15},{4,0},{5,1},{6,2},{7,3},{8,4},{9,5},{1... | collective-permute-start | bytes 589832 | tf_op jit(solution)/shard_map/ppermute | solution.py:30
  48.1 6.7 %collective-permute-start.18 = (bf16[3,64,512]{2,1,0:T(8,128)(2,1)S(1)}, bf16[3,64,512]{2,1,0:T(8,128)(2,1)S(1)}, u32[]{:S(2)}, u32[]{:S(2)}) collective-permute-start(bf16[3,64,512]{2,1,0:T(8,128)(2,1)S(1)} %get-tuple-element.22), channel_id=1, source_target_pairs={{0,8},{1,9},{2,10},{3,11},{4,12},{5,13},{6,14},{7,15},{8,0},{9,1},... | collective-permute-start | bytes 589832 | tf_op jit(solution)/shard_map/ppermute | solution.py:30
  48.4 8.1 %collective-permute-start.19 = (bf16[3,64,512]{2,1,0:T(8,128)(2,1)S(1)}, bf16[3,64,512]{2,1,0:T(8,128)(2,1)S(1)}, u32[]{:S(2)}, u32[]{:S(2)}) collective-permute-start(bf16[3,64,512]{2,1,0:T(8,128)(2,1)S(1)} %get-tuple-element.21), channel_id=1, source_target_pairs={{0,4},{1,5},{2,6},{3,7},{4,8},{5,9},{6,10},{7,11},{8,12},{9,13},{1... | collective-permute-start | bytes 589832 | tf_op jit(solution)/shard_map/ppermute | solution.py:30
  49.2 9.6 %collective-permute-start.4 = (bf16[64,512]{1,0:T(8,128)(2,1)S(1)}, bf16[64,512]{1,0:T(8,128)(2,1)S(1)}, u32[]{:S(2)}, u32[]{:S(2)}) collective-permute-start(bf16[64,512]{1,0:T(8,128)(2,1)S(1)} %fusion.21), channel_id=1, source_target_pairs={{0,3},{1,0},{2,1},{3,2},{4,7},{5,4},{6,5},{7,6},{8,11},{9,8},{10,9... | collective-permute-start | bytes 196616 | tf_op jit(solution)/shard_map/ppermute | solution.py:30
  51.2 8.2 %collective-permute-start.5 = (bf16[64,512]{1,0:T(8,128)(2,1)S(1)}, bf16[64,512]{1,0:T(8,128)(2,1)S(1)}, u32[]{:S(2)}, u32[]{:S(2)}) collective-permute-start(bf16[64,512]{1,0:T(8,128)(2,1)S(1)} %fusion.21), channel_id=1, source_target_pairs={{0,2},{1,3},{2,0},{3,1},{4,6},{5,7},{6,4},{7,5},{8,10},{9,11},{10,... | collective-permute-start | bytes 196616 | tf_op jit(solution)/shard_map/ppermute | solution.py:30
  53.0 6.5 %collective-permute-start.6 = (bf16[64,512]{1,0:T(8,128)(2,1)S(1)}, bf16[64,512]{1,0:T(8,128)(2,1)S(1)}, u32[]{:S(2)}, u32[]{:S(2)}) collective-permute-start(bf16[64,512]{1,0:T(8,128)(2,1)S(1)} %fusion.21), channel_id=1, source_target_pairs={{0,1},{1,2},{2,3},{3,0},{4,5},{5,6},{6,7},{7,4},{8,9},{9,10},{10,1... | collective-permute-start | bytes 196616 | tf_op jit(solution)/shard_map/ppermute | solution.py:30
  56.6 6.9 %collective-permute-start.20 = (bf16[3,64,512]{2,1,0:T(8,128)(2,1)S(1)}, bf16[3,64,512]{2,1,0:T(8,128)(2,1)S(1)}, u32[]{:S(2)}, u32[]{:S(2)}) collective-permute-start(bf16[3,64,512]{2,1,0:T(8,128)(2,1)S(1)} %fusion.18), channel_id=1, source_target_pairs={{0,96},{1,97},{2,98},{3,99},{4,100},{5,101},{6,102},{7,103},{8,104... | collective-permute-start | bytes 589832 | tf_op jit(solution)/shard_map/ppermute | solution.py:30
  58.7 6.1 %collective-permute-start.21 = (bf16[3,64,512]{2,1,0:T(8,128)(2,1)S(1)}, bf16[3,64,512]{2,1,0:T(8,128)(2,1)S(1)}, u32[]{:S(2)}, u32[]{:S(2)}) collective-permute-start(bf16[3,64,512]{2,1,0:T(8,128)(2,1)S(1)} %fusion.18), channel_id=1, source_target_pairs={{0,64},{1,65},{2,66},{3,67},{4,68},{5,69},{6,70},{7,71},{8,72},{9,... | collective-permute-start | bytes 589832 | tf_op jit(solution)/shard_map/ppermute | solution.py:30
  58.7 7.8 %collective-permute-start.22 = (bf16[3,64,512]{2,1,0:T(8,128)(2,1)S(1)}, bf16[3,64,512]{2,1,0:T(8,128)(2,1)S(1)}, u32[]{:S(2)}, u32[]{:S(2)}) collective-permute-start(bf16[3,64,512]{2,1,0:T(8,128)(2,1)S(1)} %fusion.18), channel_id=1, source_target_pairs={{0,32},{1,33},{2,34},{3,35},{4,36},{5,37},{6,38},{7,39},{8,40},{9,... | collective-permute-start | bytes 589832 | tf_op jit(solution)/shard_map/ppermute | solution.py:30
  59.5 13.4 %collective-permute-start.7 = (bf16[64,512]{1,0:T(8,128)(2,1)S(1)}, bf16[64,512]{1,0:T(8,128)(2,1)S(1)}, u32[]{:S(2)}, u32[]{:S(2)}) collective-permute-start(bf16[64,512]{1,0:T(8,128)(2,1)S(1)} %get-tuple-element.44), channel_id=1, source_target_pairs={{0,12},{1,13},{2,14},{3,15},{4,0},{5,1},{6,2},{7,3},{8,4},{9,5},{1... | collective-permute-start | bytes 196616 | tf_op jit(solution)/shard_map/ppermute | solution.py:30
  61.8 11.1 %collective-permute-start.8 = (bf16[64,512]{1,0:T(8,128)(2,1)S(1)}, bf16[64,512]{1,0:T(8,128)(2,1)S(1)}, u32[]{:S(2)}, u32[]{:S(2)}) collective-permute-start(bf16[64,512]{1,0:T(8,128)(2,1)S(1)} %get-tuple-element.43), channel_id=1, source_target_pairs={{0,8},{1,9},{2,10},{3,11},{4,12},{5,13},{6,14},{7,15},{8,0},{9,1},... | collective-permute-start | bytes 196616 | tf_op jit(solution)/shard_map/ppermute | solution.py:30
  63.4 9.5 %collective-permute-start.9 = (bf16[64,512]{1,0:T(8,128)(2,1)S(1)}, bf16[64,512]{1,0:T(8,128)(2,1)S(1)}, u32[]{:S(2)}, u32[]{:S(2)}) collective-permute-start(bf16[64,512]{1,0:T(8,128)(2,1)S(1)} %get-tuple-element.42), channel_id=1, source_target_pairs={{0,4},{1,5},{2,6},{3,7},{4,8},{5,9},{6,10},{7,11},{8,12},{9,13},{1... | collective-permute-start | bytes 196616 | tf_op jit(solution)/shard_map/ppermute | solution.py:30
  66.8 18.6 %collective-permute-start.23 = (bf16[3,4,64,512]{3,2,1,0:T(8,128)(2,1)S(1)}, bf16[3,4,64,512]{3,2,1,0:T(8,128)(2,1)S(1)}, u32[]{:S(2)}, u32[]{:S(2)}) collective-permute-start(bf16[3,4,64,512]{3,2,1,0:T(8,128)(2,1)S(1)} %pad_maximum_fusion.1.a_own), channel_id=1, source_target_pairs={{0,16},{1,17},{2,18},{3,19},{4,20},{5,21},{6,22},{7,23},{8,24},{9,... | collective-permute-start | bytes 2359304 | tf_op jit(solution)/shard_map/ppermute | solution.py:30
  72.9 3.2 collective-permute-start.10
  73.8 4.7 %collective-permute-start.11 = (bf16[64,512]{1,0:T(8,128)(2,1)S(1)}, bf16[64,512]{1,0:T(8,128)(2,1)S(1)}, u32[]{:S(2)}, u32[]{:S(2)}) collective-permute-start(bf16[64,512]{1,0:T(8,128)(2,1)S(1)} %select_select_fusion.4), channel_id=1, source_target_pairs={{0,64},{1,65},{2,66},{3,67},{4,68},{5,69},{6,70},{7,71},{8,72},{9,... | collective-permute-start | bytes 196616 | tf_op jit(solution)/shard_map/ppermute | solution.py:30
  73.8 5.3 %collective-permute-start.12 = (bf16[64,512]{1,0:T(8,128)(2,1)S(1)}, bf16[64,512]{1,0:T(8,128)(2,1)S(1)}, u32[]{:S(2)}, u32[]{:S(2)}) collective-permute-start(bf16[64,512]{1,0:T(8,128)(2,1)S(1)} %select_select_fusion.4), channel_id=1, source_target_pairs={{0,32},{1,33},{2,34},{3,35},{4,36},{5,37},{6,38},{7,39},{8,40},{9,... | collective-permute-start | bytes 196616 | tf_op jit(solution)/shard_map/ppermute | solution.py:30
  79.2 6.2 %collective-permute-start.13 = (bf16[256,512]{1,0:T(8,128)(2,1)S(1)}, bf16[256,512]{1,0:T(8,128)(2,1)S(1)}, u32[]{:S(2)}, u32[]{:S(2)}) collective-permute-start(bf16[256,512]{1,0:T(8,128)(2,1)S(1)} %bitcast.178), channel_id=1, source_target_pairs={{0,16},{1,17},{2,18},{3,19},{4,20},{5,21},{6,22},{7,23},{8,24},{9,... | collective-permute-start | bytes 786440 | tf_op jit(solution)/shard_map/ppermute | solution.py:30
  87.3 5.6 %collective-permute-start.26 = (bf16[256,512]{1,0:T(8,128)(2,1)S(1)}, bf16[256,512]{1,0:T(8,128)(2,1)S(1)}, u32[]{:S(2)}, u32[]{:S(2)}) collective-permute-start(bf16[256,512]{1,0:T(8,128)(2,1)S(1)} %constant_dynamic-slice_fusion), channel_id=1, source_target_pairs={{0,3},{1,0},{2,1},{3,2},{4,7},{5,4},{6,5},{7,6},{8,11},{9,8},{10,9... | collective-permute-start | bytes 786440 | tf_op jit(solution)/shard_map/ppermute | solution.py:30
  87.8 7.1 %collective-permute-start.25 = (bf16[256,512]{1,0:T(8,128)(2,1)S(1)}, bf16[256,512]{1,0:T(8,128)(2,1)S(1)}, u32[]{:S(2)}, u32[]{:S(2)}) collective-permute-start(bf16[256,512]{1,0:T(8,128)(2,1)S(1)} %constant_dynamic-slice_fusion), channel_id=1, source_target_pairs={{0,2},{1,3},{2,0},{3,1},{4,6},{5,7},{6,4},{7,5},{8,10},{9,11},{10,... | collective-permute-start | bytes 786440 | tf_op jit(solution)/shard_map/ppermute | solution.py:30
  89.0 8.6 %collective-permute-start.24 = (bf16[256,512]{1,0:T(8,128)(2,1)S(1)}, bf16[256,512]{1,0:T(8,128)(2,1)S(1)}, u32[]{:S(2)}, u32[]{:S(2)}) collective-permute-start(bf16[256,512]{1,0:T(8,128)(2,1)S(1)} %constant_dynamic-slice_fusion), channel_id=1, source_target_pairs={{0,1},{1,2},{2,3},{3,0},{4,5},{5,6},{6,7},{7,4},{8,9},{9,10},{10,1... | collective-permute-start | bytes 786440 | tf_op jit(solution)/shard_map/ppermute | solution.py:30
  97.7 60.7 %copy-start = (bf16[4,256,512]{2,1,0:T(8,128)(2,1)}, bf16[4,256,512]{2,1,0:T(8,128)(2,1)S(1)}, u32[]{:S(2)}) copy-start(bf16[4,256,512]{2,1,0:T(8,128)(2,1)S(1)} %pad_maximum_fusion.refs_0_) | copy-start | bytes 3145732
  97.7 44.8 %collective-permute-start.27 = (bf16[4,256,512]{2,1,0:T(8,128)(2,1)S(1)}, bf16[4,256,512]{2,1,0:T(8,128)(2,1)S(1)}, u32[]{:S(2)}, u32[]{:S(2)}) collective-permute-start(bf16[4,256,512]{2,1,0:T(8,128)(2,1)S(1)} %pad_maximum_fusion.refs_0_), channel_id=1, source_target_pairs={{0,4},{1,5},{2,6},{3,7},{4,8},{5,9},{6,10},{7,11},{8,12},{9,13},{1... | collective-permute-start | bytes 3145736 | tf_op jit(solution)/shard_map/ppermute | solution.py:30
  98.8 43.8 %collective-permute-start.28 = (bf16[4,256,512]{2,1,0:T(8,128)(2,1)S(1)}, bf16[4,256,512]{2,1,0:T(8,128)(2,1)}, u32[]{:S(2)}, u32[]{:S(2)}) collective-permute-start(bf16[4,256,512]{2,1,0:T(8,128)(2,1)S(1)} %pad_maximum_fusion.refs_0_), channel_id=1, source_target_pairs={{0,8},{1,9},{2,10},{3,11},{4,12},{5,13},{6,14},{7,15},{8,0},{9,1},... | collective-permute-start | bytes 3145736 | tf_op jit(solution)/shard_map/ppermute | solution.py:30
  100.7 42.4 %collective-permute-start.29 = (bf16[4,256,512]{2,1,0:T(8,128)(2,1)S(1)}, bf16[4,256,512]{2,1,0:T(8,128)(2,1)}, u32[]{:S(2)}, u32[]{:S(2)}) collective-permute-start(bf16[4,256,512]{2,1,0:T(8,128)(2,1)S(1)} %pad_maximum_fusion.refs_0_), channel_id=1, source_target_pairs={{0,12},{1,13},{2,14},{3,15},{4,0},{5,1},{6,2},{7,3},{8,4},{9,5},{1... | collective-permute-start | bytes 3145736 | tf_op jit(solution)/shard_map/ppermute | solution.py:30
  102.3 24.0 %collective-permute-start.34 = (bf16[2,64,512]{2,1,0:T(8,128)(2,1)S(1)}, bf16[2,64,512]{2,1,0:T(8,128)(2,1)S(1)}, u32[]{:S(2)}, u32[]{:S(2)}) collective-permute-start(bf16[2,64,512]{2,1,0:T(8,128)(2,1)S(1)} %terms.1), channel_id=1, source_target_pairs={{0,12},{1,13},{2,14},{3,15},{4,0},{5,1},{6,2},{7,3},{8,4},{9,5},{1... | collective-permute-start | bytes 393224 | tf_op jit(solution)/shard_map/ppermute | solution.py:30
  103.5 30.6 %collective-permute-start.35 = (bf16[2,64,512]{2,1,0:T(8,128)(2,1)S(1)}, bf16[2,64,512]{2,1,0:T(8,128)(2,1)S(1)}, u32[]{:S(2)}, u32[]{:S(2)}) collective-permute-start(bf16[2,64,512]{2,1,0:T(8,128)(2,1)S(1)} %terms.1), channel_id=1, source_target_pairs={{0,8},{1,9},{2,10},{3,11},{4,12},{5,13},{6,14},{7,15},{8,0},{9,1},... | collective-permute-start | bytes 393224 | tf_op jit(solution)/shard_map/ppermute | solution.py:30
  126.3 7.8 %collective-permute-start.36 = (bf16[2,64,512]{2,1,0:T(8,128)(2,1)S(1)}, bf16[2,64,512]{2,1,0:T(8,128)(2,1)S(1)}, u32[]{:S(2)}, u32[]{:S(2)}) collective-permute-start(bf16[2,64,512]{2,1,0:T(8,128)(2,1)S(1)} %terms.1), channel_id=1, source_target_pairs={{0,4},{1,5},{2,6},{3,7},{4,8},{5,9},{6,10},{7,11},{8,12},{9,13},{1... | collective-permute-start | bytes 393224 | tf_op jit(solution)/shard_map/ppermute | solution.py:30
  134.2 3.9 collective-permute-start.37
  135.2 8.8 %collective-permute-start.38 = (bf16[2,64,512]{2,1,0:T(8,128)(2,1)S(1)}, bf16[2,64,512]{2,1,0:T(8,128)(2,1)S(1)}, u32[]{:S(2)}, u32[]{:S(2)}) collective-permute-start(bf16[2,64,512]{2,1,0:T(8,128)(2,1)S(1)} %get-tuple-element.36), channel_id=1, source_target_pairs={{0,2},{1,3},{2,0},{3,1},{4,6},{5,7},{6,4},{7,5},{8,10},{9,11},{10,... | collective-permute-start | bytes 393224 | tf_op jit(solution)/shard_map/ppermute | solution.py:30
  138.1 20.4 %collective-permute-start.30 = (bf16[4,256,512]{2,1,0:T(8,128)(2,1)S(1)}, bf16[4,256,512]{2,1,0:T(8,128)(2,1)}, u32[]{:S(2)}, u32[]{:S(2)}) collective-permute-start(bf16[4,256,512]{2,1,0:T(8,128)(2,1)S(1)} %pad_maximum_fusion.refs_0_), channel_id=1, source_target_pairs={{0,16},{1,17},{2,18},{3,19},{4,20},{5,21},{6,22},{7,23},{8,24},{9,... | collective-permute-start | bytes 3145736 | tf_op jit(solution)/shard_map/ppermute | solution.py:30
  142.6 15.9 %copy-start.2 = (bf16[4,256,512]{2,1,0:T(8,128)(2,1)}, bf16[4,256,512]{2,1,0:T(8,128)(2,1)S(1)}, u32[]{:S(2)}) copy-start(bf16[4,256,512]{2,1,0:T(8,128)(2,1)S(1)} %collective-permute-done.27.refs_1_) | copy-start | bytes 3145732
  142.6 15.9 %collective-permute-start.31 = (bf16[4,256,512]{2,1,0:T(8,128)(2,1)S(1)}, bf16[4,256,512]{2,1,0:T(8,128)(2,1)}, u32[]{:S(2)}, u32[]{:S(2)}) collective-permute-start(bf16[4,256,512]{2,1,0:T(8,128)(2,1)S(1)} %collective-permute-done.27.refs_1_), channel_id=1, source_target_pairs={{0,16},{1,17},{2,18},{3,19},{4,20},{5,21},{6,22},{7,23},{8,24},{9,... | collective-permute-start | bytes 3145736 | tf_op jit(solution)/shard_map/ppermute | solution.py:30
  142.7 15.8 %collective-permute-start.32 = (bf16[4,256,512]{2,1,0:T(8,128)(2,1)}, bf16[4,256,512]{2,1,0:T(8,128)(2,1)}, u32[]{:S(2)}, u32[]{:S(2)}) collective-permute-start(bf16[4,256,512]{2,1,0:T(8,128)(2,1)} %collective-permute-done.28.refs_2_), channel_id=1, source_target_pairs={{0,16},{1,17},{2,18},{3,19},{4,20},{5,21},{6,22},{7,23},{8,24},{9,... | collective-permute-start | bytes 3145736 | tf_op jit(solution)/shard_map/ppermute | solution.py:30
  143.1 15.4 %collective-permute-start.33 = (bf16[4,256,512]{2,1,0:T(8,128)(2,1)}, bf16[4,256,512]{2,1,0:T(8,128)(2,1)}, u32[]{:S(2)}, u32[]{:S(2)}) collective-permute-start(bf16[4,256,512]{2,1,0:T(8,128)(2,1)} %collective-permute-done.29.refs_3_), channel_id=1, source_target_pairs={{0,16},{1,17},{2,18},{3,19},{4,20},{5,21},{6,22},{7,23},{8,24},{9,... | collective-permute-start | bytes 3145736 | tf_op jit(solution)/shard_map/ppermute | solution.py:30
  144.0 14.2 %collective-permute-start.39 = (bf16[2,64,512]{2,1,0:T(8,128)(2,1)S(1)}, bf16[2,64,512]{2,1,0:T(8,128)(2,1)S(1)}, u32[]{:S(2)}, u32[]{:S(2)}) collective-permute-start(bf16[2,64,512]{2,1,0:T(8,128)(2,1)S(1)} %get-tuple-element.35), channel_id=1, source_target_pairs={{0,1},{1,2},{2,3},{3,0},{4,5},{5,6},{6,7},{7,4},{8,9},{9,10},{10,1... | collective-permute-start | bytes 393224 | tf_op jit(solution)/shard_map/ppermute | solution.py:30
  158.4 257.3 %copy-start.1 = (f32[1,3,64,512]{3,2,1,0:T(8,128)S(1)}, f32[1,3,64,512]{3,2,1,0:T(8,128)}, u32[]{:S(2)}) copy-start(f32[1,3,64,512]{3,2,1,0:T(8,128)} %param.15) | copy-start | bytes 1179652

commit v2 on v0

v2 whole, which is shorter than its diff:
```python
import functools

import jax
import jax.numpy as jnp
from jax import lax
from jax.experimental import pallas as pl
from jax.experimental.pallas import tpu as pltpu
from jax.sharding import PartitionSpec as P

decay_stats = 0.95
decay_moment = 0.9
epsilon = 1e-06

AXES = ("dp", "group")
X, CORES, SIDE, SLOTS = 4, 2, 4, 3
BLOCKS = SIDE * SIDE
BS = 512
ROWS = BS // (X * CORES)
HALF = BS // CORES
NEAR = SIDE * HALF
half_type = jnp.bfloat16
wide_type = jnp.float32

SMEM = pl.BlockSpec(memory_space=pltpu.SMEM)
VMEM = pl.BlockSpec(memory_space=pltpu.VMEM)
ANY = pl.BlockSpec(memory_space=pl.ANY)

GRAD_PICK, GRAD_LAST, ROOT_PICK, ROOT_LAST = 0, 4, 5, 9
SLOT_PICK, TERM_PICK, TERM_LAST, SLOT_LIVE, SLOT_BLOCK, LANDING = 10, 14, 18, 21, 24, 27
CHOICES = LANDING + 32


def permute(value, target):
    pairs = []
    for x in range(X):
        for c in range(CORES):
            for z in range(SIDE):
                for y in range(SIDE):
                    tx, tc, tz, ty = target(x, c, z, y)
                    pairs.append(
                        ((x * 2 + c) * 16 + z * 4 + y, ((tx % 4) * 2 + tc) * 16 + (tz % 4) * 4 + ty % 4)
                    )
    return lax.ppermute(value, AXES, pairs)


def to_core(value):
    return permute(value, lambda x, c, z, y: (x, 1 - c, z, y))


def to_x(value, k):
    return permute(value, lambda x, c, z, y: (x + k, c, z, y))


def to_u(value, k):
    return permute(value, lambda x, c, z, y: (x, c, z, y + k) if c == 0 else (x, c, z + k, y))


def to_v(value, k):
    return permute(value, lambda x, c, z, y: (x, c, z + k, y) if c == 0 else (x, c, z, y + k))


def along(send, values):
    got = [values[0], None, None, None]
    for k in (1, 3, 2):
        got[k] = send(values[k], k)
    return got


def position():
    dp, me = lax.axis_index("dp"), lax.axis_index("group")
    return dp >> 1, dp & 1, me >> 2, me & 3


def choice_kernel(order_ref, count_ref, out, start_ref, owner_ref):
    x, c, z, y = position()
    me = z * 4 + y
    first = c == 0
    u, v = jnp.where(first, y, z), jnp.where(first, z, y)

    def place_at(uu, vv):
        yy, zz = jnp.where(first, uu, vv), jnp.where(first, vv, uu)
        return 4 * ((zz - yy) & 3) + yy

    def uv_of_member(g):
        yy, zz = g & 3, g >> 2
        return jnp.where(first, yy, zz), jnp.where(first, zz, yy)

    def uv_of_place(q):
        yy = q & 3
        zz = (yy + (q >> 2)) & 3
        return jnp.where(first, yy, zz), jnp.where(first, zz, yy)

    place = jnp.int32(0)
    for o in range(BLOCKS):
        start_ref[o] = place
        for s in range(SLOTS):

            @pl.when(s < count_ref[o])
            def _():
                owner_ref[start_ref[o] + s] = o

        place = place + count_ref[o]

    for k in range(4):
        q = place_at(u, (v + k) & 3)
        block = order_ref[q]
        bu, bv = uv_of_member(block)
        out[GRAD_PICK + k] = (u - bu) & 3
        ou, ov = uv_of_member(owner_ref[q])
        out[ROOT_PICK + k] = (u - ou) & 3
        if k == 0:
            out[GRAD_LAST] = (v - bv) & 3
            out[ROOT_LAST] = (v - ov) & 3
    my_start, my_count = start_ref[me], count_ref[me]
    slot_u = []
    for s in range(SLOTS):
        q = jnp.minimum(my_start + s, BLOCKS - 1)
        su, sv = uv_of_place(q)
        slot_u.append(su)
        out[TERM_LAST + s] = (v - sv) & 3
        out[SLOT_LIVE + s] = (s < my_count).astype(jnp.int32)
        out[SLOT_BLOCK + s] = order_ref[q]
    for k in range(4):
        far = (u + k) & 3
        chosen = jnp.int32(0)
        for s in range(SLOTS):
            chosen = jnp.where((s < my_count) & (slot_u[s] == far), s, chosen)
        out[SLOT_PICK + k] = chosen
        far = (v + k) & 3
        member = jnp.where(first, 4 * far + u, 4 * u + far)
        chosen = jnp.int32(0)
        for s in range(SLOTS):
            fu, fv = uv_of_place(start_ref[member] + s)
            chosen = jnp.where((s < count_ref[member]) & (fv == v), (u - fu) & 3, chosen)
        out[TERM_PICK + k] = chosen
    for k in range(4):
        for j in range(4):
            out[LANDING + k * 4 + j] = order_ref[place_at((u - j) & 3, (v - k) & 3)]
            out[LANDING + 16 + k * 4 + j] = order_ref[place_at((u - k) & 3, (v - j) & 3)]


def choices(block_order, owner_count):
    return pl.pallas_call(
        choice_kernel,
        out_shape=jax.ShapeDtypeStruct((CHOICES,), jnp.int32),
        in_specs=[SMEM, SMEM],
        out_specs=SMEM,
        scratch_shapes=[pltpu.SMEM((BLOCKS,), jnp.int32), pltpu.SMEM((BLOCKS,), jnp.int32)],
        name="choices",
    )(block_order, owner_count)


def cost(flops, *arrays):
    moved = sum(a.size * a.dtype.itemsize for a in arrays)
    return pl.CostEstimate(flops=flops, bytes_accessed=moved, transcendentals=0)


def small_call(body, outs, name, *args, aliases=None, flops=0, scratch=()):
    return pl.pallas_call(
        body,
        out_shape=outs,
        in_specs=[SMEM if a.dtype == jnp.int32 else VMEM for a in args],
        out_specs=jax.tree.map(lambda _: VMEM, outs),
        scratch_shapes=scratch,
        input_output_aliases=aliases or {},
        compiler_params=pltpu.CompilerParams(vmem_limit_bytes=12 << 20),
        cost_estimate=cost(flops, *args, *jax.tree.leaves(outs)),
        name=name,
    )(*args)


def copy_chosen(index, options, out, at):
    for n, option in enumerate(options):

        @pl.when(index == n)
        def _():
            out[...] = option[at]


def pair_kernel(mine, theirs, own, *sends):
    x, c, _, _ = position()
    for k in range(4):
        at = pl.ds(pl.multiple_of(c * HALF + ((x + k) & 3) * ROWS, ROWS), ROWS)
        both = mine[at, :].astype(wide_type) + theirs[at, :].astype(wide_type)
        if k == 0:
            own[...] = both
        else:
            sends[k - 1][...] = both.astype(half_type)


def pack_kernel(spot, left, right, moment, *outs):
    for k, out in enumerate(outs):
        slot = spot[SLOT_PICK + k]
        out[0] = left[slot].astype(half_type)
        out[1] = right[slot].astype(half_type)
        out[2] = moment[slot].astype(half_type)


def total_kernel(own, a, b, c, *packs):
    total = own[...] + a[...].astype(wide_type)
    total = total + b[...].astype(wide_type)
    total = (total + c[...].astype(wide_type)).astype(half_type)
    for out in packs[4:]:
        out[3] = total


def turn_kernel(spot, a, b, c, d, *outs):
    for k, out in enumerate(outs):
        copy_chosen(spot[ROOT_PICK + k], (a, b, c, d), out.at[:3], pl.ds(0, 3))
        copy_chosen(spot[GRAD_PICK + k], (a, b, c, d), out.at[3:], pl.ds(3, 1))


def here_kernel(spot, a, b, c, d, out):
    copy_chosen(spot[ROOT_LAST], (a, b, c, d), out.at[:3], pl.ds(0, 3))
    copy_chosen(spot[GRAD_LAST], (a, b, c, d), out.at[3:], pl.ds(3, 1))


def line_kernel(*refs):
    out = refs[4]
    x = position()[0]
    for k in range(4):
        out[(x - k) & 3] = refs[k][...]


def line_up(got, name):
    shape = jax.ShapeDtypeStruct((4,) + got[0].shape, got[0].dtype)
    return small_call(line_kernel, shape, name, *got)


def step_kernel(mine, other, out, grad, full, held):
    x, c, _, _ = position()
    for n in range(X):
        for core, source in ((c, mine), (1 - c, other)):
            rows = pl.ds(pl.multiple_of((2 * n + core) * ROWS, ROWS), ROWS)
            for which in range(3):
                full[which, rows, :] = source[n, which]
            grad[pl.ds(pl.multiple_of(core * HALF + n * ROWS, ROWS), ROWS), :] = source[n, 3]
    g = grad[...]
    wide = g.astype(wide_type)
    grad_square = jnp.sum(wide * wide)
    precond = jnp.dot(full[0], g, preferred_element_type=wide_type).astype(half_type)
    held[...] = jnp.dot(precond, full[1], preferred_element_type=wide_type)
    dir_square = jnp.sum(held[...] * held[...])
    entries = float(BS * BS)
    top = jnp.sqrt(jnp.full((1, BS), grad_square / entries, wide_type))
    graft = top / jnp.sqrt(jnp.full((1, BS), dir_square / entries + epsilon, wide_type))
    half = pl.ds(pl.multiple_of(c * HALF, HALF), HALF)
    fresh = decay_moment * full[2, half, :].astype(wide_type) + graft * held[half, :]
    out[:HALF, :] = fresh.astype(half_type)
    rows = grad[pl.ds(pl.multiple_of((2 * x + c) * ROWS, ROWS), ROWS), :]
    out[HALF : HALF + ROWS, :] = lax.dot_general(
        rows, g, (((1,), (1,)), ((), ())), preferred_element_type=wide_type
    ).astype(half_type)
    columns = grad[:, pl.ds(pl.multiple_of(x * 2 * ROWS, 2 * ROWS), 2 * ROWS)]
    held[: 2 * ROWS, :] = lax.dot_general(
        columns, g, (((0,), (0,)), ((), ())), preferred_element_type=wide_type
    )
    term = held[pl.ds(pl.multiple_of(c * ROWS, ROWS), ROWS), :]
    out[HALF + ROWS :, :] = term.astype(half_type)


def near_kernel(spot, a, b, c, d, *outs):
    for k, out in enumerate(outs):
        for j, source in enumerate((a, b, c, d)):
            out[j * HALF : (j + 1) * HALF, :] = source[:HALF, :]
        copy_chosen(spot[TERM_PICK + k], (a, b, c, d), out.at[NEAR:], pl.ds(HALF, 2 * ROWS))


def placed_copies(spot, sources, out, sems):
    _, c, _, _ = position()
    copies = []
    for n, (which, source) in enumerate(sources):
        half = c if which < 4 else 1 - c
        for j in range(4):
            copies.append(
                pltpu.make_async_copy(
                    source.at[pl.ds(j * HALF, HALF), :],
                    out.at[
                        spot[LANDING + which * 4 + j],
                        pl.ds(pl.multiple_of(half * HALF, HALF), HALF),
                        :,
                    ],
                    sems.at[n * 4 + j],
                )
            )
    return copies


def place_kernel(which, spot, *refs):
    mine, other, out, sems = refs[-4:]
    copies = placed_copies(spot, ((which, mine), (which + 4, other)), out, sems)
    for copy in copies:
        copy.start()
    for copy in copies:
        copy.wait()


def place(which, spot, begun, mine, other):
    given = [mine, other] if begun is None else [begun, mine, other]
    out = jax.ShapeDtypeStruct((BLOCKS, BS, BS), half_type)
    return pl.pallas_call(
        functools.partial(place_kernel, which),
        out_shape=out,
        in_specs=[SMEM] + [ANY] * (len(given) - 2) + [VMEM] * 2,
        out_specs=ANY,
        scratch_shapes=[pltpu.SemaphoreType.DMA((8,))],
        input_output_aliases={} if begun is None else {1: 0},
        compiler_params=pltpu.CompilerParams(vmem_limit_bytes=4 << 20),
        cost_estimate=cost(0, mine, other, mine, other),
        name="place",
    )(spot, *given)


def finish_kernel(spot, begun, moment, *refs):
    del begun
    sources, (out, out_moment, sems) = refs[:8], refs[8:]
    copies = placed_copies(
        spot, [(n, sources[n]) for n in (3, 2, 7, 6)], out, sems
    )
    for copy in copies:
        copy.start()
    x, c, _, _ = position()
    row = (2 * x + c) * ROWS
    in_half = row & (HALF - 1)
    for s in range(SLOTS):
        live = spot[SLOT_LIVE + s] == 1
        block = spot[SLOT_BLOCK + s]
        out_moment[s] = moment[s]
        for n, source in enumerate(sources):
            half = c if n < 4 else 1 - c
            for j in range(4):

                @pl.when(live & (spot[LANDING + n * 4 + j] == block) & ((row >> 8) == half))
                def _():
                    at = pl.ds(pl.multiple_of(j * HALF + in_half, ROWS), ROWS)
                    out_moment[s] = source[at, :].astype(wide_type)

    for copy in copies:
        copy.wait()


def stats_kernel(spot, left, right, *refs):
    sources, outs = refs[:4], refs[4:]
    for s in range(SLOTS):
        for old, out in zip((left, right), outs):
            out[s] = old[s]
        for n, source in enumerate(sources):

            @pl.when((spot[SLOT_LIVE + s] == 1) & (spot[TERM_LAST + s] == n))
            def _():
                for i, (old, out) in enumerate(zip((left, right), outs)):
                    at = pl.ds(NEAR + i * ROWS, ROWS)
                    term = source[at, :].astype(wide_type)
                    out[s] = decay_stats * old[s] + (1.0 - decay_stats) * term


def local(
    gradients, block_order, owner_count, stat_left, stat_right, root_left, root_right, momentum
):
    chunk_type = jax.ShapeDtypeStruct((ROWS, BS), half_type)
    pack_type = jax.ShapeDtypeStruct((4, ROWS, BS), half_type)
    stat_type = jax.ShapeDtypeStruct((SLOTS, ROWS, BS), wide_type)
    spot = choices(block_order, owner_count)
    hold = lax.optimization_barrier

    mine = gradients[0, 0]
    own, *sends = small_call(
        pair_kernel,
        [jax.ShapeDtypeStruct((ROWS, BS), wide_type)] + [chunk_type] * 3,
        "pair",
        mine,
        to_core(mine),
    )
    sends, left, right, moment = hold((sends, root_left[0], root_right[0], momentum[0]))
    packs = small_call(pack_kernel, [pack_type] * 4, "packs", spot, left, right, moment)
    got = along(to_x, [own] + sends)

    packs = small_call(
        total_kernel, [pack_type] * 4, "total", *got, *packs, aliases={4: 0, 5: 1, 6: 2, 7: 3}
    )
    row = along(to_u, packs)
    column = along(to_v, small_call(turn_kernel, [pack_type] * 4, "turn", spot, *row))
    pack = small_call(here_kernel, pack_type, "here", spot, *column)
    full = line_up(along(to_x, [pack] * 4), "line")
    send = small_call(
        step_kernel,
        jax.ShapeDtypeStruct((HALF + 2 * ROWS, BS), half_type),
        "step",
        full,
        to_core(full),
        flops=6 * BS**3,
        scratch=[
            pltpu.VMEM((BS, BS), half_type),
            pltpu.VMEM((3, BS, BS), half_type),
            pltpu.VMEM((BS, BS), wide_type),
        ],
    )

    row = along(to_u, [send] * 4)
    near_type = jax.ShapeDtypeStruct((NEAR + 2 * ROWS, BS), half_type)
    nears = small_call(near_kernel, [near_type] * 4, "near", spot, *row)
    held = along(to_v, nears)
    across = [to_core(value) for value in held]
    begun = place(0, spot, None, held[0], across[0])
    begun = place(1, spot, begun, held[1], across[1])
    left_stats, right_stats = small_call(
        stats_kernel, [stat_type] * 2, "stats", spot, stat_left[0], stat_right[0], *held
    )
    update_blocks, new_momentum = pl.pallas_call(
        finish_kernel,
        out_shape=[jax.ShapeDtypeStruct((BLOCKS, BS, BS), half_type), stat_type],
        in_specs=[SMEM, ANY] + [VMEM] * 9,
        out_specs=[ANY, VMEM],
        scratch_shapes=[pltpu.SemaphoreType.DMA((16,))],
        input_output_aliases={1: 0},
        compiler_params=pltpu.CompilerParams(vmem_limit_bytes=16 << 20),
        cost_estimate=cost(0, *held, *held),
        name="finish",
    )(spot, begun, momentum[0], *held, *across)
    return (update_blocks, left_stats[None], right_stats[None], new_momentum[None])


def solution(mesh):
    placed = (
        P("dp", "group", None, None),
        P(),
        P(),
        P("group", None, "dp", None),
        P("group", None, "dp", None),
        P("group", None, "dp", None),
        P("group", None, "dp", None),
        P("group", None, "dp", None),
    )
    return jax.shard_map(
        local,
        mesh=mesh,
        in_specs=placed,
        out_specs=(
            P(),
            P("group", None, "dp", None),
            P("group", None, "dp", None),
            P("group", None, "dp", None),
        ),
        check_vma=False,
    )
```

time: 304 us -> 113 us (0.37)
  waiting for transfers between devices: 250 us -> 55.4 us
  starting transfers between devices: 0.2 us -> 39.2 us
  Pallas kernels: 0 us -> 14.6 us
  local copies, waits for them, and re-layouts: 16.8 us -> 2.71 us
  between operations: 13.9 us -> 0.83 us
  blocking collectives: 12.1 us -> 0 us
  other arithmetic: 5.46 us -> 0 us
  matrix products: 4.86 us -> 0 us
    all_gather x4 -> x0, waiting for transfers between devices: 185 us -> none  [the longest x1 69.6 us: local(): every_block = lax.all_gather(summed[None], 'group', axis=0, tiled=True)]
    psum x1 -> x0, waiting for transfers between devices: 64.2 us -> none  [local(): summed = lax.psum(own_term.astype(jnp.bfloat16), 'dp')]
    ppermute x0 -> x24, waiting for transfers between devices: none -> 55.4 us  [permute(): return lax.ppermute(value, AXES, pairs)]
    ppermute x0 -> x24, starting transfers between devices: none -> 39.2 us  [permute(): return lax.ppermute(value, AXES, pairs)]
    pallas_call x0 -> x13, Pallas kernels: none -> 14.6 us  [the longest x9 5.93 us: small_call(): pl.pallas_call(body, out_shape=outs, in_specs=[SMEM if a.dtype == jnp.int...]
    psum x1 -> x0, blocking collectives: 12.1 us -> none  [local(): lax.psum((jnp.sum(direction * direction, axis=(1, 2)), jnp.sum(grad_wide...]
    gather x5 -> x0, local copies, waits for them, and re-layouts: 8.04 us -> none  [the longest x1 4.03 us: local(): jnp.take(every_block, my_blocks, axis=0)]
    unnamed x17 -> x16, local copies, waits for them, and re-layouts: 8.05 us -> 2.71 us
  transfers between devices with their start and end apart: 5 -> 24, of which waited for: 5 -> 12; matrix products, arithmetic and copies ran while one was open for 4% -> 0% of each run, Pallas kernels for 0% -> 7%
where the time goes in v2:
time: 113 us
  waiting for transfers between devices  55.4 us (49%)
  starting transfers between devices  39.2 us (35%)
  Pallas kernels  14.6 us (13%)
  local copies, waits for them, and re-layouts  2.71 us (2%)
    ppermute x24, waiting for transfers between devices, permute(): return lax.ppermute(value, AXES, pairs)  55.4 us
    ppermute x24, starting transfers between devices, permute(): return lax.ppermute(value, AXES, pairs)  39.2 us
    pallas_call x9, Pallas kernels, small_call(): pl.pallas_call(body, out_shape=outs, in_specs=[SMEM if a.dtype == jnp.int...  5.93 us
    pallas_call x2, Pallas kernels, place(): pl.pallas_call(functools.partial(place_kernel, which), out_shape=out, in_...  3.85 us
    pallas_call x1, Pallas kernels, local(): pl.pallas_call(finish_kernel, out_shape=[jax.ShapeDtypeStruct((BLOCKS, BS...  3.44 us
    unnamed x16, local copies, waits for them, and re-layouts  2.71 us
  transfers between devices with their start and end apart: 24, of which 12 were waited for; matrix products, arithmetic and copies ran while one was open for 0% of the time, Pallas kernels for 7%

profile of v2, /device:TPU:1, one launch (start us, length us, event | category | flops | bytes accessed | tf_op | source)
XLA Modules:
  0.0 112.7 jit_solution(10310781030371324487)
XLA Ops:
  0.6 1.5 %collective-permute-start = (bf16[512,512]{1,0:T(8,128)(2,1)}, bf16[512,512]{1,0:T(8,128)(2,1)S(1)}, u32[]{:S(2)}, u32[]{:S(2)}) collective-permute-start(bf16[512,512]{1,0:T(8,128)(2,1)} %bitcast.11), channel_id=1, source_target_pairs={{0,16},{1,17},{2,18},{3,19},{4,20},{5,21},{6,22},{7,23},{8,24},{9,... | collective-permute-start | bytes 1572872 | tf_op jit(solution)/shard_map/ppermute | solution.py:43
  2.1 1.7 %collective-permute-done.theirs = bf16[512,512]{1,0:T(8,128)(2,1)S(1)} collective-permute-done((bf16[512,512]{1,0:T(8,128)(2,1)}, bf16[512,512]{1,0:T(8,128)(2,1)S(1)}, u32[]{:S(2)}, u32[]{:S(2)}) %collective-permute-start) | collective-permute-done | bytes 524320 | tf_op jit(solution)/shard_map/ppermute | solution.py:43
  3.9 1.0 copy-done.1
  4.9 0.1 pair.1
  5.0 1.4 %collective-permute-start.1 = (bf16[64,512]{1,0:T(8,128)(2,1)S(1)}, bf16[64,512]{1,0:T(8,128)(2,1)S(1)}, u32[]{:S(2)}, u32[]{:S(2)}) collective-permute-start(bf16[64,512]{1,0:T(8,128)(2,1)S(1)} %get-tuple-element.38), channel_id=1, source_target_pairs={{0,32},{1,33},{2,34},{3,35},{4,36},{5,37},{6,38},{7,39},{8,40},{9,... | collective-permute-start | bytes 196616 | tf_op jit(solution)/shard_map/ppermute | solution.py:43
  6.4 2.5 %collective-permute-start.2 = (bf16[64,512]{1,0:T(8,128)(2,1)S(1)}, bf16[64,512]{1,0:T(8,128)(2,1)S(1)}, u32[]{:S(2)}, u32[]{:S(2)}) collective-permute-start(bf16[64,512]{1,0:T(8,128)(2,1)S(1)} %get-tuple-element.39), channel_id=1, source_target_pairs={{0,64},{1,65},{2,66},{3,67},{4,68},{5,69},{6,70},{7,71},{8,72},{9,... | collective-permute-start | bytes 196616 | tf_op jit(solution)/shard_map/ppermute | solution.py:43
  8.8 1.2 %collective-permute-start.3 = (bf16[64,512]{1,0:T(8,128)(2,1)S(1)}, bf16[64,512]{1,0:T(8,128)(2,1)S(1)}, u32[]{:S(2)}, u32[]{:S(2)}) collective-permute-start(bf16[64,512]{1,0:T(8,128)(2,1)S(1)} %get-tuple-element.40), channel_id=1, source_target_pairs={{0,96},{1,97},{2,98},{3,99},{4,100},{5,101},{6,102},{7,103},{8,104... | collective-permute-start | bytes 196616 | tf_op jit(solution)/shard_map/ppermute | solution.py:43
  10.0 1.4 %choices.1.spot = s32[59]{0:T(128)} custom-call(s32[16]{0:T(128)} %order_ref.1, s32[16]{0:T(128)} %count_ref.1), custom_call_target="tpu_custom_call" | custom-call | tf_op jit(solution)/shard_map/choices/pallas_call | solution.py:143
  11.4 0.0 copy-start.5
  11.4 1.0 copy-done.5
  12.4 0.7 copy-done.6
  13.1 0.6 packs.1
  13.7 0.0 collective-permute-done.1.a
  13.7 0.0 collective-permute-done.2.b
  13.7 0.0 collective-permute-done.3.c
  13.8 1.7 %collective-permute-start.4 = (bf16[4,64,512]{2,1,0:T(8,128)(2,1)S(1)}, bf16[4,64,512]{2,1,0:T(8,128)(2,1)S(1)}, u32[]{:S(2)}, u32[]{:S(2)}) collective-permute-start(bf16[4,64,512]{2,1,0:T(8,128)(2,1)S(1)} %get-tuple-element.49), channel_id=1, source_target_pairs={{0,1},{1,2},{2,3},{3,0},{4,5},{5,6},{6,7},{7,4},{8,9},{9,10},{10,1... | collective-permute-start | bytes 786440 | tf_op jit(solution)/shard_map/ppermute | solution.py:43
  15.5 3.3 %collective-permute-start.5 = (bf16[4,64,512]{2,1,0:T(8,128)(2,1)S(1)}, bf16[4,64,512]{2,1,0:T(8,128)(2,1)S(1)}, u32[]{:S(2)}, u32[]{:S(2)}) collective-permute-start(bf16[4,64,512]{2,1,0:T(8,128)(2,1)S(1)} %get-tuple-element.50), channel_id=1, source_target_pairs={{0,2},{1,3},{2,0},{3,1},{4,6},{5,7},{6,4},{7,5},{8,10},{9,11},{10,... | collective-permute-start | bytes 786440 | tf_op jit(solution)/shard_map/ppermute | solution.py:43
  18.8 0.7 collective-permute-start.6
  19.5 2.1 %collective-permute-done.4.b = bf16[4,64,512]{2,1,0:T(8,128)(2,1)S(1)} collective-permute-done((bf16[4,64,512]{2,1,0:T(8,128)(2,1)S(1)}, bf16[4,64,512]{2,1,0:T(8,128)(2,1)S(1)}, u32[]{:S(2)}, u32[]{:S(2)}) %collective-permute-start.4) | collective-permute-done | bytes 262176 | tf_op jit(solution)/shard_map/ppermute | solution.py:43
  21.7 4.0 %collective-permute-done.5.c = bf16[4,64,512]{2,1,0:T(8,128)(2,1)S(1)} collective-permute-done((bf16[4,64,512]{2,1,0:T(8,128)(2,1)S(1)}, bf16[4,64,512]{2,1,0:T(8,128)(2,1)S(1)}, u32[]{:S(2)}, u32[]{:S(2)}) %collective-permute-start.5) | collective-permute-done | bytes 262176 | tf_op jit(solution)/shard_map/ppermute | solution.py:43
  25.6 0.0 collective-permute-done.6.d
  25.6 0.8 turn.1
  26.4 1.1 collective-permute-start.7
  27.5 2.6 %collective-permute-start.8 = (bf16[4,64,512]{2,1,0:T(8,128)(2,1)S(1)}, bf16[4,64,512]{2,1,0:T(8,128)(2,1)S(1)}, u32[]{:S(2)}, u32[]{:S(2)}) collective-permute-start(bf16[4,64,512]{2,1,0:T(8,128)(2,1)S(1)} %get-tuple-element.54), channel_id=1, source_target_pairs={{0,8},{1,9},{2,10},{3,11},{4,12},{5,13},{6,14},{7,15},{8,0},{9,1},... | collective-permute-start | bytes 786440 | tf_op jit(solution)/shard_map/ppermute | solution.py:43
  30.1 1.1 collective-permute-start.9
  31.2 2.0 %collective-permute-done.7.b = bf16[4,64,512]{2,1,0:T(8,128)(2,1)S(1)} collective-permute-done((bf16[4,64,512]{2,1,0:T(8,128)(2,1)S(1)}, bf16[4,64,512]{2,1,0:T(8,128)(2,1)S(1)}, u32[]{:S(2)}, u32[]{:S(2)}) %collective-permute-start.7) | collective-permute-done | bytes 262176 | tf_op jit(solution)/shard_map/ppermute | solution.py:43
  33.2 3.5 %collective-permute-done.8.c = bf16[4,64,512]{2,1,0:T(8,128)(2,1)S(1)} collective-permute-done((bf16[4,64,512]{2,1,0:T(8,128)(2,1)S(1)}, bf16[4,64,512]{2,1,0:T(8,128)(2,1)S(1)}, u32[]{:S(2)}, u32[]{:S(2)}) %collective-permute-start.8) | collective-permute-done | bytes 262176 | tf_op jit(solution)/shard_map/ppermute | solution.py:43
  36.7 0.0 collective-permute-done.9.d
  36.7 0.6 here.1.refs_0_
  37.3 0.4 collective-permute-start.10
  37.7 1.4 %collective-permute-start.11 = (bf16[4,64,512]{2,1,0:T(8,128)(2,1)S(1)}, bf16[4,64,512]{2,1,0:T(8,128)(2,1)S(1)}, u32[]{:S(2)}, u32[]{:S(2)}) collective-permute-start(bf16[4,64,512]{2,1,0:T(8,128)(2,1)S(1)} %here.1.refs_0_), channel_id=1, source_target_pairs={{0,64},{1,65},{2,66},{3,67},{4,68},{5,69},{6,70},{7,71},{8,72},{9,... | collective-permute-start | bytes 786440 | tf_op jit(solution)/shard_map/ppermute | solution.py:43
  39.1 1.1 collective-permute-start.12
  40.1 7.5 %collective-permute-done.10.refs_1_ = bf16[4,64,512]{2,1,0:T(8,128)(2,1)S(1)} collective-permute-done((bf16[4,64,512]{2,1,0:T(8,128)(2,1)S(1)}, bf16[4,64,512]{2,1,0:T(8,128)(2,1)S(1)}, u32[]{:S(2)}, u32[]{:S(2)}) %collective-permute-start.10) | collective-permute-done | bytes 262176 | tf_op jit(solution)/shard_map/ppermute | solution.py:43
  47.6 0.0 collective-permute-done.11.refs_2_
  47.6 2.4 %collective-permute-done.12.refs_3_ = bf16[4,64,512]{2,1,0:T(8,128)(2,1)S(1)} collective-permute-done((bf16[4,64,512]{2,1,0:T(8,128)(2,1)S(1)}, bf16[4,64,512]{2,1,0:T(8,128)(2,1)S(1)}, u32[]{:S(2)}, u32[]{:S(2)}) %collective-permute-start.12) | collective-permute-done | bytes 262176 | tf_op jit(solution)/shard_map/ppermute | solution.py:43
  50.0 0.1 line.1.mine
  50.1 0.0 copy-start.7
  50.1 3.6 %collective-permute-start.13 = (bf16[4,4,64,512]{3,2,1,0:T(8,128)(2,1)S(1)}, bf16[4,4,64,512]{3,2,1,0:T(8,128)(2,1)S(1)}, u32[]{:S(2)}, u32[]{:S(2)}) collective-permute-start(bf16[4,4,64,512]{3,2,1,0:T(8,128)(2,1)S(1)} %line.1.mine), channel_id=1, source_target_pairs={{0,16},{1,17},{2,18},{3,19},{4,20},{5,21},{6,22},{7,23},{8,24},{9,... | collective-permute-start | bytes 3145736 | tf_op jit(solution)/shard_map/ppermute | solution.py:43
  53.7 2.3 %collective-permute-done.13.other = bf16[4,4,64,512]{3,2,1,0:T(8,128)(2,1)S(1)} collective-permute-done((bf16[4,4,64,512]{3,2,1,0:T(8,128)(2,1)S(1)}, bf16[4,4,64,512]{3,2,1,0:T(8,128)(2,1)S(1)}, u32[]{:S(2)}, u32[]{:S(2)}) %collective-permute-start.13) | collective-permute-done | bytes 1048608 | tf_op jit(solution)/shard_map/ppermute | solution.py:43
  56.0 1.3 %step.1.a = bf16[384,512]{1,0:T(8,128)(2,1)S(1)} custom-call(bf16[4,4,64,512]{3,2,1,0:T(8,128)(2,1)S(1)} %line.1.mine, bf16[4,4,64,512]{3,2,1,0:T(8,128)(2,1)S(1)} %collective-permute-done.13.other), custom_call_target="tpu_custom_call" | custom-call | flops 805306368 | bytes 2490368 | tf_op jit(solution)/shard_map/step/pallas_call | solution.py:159
  57.4 1.3 %collective-permute-start.14 = (bf16[384,512]{1,0:T(8,128)(2,1)S(1)}, bf16[384,512]{1,0:T(8,128)(2,1)S(1)}, u32[]{:S(2)}, u32[]{:S(2)}) collective-permute-start(bf16[384,512]{1,0:T(8,128)(2,1)S(1)} %step.1.a), channel_id=1, source_target_pairs={{0,1},{1,2},{2,3},{3,0},{4,5},{5,6},{6,7},{7,4},{8,9},{9,10},{10,1... | collective-permute-start | bytes 1179656 | tf_op jit(solution)/shard_map/ppermute | solution.py:43
  58.7 2.1 %collective-permute-start.15 = (bf16[384,512]{1,0:T(8,128)(2,1)S(1)}, bf16[384,512]{1,0:T(8,128)(2,1)S(1)}, u32[]{:S(2)}, u32[]{:S(2)}) collective-permute-start(bf16[384,512]{1,0:T(8,128)(2,1)S(1)} %step.1.a), channel_id=1, source_target_pairs={{0,2},{1,3},{2,0},{3,1},{4,6},{5,7},{6,4},{7,5},{8,10},{9,11},{10,... | collective-permute-start | bytes 1179656 | tf_op jit(solution)/shard_map/ppermute | solution.py:43
  60.8 1.0 collective-permute-start.16
  61.8 3.8 %collective-permute-done.14.b = bf16[384,512]{1,0:T(8,128)(2,1)S(1)} collective-permute-done((bf16[384,512]{1,0:T(8,128)(2,1)S(1)}, bf16[384,512]{1,0:T(8,128)(2,1)S(1)}, u32[]{:S(2)}, u32[]{:S(2)}) %collective-permute-start.14) | collective-permute-done | bytes 393248 | tf_op jit(solution)/shard_map/ppermute | solution.py:43
  65.6 4.9 %collective-permute-done.15.c = bf16[384,512]{1,0:T(8,128)(2,1)S(1)} collective-permute-done((bf16[384,512]{1,0:T(8,128)(2,1)S(1)}, bf16[384,512]{1,0:T(8,128)(2,1)S(1)}, u32[]{:S(2)}, u32[]{:S(2)}) %collective-permute-start.15) | collective-permute-done | bytes 393248 | tf_op jit(solution)/shard_map/ppermute | solution.py:43
  70.5 0.0 collective-permute-done.16.d
  70.5 0.9 near.1
  71.4 1.4 %collective-permute-start.18 = (bf16[1152,512]{1,0:T(8,128)(2,1)S(1)}, bf16[1152,512]{1,0:T(8,128)(2,1)S(1)}, u32[]{:S(2)}, u32[]{:S(2)}) collective-permute-start(bf16[1152,512]{1,0:T(8,128)(2,1)S(1)} %get-tuple-element.57), channel_id=1, source_target_pairs={{0,4},{1,5},{2,6},{3,7},{4,8},{5,9},{6,10},{7,11},{8,12},{9,13},{1... | collective-permute-start | bytes 3538952 | tf_op jit(solution)/shard_map/ppermute | solution.py:43
  72.8 2.1 %collective-permute-start.20 = (bf16[1152,512]{1,0:T(8,128)(2,1)S(1)}, bf16[1152,512]{1,0:T(8,128)(2,1)S(1)}, u32[]{:S(2)}, u32[]{:S(2)}) collective-permute-start(bf16[1152,512]{1,0:T(8,128)(2,1)S(1)} %get-tuple-element.58), channel_id=1, source_target_pairs={{0,8},{1,9},{2,10},{3,11},{4,12},{5,13},{6,14},{7,15},{8,0},{9,1},... | collective-permute-start | bytes 3538952 | tf_op jit(solution)/shard_map/ppermute | solution.py:43
  74.9 1.1 %collective-permute-start.21 = (bf16[1152,512]{1,0:T(8,128)(2,1)S(1)}, bf16[1152,512]{1,0:T(8,128)(2,1)S(1)}, u32[]{:S(2)}, u32[]{:S(2)}) collective-permute-start(bf16[1152,512]{1,0:T(8,128)(2,1)S(1)} %get-tuple-element.59), channel_id=1, source_target_pairs={{0,12},{1,13},{2,14},{3,15},{4,0},{5,1},{6,2},{7,3},{8,4},{9,5},{1... | collective-permute-start | bytes 3538952 | tf_op jit(solution)/shard_map/ppermute | solution.py:43
  76.0 2.0 %collective-permute-start.17 = (bf16[1152,512]{1,0:T(8,128)(2,1)S(1)}, bf16[1152,512]{1,0:T(8,128)(2,1)S(1)}, u32[]{:S(2)}, u32[]{:S(2)}) collective-permute-start(bf16[1152,512]{1,0:T(8,128)(2,1)S(1)} %get-tuple-element.56.refs_0_), channel_id=1, source_target_pairs={{0,16},{1,17},{2,18},{3,19},{4,20},{5,21},{6,22},{7,23},{8,24},{9,... | collective-permute-start | bytes 3538952 | tf_op jit(solution)/shard_map/ppermute | solution.py:43
  78.1 10.0 %collective-permute-done.18.refs_1_ = bf16[1152,512]{1,0:T(8,128)(2,1)S(1)} collective-permute-done((bf16[1152,512]{1,0:T(8,128)(2,1)S(1)}, bf16[1152,512]{1,0:T(8,128)(2,1)S(1)}, u32[]{:S(2)}, u32[]{:S(2)}) %collective-permute-start.18) | collective-permute-done | bytes 1179680 | tf_op jit(solution)/shard_map/ppermute | solution.py:43
  88.0 2.3 %collective-permute-start.19 = (bf16[1152,512]{1,0:T(8,128)(2,1)S(1)}, bf16[1152,512]{1,0:T(8,128)(2,1)S(1)}, u32[]{:S(2)}, u32[]{:S(2)}) collective-permute-start(bf16[1152,512]{1,0:T(8,128)(2,1)S(1)} %collective-permute-done.18.refs_1_), channel_id=1, source_target_pairs={{0,16},{1,17},{2,18},{3,19},{4,20},{5,21},{6,22},{7,23},{8,24},{9,... | collective-permute-start | bytes 3538952 | tf_op jit(solution)/shard_map/ppermute | solution.py:43
  90.3 11.1 %collective-permute-done.20.refs_2_ = bf16[1152,512]{1,0:T(8,128)(2,1)S(1)} collective-permute-done((bf16[1152,512]{1,0:T(8,128)(2,1)S(1)}, bf16[1152,512]{1,0:T(8,128)(2,1)S(1)}, u32[]{:S(2)}, u32[]{:S(2)}) %collective-permute-start.20) | collective-permute-done | bytes 1179680 | tf_op jit(solution)/shard_map/ppermute | solution.py:43
  101.4 2.2 %collective-permute-start.22 = (bf16[1152,512]{1,0:T(8,128)(2,1)S(1)}, bf16[1152,512]{1,0:T(8,128)(2,1)S(1)}, u32[]{:S(2)}, u32[]{:S(2)}) collective-permute-start(bf16[1152,512]{1,0:T(8,128)(2,1)S(1)} %collective-permute-done.20.refs_2_), channel_id=1, source_target_pairs={{0,16},{1,17},{2,18},{3,19},{4,20},{5,21},{6,22},{7,23},{8,24},{9,... | collective-permute-start | bytes 3538952 | tf_op jit(solution)/shard_map/ppermute | solution.py:43
  103.6 0.0 collective-permute-done.21.refs_3_
  103.6 0.2 collective-permute-start.23
  103.8 0.0 collective-permute-done.17.refs_1_.refs_4_
  103.8 1.9 %place.2.refs_0_ = bf16[16,512,512]{2,1,0:T(8,128)(2,1)} custom-call(s32[59]{0:T(128)S(1)} %copy-done.7, bf16[1152,512]{1,0:T(8,128)(2,1)S(1)} %get-tuple-element.56.refs_0_, bf16[1152,512]{1,0:T(8,128)(2,1)S(1)} %collective-permute-done.17.refs_1_.refs_4_), custom_call_target="tpu_custom_call" | custom-call | bytes 4718592 | tf_op jit(solution)/shard_map/place/pallas_call | solution.py:301
  105.8 1.5 %stats.1 = (f32[3,64,512]{2,1,0:T(8,128)}, f32[3,64,512]{2,1,0:T(8,128)}) custom-call(s32[59]{0:T(128)S(1)} %copy-done.7, f32[3,64,512]{2,1,0:T(8,128)S(1)} %bitcast.13, f32[3,64,512]{2,1,0:T(8,128)S(1)} %bitcast.14, bf16[1152,512]{1,0:T(8,128)(2,1)S(1)} %get-tuple-element.56.refs_0_, bf16[1152,512]{1,0:T(8,128)(2,1)S(1)} %collective-permute-done.18.refs_1_, ...), custom_call_target="tpu_custom_call" | custom-call | bytes 6291692 | tf_op jit(solution)/shard_map/stats/pallas_call | solution.py:159
  107.3 0.0 collective-permute-done.19.refs_2_.refs_5_
  107.3 1.9 %place.3.begun = bf16[16,512,512]{2,1,0:T(8,128)(2,1)} custom-call(s32[59]{0:T(128)S(1)} %copy-done.7, bf16[16,512,512]{2,1,0:T(8,128)(2,1)} %place.2.refs_0_, bf16[1152,512]{1,0:T(8,128)(2,1)S(1)} %collective-permute-done.18.refs_1_, bf16[1152,512]{1,0:T(8,128)(2,1)S(1)} %collective-permute-done.19.refs_2_.refs_5_), custom_call_target="tpu_custom_call", output_to_operand_aliasing={{}: (1, {})} | custom-call | bytes 4718592 | tf_op jit(solution)/shard_map/place/pallas_call | solution.py:301
  109.3 0.0 collective-permute-done.22.refs_6_
  109.3 3.4 %finish.1 = (bf16[16,512,512]{2,1,0:T(8,128)(2,1)}, f32[3,64,512]{2,1,0:T(8,128)}) custom-call(s32[59]{0:T(128)S(1)} %copy-done.7, bf16[16,512,512]{2,1,0:T(8,128)(2,1)} %place.3.begun, f32[3,64,512]{2,1,0:T(8,128)S(1)} %bitcast.10, bf16[1152,512]{1,0:T(8,128)(2,1)S(1)} %get-tuple-element.56.refs_0_, ...), custom_call_target="tpu_custom_call", output_to_operand_aliasing={{0}: (1, {})} | custom-call | bytes 9437184 | tf_op jit(solution)/shard_map/finish/pallas_call | solution.py:409
  (13 shorter events, 0.1 us)
Async XLA Ops:
  0.6 10.8 %copy-start = (f32[1,3,64,512]{3,2,1,0:T(8,128)S(1)}, f32[1,3,64,512]{3,2,1,0:T(8,128)}, u32[]{:S(2)}) copy-start(f32[1,3,64,512]{3,2,1,0:T(8,128)} %param.15) | copy-start | bytes 1179652
  0.6 3.2 %collective-permute-start = (bf16[512,512]{1,0:T(8,128)(2,1)}, bf16[512,512]{1,0:T(8,128)(2,1)S(1)}, u32[]{:S(2)}, u32[]{:S(2)}) collective-permute-start(bf16[512,512]{1,0:T(8,128)(2,1)} %bitcast.11), channel_id=1, source_target_pairs={{0,16},{1,17},{2,18},{3,19},{4,20},{5,21},{6,22},{7,23},{8,24},{9,... | collective-permute-start | bytes 1572872 | tf_op jit(solution)/shard_map/ppermute | solution.py:43
  3.9 1.0 copy-start.1
  4.9 6.5 %copy-start.4 = (f32[1,3,64,512]{3,2,1,0:T(8,128)S(1)}, f32[1,3,64,512]{3,2,1,0:T(8,128)}, u32[]{:S(2)}) copy-start(f32[1,3,64,512]{3,2,1,0:T(8,128)} %param.13) | copy-start | bytes 1179652
  5.0 8.7 %collective-permute-start.1 = (bf16[64,512]{1,0:T(8,128)(2,1)S(1)}, bf16[64,512]{1,0:T(8,128)(2,1)S(1)}, u32[]{:S(2)}, u32[]{:S(2)}) collective-permute-start(bf16[64,512]{1,0:T(8,128)(2,1)S(1)} %get-tuple-element.38), channel_id=1, source_target_pairs={{0,32},{1,33},{2,34},{3,35},{4,36},{5,37},{6,38},{7,39},{8,40},{9,... | collective-permute-start | bytes 196616 | tf_op jit(solution)/shard_map/ppermute | solution.py:43
  6.4 7.3 %collective-permute-start.2 = (bf16[64,512]{1,0:T(8,128)(2,1)S(1)}, bf16[64,512]{1,0:T(8,128)(2,1)S(1)}, u32[]{:S(2)}, u32[]{:S(2)}) collective-permute-start(bf16[64,512]{1,0:T(8,128)(2,1)S(1)} %get-tuple-element.39), channel_id=1, source_target_pairs={{0,64},{1,65},{2,66},{3,67},{4,68},{5,69},{6,70},{7,71},{8,72},{9,... | collective-permute-start | bytes 196616 | tf_op jit(solution)/shard_map/ppermute | solution.py:43
  8.8 4.9 %collective-permute-start.3 = (bf16[64,512]{1,0:T(8,128)(2,1)S(1)}, bf16[64,512]{1,0:T(8,128)(2,1)S(1)}, u32[]{:S(2)}, u32[]{:S(2)}) collective-permute-start(bf16[64,512]{1,0:T(8,128)(2,1)S(1)} %get-tuple-element.40), channel_id=1, source_target_pairs={{0,96},{1,97},{2,98},{3,99},{4,100},{5,101},{6,102},{7,103},{8,104... | collective-permute-start | bytes 196616 | tf_op jit(solution)/shard_map/ppermute | solution.py:43
  11.4 1.0 copy-start.5
  12.4 0.7 copy-start.6
  13.8 7.9 %collective-permute-start.4 = (bf16[4,64,512]{2,1,0:T(8,128)(2,1)S(1)}, bf16[4,64,512]{2,1,0:T(8,128)(2,1)S(1)}, u32[]{:S(2)}, u32[]{:S(2)}) collective-permute-start(bf16[4,64,512]{2,1,0:T(8,128)(2,1)S(1)} %get-tuple-element.49), channel_id=1, source_target_pairs={{0,1},{1,2},{2,3},{3,0},{4,5},{5,6},{6,7},{7,4},{8,9},{9,10},{10,1... | collective-permute-start | bytes 786440 | tf_op jit(solution)/shard_map/ppermute | solution.py:43
  15.5 10.2 %collective-permute-start.5 = (bf16[4,64,512]{2,1,0:T(8,128)(2,1)S(1)}, bf16[4,64,512]{2,1,0:T(8,128)(2,1)S(1)}, u32[]{:S(2)}, u32[]{:S(2)}) collective-permute-start(bf16[4,64,512]{2,1,0:T(8,128)(2,1)S(1)} %get-tuple-element.50), channel_id=1, source_target_pairs={{0,2},{1,3},{2,0},{3,1},{4,6},{5,7},{6,4},{7,5},{8,10},{9,11},{10,... | collective-permute-start | bytes 786440 | tf_op jit(solution)/shard_map/ppermute | solution.py:43
  18.8 6.9 %collective-permute-start.6 = (bf16[4,64,512]{2,1,0:T(8,128)(2,1)S(1)}, bf16[4,64,512]{2,1,0:T(8,128)(2,1)S(1)}, u32[]{:S(2)}, u32[]{:S(2)}) collective-permute-start(bf16[4,64,512]{2,1,0:T(8,128)(2,1)S(1)} %get-tuple-element.51), channel_id=1, source_target_pairs={{0,3},{1,0},{2,1},{3,2},{4,7},{5,4},{6,5},{7,6},{8,11},{9,8},{10,9... | collective-permute-start | bytes 786440 | tf_op jit(solution)/shard_map/ppermute | solution.py:43
  26.4 6.8 %collective-permute-start.7 = (bf16[4,64,512]{2,1,0:T(8,128)(2,1)S(1)}, bf16[4,64,512]{2,1,0:T(8,128)(2,1)S(1)}, u32[]{:S(2)}, u32[]{:S(2)}) collective-permute-start(bf16[4,64,512]{2,1,0:T(8,128)(2,1)S(1)} %get-tuple-element.53), channel_id=1, source_target_pairs={{0,4},{1,5},{2,6},{3,7},{4,8},{5,9},{6,10},{7,11},{8,12},{9,13},{1... | collective-permute-start | bytes 786440 | tf_op jit(solution)/shard_map/ppermute | solution.py:43
  27.5 9.2 %collective-permute-start.8 = (bf16[4,64,512]{2,1,0:T(8,128)(2,1)S(1)}, bf16[4,64,512]{2,1,0:T(8,128)(2,1)S(1)}, u32[]{:S(2)}, u32[]{:S(2)}) collective-permute-start(bf16[4,64,512]{2,1,0:T(8,128)(2,1)S(1)} %get-tuple-element.54), channel_id=1, source_target_pairs={{0,8},{1,9},{2,10},{3,11},{4,12},{5,13},{6,14},{7,15},{8,0},{9,1},... | collective-permute-start | bytes 786440 | tf_op jit(solution)/shard_map/ppermute | solution.py:43
  30.1 6.6 %collective-permute-start.9 = (bf16[4,64,512]{2,1,0:T(8,128)(2,1)S(1)}, bf16[4,64,512]{2,1,0:T(8,128)(2,1)S(1)}, u32[]{:S(2)}, u32[]{:S(2)}) collective-permute-start(bf16[4,64,512]{2,1,0:T(8,128)(2,1)S(1)} %get-tuple-element.55), channel_id=1, source_target_pairs={{0,12},{1,13},{2,14},{3,15},{4,0},{5,1},{6,2},{7,3},{8,4},{9,5},{1... | collective-permute-start | bytes 786440 | tf_op jit(solution)/shard_map/ppermute | solution.py:43
  37.3 10.4 %collective-permute-start.10 = (bf16[4,64,512]{2,1,0:T(8,128)(2,1)S(1)}, bf16[4,64,512]{2,1,0:T(8,128)(2,1)S(1)}, u32[]{:S(2)}, u32[]{:S(2)}) collective-permute-start(bf16[4,64,512]{2,1,0:T(8,128)(2,1)S(1)} %here.1.refs_0_), channel_id=1, source_target_pairs={{0,32},{1,33},{2,34},{3,35},{4,36},{5,37},{6,38},{7,39},{8,40},{9,... | collective-permute-start | bytes 786440 | tf_op jit(solution)/shard_map/ppermute | solution.py:43
  37.7 10.0 %collective-permute-start.11 = (bf16[4,64,512]{2,1,0:T(8,128)(2,1)S(1)}, bf16[4,64,512]{2,1,0:T(8,128)(2,1)S(1)}, u32[]{:S(2)}, u32[]{:S(2)}) collective-permute-start(bf16[4,64,512]{2,1,0:T(8,128)(2,1)S(1)} %here.1.refs_0_), channel_id=1, source_target_pairs={{0,64},{1,65},{2,66},{3,67},{4,68},{5,69},{6,70},{7,71},{8,72},{9,... | collective-permute-start | bytes 786440 | tf_op jit(solution)/shard_map/ppermute | solution.py:43
  39.1 10.9 %collective-permute-start.12 = (bf16[4,64,512]{2,1,0:T(8,128)(2,1)S(1)}, bf16[4,64,512]{2,1,0:T(8,128)(2,1)S(1)}, u32[]{:S(2)}, u32[]{:S(2)}) collective-permute-start(bf16[4,64,512]{2,1,0:T(8,128)(2,1)S(1)} %here.1.refs_0_), channel_id=1, source_target_pairs={{0,96},{1,97},{2,98},{3,99},{4,100},{5,101},{6,102},{7,103},{8,104... | collective-permute-start | bytes 786440 | tf_op jit(solution)/shard_map/ppermute | solution.py:43
  50.1 20.4 %copy-start.7 = (s32[59]{0:T(128)S(1)}, s32[59]{0:T(128)}, u32[]{:S(2)}) copy-start(s32[59]{0:T(128)} %choices.1.spot) | copy-start | bytes 712
  50.1 5.9 %collective-permute-start.13 = (bf16[4,4,64,512]{3,2,1,0:T(8,128)(2,1)S(1)}, bf16[4,4,64,512]{3,2,1,0:T(8,128)(2,1)S(1)}, u32[]{:S(2)}, u32[]{:S(2)}) collective-permute-start(bf16[4,4,64,512]{3,2,1,0:T(8,128)(2,1)S(1)} %line.1.mine), channel_id=1, source_target_pairs={{0,16},{1,17},{2,18},{3,19},{4,20},{5,21},{6,22},{7,23},{8,24},{9,... | collective-permute-start | bytes 3145736 | tf_op jit(solution)/shard_map/ppermute | solution.py:43
  57.4 8.2 %collective-permute-start.14 = (bf16[384,512]{1,0:T(8,128)(2,1)S(1)}, bf16[384,512]{1,0:T(8,128)(2,1)S(1)}, u32[]{:S(2)}, u32[]{:S(2)}) collective-permute-start(bf16[384,512]{1,0:T(8,128)(2,1)S(1)} %step.1.a), channel_id=1, source_target_pairs={{0,1},{1,2},{2,3},{3,0},{4,5},{5,6},{6,7},{7,4},{8,9},{9,10},{10,1... | collective-permute-start | bytes 1179656 | tf_op jit(solution)/shard_map/ppermute | solution.py:43
  58.7 11.8 %collective-permute-start.15 = (bf16[384,512]{1,0:T(8,128)(2,1)S(1)}, bf16[384,512]{1,0:T(8,128)(2,1)S(1)}, u32[]{:S(2)}, u32[]{:S(2)}) collective-permute-start(bf16[384,512]{1,0:T(8,128)(2,1)S(1)} %step.1.a), channel_id=1, source_target_pairs={{0,2},{1,3},{2,0},{3,1},{4,6},{5,7},{6,4},{7,5},{8,10},{9,11},{10,... | collective-permute-start | bytes 1179656 | tf_op jit(solution)/shard_map/ppermute | solution.py:43
  60.8 9.7 %collective-permute-start.16 = (bf16[384,512]{1,0:T(8,128)(2,1)S(1)}, bf16[384,512]{1,0:T(8,128)(2,1)S(1)}, u32[]{:S(2)}, u32[]{:S(2)}) collective-permute-start(bf16[384,512]{1,0:T(8,128)(2,1)S(1)} %step.1.a), channel_id=1, source_target_pairs={{0,3},{1,0},{2,1},{3,2},{4,7},{5,4},{6,5},{7,6},{8,11},{9,8},{10,9... | collective-permute-start | bytes 1179656 | tf_op jit(solution)/shard_map/ppermute | solution.py:43
  71.4 16.6 %collective-permute-start.18 = (bf16[1152,512]{1,0:T(8,128)(2,1)S(1)}, bf16[1152,512]{1,0:T(8,128)(2,1)S(1)}, u32[]{:S(2)}, u32[]{:S(2)}) collective-permute-start(bf16[1152,512]{1,0:T(8,128)(2,1)S(1)} %get-tuple-element.57), channel_id=1, source_target_pairs={{0,4},{1,5},{2,6},{3,7},{4,8},{5,9},{6,10},{7,11},{8,12},{9,13},{1... | collective-permute-start | bytes 3538952 | tf_op jit(solution)/shard_map/ppermute | solution.py:43
  72.8 28.6 %collective-permute-start.20 = (bf16[1152,512]{1,0:T(8,128)(2,1)S(1)}, bf16[1152,512]{1,0:T(8,128)(2,1)S(1)}, u32[]{:S(2)}, u32[]{:S(2)}) collective-permute-start(bf16[1152,512]{1,0:T(8,128)(2,1)S(1)} %get-tuple-element.58), channel_id=1, source_target_pairs={{0,8},{1,9},{2,10},{3,11},{4,12},{5,13},{6,14},{7,15},{8,0},{9,1},... | collective-permute-start | bytes 3538952 | tf_op jit(solution)/shard_map/ppermute | solution.py:43
  74.9 28.7 %collective-permute-start.21 = (bf16[1152,512]{1,0:T(8,128)(2,1)S(1)}, bf16[1152,512]{1,0:T(8,128)(2,1)S(1)}, u32[]{:S(2)}, u32[]{:S(2)}) collective-permute-start(bf16[1152,512]{1,0:T(8,128)(2,1)S(1)} %get-tuple-element.59), channel_id=1, source_target_pairs={{0,12},{1,13},{2,14},{3,15},{4,0},{5,1},{6,2},{7,3},{8,4},{9,5},{1... | collective-permute-start | bytes 3538952 | tf_op jit(solution)/shard_map/ppermute | solution.py:43
  76.0 29.7 %copy-start.2 = (f32[1,3,64,512]{3,2,1,0:T(8,128)S(1)}, f32[1,3,64,512]{3,2,1,0:T(8,128)}, u32[]{:S(2)}) copy-start(f32[1,3,64,512]{3,2,1,0:T(8,128)} %param.11) | copy-start | bytes 1179652
  76.0 29.8 %copy-start.3 = (f32[1,3,64,512]{3,2,1,0:T(8,128)S(1)}, f32[1,3,64,512]{3,2,1,0:T(8,128)}, u32[]{:S(2)}) copy-start(f32[1,3,64,512]{3,2,1,0:T(8,128)} %param.12) | copy-start | bytes 1179652
  76.0 27.8 %collective-permute-start.17 = (bf16[1152,512]{1,0:T(8,128)(2,1)S(1)}, bf16[1152,512]{1,0:T(8,128)(2,1)S(1)}, u32[]{:S(2)}, u32[]{:S(2)}) collective-permute-start(bf16[1152,512]{1,0:T(8,128)(2,1)S(1)} %get-tuple-element.56.refs_0_), channel_id=1, source_target_pairs={{0,16},{1,17},{2,18},{3,19},{4,20},{5,21},{6,22},{7,23},{8,24},{9,... | collective-permute-start | bytes 3538952 | tf_op jit(solution)/shard_map/ppermute | solution.py:43
  88.0 19.3 %collective-permute-start.19 = (bf16[1152,512]{1,0:T(8,128)(2,1)S(1)}, bf16[1152,512]{1,0:T(8,128)(2,1)S(1)}, u32[]{:S(2)}, u32[]{:S(2)}) collective-permute-start(bf16[1152,512]{1,0:T(8,128)(2,1)S(1)} %collective-permute-done.18.refs_1_), channel_id=1, source_target_pairs={{0,16},{1,17},{2,18},{3,19},{4,20},{5,21},{6,22},{7,23},{8,24},{9,... | collective-permute-start | bytes 3538952 | tf_op jit(solution)/shard_map/ppermute | solution.py:43
  101.4 7.9 %collective-permute-start.22 = (bf16[1152,512]{1,0:T(8,128)(2,1)S(1)}, bf16[1152,512]{1,0:T(8,128)(2,1)S(1)}, u32[]{:S(2)}, u32[]{:S(2)}) collective-permute-start(bf16[1152,512]{1,0:T(8,128)(2,1)S(1)} %collective-permute-done.20.refs_2_), channel_id=1, source_target_pairs={{0,16},{1,17},{2,18},{3,19},{4,20},{5,21},{6,22},{7,23},{8,24},{9,... | collective-permute-start | bytes 3538952 | tf_op jit(solution)/shard_map/ppermute | solution.py:43
  103.6 5.7 %collective-permute-start.23 = (bf16[1152,512]{1,0:T(8,128)(2,1)S(1)}, bf16[1152,512]{1,0:T(8,128)(2,1)S(1)}, u32[]{:S(2)}, u32[]{:S(2)}) collective-permute-start(bf16[1152,512]{1,0:T(8,128)(2,1)S(1)} %collective-permute-done.21.refs_3_), channel_id=1, source_target_pairs={{0,16},{1,17},{2,18},{3,19},{4,20},{5,21},{6,22},{7,23},{8,24},{9,... | collective-permute-start | bytes 3538952 | tf_op jit(solution)/shard_map/ppermute | solution.py:43

commit v3 on v2

--- a/solution.py
+++ b/solution.py
@@ -26,7 +26,8 @@
 ANY = pl.BlockSpec(memory_space=pl.ANY)
 
 GRAD_PICK, GRAD_LAST, ROOT_PICK, ROOT_LAST = 0, 4, 5, 9
-SLOT_PICK, TERM_PICK, TERM_LAST, SLOT_LIVE, SLOT_BLOCK, LANDING = 10, 14, 18, 21, 24, 27
+SLOT_PICK, TERM_PICK, TERM_LAST, SLOT_LIVE, SLOT_FROM, SLOT_ROW = 10, 14, 18, 21, 24, 27
+LANDING = 30
 CHOICES = LANDING + 32
 
 
@@ -59,11 +60,8 @@
     return permute(value, lambda x, c, z, y: (x, c, z + k, y) if c == 0 else (x, c, z, y + k))
 
 
-def along(send, values):
-    got = [values[0], None, None, None]
-    for k in (1, 3, 2):
-        got[k] = send(values[k], k)
-    return got
+def along(send, values, shifts=(1, 3, 2)):
+    return [values[0]] + [send(values[k], k) for k in shifts]
 
 
 def position():
@@ -119,7 +117,10 @@
         slot_u.append(su)
         out[TERM_LAST + s] = (v - sv) & 3
         out[SLOT_LIVE + s] = (s < my_count).astype(jnp.int32)
-        out[SLOT_BLOCK + s] = order_ref[q]
+        near, far = (u - su) & 3, (v - sv) & 3
+        same = ((2 * x + c) >> 2) == c
+        out[SLOT_FROM + s] = jnp.where(s < my_count, jnp.where(same, far, 4 + near), 8)
+        out[SLOT_ROW + s] = jnp.where(same, near, far)
     for k in range(4):
         far = (u + k) & 3
         chosen = jnp.int32(0)
@@ -146,6 +147,7 @@
         in_specs=[SMEM, SMEM],
         out_specs=SMEM,
         scratch_shapes=[pltpu.SMEM((BLOCKS,), jnp.int32), pltpu.SMEM((BLOCKS,), jnp.int32)],
+        cost_estimate=pl.CostEstimate(flops=0, bytes_accessed=4 << 20, transcendentals=0),
         name="choices",
     )(block_order, owner_count)
 
@@ -196,7 +198,7 @@
         out[2] = moment[slot].astype(half_type)
 
 
-def total_kernel(own, a, b, c, *packs):
+def total_kernel(own, a, c, b, *packs):
     total = own[...] + a[...].astype(wide_type)
     total = total + b[...].astype(wide_type)
     total = (total + c[...].astype(wide_type)).astype(half_type)
@@ -204,13 +206,13 @@
         out[3] = total
 
 
-def turn_kernel(spot, a, b, c, d, *outs):
+def turn_kernel(spot, a, b, d, c, *outs):
     for k, out in enumerate(outs):
         copy_chosen(spot[ROOT_PICK + k], (a, b, c, d), out.at[:3], pl.ds(0, 3))
         copy_chosen(spot[GRAD_PICK + k], (a, b, c, d), out.at[3:], pl.ds(3, 1))
 
 
-def here_kernel(spot, a, b, c, d, out):
+def here_kernel(spot, a, b, d, c, out):
     copy_chosen(spot[ROOT_LAST], (a, b, c, d), out.at[:3], pl.ds(0, 3))
     copy_chosen(spot[GRAD_LAST], (a, b, c, d), out.at[3:], pl.ds(3, 1))
 
@@ -218,8 +220,8 @@
 def line_kernel(*refs):
     out = refs[4]
     x = position()[0]
-    for k in range(4):
-        out[(x - k) & 3] = refs[k][...]
+    for n, k in enumerate((0, 2, 3, 1)):
+        out[(x - k) & 3] = refs[n][...]
 
 
 def line_up(got, name):
@@ -259,28 +261,31 @@
     out[HALF + ROWS :, :] = term.astype(half_type)
 
 
-def near_kernel(spot, a, b, c, d, *outs):
-    for k, out in enumerate(outs):
-        for j, source in enumerate((a, b, c, d)):
-            out[j * HALF : (j + 1) * HALF, :] = source[:HALF, :]
-        copy_chosen(spot[TERM_PICK + k], (a, b, c, d), out.at[NEAR:], pl.ds(HALF, 2 * ROWS))
+def near_kernel(spot, a, c, d, b, near, ahead, back):
+    sources = (a, b, c, d)
+    for out, first in ((near, 0), (ahead, ROWS), (back, 0)):
+        for j, source in enumerate(sources):
+            out[first + j * HALF : first + (j + 1) * HALF, :] = source[:HALF, :]
+    both, left, right = pl.ds(HALF, 2 * ROWS), pl.ds(HALF, ROWS), pl.ds(HALF + ROWS, ROWS)
+    copy_chosen(spot[TERM_PICK], sources, near.at[NEAR:], both)
+    copy_chosen(spot[TERM_PICK + 1], sources, ahead.at[NEAR + ROWS :], both)
+    copy_chosen(spot[TERM_PICK + 3], sources, back.at[NEAR + ROWS :], both)
+    copy_chosen(spot[TERM_PICK + 2], sources, ahead.at[:ROWS], left)
+    copy_chosen(spot[TERM_PICK + 2], sources, back.at[NEAR : NEAR + ROWS], right)
 
 
 def placed_copies(spot, sources, out, sems):
     _, c, _, _ = position()
     copies = []
-    for n, (which, source) in enumerate(sources):
+    for which, first, count, skip, source in sources:
         half = c if which < 4 else 1 - c
-        for j in range(4):
+        rows = pl.ds(pl.multiple_of(half * HALF, HALF), HALF)
+        for j in range(count):
             copies.append(
                 pltpu.make_async_copy(
-                    source.at[pl.ds(j * HALF, HALF), :],
-                    out.at[
-                        spot[LANDING + which * 4 + j],
-                        pl.ds(pl.multiple_of(half * HALF, HALF), HALF),
-                        :,
-                    ],
-                    sems.at[n * 4 + j],
+                    source.at[pl.ds(skip + j * HALF, HALF), :],
+                    out.at[spot[LANDING + which * 4 + first + j], rows, :],
+                    sems.at[len(copies)],
                 )
             )
     return copies
@@ -288,7 +293,9 @@
 
 def place_kernel(which, spot, *refs):
     mine, other, out, sems = refs[-4:]
-    copies = placed_copies(spot, ((which, mine), (which + 4, other)), out, sems)
+    skip = ROWS if which == 1 else 0
+    sources = ((which, 0, 4, skip, mine), (which + 4, 0, 4, skip, other))
+    copies = placed_copies(spot, sources, out, sems)
     for copy in copies:
         copy.start()
     for copy in copies:
@@ -313,45 +320,58 @@
 
 def finish_kernel(spot, begun, moment, *refs):
     del begun
-    sources, (out, out_moment, sems) = refs[:8], refs[8:]
-    copies = placed_copies(
-        spot, [(n, sources[n]) for n in (3, 2, 7, 6)], out, sems
-    )
+    whole, halves, (out, out_moment, sems) = refs[:6], refs[6:10], refs[10:]
+    near, near_other, one, one_other, three, three_other = whole
+    low, high, low_other, high_other = halves
+    sources = ((2, 0, 2, ROWS, low), (2, 2, 2, 0, high))
+    sources += ((6, 0, 2, ROWS, low_other), (6, 2, 2, 0, high_other))
+    copies = placed_copies(spot, sources, out, sems)
     for copy in copies:
         copy.start()
     x, c, _, _ = position()
-    row = (2 * x + c) * ROWS
-    in_half = row & (HALF - 1)
+    in_half = ((2 * x + c) & 3) * ROWS
     for s in range(SLOTS):
-        live = spot[SLOT_LIVE + s] == 1
-        block = spot[SLOT_BLOCK + s]
         out_moment[s] = moment[s]
-        for n, source in enumerate(sources):
-            half = c if n < 4 else 1 - c
-            for j in range(4):
-
-                @pl.when(live & (spot[LANDING + n * 4 + j] == block) & ((row >> 8) == half))
-                def _():
-                    at = pl.ds(pl.multiple_of(j * HALF + in_half, ROWS), ROWS)
-                    out_moment[s] = source[at, :].astype(wide_type)
-
+        which, place = spot[SLOT_FROM + s], spot[SLOT_ROW + s]
+
+        def take(here, source, first, skip=0):
+            @pl.when(here)
+            def _():
+                at = pl.ds(pl.multiple_of(skip + (place - first) * HALF + in_half, ROWS), ROWS)
+                out_moment[s] = source[at, :].astype(wide_type)
+
+        take(which == 0, near, 0)
+        take(which == 1, one, 0, ROWS)
+        take(which == 3, three, 0)
+        take(which == 4, near_other, 0)
+        take(which == 5, one_other, 0, ROWS)
+        take(which == 7, three_other, 0)
+        take((which == 2) & (place < 2), low, 0, ROWS)
+        take((which == 2) & (place >= 2), high, 2)
+        take((which == 6) & (place < 2), low_other, 0, ROWS)
+        take((which == 6) & (place >= 2), high_other, 2)
     for copy in copies:
         copy.wait()
 
 
-def stats_kernel(spot, left, right, *refs):
-    sources, outs = refs[:4], refs[4:]
+def stats_kernel(spot, left, right, near, one, low, high, three, out_left, out_right):
+    last = NEAR + ROWS
+    terms = (
+        (near.at[NEAR : NEAR + ROWS], near.at[NEAR + ROWS :]),
+        (one.at[last : last + ROWS], one.at[last + ROWS :]),
+        (low.at[:ROWS], high.at[2 * HALF :]),
+        (three.at[last : last + ROWS], three.at[last + ROWS :]),
+    )
     for s in range(SLOTS):
-        for old, out in zip((left, right), outs):
-            out[s] = old[s]
-        for n, source in enumerate(sources):
+        out_left[s] = left[s]
+        out_right[s] = right[s]
+        for n, (left_term, right_term) in enumerate(terms):
 
             @pl.when((spot[SLOT_LIVE + s] == 1) & (spot[TERM_LAST + s] == n))
             def _():
-                for i, (old, out) in enumerate(zip((left, right), outs)):
-                    at = pl.ds(NEAR + i * ROWS, ROWS)
-                    term = source[at, :].astype(wide_type)
-                    out[s] = decay_stats * old[s] + (1.0 - decay_stats) * term
+                for old, out, term in ((left, out_left, left_term), (right, out_right, right_term)):
+                    new = term[...].astype(wide_type)
+                    out[s] = decay_stats * old[s] + (1.0 - decay_stats) * new
 
 
 def local(
@@ -360,16 +380,17 @@
     chunk_type = jax.ShapeDtypeStruct((ROWS, BS), half_type)
     pack_type = jax.ShapeDtypeStruct((4, ROWS, BS), half_type)
     stat_type = jax.ShapeDtypeStruct((SLOTS, ROWS, BS), wide_type)
-    spot = choices(block_order, owner_count)
     hold = lax.optimization_barrier
 
     mine = gradients[0, 0]
+    theirs = to_core(mine)
+    spot, theirs = hold((choices(block_order, owner_count), theirs))
     own, *sends = small_call(
         pair_kernel,
         [jax.ShapeDtypeStruct((ROWS, BS), wide_type)] + [chunk_type] * 3,
         "pair",
         mine,
-        to_core(mine),
+        theirs,
     )
     sends, left, right, moment = hold((sends, root_left[0], root_right[0], momentum[0]))
     packs = small_call(pack_kernel, [pack_type] * 4, "packs", spot, left, right, moment)
@@ -381,7 +402,7 @@
     row = along(to_u, packs)
     column = along(to_v, small_call(turn_kernel, [pack_type] * 4, "turn", spot, *row))
     pack = small_call(here_kernel, pack_type, "here", spot, *column)
-    full = line_up(along(to_x, [pack] * 4), "line")
+    full = line_up(along(to_x, [pack] * 4, (2, 3, 1)), "line")
     send = small_call(
         step_kernel,
         jax.ShapeDtypeStruct((HALF + 2 * ROWS, BS), half_type),
@@ -396,27 +417,47 @@
         ],
     )
 
-    row = along(to_u, [send] * 4)
+    row = along(to_u, [send] * 4, (2, 3, 1))
     near_type = jax.ShapeDtypeStruct((NEAR + 2 * ROWS, BS), half_type)
-    nears = small_call(near_kernel, [near_type] * 4, "near", spot, *row)
-    held = along(to_v, nears)
-    across = [to_core(value) for value in held]
-    begun = place(0, spot, None, held[0], across[0])
-    begun = place(1, spot, begun, held[1], across[1])
+    sent_type = jax.ShapeDtypeStruct((NEAR + 3 * ROWS, BS), half_type)
+    near, ahead, back = small_call(
+        near_kernel, [near_type, sent_type, sent_type], "near", spot, *row
+    )
+    one, three = to_v(ahead, 1), to_v(back, 3)
+    near_other = to_core(near)
+    low = to_v(one[: ROWS + 2 * HALF], 1)
+    high = to_v(three[2 * HALF : NEAR + ROWS], 3)
+    one_other, three_other = to_core(one), to_core(three)
+    begun = place(0, spot, None, near, near_other)
+    begun = place(1, spot, begun, one, one_other)
+    begun = place(3, spot, begun, three, three_other)
+    low, high, begun = hold((low, high, begun))
     left_stats, right_stats = small_call(
-        stats_kernel, [stat_type] * 2, "stats", spot, stat_left[0], stat_right[0], *held
-    )
+        stats_kernel,
+        [stat_type] * 2,
+        "stats",
+        spot,
+        stat_left[0],
+        stat_right[0],
+        near,
+        one,
+        low,
+        high,
+        three,
+    )
+    given = [near, near_other, one, one_other, three, three_other]
+    given += [low, high, to_core(low), to_core(high)]
     update_blocks, new_momentum = pl.pallas_call(
         finish_kernel,
         out_shape=[jax.ShapeDtypeStruct((BLOCKS, BS, BS), half_type), stat_type],
-        in_specs=[SMEM, ANY] + [VMEM] * 9,
+        in_specs=[SMEM, ANY] + [VMEM] * (1 + len(given)),
         out_specs=[ANY, VMEM],
-        scratch_shapes=[pltpu.SemaphoreType.DMA((16,))],
+        scratch_shapes=[pltpu.SemaphoreType.DMA((8,))],
         input_output_aliases={1: 0},
         compiler_params=pltpu.CompilerParams(vmem_limit_bytes=16 << 20),
-        cost_estimate=cost(0, *held, *held),
+        cost_estimate=cost(0, *given),
         name="finish",
-    )(spot, begun, momentum[0], *held, *across)
+    )(spot, begun, momentum[0], *given)
     return (update_blocks, left_stats[None], right_stats[None], new_momentum[None])
 
 

time: 113 us -> 106 us (0.938)
  starting transfers between devices: 39.2 us -> 35.2 us
  waiting for transfers between devices: 55.4 us -> 51.6 us
  Pallas kernels: 14.6 us -> 15.8 us
    ppermute x24 -> x26, starting transfers between devices: 39.2 us -> 35.2 us  [permute(): return lax.ppermute(value, AXES, pairs)]
    ppermute x24 -> x26, waiting for transfers between devices: 55.4 us -> 51.6 us  [permute(): return lax.ppermute(value, AXES, pairs)]
    pallas_call x2 -> x3, Pallas kernels: 3.85 us -> 5.79 us  [place(): pl.pallas_call(functools.partial(place_kernel, which), out_shape=out, in_...]
  transfers between devices with their start and end apart: 24 -> 26, of which waited for: 12 -> 18; matrix products, arithmetic and copies ran while one was open for 0% -> 0% of each run, Pallas kernels for 7% -> 9%
where the time goes in v3:
time: 106 us
  waiting for transfers between devices  51.6 us (49%)
  starting transfers between devices  35.2 us (33%)
  Pallas kernels  15.8 us (15%)
  local copies, waits for them, and re-layouts  2.8 us (3%)
    ppermute x26, waiting for transfers between devices, permute(): return lax.ppermute(value, AXES, pairs)  51.6 us
    ppermute x26, starting transfers between devices, permute(): return lax.ppermute(value, AXES, pairs)  35.2 us
    pallas_call x9, Pallas kernels, small_call(): pl.pallas_call(body, out_shape=outs, in_specs=[SMEM if a.dtype == jnp.int...  5.96 us
    pallas_call x3, Pallas kernels, place(): pl.pallas_call(functools.partial(place_kernel, which), out_shape=out, in_...  5.79 us
    unnamed x16, local copies, waits for them, and re-layouts  2.72 us
    pallas_call x1, Pallas kernels, local(): pl.pallas_call(finish_kernel, out_shape=[jax.ShapeDtypeStruct((BLOCKS, BS...  2.67 us
  transfers between devices with their start and end apart: 26, of which 18 were waited for; matrix products, arithmetic and copies ran while one was open for 0% of the time, Pallas kernels for 9%

profile of v3, /device:TPU:1, one launch (start us, length us, event | category | flops | bytes accessed | tf_op | source)
XLA Modules:
  0.0 106.2 jit_solution(17550283682548973357)
XLA Ops:
  0.6 1.5 %collective-permute-start = (bf16[512,512]{1,0:T(8,128)(2,1)}, bf16[512,512]{1,0:T(8,128)(2,1)S(1)}, u32[]{:S(2)}, u32[]{:S(2)}) collective-permute-start(bf16[512,512]{1,0:T(8,128)(2,1)} %bitcast.11), channel_id=1, source_target_pairs={{0,16},{1,17},{2,18},{3,19},{4,20},{5,21},{6,22},{7,23},{8,24},{9,... | collective-permute-start | bytes 1572872 | tf_op jit(solution)/shard_map/ppermute | solution.py:44
  2.1 1.4 %choices.1.spot = s32[62]{0:T(128)} custom-call(s32[16]{0:T(128)} %order_ref.1, s32[16]{0:T(128)} %count_ref.1), custom_call_target="tpu_custom_call" | custom-call | bytes 4194304 | tf_op jit(solution)/shard_map/choices/pallas_call | solution.py:144
  3.6 0.3 collective-permute-done.theirs
  3.9 1.0 copy-done.1
  4.9 0.1 pair.1
  5.0 1.4 %collective-permute-start.1 = (bf16[64,512]{1,0:T(8,128)(2,1)S(1)}, bf16[64,512]{1,0:T(8,128)(2,1)S(1)}, u32[]{:S(2)}, u32[]{:S(2)}) collective-permute-start(bf16[64,512]{1,0:T(8,128)(2,1)S(1)} %get-tuple-element.44), channel_id=1, source_target_pairs={{0,32},{1,33},{2,34},{3,35},{4,36},{5,37},{6,38},{7,39},{8,40},{9,... | collective-permute-start | bytes 196616 | tf_op jit(solution)/shard_map/ppermute | solution.py:44
  6.4 1.4 %collective-permute-start.2 = (bf16[64,512]{1,0:T(8,128)(2,1)S(1)}, bf16[64,512]{1,0:T(8,128)(2,1)S(1)}, u32[]{:S(2)}, u32[]{:S(2)}) collective-permute-start(bf16[64,512]{1,0:T(8,128)(2,1)S(1)} %get-tuple-element.45), channel_id=1, source_target_pairs={{0,96},{1,97},{2,98},{3,99},{4,100},{5,101},{6,102},{7,103},{8,104... | collective-permute-start | bytes 196616 | tf_op jit(solution)/shard_map/ppermute | solution.py:44
  7.7 1.6 %collective-permute-start.3 = (bf16[64,512]{1,0:T(8,128)(2,1)S(1)}, bf16[64,512]{1,0:T(8,128)(2,1)S(1)}, u32[]{:S(2)}, u32[]{:S(2)}) collective-permute-start(bf16[64,512]{1,0:T(8,128)(2,1)S(1)} %get-tuple-element.46), channel_id=1, source_target_pairs={{0,64},{1,65},{2,66},{3,67},{4,68},{5,69},{6,70},{7,71},{8,72},{9,... | collective-permute-start | bytes 196616 | tf_op jit(solution)/shard_map/ppermute | solution.py:44
  9.4 1.0 copy-done.5
  10.4 0.7 copy-done.6
  11.0 0.6 packs.1
  11.7 0.0 collective-permute-done.2.c
  11.7 0.7 collective-permute-done.3.b
  12.4 1.8 %collective-permute-start.4 = (bf16[4,64,512]{2,1,0:T(8,128)(2,1)S(1)}, bf16[4,64,512]{2,1,0:T(8,128)(2,1)S(1)}, u32[]{:S(2)}, u32[]{:S(2)}) collective-permute-start(bf16[4,64,512]{2,1,0:T(8,128)(2,1)S(1)} %get-tuple-element.55), channel_id=1, source_target_pairs={{0,1},{1,2},{2,3},{3,0},{4,5},{5,6},{6,7},{7,4},{8,9},{9,10},{10,1... | collective-permute-start | bytes 786440 | tf_op jit(solution)/shard_map/ppermute | solution.py:44
  14.2 2.2 %collective-permute-start.5 = (bf16[4,64,512]{2,1,0:T(8,128)(2,1)S(1)}, bf16[4,64,512]{2,1,0:T(8,128)(2,1)S(1)}, u32[]{:S(2)}, u32[]{:S(2)}) collective-permute-start(bf16[4,64,512]{2,1,0:T(8,128)(2,1)S(1)} %get-tuple-element.56), channel_id=1, source_target_pairs={{0,3},{1,0},{2,1},{3,2},{4,7},{5,4},{6,5},{7,6},{8,11},{9,8},{10,9... | collective-permute-start | bytes 786440 | tf_op jit(solution)/shard_map/ppermute | solution.py:44
  16.4 1.2 %collective-permute-start.6 = (bf16[4,64,512]{2,1,0:T(8,128)(2,1)S(1)}, bf16[4,64,512]{2,1,0:T(8,128)(2,1)S(1)}, u32[]{:S(2)}, u32[]{:S(2)}) collective-permute-start(bf16[4,64,512]{2,1,0:T(8,128)(2,1)S(1)} %get-tuple-element.57), channel_id=1, source_target_pairs={{0,2},{1,3},{2,0},{3,1},{4,6},{5,7},{6,4},{7,5},{8,10},{9,11},{10,... | collective-permute-start | bytes 786440 | tf_op jit(solution)/shard_map/ppermute | solution.py:44
  17.6 2.7 %collective-permute-done.4.b = bf16[4,64,512]{2,1,0:T(8,128)(2,1)S(1)} collective-permute-done((bf16[4,64,512]{2,1,0:T(8,128)(2,1)S(1)}, bf16[4,64,512]{2,1,0:T(8,128)(2,1)S(1)}, u32[]{:S(2)}, u32[]{:S(2)}) %collective-permute-start.4) | collective-permute-done | bytes 262176 | tf_op jit(solution)/shard_map/ppermute | solution.py:44
  20.4 2.2 %collective-permute-done.5.d = bf16[4,64,512]{2,1,0:T(8,128)(2,1)S(1)} collective-permute-done((bf16[4,64,512]{2,1,0:T(8,128)(2,1)S(1)}, bf16[4,64,512]{2,1,0:T(8,128)(2,1)S(1)}, u32[]{:S(2)}, u32[]{:S(2)}) %collective-permute-start.5) | collective-permute-done | bytes 262176 | tf_op jit(solution)/shard_map/ppermute | solution.py:44
  22.5 1.8 %collective-permute-done.6.c = bf16[4,64,512]{2,1,0:T(8,128)(2,1)S(1)} collective-permute-done((bf16[4,64,512]{2,1,0:T(8,128)(2,1)S(1)}, bf16[4,64,512]{2,1,0:T(8,128)(2,1)S(1)}, u32[]{:S(2)}, u32[]{:S(2)}) %collective-permute-start.6) | collective-permute-done | bytes 262176 | tf_op jit(solution)/shard_map/ppermute | solution.py:44
  24.4 0.8 turn.1
  25.1 1.1 %collective-permute-start.7 = (bf16[4,64,512]{2,1,0:T(8,128)(2,1)S(1)}, bf16[4,64,512]{2,1,0:T(8,128)(2,1)S(1)}, u32[]{:S(2)}, u32[]{:S(2)}) collective-permute-start(bf16[4,64,512]{2,1,0:T(8,128)(2,1)S(1)} %get-tuple-element.59), channel_id=1, source_target_pairs={{0,4},{1,5},{2,6},{3,7},{4,8},{5,9},{6,10},{7,11},{8,12},{9,13},{1... | collective-permute-start | bytes 786440 | tf_op jit(solution)/shard_map/ppermute | solution.py:44
  26.2 1.8 %collective-permute-start.8 = (bf16[4,64,512]{2,1,0:T(8,128)(2,1)S(1)}, bf16[4,64,512]{2,1,0:T(8,128)(2,1)S(1)}, u32[]{:S(2)}, u32[]{:S(2)}) collective-permute-start(bf16[4,64,512]{2,1,0:T(8,128)(2,1)S(1)} %get-tuple-element.60), channel_id=1, source_target_pairs={{0,12},{1,13},{2,14},{3,15},{4,0},{5,1},{6,2},{7,3},{8,4},{9,5},{1... | collective-permute-start | bytes 786440 | tf_op jit(solution)/shard_map/ppermute | solution.py:44
  28.0 1.3 %collective-permute-start.9 = (bf16[4,64,512]{2,1,0:T(8,128)(2,1)S(1)}, bf16[4,64,512]{2,1,0:T(8,128)(2,1)S(1)}, u32[]{:S(2)}, u32[]{:S(2)}) collective-permute-start(bf16[4,64,512]{2,1,0:T(8,128)(2,1)S(1)} %get-tuple-element.61), channel_id=1, source_target_pairs={{0,8},{1,9},{2,10},{3,11},{4,12},{5,13},{6,14},{7,15},{8,0},{9,1},... | collective-permute-start | bytes 786440 | tf_op jit(solution)/shard_map/ppermute | solution.py:44
  29.3 2.4 %collective-permute-done.7.b = bf16[4,64,512]{2,1,0:T(8,128)(2,1)S(1)} collective-permute-done((bf16[4,64,512]{2,1,0:T(8,128)(2,1)S(1)}, bf16[4,64,512]{2,1,0:T(8,128)(2,1)S(1)}, u32[]{:S(2)}, u32[]{:S(2)}) %collective-permute-start.7) | collective-permute-done | bytes 262176 | tf_op jit(solution)/shard_map/ppermute | solution.py:44
  31.7 2.4 %collective-permute-done.8.d = bf16[4,64,512]{2,1,0:T(8,128)(2,1)S(1)} collective-permute-done((bf16[4,64,512]{2,1,0:T(8,128)(2,1)S(1)}, bf16[4,64,512]{2,1,0:T(8,128)(2,1)S(1)}, u32[]{:S(2)}, u32[]{:S(2)}) %collective-permute-start.8) | collective-permute-done | bytes 262176 | tf_op jit(solution)/shard_map/ppermute | solution.py:44
  34.1 1.5 %collective-permute-done.9.c = bf16[4,64,512]{2,1,0:T(8,128)(2,1)S(1)} collective-permute-done((bf16[4,64,512]{2,1,0:T(8,128)(2,1)S(1)}, bf16[4,64,512]{2,1,0:T(8,128)(2,1)S(1)}, u32[]{:S(2)}, u32[]{:S(2)}) %collective-permute-start.9) | collective-permute-done | bytes 262176 | tf_op jit(solution)/shard_map/ppermute | solution.py:44
  35.7 0.6 here.1.refs_0_
  36.3 0.5 collective-permute-start.12
  36.7 2.3 %collective-permute-start.11 = (bf16[4,64,512]{2,1,0:T(8,128)(2,1)S(1)}, bf16[4,64,512]{2,1,0:T(8,128)(2,1)S(1)}, u32[]{:S(2)}, u32[]{:S(2)}) collective-permute-start(bf16[4,64,512]{2,1,0:T(8,128)(2,1)S(1)} %here.1.refs_0_), channel_id=1, source_target_pairs={{0,96},{1,97},{2,98},{3,99},{4,100},{5,101},{6,102},{7,103},{8,104... | collective-permute-start | bytes 786440 | tf_op jit(solution)/shard_map/ppermute | solution.py:44
  39.0 0.3 collective-permute-start.10
  39.3 3.4 %collective-permute-done.12.refs_3_ = bf16[4,64,512]{2,1,0:T(8,128)(2,1)S(1)} collective-permute-done((bf16[4,64,512]{2,1,0:T(8,128)(2,1)S(1)}, bf16[4,64,512]{2,1,0:T(8,128)(2,1)S(1)}, u32[]{:S(2)}, u32[]{:S(2)}) %collective-permute-start.12) | collective-permute-done | bytes 262176 | tf_op jit(solution)/shard_map/ppermute | solution.py:44
  42.8 2.3 %collective-permute-done.11.refs_2_ = bf16[4,64,512]{2,1,0:T(8,128)(2,1)S(1)} collective-permute-done((bf16[4,64,512]{2,1,0:T(8,128)(2,1)S(1)}, bf16[4,64,512]{2,1,0:T(8,128)(2,1)S(1)}, u32[]{:S(2)}, u32[]{:S(2)}) %collective-permute-start.11) | collective-permute-done | bytes 262176 | tf_op jit(solution)/shard_map/ppermute | solution.py:44
  45.1 2.1 %collective-permute-done.10.refs_1_ = bf16[4,64,512]{2,1,0:T(8,128)(2,1)S(1)} collective-permute-done((bf16[4,64,512]{2,1,0:T(8,128)(2,1)S(1)}, bf16[4,64,512]{2,1,0:T(8,128)(2,1)S(1)}, u32[]{:S(2)}, u32[]{:S(2)}) %collective-permute-start.10) | collective-permute-done | bytes 262176 | tf_op jit(solution)/shard_map/ppermute | solution.py:44
  47.2 0.1 line.1.mine
  47.2 0.0 copy-start.7
  47.3 5.1 %collective-permute-start.13 = (bf16[4,4,64,512]{3,2,1,0:T(8,128)(2,1)S(1)}, bf16[4,4,64,512]{3,2,1,0:T(8,128)(2,1)S(1)}, u32[]{:S(2)}, u32[]{:S(2)}) collective-permute-start(bf16[4,4,64,512]{3,2,1,0:T(8,128)(2,1)S(1)} %line.1.mine), channel_id=1, source_target_pairs={{0,16},{1,17},{2,18},{3,19},{4,20},{5,21},{6,22},{7,23},{8,24},{9,... | collective-permute-start | bytes 3145736 | tf_op jit(solution)/shard_map/ppermute | solution.py:44
  52.3 2.3 %collective-permute-done.13.other = bf16[4,4,64,512]{3,2,1,0:T(8,128)(2,1)S(1)} collective-permute-done((bf16[4,4,64,512]{3,2,1,0:T(8,128)(2,1)S(1)}, bf16[4,4,64,512]{3,2,1,0:T(8,128)(2,1)S(1)}, u32[]{:S(2)}, u32[]{:S(2)}) %collective-permute-start.13) | collective-permute-done | bytes 1048608 | tf_op jit(solution)/shard_map/ppermute | solution.py:44
  54.6 1.3 %step.1.a = bf16[384,512]{1,0:T(8,128)(2,1)S(1)} custom-call(bf16[4,4,64,512]{3,2,1,0:T(8,128)(2,1)S(1)} %line.1.mine, bf16[4,4,64,512]{3,2,1,0:T(8,128)(2,1)S(1)} %collective-permute-done.13.other), custom_call_target="tpu_custom_call" | custom-call | flops 805306368 | bytes 2490368 | tf_op jit(solution)/shard_map/step/pallas_call | solution.py:161
  55.9 0.9 collective-permute-start.16
  56.9 1.8 %collective-permute-start.15 = (bf16[384,512]{1,0:T(8,128)(2,1)S(1)}, bf16[384,512]{1,0:T(8,128)(2,1)S(1)}, u32[]{:S(2)}, u32[]{:S(2)}) collective-permute-start(bf16[384,512]{1,0:T(8,128)(2,1)S(1)} %step.1.a), channel_id=1, source_target_pairs={{0,3},{1,0},{2,1},{3,2},{4,7},{5,4},{6,5},{7,6},{8,11},{9,8},{10,9... | collective-permute-start | bytes 1179656 | tf_op jit(solution)/shard_map/ppermute | solution.py:44
  58.7 0.1 collective-permute-start.14
  58.8 5.4 %collective-permute-done.16.b = bf16[384,512]{1,0:T(8,128)(2,1)S(1)} collective-permute-done((bf16[384,512]{1,0:T(8,128)(2,1)S(1)}, bf16[384,512]{1,0:T(8,128)(2,1)S(1)}, u32[]{:S(2)}, u32[]{:S(2)}) %collective-permute-start.16) | collective-permute-done | bytes 393248 | tf_op jit(solution)/shard_map/ppermute | solution.py:44
  64.1 3.5 %collective-permute-done.15.d = bf16[384,512]{1,0:T(8,128)(2,1)S(1)} collective-permute-done((bf16[384,512]{1,0:T(8,128)(2,1)S(1)}, bf16[384,512]{1,0:T(8,128)(2,1)S(1)}, u32[]{:S(2)}, u32[]{:S(2)}) %collective-permute-start.15) | collective-permute-done | bytes 393248 | tf_op jit(solution)/shard_map/ppermute | solution.py:44
  67.6 0.8 collective-permute-done.14.c
  68.5 0.9 near.1
  69.3 0.9 collective-permute-start.17
  70.3 1.8 %collective-permute-start.19 = (bf16[1216,512]{1,0:T(8,128)(2,1)S(1)}, bf16[1216,512]{1,0:T(8,128)(2,1)S(1)}, u32[]{:S(2)}, u32[]{:S(2)}) collective-permute-start(bf16[1216,512]{1,0:T(8,128)(2,1)S(1)} %get-tuple-element.63), channel_id=1, source_target_pairs={{0,12},{1,13},{2,14},{3,15},{4,0},{5,1},{6,2},{7,3},{8,4},{9,5},{1... | collective-permute-start | bytes 3735560 | tf_op jit(solution)/shard_map/ppermute | solution.py:44
  72.1 14.6 %collective-permute-done.17.refs_1_.refs_2_.one = bf16[1216,512]{1,0:T(8,128)(2,1)S(1)} collective-permute-done((bf16[1216,512]{1,0:T(8,128)(2,1)S(1)}, bf16[1216,512]{1,0:T(8,128)(2,1)S(1)}, u32[]{:S(2)}, u32[]{:S(2)}) %collective-permute-start.17) | collective-permute-done | bytes 1245216 | tf_op jit(solution)/shard_map/ppermute | solution.py:44
  86.7 2.1 %collective-permute-start.22 = (bf16[1216,512]{1,0:T(8,128)(2,1)S(1)}, bf16[1216,512]{1,0:T(8,128)(2,1)S(1)}, u32[]{:S(2)}, u32[]{:S(2)}) collective-permute-start(bf16[1216,512]{1,0:T(8,128)(2,1)S(1)} %collective-permute-done.17.refs_1_.refs_2_.one), channel_id=1, source_target_pairs={{0,16},{1,17},{2,18},{3,19},{4,20},{5,21},{6,22},{7,23},{8,24},{9,... | collective-permute-start | bytes 3735560 | tf_op jit(solution)/shard_map/ppermute | solution.py:44
  88.7 0.0 collective-permute-start.23
  88.7 0.5 collective-permute-start.21
  89.3 1.2 %collective-permute-start.18 = (bf16[576,512]{1,0:T(8,128)(2,1)S(1)}, bf16[576,512]{1,0:T(8,128)(2,1)S(1)}, u32[]{:S(2)}, u32[]{:S(2)}) collective-permute-start(bf16[576,512]{1,0:T(8,128)(2,1)S(1)} %slice.8), channel_id=1, source_target_pairs={{0,4},{1,5},{2,6},{3,7},{4,8},{5,9},{6,10},{7,11},{8,12},{9,13},{1... | collective-permute-start | bytes 1769480 | tf_op jit(solution)/shard_map/ppermute | solution.py:44
  90.5 1.8 %collective-permute-start.20 = (bf16[576,512]{1,0:T(8,128)(2,1)S(1)}, bf16[576,512]{1,0:T(8,128)(2,1)S(1)}, u32[]{:S(2)}, u32[]{:S(2)}) collective-permute-start(bf16[576,512]{1,0:T(8,128)(2,1)S(1)} %slice.9), channel_id=1, source_target_pairs={{0,12},{1,13},{2,14},{3,15},{4,0},{5,1},{6,2},{7,3},{8,4},{9,5},{1... | collective-permute-start | bytes 1769480 | tf_op jit(solution)/shard_map/ppermute | solution.py:44
  92.4 2.4 %collective-permute-done.21.refs_1_ = bf16[1152,512]{1,0:T(8,128)(2,1)S(1)} collective-permute-done((bf16[1152,512]{1,0:T(8,128)(2,1)S(1)}, bf16[1152,512]{1,0:T(8,128)(2,1)S(1)}, u32[]{:S(2)}, u32[]{:S(2)}) %collective-permute-start.21) | collective-permute-done | bytes 1179680 | tf_op jit(solution)/shard_map/ppermute | solution.py:44
  94.8 1.9 %place.3.refs_0_ = bf16[16,512,512]{2,1,0:T(8,128)(2,1)} custom-call(s32[62]{0:T(128)S(1)} %copy-done.7, bf16[1152,512]{1,0:T(8,128)(2,1)S(1)} %get-tuple-element.64.refs_0_.near, bf16[1152,512]{1,0:T(8,128)(2,1)S(1)} %collective-permute-done.21.refs_1_), custom_call_target="tpu_custom_call" | custom-call | bytes 4718592 | tf_op jit(solution)/shard_map/place/pallas_call | solution.py:308
  96.7 1.9 %place.4.refs_0_ = bf16[16,512,512]{2,1,0:T(8,128)(2,1)} custom-call(s32[62]{0:T(128)S(1)} %copy-done.7, bf16[16,512,512]{2,1,0:T(8,128)(2,1)} %place.3.refs_0_, bf16[1216,512]{1,0:T(8,128)(2,1)S(1)} %collective-permute-done.17.refs_1_.refs_2_.one, bf16[1216,512]{1,0:T(8,128)(2,1)S(1)} %collective-permute-done.22.refs_2_.refs_3_), custom_call_target="tpu_custom_call", output_to_operand_aliasing={{}: (1, {})} | custom-call | bytes 4980736 | tf_op jit(solution)/shard_map/place/pallas_call | solution.py:308
  98.7 0.0 copy-start.2
  98.7 0.0 copy-start.3
  98.7 1.9 %place.5.begun = bf16[16,512,512]{2,1,0:T(8,128)(2,1)} custom-call(s32[62]{0:T(128)S(1)} %copy-done.7, bf16[16,512,512]{2,1,0:T(8,128)(2,1)} %place.4.refs_0_, bf16[1216,512]{1,0:T(8,128)(2,1)S(1)} %collective-permute-done.19.refs_1_.refs_4_.three, bf16[1216,512]{1,0:T(8,128)(2,1)S(1)} %collective-permute-done.23.refs_2_.refs_5_), custom_call_target="tpu_custom_call", output_to_operand_aliasing={{}: (1, {})} | custom-call | bytes 4980736 | tf_op jit(solution)/shard_map/place/pallas_call | solution.py:308
  100.6 0.5 collective-permute-start.24
  101.1 0.1 collective-permute-start.25
  101.2 1.6 %stats.1 = (f32[3,64,512]{2,1,0:T(8,128)}, f32[3,64,512]{2,1,0:T(8,128)}) custom-call(s32[62]{0:T(128)S(1)} %copy-done.7, f32[3,64,512]{2,1,0:T(8,128)S(1)} %bitcast.13, f32[3,64,512]{2,1,0:T(8,128)S(1)} %bitcast.14, bf16[1152,512]{1,0:T(8,128)(2,1)S(1)} %get-tuple-element.64.refs_0_.near, bf16[1216,512]{1,0:T(8,128)(2,1)S(1)} %collective-permute-done.17.refs_1_.refs_2_.one, ...), custom_call_target="tpu_custom_call" | custom-call | bytes 6422776 | tf_op jit(solution)/shard_map/stats/pallas_call | solution.py:161
  102.9 0.7 collective-permute-done.25.refs_9_
  103.6 2.7 %finish.1 = (bf16[16,512,512]{2,1,0:T(8,128)(2,1)}, f32[3,64,512]{2,1,0:T(8,128)}) custom-call(s32[62]{0:T(128)S(1)} %copy-done.7, bf16[16,512,512]{2,1,0:T(8,128)(2,1)} %place.5.begun, f32[3,64,512]{2,1,0:T(8,128)S(1)} %bitcast.10, bf16[1152,512]{1,0:T(8,128)(2,1)S(1)} %get-tuple-element.64.refs_0_.near, ...), custom_call_target="tpu_custom_call", output_to_operand_aliasing={{0}: (1, {})} | custom-call | bytes 9699328 | tf_op jit(solution)/shard_map/finish/pallas_call | solution.py:450
  (20 shorter events, 0.2 us)
Async XLA Ops:
  0.6 8.7 %copy-start = (f32[1,3,64,512]{3,2,1,0:T(8,128)S(1)}, f32[1,3,64,512]{3,2,1,0:T(8,128)}, u32[]{:S(2)}) copy-start(f32[1,3,64,512]{3,2,1,0:T(8,128)} %param.15) | copy-start | bytes 1179652
  0.6 3.2 %collective-permute-start = (bf16[512,512]{1,0:T(8,128)(2,1)}, bf16[512,512]{1,0:T(8,128)(2,1)S(1)}, u32[]{:S(2)}, u32[]{:S(2)}) collective-permute-start(bf16[512,512]{1,0:T(8,128)(2,1)} %bitcast.11), channel_id=1, source_target_pairs={{0,16},{1,17},{2,18},{3,19},{4,20},{5,21},{6,22},{7,23},{8,24},{9,... | collective-permute-start | bytes 1572872 | tf_op jit(solution)/shard_map/ppermute | solution.py:44
  3.9 1.0 copy-start.1
  4.9 4.4 %copy-start.4 = (f32[1,3,64,512]{3,2,1,0:T(8,128)S(1)}, f32[1,3,64,512]{3,2,1,0:T(8,128)}, u32[]{:S(2)}) copy-start(f32[1,3,64,512]{3,2,1,0:T(8,128)} %param.13) | copy-start | bytes 1179652
  5.0 6.7 %collective-permute-start.1 = (bf16[64,512]{1,0:T(8,128)(2,1)S(1)}, bf16[64,512]{1,0:T(8,128)(2,1)S(1)}, u32[]{:S(2)}, u32[]{:S(2)}) collective-permute-start(bf16[64,512]{1,0:T(8,128)(2,1)S(1)} %get-tuple-element.44), channel_id=1, source_target_pairs={{0,32},{1,33},{2,34},{3,35},{4,36},{5,37},{6,38},{7,39},{8,40},{9,... | collective-permute-start | bytes 196616 | tf_op jit(solution)/shard_map/ppermute | solution.py:44
  6.4 5.3 %collective-permute-start.2 = (bf16[64,512]{1,0:T(8,128)(2,1)S(1)}, bf16[64,512]{1,0:T(8,128)(2,1)S(1)}, u32[]{:S(2)}, u32[]{:S(2)}) collective-permute-start(bf16[64,512]{1,0:T(8,128)(2,1)S(1)} %get-tuple-element.45), channel_id=1, source_target_pairs={{0,96},{1,97},{2,98},{3,99},{4,100},{5,101},{6,102},{7,103},{8,104... | collective-permute-start | bytes 196616 | tf_op jit(solution)/shard_map/ppermute | solution.py:44
  7.7 4.6 %collective-permute-start.3 = (bf16[64,512]{1,0:T(8,128)(2,1)S(1)}, bf16[64,512]{1,0:T(8,128)(2,1)S(1)}, u32[]{:S(2)}, u32[]{:S(2)}) collective-permute-start(bf16[64,512]{1,0:T(8,128)(2,1)S(1)} %get-tuple-element.46), channel_id=1, source_target_pairs={{0,64},{1,65},{2,66},{3,67},{4,68},{5,69},{6,70},{7,71},{8,72},{9,... | collective-permute-start | bytes 196616 | tf_op jit(solution)/shard_map/ppermute | solution.py:44
  9.4 1.0 copy-start.5
  10.4 0.7 copy-start.6
  12.4 8.0 %collective-permute-start.4 = (bf16[4,64,512]{2,1,0:T(8,128)(2,1)S(1)}, bf16[4,64,512]{2,1,0:T(8,128)(2,1)S(1)}, u32[]{:S(2)}, u32[]{:S(2)}) collective-permute-start(bf16[4,64,512]{2,1,0:T(8,128)(2,1)S(1)} %get-tuple-element.55), channel_id=1, source_target_pairs={{0,1},{1,2},{2,3},{3,0},{4,5},{5,6},{6,7},{7,4},{8,9},{9,10},{10,1... | collective-permute-start | bytes 786440 | tf_op jit(solution)/shard_map/ppermute | solution.py:44
  14.2 8.3 %collective-permute-start.5 = (bf16[4,64,512]{2,1,0:T(8,128)(2,1)S(1)}, bf16[4,64,512]{2,1,0:T(8,128)(2,1)S(1)}, u32[]{:S(2)}, u32[]{:S(2)}) collective-permute-start(bf16[4,64,512]{2,1,0:T(8,128)(2,1)S(1)} %get-tuple-element.56), channel_id=1, source_target_pairs={{0,3},{1,0},{2,1},{3,2},{4,7},{5,4},{6,5},{7,6},{8,11},{9,8},{10,9... | collective-permute-start | bytes 786440 | tf_op jit(solution)/shard_map/ppermute | solution.py:44
  16.4 8.0 %collective-permute-start.6 = (bf16[4,64,512]{2,1,0:T(8,128)(2,1)S(1)}, bf16[4,64,512]{2,1,0:T(8,128)(2,1)S(1)}, u32[]{:S(2)}, u32[]{:S(2)}) collective-permute-start(bf16[4,64,512]{2,1,0:T(8,128)(2,1)S(1)} %get-tuple-element.57), channel_id=1, source_target_pairs={{0,2},{1,3},{2,0},{3,1},{4,6},{5,7},{6,4},{7,5},{8,10},{9,11},{10,... | collective-permute-start | bytes 786440 | tf_op jit(solution)/shard_map/ppermute | solution.py:44
  25.1 6.6 %collective-permute-start.7 = (bf16[4,64,512]{2,1,0:T(8,128)(2,1)S(1)}, bf16[4,64,512]{2,1,0:T(8,128)(2,1)S(1)}, u32[]{:S(2)}, u32[]{:S(2)}) collective-permute-start(bf16[4,64,512]{2,1,0:T(8,128)(2,1)S(1)} %get-tuple-element.59), channel_id=1, source_target_pairs={{0,4},{1,5},{2,6},{3,7},{4,8},{5,9},{6,10},{7,11},{8,12},{9,13},{1... | collective-permute-start | bytes 786440 | tf_op jit(solution)/shard_map/ppermute | solution.py:44
  26.2 7.9 %collective-permute-start.8 = (bf16[4,64,512]{2,1,0:T(8,128)(2,1)S(1)}, bf16[4,64,512]{2,1,0:T(8,128)(2,1)S(1)}, u32[]{:S(2)}, u32[]{:S(2)}) collective-permute-start(bf16[4,64,512]{2,1,0:T(8,128)(2,1)S(1)} %get-tuple-element.60), channel_id=1, source_target_pairs={{0,12},{1,13},{2,14},{3,15},{4,0},{5,1},{6,2},{7,3},{8,4},{9,5},{1... | collective-permute-start | bytes 786440 | tf_op jit(solution)/shard_map/ppermute | solution.py:44
  28.0 7.7 %collective-permute-start.9 = (bf16[4,64,512]{2,1,0:T(8,128)(2,1)S(1)}, bf16[4,64,512]{2,1,0:T(8,128)(2,1)S(1)}, u32[]{:S(2)}, u32[]{:S(2)}) collective-permute-start(bf16[4,64,512]{2,1,0:T(8,128)(2,1)S(1)} %get-tuple-element.61), channel_id=1, source_target_pairs={{0,8},{1,9},{2,10},{3,11},{4,12},{5,13},{6,14},{7,15},{8,0},{9,1},... | collective-permute-start | bytes 786440 | tf_op jit(solution)/shard_map/ppermute | solution.py:44
  36.3 6.5 %collective-permute-start.12 = (bf16[4,64,512]{2,1,0:T(8,128)(2,1)S(1)}, bf16[4,64,512]{2,1,0:T(8,128)(2,1)S(1)}, u32[]{:S(2)}, u32[]{:S(2)}) collective-permute-start(bf16[4,64,512]{2,1,0:T(8,128)(2,1)S(1)} %here.1.refs_0_), channel_id=1, source_target_pairs={{0,32},{1,33},{2,34},{3,35},{4,36},{5,37},{6,38},{7,39},{8,40},{9,... | collective-permute-start | bytes 786440 | tf_op jit(solution)/shard_map/ppermute | solution.py:44
  36.7 8.3 %collective-permute-start.11 = (bf16[4,64,512]{2,1,0:T(8,128)(2,1)S(1)}, bf16[4,64,512]{2,1,0:T(8,128)(2,1)S(1)}, u32[]{:S(2)}, u32[]{:S(2)}) collective-permute-start(bf16[4,64,512]{2,1,0:T(8,128)(2,1)S(1)} %here.1.refs_0_), channel_id=1, source_target_pairs={{0,96},{1,97},{2,98},{3,99},{4,100},{5,101},{6,102},{7,103},{8,104... | collective-permute-start | bytes 786440 | tf_op jit(solution)/shard_map/ppermute | solution.py:44
  39.0 8.1 %collective-permute-start.10 = (bf16[4,64,512]{2,1,0:T(8,128)(2,1)S(1)}, bf16[4,64,512]{2,1,0:T(8,128)(2,1)S(1)}, u32[]{:S(2)}, u32[]{:S(2)}) collective-permute-start(bf16[4,64,512]{2,1,0:T(8,128)(2,1)S(1)} %here.1.refs_0_), channel_id=1, source_target_pairs={{0,64},{1,65},{2,66},{3,67},{4,68},{5,69},{6,70},{7,71},{8,72},{9,... | collective-permute-start | bytes 786440 | tf_op jit(solution)/shard_map/ppermute | solution.py:44
  47.2 21.2 %copy-start.7 = (s32[62]{0:T(128)S(1)}, s32[62]{0:T(128)}, u32[]{:S(2)}) copy-start(s32[62]{0:T(128)} %choices.1.spot) | copy-start | bytes 748
  47.3 7.4 %collective-permute-start.13 = (bf16[4,4,64,512]{3,2,1,0:T(8,128)(2,1)S(1)}, bf16[4,4,64,512]{3,2,1,0:T(8,128)(2,1)S(1)}, u32[]{:S(2)}, u32[]{:S(2)}) collective-permute-start(bf16[4,4,64,512]{3,2,1,0:T(8,128)(2,1)S(1)} %line.1.mine), channel_id=1, source_target_pairs={{0,16},{1,17},{2,18},{3,19},{4,20},{5,21},{6,22},{7,23},{8,24},{9,... | collective-permute-start | bytes 3145736 | tf_op jit(solution)/shard_map/ppermute | solution.py:44
  55.9 8.2 %collective-permute-start.16 = (bf16[384,512]{1,0:T(8,128)(2,1)S(1)}, bf16[384,512]{1,0:T(8,128)(2,1)S(1)}, u32[]{:S(2)}, u32[]{:S(2)}) collective-permute-start(bf16[384,512]{1,0:T(8,128)(2,1)S(1)} %step.1.a), channel_id=1, source_target_pairs={{0,1},{1,2},{2,3},{3,0},{4,5},{5,6},{6,7},{7,4},{8,9},{9,10},{10,1... | collective-permute-start | bytes 1179656 | tf_op jit(solution)/shard_map/ppermute | solution.py:44
  56.9 10.8 %collective-permute-start.15 = (bf16[384,512]{1,0:T(8,128)(2,1)S(1)}, bf16[384,512]{1,0:T(8,128)(2,1)S(1)}, u32[]{:S(2)}, u32[]{:S(2)}) collective-permute-start(bf16[384,512]{1,0:T(8,128)(2,1)S(1)} %step.1.a), channel_id=1, source_target_pairs={{0,3},{1,0},{2,1},{3,2},{4,7},{5,4},{6,5},{7,6},{8,11},{9,8},{10,9... | collective-permute-start | bytes 1179656 | tf_op jit(solution)/shard_map/ppermute | solution.py:44
  58.7 9.8 %collective-permute-start.14 = (bf16[384,512]{1,0:T(8,128)(2,1)S(1)}, bf16[384,512]{1,0:T(8,128)(2,1)S(1)}, u32[]{:S(2)}, u32[]{:S(2)}) collective-permute-start(bf16[384,512]{1,0:T(8,128)(2,1)S(1)} %step.1.a), channel_id=1, source_target_pairs={{0,2},{1,3},{2,0},{3,1},{4,6},{5,7},{6,4},{7,5},{8,10},{9,11},{10,... | collective-permute-start | bytes 1179656 | tf_op jit(solution)/shard_map/ppermute | solution.py:44
  69.3 17.3 %collective-permute-start.17 = (bf16[1216,512]{1,0:T(8,128)(2,1)S(1)}, bf16[1216,512]{1,0:T(8,128)(2,1)S(1)}, u32[]{:S(2)}, u32[]{:S(2)}) collective-permute-start(bf16[1216,512]{1,0:T(8,128)(2,1)S(1)} %get-tuple-element.62), channel_id=1, source_target_pairs={{0,4},{1,5},{2,6},{3,7},{4,8},{5,9},{6,10},{7,11},{8,12},{9,13},{1... | collective-permute-start | bytes 3735560 | tf_op jit(solution)/shard_map/ppermute | solution.py:44
  70.3 18.5 %collective-permute-start.19 = (bf16[1216,512]{1,0:T(8,128)(2,1)S(1)}, bf16[1216,512]{1,0:T(8,128)(2,1)S(1)}, u32[]{:S(2)}, u32[]{:S(2)}) collective-permute-start(bf16[1216,512]{1,0:T(8,128)(2,1)S(1)} %get-tuple-element.63), channel_id=1, source_target_pairs={{0,12},{1,13},{2,14},{3,15},{4,0},{5,1},{6,2},{7,3},{8,4},{9,5},{1... | collective-permute-start | bytes 3735560 | tf_op jit(solution)/shard_map/ppermute | solution.py:44
  86.7 10.0 %collective-permute-start.22 = (bf16[1216,512]{1,0:T(8,128)(2,1)S(1)}, bf16[1216,512]{1,0:T(8,128)(2,1)S(1)}, u32[]{:S(2)}, u32[]{:S(2)}) collective-permute-start(bf16[1216,512]{1,0:T(8,128)(2,1)S(1)} %collective-permute-done.17.refs_1_.refs_2_.one), channel_id=1, source_target_pairs={{0,16},{1,17},{2,18},{3,19},{4,20},{5,21},{6,22},{7,23},{8,24},{9,... | collective-permute-start | bytes 3735560 | tf_op jit(solution)/shard_map/ppermute | solution.py:44
  88.7 9.9 %collective-permute-start.23 = (bf16[1216,512]{1,0:T(8,128)(2,1)S(1)}, bf16[1216,512]{1,0:T(8,128)(2,1)S(1)}, u32[]{:S(2)}, u32[]{:S(2)}) collective-permute-start(bf16[1216,512]{1,0:T(8,128)(2,1)S(1)} %collective-permute-done.19.refs_1_.refs_4_.three), channel_id=1, source_target_pairs={{0,16},{1,17},{2,18},{3,19},{4,20},{5,21},{6,22},{7,23},{8,24},{9,... | collective-permute-start | bytes 3735560 | tf_op jit(solution)/shard_map/ppermute | solution.py:44
  88.7 6.0 %collective-permute-start.21 = (bf16[1152,512]{1,0:T(8,128)(2,1)S(1)}, bf16[1152,512]{1,0:T(8,128)(2,1)S(1)}, u32[]{:S(2)}, u32[]{:S(2)}) collective-permute-start(bf16[1152,512]{1,0:T(8,128)(2,1)S(1)} %get-tuple-element.64.refs_0_.near), channel_id=1, source_target_pairs={{0,16},{1,17},{2,18},{3,19},{4,20},{5,21},{6,22},{7,23},{8,24},{9,... | collective-permute-start | bytes 3538952 | tf_op jit(solution)/shard_map/ppermute | solution.py:44
  89.3 11.3 %collective-permute-start.18 = (bf16[576,512]{1,0:T(8,128)(2,1)S(1)}, bf16[576,512]{1,0:T(8,128)(2,1)S(1)}, u32[]{:S(2)}, u32[]{:S(2)}) collective-permute-start(bf16[576,512]{1,0:T(8,128)(2,1)S(1)} %slice.8), channel_id=1, source_target_pairs={{0,4},{1,5},{2,6},{3,7},{4,8},{5,9},{6,10},{7,11},{8,12},{9,13},{1... | collective-permute-start | bytes 1769480 | tf_op jit(solution)/shard_map/ppermute | solution.py:44
  90.5 10.1 %collective-permute-start.20 = (bf16[576,512]{1,0:T(8,128)(2,1)S(1)}, bf16[576,512]{1,0:T(8,128)(2,1)S(1)}, u32[]{:S(2)}, u32[]{:S(2)}) collective-permute-start(bf16[576,512]{1,0:T(8,128)(2,1)S(1)} %slice.9), channel_id=1, source_target_pairs={{0,12},{1,13},{2,14},{3,15},{4,0},{5,1},{6,2},{7,3},{8,4},{9,5},{1... | collective-permute-start | bytes 1769480 | tf_op jit(solution)/shard_map/ppermute | solution.py:44
  98.7 2.6 %copy-start.2 = (f32[1,3,64,512]{3,2,1,0:T(8,128)S(1)}, f32[1,3,64,512]{3,2,1,0:T(8,128)}, u32[]{:S(2)}) copy-start(f32[1,3,64,512]{3,2,1,0:T(8,128)} %param.11) | copy-start | bytes 1179652
  98.7 2.6 %copy-start.3 = (f32[1,3,64,512]{3,2,1,0:T(8,128)S(1)}, f32[1,3,64,512]{3,2,1,0:T(8,128)}, u32[]{:S(2)}) copy-start(f32[1,3,64,512]{3,2,1,0:T(8,128)} %param.12) | copy-start | bytes 1179652
  100.6 2.2 %collective-permute-start.24 = (bf16[576,512]{1,0:T(8,128)(2,1)S(1)}, bf16[576,512]{1,0:T(8,128)(2,1)S(1)}, u32[]{:S(2)}, u32[]{:S(2)}) collective-permute-start(bf16[576,512]{1,0:T(8,128)(2,1)S(1)} %collective-permute-done.18.refs_6_.low), channel_id=1, source_target_pairs={{0,16},{1,17},{2,18},{3,19},{4,20},{5,21},{6,22},{7,23},{8,24},{9,... | collective-permute-start | bytes 1769480 | tf_op jit(solution)/shard_map/ppermute | solution.py:44
  101.1 2.5 %collective-permute-start.25 = (bf16[576,512]{1,0:T(8,128)(2,1)S(1)}, bf16[576,512]{1,0:T(8,128)(2,1)S(1)}, u32[]{:S(2)}, u32[]{:S(2)}) collective-permute-start(bf16[576,512]{1,0:T(8,128)(2,1)S(1)} %collective-permute-done.20.refs_7_.high), channel_id=1, source_target_pairs={{0,16},{1,17},{2,18},{3,19},{4,20},{5,21},{6,22},{7,23},{8,24},{9,... | collective-permute-start | bytes 1769480 | tf_op jit(solution)/shard_map/ppermute | solution.py:44

commit v4 on v3

v4 whole, which is shorter than its diff:
```python
import functools

import jax
import jax.numpy as jnp
from jax import lax
from jax.experimental import pallas as pl
from jax.experimental.pallas import tpu as pltpu
from jax.sharding import PartitionSpec as P

decay_stats = 0.95
decay_moment = 0.9
epsilon = 1e-06

AXES = ("dp", "group")
X, CORES, SIDE, SLOTS = 4, 2, 4, 3
BLOCKS = SIDE * SIDE
BS = 512
ROWS = BS // (X * CORES)
HALF = BS // CORES
NEAR = SIDE * HALF
half_type = jnp.bfloat16
wide_type = jnp.float32

SMEM = pl.BlockSpec(memory_space=pltpu.SMEM)
VMEM = pl.BlockSpec(memory_space=pltpu.VMEM)
ANY = pl.BlockSpec(memory_space=pl.ANY)

GRAD_PICK, GRAD_LAST, ROOT_PICK, ROOT_LAST, TERM_PICK, TILES = 0, 4, 5, 9, 10, 14
SLOT_PICK, TERM_LAST, SLOT_LIVE, SLOT_FROM, SLOT_ROW = 14, 18, 21, 24, 27
LANDING = 30
CHOICES = LANDING + 32


def permute(value, target):
    pairs = []
    for x in range(X):
        for c in range(CORES):
            for z in range(SIDE):
                for y in range(SIDE):
                    tx, tc, tz, ty = target(x, c, z, y)
                    pairs.append(
                        ((x * 2 + c) * 16 + z * 4 + y, ((tx % 4) * 2 + tc) * 16 + (tz % 4) * 4 + ty % 4)
                    )
    return lax.ppermute(value, AXES, pairs)


def to_core(value):
    return permute(value, lambda x, c, z, y: (x, 1 - c, z, y))


def to_x(value, k):
    return permute(value, lambda x, c, z, y: (x + k, c, z, y))


def to_u(value, k):
    return permute(value, lambda x, c, z, y: (x, c, z, y + k) if c == 0 else (x, c, z + k, y))


def to_v(value, k):
    return permute(value, lambda x, c, z, y: (x, c, z + k, y) if c == 0 else (x, c, z, y + k))


def along(send, values, shifts=(1, 3, 2)):
    return [values[0]] + [send(values[k], k) for k in shifts]


def position():
    dp, me = lax.axis_index("dp"), lax.axis_index("group")
    return dp >> 1, dp & 1, me >> 2, me & 3


def choice_kernel(order_ref, count_ref, out, tiles, start_ref, owner_ref):
    x, c, z, y = position()
    me = z * 4 + y
    first = c == 0
    u, v = jnp.where(first, y, z), jnp.where(first, z, y)

    def place_at(uu, vv):
        yy, zz = jnp.where(first, uu, vv), jnp.where(first, vv, uu)
        return 4 * ((zz - yy) & 3) + yy

    def uv_of_member(g):
        yy, zz = g & 3, g >> 2
        return jnp.where(first, yy, zz), jnp.where(first, zz, yy)

    def uv_of_place(q):
        yy = q & 3
        zz = (yy + (q >> 2)) & 3
        return jnp.where(first, yy, zz), jnp.where(first, zz, yy)

    place = jnp.int32(0)
    for o in range(BLOCKS):
        start_ref[o] = place
        for s in range(SLOTS):

            @pl.when(s < count_ref[o])
            def _():
                owner_ref[start_ref[o] + s] = o

        place = place + count_ref[o]

    for k in range(4):
        q = place_at(u, (v + k) & 3)
        block = order_ref[q]
        bu, bv = uv_of_member(block)
        out[GRAD_PICK + k] = (u - bu) & 3
        ou, ov = uv_of_member(owner_ref[q])
        out[ROOT_PICK + k] = (u - ou) & 3
        if k == 0:
            out[GRAD_LAST] = (v - bv) & 3
            out[ROOT_LAST] = (v - ov) & 3
    my_start, my_count = start_ref[me], count_ref[me]
    slot_u = []
    for s in range(SLOTS):
        q = jnp.minimum(my_start + s, BLOCKS - 1)
        su, sv = uv_of_place(q)
        slot_u.append(su)
        out[TERM_LAST + s] = (v - sv) & 3
        out[SLOT_LIVE + s] = (s < my_count).astype(jnp.int32)
        out[SLOT_FROM + s] = jnp.where(s < my_count, (v - sv) & 3, 8)
        out[SLOT_ROW + s] = (u - su) & 3
    for k in range(4):
        far = (u + k) & 3
        chosen = jnp.int32(0)
        for s in range(SLOTS):
            chosen = jnp.where((s < my_count) & (slot_u[s] == far), s, chosen)
        out[SLOT_PICK + k] = chosen
        far = (v + k) & 3
        member = jnp.where(first, 4 * far + u, 4 * u + far)
        chosen = jnp.int32(0)
        for s in range(SLOTS):
            fu, fv = uv_of_place(start_ref[member] + s)
            chosen = jnp.where((s < count_ref[member]) & (fv == v), (u - fu) & 3, chosen)
        out[TERM_PICK + k] = chosen
    for k in range(4):
        for j in range(4):
            out[LANDING + k * 4 + j] = order_ref[place_at((u - j) & 3, (v - k) & 3)]
            out[LANDING + 16 + k * 4 + j] = order_ref[place_at((u - k) & 3, (v - j) & 3)]
    for n in range(TILES):
        tiles[n] = jnp.full((16, BS), out[n].astype(wide_type), wide_type).astype(half_type)


def choices(block_order, owner_count):
    return pl.pallas_call(
        choice_kernel,
        out_shape=[
            jax.ShapeDtypeStruct((CHOICES,), jnp.int32),
            jax.ShapeDtypeStruct((TILES, 16, BS), half_type),
        ],
        in_specs=[SMEM, SMEM],
        out_specs=[SMEM, VMEM],
        scratch_shapes=[pltpu.SMEM((BLOCKS,), jnp.int32), pltpu.SMEM((BLOCKS,), jnp.int32)],
        cost_estimate=pl.CostEstimate(flops=0, bytes_accessed=4 << 20, transcendentals=0),
        name="choices",
    )(block_order, owner_count)


def cost(flops, *arrays):
    moved = sum(a.size * a.dtype.itemsize for a in arrays)
    return pl.CostEstimate(flops=flops, bytes_accessed=moved, transcendentals=0)


def small_call(body, outs, name, *args, aliases=None, flops=0, scratch=()):
    return pl.pallas_call(
        body,
        out_shape=outs,
        in_specs=[SMEM if a.dtype == jnp.int32 else VMEM for a in args],
        out_specs=jax.tree.map(lambda _: VMEM, outs),
        scratch_shapes=scratch,
        input_output_aliases=aliases or {},
        compiler_params=pltpu.CompilerParams(vmem_limit_bytes=12 << 20),
        cost_estimate=cost(flops, *args, *jax.tree.leaves(outs)),
        name=name,
    )(*args)


def blend(choice, options):
    rows = options[0].shape[0]
    parts = [option.reshape(rows // 16, 16, BS) for option in options]
    out = parts[3]
    for n in (2, 1, 0):
        out = jnp.where(choice[None] == n, parts[n], out)
    return out.reshape(rows, BS)


def half_kernel(given, out):
    c = position()[1]
    out[...] = given[pl.ds(pl.multiple_of(c * HALF, HALF), HALF), :]


def pair_kernel(mine, theirs, own, *sends):
    x, c, _, _ = position()
    for k in range(4):
        row = ((x + k) & 3) * ROWS
        at = pl.ds(pl.multiple_of(row, ROWS), ROWS)
        far = pl.ds(pl.multiple_of(c * HALF + row, ROWS), ROWS)
        both = mine[at, :].astype(wide_type) + theirs[far, :].astype(wide_type)
        if k == 0:
            own[...] = both
        else:
            sends[k - 1][...] = both.astype(half_type)


def pack_kernel(spot, left, right, moment, *outs):
    for k, out in enumerate(outs):
        slot = spot[SLOT_PICK + k]
        out[0] = left[slot].astype(half_type)
        out[1] = right[slot].astype(half_type)
        out[2] = moment[slot].astype(half_type)


def total_kernel(own, a, c, b, *packs):
    total = own[...] + a[...].astype(wide_type)
    total = total + b[...].astype(wide_type)
    total = (total + c[...].astype(wide_type)).astype(half_type)
    for out in packs[4:]:
        out[3] = total


def turn_kernel(tiles, a, b, d, c, *outs):
    for n in range(4):
        options = [source[n] for source in (a, b, c, d)]
        base = GRAD_PICK if n == 3 else ROOT_PICK
        for k, out in enumerate(outs):
            out[n] = blend(tiles[base + k], options)


def here_kernel(tiles, a, b, d, c, out):
    for n in range(4):
        options = [source[n] for source in (a, b, c, d)]
        out[n] = blend(tiles[GRAD_LAST if n == 3 else ROOT_LAST], options)


def line_kernel(*refs):
    shared, moment = refs[4:]
    x = position()[0]
    for i, k in enumerate((0, 2, 3, 1)):
        n = (x - k) & 3
        shared[n, 0] = refs[i][0]
        shared[n, 1] = refs[i][1]
        shared[n, 2] = refs[i][3]
        moment[n] = refs[i][2]


def step_kernel(mine, moment, other, out, grad, full, held):
    x, c, _, _ = position()
    for n in range(X):
        for core, source in ((c, mine), (1 - c, other)):
            rows = pl.ds(pl.multiple_of((2 * n + core) * ROWS, ROWS), ROWS)
            for which in range(2):
                full[which, rows, :] = source[n, which]
            grad[pl.ds(pl.multiple_of(core * HALF + n * ROWS, ROWS), ROWS), :] = source[n, 2]
    g = grad[...]
    wide = g.astype(wide_type)
    grad_square = jnp.sum(wide * wide)
    precond = jnp.dot(full[0], g, preferred_element_type=wide_type).astype(half_type)
    held[...] = jnp.dot(precond, full[1], preferred_element_type=wide_type)
    dir_square = jnp.sum(held[...] * held[...])
    entries = float(BS * BS)
    top = jnp.sqrt(jnp.full((1, BS), grad_square / entries, wide_type))
    graft = top / jnp.sqrt(jnp.full((1, BS), dir_square / entries + epsilon, wide_type))
    for n in range(X):
        rows = pl.ds(pl.multiple_of((2 * n + c) * ROWS, ROWS), ROWS)
        fresh = decay_moment * moment[n].astype(wide_type) + graft * held[rows, :]
        out[n] = fresh.astype(half_type)
    rows = grad[pl.ds(pl.multiple_of((2 * x + c) * ROWS, ROWS), ROWS), :]
    out[4] = lax.dot_general(
        rows, g, (((1,), (1,)), ((), ())), preferred_element_type=wide_type
    ).astype(half_type)
    columns = grad[:, pl.ds(pl.multiple_of(x * 2 * ROWS, 2 * ROWS), 2 * ROWS)]
    held[: 2 * ROWS, :] = lax.dot_general(
        columns, g, (((0,), (0,)), ((), ())), preferred_element_type=wide_type
    )
    out[5] = held[pl.ds(pl.multiple_of(c * ROWS, ROWS), ROWS), :].astype(half_type)


def near_kernel(tiles, a, c, d, b, near, ahead, back):
    sources = (a, b, c, d)
    for out, first in ((near, 0), (ahead, 1), (back, 0)):
        for j, source in enumerate(sources):
            out[first + j * 4 : first + j * 4 + 4] = source[:4]
    left = [source[4] for source in sources]
    right = [source[5] for source in sources]
    for k, out, first in ((0, near, 16), (1, ahead, 17), (3, back, 17)):
        out[first] = blend(tiles[TERM_PICK + k], left)
        out[first + 1] = blend(tiles[TERM_PICK + k], right)
    ahead[0] = blend(tiles[TERM_PICK + 2], left)
    back[16] = blend(tiles[TERM_PICK + 2], right)


def placed_copies(spot, sources, out, sems):
    _, c, _, _ = position()
    copies = []
    for which, first, count, skip, source in sources:
        half = c if which < 4 else 1 - c
        for j in range(count):
            copies.append(
                pltpu.make_async_copy(
                    source.at[pl.ds(skip + j * 4, 4)],
                    out.at[spot[LANDING + which * 4 + first + j], :, half],
                    sems.at[len(copies)],
                )
            )
    return copies


def place_kernel(which, spot, *refs):
    mine, other, out, sems = refs[-4:]
    skip = 1 if which == 1 else 0
    sources = ((which, 0, 4, skip, mine), (which + 4, 0, 4, skip, other))
    copies = placed_copies(spot, sources, out, sems)
    for copy in copies:
        copy.start()
    for copy in copies:
        copy.wait()


def place(which, spot, begun, mine, other):
    given = [mine, other] if begun is None else [begun, mine, other]
    return pl.pallas_call(
        functools.partial(place_kernel, which),
        out_shape=jax.ShapeDtypeStruct((BLOCKS, X, CORES, ROWS, BS), half_type),
        in_specs=[SMEM] + [ANY] * (len(given) - 2) + [VMEM] * 2,
        out_specs=ANY,
        scratch_shapes=[pltpu.SemaphoreType.DMA((8,))],
        input_output_aliases={} if begun is None else {1: 0},
        compiler_params=pltpu.CompilerParams(vmem_limit_bytes=4 << 20),
        cost_estimate=cost(0, mine, other, mine, other),
        name="place",
    )(spot, *given)


def finish_kernel(spot, begun, moment, near, one, three, low, high, low_other, high_other, *refs):
    del begun
    out, out_moment, fresh, sems, more = refs
    sources = ((2, 0, 2, 1, low), (2, 2, 2, 0, high))
    sources += ((6, 0, 2, 1, low_other), (6, 2, 2, 0, high_other))
    copies = placed_copies(spot, sources, out, sems)
    for copy in copies:
        copy.start()
    x = position()[0]
    parts = ((0, 0, 4, 0, near), (1, 0, 4, 1, one), (3, 0, 4, 0, three)) + sources[:2]
    for s in range(SLOTS):
        fresh[s] = moment[s]
        came, place = spot[SLOT_FROM + s], spot[SLOT_ROW + s]
        for which, first, count, skip, source in parts:

            @pl.when((came == which) & (place >= first) & (place < first + count))
            def _():
                fresh[s] = source[skip + (place - first) * 4 + x].astype(wide_type)

        copy = pltpu.make_async_copy(fresh.at[s], out_moment.at[s], more.at[s])
        copy.start()
        copies.append(copy)
    for copy in copies:
        copy.wait()


def stats_kernel(spot, left, right, near, one, low, high, three, out_left, out_right):
    terms = ((near, 16, near, 17), (one, 17, one, 18), (low, 0, high, 8), (three, 17, three, 18))
    for s in range(SLOTS):
        out_left[s] = left[s]
        out_right[s] = right[s]
        for n, (left_from, m, right_from, r) in enumerate(terms):

            @pl.when((spot[SLOT_LIVE + s] == 1) & (spot[TERM_LAST + s] == n))
            def _():
                new = left_from[m].astype(wide_type)
                out_left[s] = decay_stats * left[s] + (1.0 - decay_stats) * new
                new = right_from[r].astype(wide_type)
                out_right[s] = decay_stats * right[s] + (1.0 - decay_stats) * new


def local(
    gradients, block_order, owner_count, stat_left, stat_right, root_left, root_right, momentum
):
    chunk_type = jax.ShapeDtypeStruct((ROWS, BS), half_type)
    pack_type = jax.ShapeDtypeStruct((4, ROWS, BS), half_type)
    stat_type = jax.ShapeDtypeStruct((SLOTS, ROWS, BS), wide_type)
    hold = lax.optimization_barrier

    mine = gradients[0, 0]
    theirs = to_core(mine)
    mine = small_call(half_kernel, jax.ShapeDtypeStruct((HALF, BS), half_type), "half", mine)
    mine, theirs = hold((mine, theirs))
    own, *sends = small_call(
        pair_kernel,
        [jax.ShapeDtypeStruct((ROWS, BS), wide_type)] + [chunk_type] * 3,
        "pair",
        mine,
        theirs,
    )
    sends, order, count, left, right, moment = hold(
        (sends, block_order, owner_count, root_left[0], root_right[0], momentum[0])
    )
    spot, tiles = choices(order, count)
    packs = small_call(pack_kernel, [pack_type] * 4, "packs", spot, left, right, moment)
    got = along(to_x, [own] + sends)

    packs = small_call(
        total_kernel, [pack_type] * 4, "total", *got, *packs, aliases={4: 0, 5: 1, 6: 2, 7: 3}
    )
    row = along(to_u, packs)
    column = along(to_v, small_call(turn_kernel, [pack_type] * 4, "turn", tiles, *row))
    pack = small_call(here_kernel, pack_type, "here", tiles, *column)
    shared, moment = small_call(
        line_kernel,
        [
            jax.ShapeDtypeStruct((X, 3, ROWS, BS), half_type),
            jax.ShapeDtypeStruct((X, ROWS, BS), half_type),
        ],
        "line",
        *along(to_x, [pack] * 4, (2, 3, 1)),
    )
    send = small_call(
        step_kernel,
        jax.ShapeDtypeStruct((6, ROWS, BS), half_type),
        "step",
        shared,
        moment,
        to_core(shared),
        flops=6 * BS**3,
        scratch=[
            pltpu.VMEM((BS, BS), half_type),
            pltpu.VMEM((2, BS, BS), half_type),
            pltpu.VMEM((BS, BS), wide_type),
        ],
    )

    row = along(to_u, [send] * 4, (2, 3, 1))
    near_type = jax.ShapeDtypeStruct((18, ROWS, BS), half_type)
    sent_type = jax.ShapeDtypeStruct((19, ROWS, BS), half_type)
    near, ahead, back = small_call(
        near_kernel, [near_type, sent_type, sent_type], "near", tiles, *row
    )
    one, three = to_v(ahead, 1), to_v(back, 3)
    near_other = to_core(near)
    low = to_v(one[:9], 1)
    high = to_v(three[8:17], 3)
    one_other, three_other = to_core(one), to_core(three)
    begun = place(0, spot, None, near, near_other)
    begun = place(1, spot, begun, one, one_other)
    begun = place(3, spot, begun, three, three_other)
    low, high, begun = hold((low, high, begun))
    left_stats, right_stats = small_call(
        stats_kernel,
        [stat_type] * 2,
        "stats",
        spot,
        stat_left[0],
        stat_right[0],
        near,
        one,
        low,
        high,
        three,
    )
    given = [near, one, three, low, high, to_core(low), to_core(high)]
    update_blocks, new_momentum = pl.pallas_call(
        finish_kernel,
        out_shape=[jax.ShapeDtypeStruct(begun.shape, half_type), stat_type],
        in_specs=[SMEM, ANY] + [VMEM] * (1 + len(given)),
        out_specs=[ANY, ANY],
        scratch_shapes=[
            pltpu.VMEM((SLOTS, ROWS, BS), wide_type),
            pltpu.SemaphoreType.DMA((8,)),
            pltpu.SemaphoreType.DMA((SLOTS,)),
        ],
        input_output_aliases={1: 0},
        compiler_params=pltpu.CompilerParams(vmem_limit_bytes=16 << 20),
        cost_estimate=cost(0, *given),
        name="finish",
    )(spot, begun, momentum[0], *given)
    update_blocks = update_blocks.reshape(BLOCKS, BS, BS)
    return (update_blocks, left_stats[None], right_stats[None], new_momentum[None])


def solution(mesh):
    placed = (
        P("dp", "group", None, None),
        P(),
        P(),
        P("group", None, "dp", None),
        P("group", None, "dp", None),
        P("group", None, "dp", None),
        P("group", None, "dp", None),
        P("group", None, "dp", None),
    )
    return jax.shard_map(
        local,
        mesh=mesh,
        in_specs=placed,
        out_specs=(
            P(),
            P("group", None, "dp", None),
            P("group", None, "dp", None),
            P("group", None, "dp", None),
        ),
        check_vma=False,
    )
```

time: 106 us -> 103 us (0.972)
  Pallas kernels: 15.8 us -> 13.7 us
    pallas_call x9 -> x10, Pallas kernels: 5.96 us -> 4.22 us  [small_call(): pl.pallas_call(body, out_shape=outs, in_specs=[SMEM if a.dtype == jnp.int...]
    unnamed x16 -> x18, local copies, waits for them, and re-layouts: 2.72 us -> 1.73 us
  transfers between devices with their start and end apart: 26 -> 26, of which waited for: 18 -> 16; matrix products, arithmetic and copies ran while one was open for 0% -> 0% of each run, Pallas kernels for 9% -> 9%
where the time goes in v4:
time: 103 us
  waiting for transfers between devices  51.1 us (50%)
  starting transfers between devices  35.3 us (34%)
  Pallas kernels  13.7 us (13%)
  local copies, waits for them, and re-layouts  1.8 us (2%)
    ppermute x26, waiting for transfers between devices, permute(): return lax.ppermute(value, AXES, pairs)  51.1 us
    ppermute x26, starting transfers between devices, permute(): return lax.ppermute(value, AXES, pairs)  35.3 us
    pallas_call x3, Pallas kernels, place(): pl.pallas_call(functools.partial(place_kernel, which), out_shape=jax.Shap...  5.78 us
    pallas_call x10, Pallas kernels, small_call(): pl.pallas_call(body, out_shape=outs, in_specs=[SMEM if a.dtype == jnp.int...  4.22 us
    pallas_call x1, Pallas kernels, local(): pl.pallas_call(finish_kernel, out_shape=[jax.ShapeDtypeStruct(begun.shape...  2.07 us
  transfers between devices with their start and end apart: 26, of which 16 were waited for; matrix products, arithmetic and copies ran while one was open for 0% of the time, Pallas kernels for 9%

profile of v4, /device:TPU:1, one launch (start us, length us, event | category | flops | bytes accessed | tf_op | source)
XLA Modules:
  0.0 102.8 jit_solution(3048652794360536770)
XLA Ops:
  0.6 1.5 %collective-permute-start = (bf16[512,512]{1,0:T(8,128)(2,1)}, bf16[512,512]{1,0:T(8,128)(2,1)S(1)}, u32[]{:S(2)}, u32[]{:S(2)}) collective-permute-start(bf16[512,512]{1,0:T(8,128)(2,1)} %bitcast.12), channel_id=1, source_target_pairs={{0,16},{1,17},{2,18},{3,19},{4,20},{5,21},{6,22},{7,23},{8,24},{9,... | collective-permute-start | bytes 1572872 | tf_op jit(solution)/shard_map/ppermute | solution.py:44
  2.1 1.0 %copy-done.2 = bf16[1,1,512,512]{3,2,1,0:T(8,128)(2,1)S(1)} copy-done((bf16[1,1,512,512]{3,2,1,0:T(8,128)(2,1)S(1)}, bf16[1,1,512,512]{3,2,1,0:T(8,128)(2,1)}, u32[]{:S(2)}) %copy-start.2) | copy-done | bytes 524312
  3.2 0.7 collective-permute-done.theirs
  3.9 0.1 pair.1
  4.0 1.4 %collective-permute-start.1 = (bf16[64,512]{1,0:T(8,128)(2,1)S(1)}, bf16[64,512]{1,0:T(8,128)(2,1)S(1)}, u32[]{:S(2)}, u32[]{:S(2)}) collective-permute-start(bf16[64,512]{1,0:T(8,128)(2,1)S(1)} %get-tuple-element.54), channel_id=1, source_target_pairs={{0,32},{1,33},{2,34},{3,35},{4,36},{5,37},{6,38},{7,39},{8,40},{9,... | collective-permute-start | bytes 196616 | tf_op jit(solution)/shard_map/ppermute | solution.py:44
  5.3 1.4 %collective-permute-start.2 = (bf16[64,512]{1,0:T(8,128)(2,1)S(1)}, bf16[64,512]{1,0:T(8,128)(2,1)S(1)}, u32[]{:S(2)}, u32[]{:S(2)}) collective-permute-start(bf16[64,512]{1,0:T(8,128)(2,1)S(1)} %get-tuple-element.55), channel_id=1, source_target_pairs={{0,96},{1,97},{2,98},{3,99},{4,100},{5,101},{6,102},{7,103},{8,104... | collective-permute-start | bytes 196616 | tf_op jit(solution)/shard_map/ppermute | solution.py:44
  6.7 1.6 %collective-permute-start.3 = (bf16[64,512]{1,0:T(8,128)(2,1)S(1)}, bf16[64,512]{1,0:T(8,128)(2,1)S(1)}, u32[]{:S(2)}, u32[]{:S(2)}) collective-permute-start(bf16[64,512]{1,0:T(8,128)(2,1)S(1)} %get-tuple-element.56), channel_id=1, source_target_pairs={{0,64},{1,65},{2,66},{3,67},{4,68},{5,69},{6,70},{7,71},{8,72},{9,... | collective-permute-start | bytes 196616 | tf_op jit(solution)/shard_map/ppermute | solution.py:44
  8.3 1.6 %choices.1 = (s32[62]{0:T(128)}, bf16[14,16,512]{2,1,0:T(8,128)(2,1)}) custom-call(s32[16]{0:T(128)} %order_ref, s32[16]{0:T(128)} %count_ref), custom_call_target="tpu_custom_call" | custom-call | bytes 4194304 | tf_op jit(solution)/shard_map/choices/pallas_call | solution.py:144
  10.0 0.0 copy-start.7
  10.0 0.6 copy-done.7
  10.6 0.6 packs.1
  11.2 0.0 collective-permute-done.1.a
  11.3 0.0 collective-permute-done.2.c
  11.3 0.1 collective-permute-done.3.b
  11.4 1.8 %collective-permute-start.4 = (bf16[4,64,512]{2,1,0:T(8,128)(2,1)S(1)}, bf16[4,64,512]{2,1,0:T(8,128)(2,1)S(1)}, u32[]{:S(2)}, u32[]{:S(2)}) collective-permute-start(bf16[4,64,512]{2,1,0:T(8,128)(2,1)S(1)} %get-tuple-element.65), channel_id=1, source_target_pairs={{0,1},{1,2},{2,3},{3,0},{4,5},{5,6},{6,7},{7,4},{8,9},{9,10},{10,1... | collective-permute-start | bytes 786440 | tf_op jit(solution)/shard_map/ppermute | solution.py:44
  13.1 2.2 %collective-permute-start.5 = (bf16[4,64,512]{2,1,0:T(8,128)(2,1)S(1)}, bf16[4,64,512]{2,1,0:T(8,128)(2,1)S(1)}, u32[]{:S(2)}, u32[]{:S(2)}) collective-permute-start(bf16[4,64,512]{2,1,0:T(8,128)(2,1)S(1)} %get-tuple-element.66), channel_id=1, source_target_pairs={{0,3},{1,0},{2,1},{3,2},{4,7},{5,4},{6,5},{7,6},{8,11},{9,8},{10,9... | collective-permute-start | bytes 786440 | tf_op jit(solution)/shard_map/ppermute | solution.py:44
  15.3 1.2 %collective-permute-start.6 = (bf16[4,64,512]{2,1,0:T(8,128)(2,1)S(1)}, bf16[4,64,512]{2,1,0:T(8,128)(2,1)S(1)}, u32[]{:S(2)}, u32[]{:S(2)}) collective-permute-start(bf16[4,64,512]{2,1,0:T(8,128)(2,1)S(1)} %get-tuple-element.67), channel_id=1, source_target_pairs={{0,2},{1,3},{2,0},{3,1},{4,6},{5,7},{6,4},{7,5},{8,10},{9,11},{10,... | collective-permute-start | bytes 786440 | tf_op jit(solution)/shard_map/ppermute | solution.py:44
  16.6 2.7 %collective-permute-done.4.b = bf16[4,64,512]{2,1,0:T(8,128)(2,1)S(1)} collective-permute-done((bf16[4,64,512]{2,1,0:T(8,128)(2,1)S(1)}, bf16[4,64,512]{2,1,0:T(8,128)(2,1)S(1)}, u32[]{:S(2)}, u32[]{:S(2)}) %collective-permute-start.4) | collective-permute-done | bytes 262176 | tf_op jit(solution)/shard_map/ppermute | solution.py:44
  19.3 2.2 %collective-permute-done.5.d = bf16[4,64,512]{2,1,0:T(8,128)(2,1)S(1)} collective-permute-done((bf16[4,64,512]{2,1,0:T(8,128)(2,1)S(1)}, bf16[4,64,512]{2,1,0:T(8,128)(2,1)S(1)}, u32[]{:S(2)}, u32[]{:S(2)}) %collective-permute-start.5) | collective-permute-done | bytes 262176 | tf_op jit(solution)/shard_map/ppermute | solution.py:44
  21.5 1.8 %collective-permute-done.6.c = bf16[4,64,512]{2,1,0:T(8,128)(2,1)S(1)} collective-permute-done((bf16[4,64,512]{2,1,0:T(8,128)(2,1)S(1)}, bf16[4,64,512]{2,1,0:T(8,128)(2,1)S(1)}, u32[]{:S(2)}, u32[]{:S(2)}) %collective-permute-start.6) | collective-permute-done | bytes 262176 | tf_op jit(solution)/shard_map/ppermute | solution.py:44
  23.3 0.3 turn.1
  23.6 1.1 %collective-permute-start.7 = (bf16[4,64,512]{2,1,0:T(8,128)(2,1)S(1)}, bf16[4,64,512]{2,1,0:T(8,128)(2,1)S(1)}, u32[]{:S(2)}, u32[]{:S(2)}) collective-permute-start(bf16[4,64,512]{2,1,0:T(8,128)(2,1)S(1)} %get-tuple-element.69), channel_id=1, source_target_pairs={{0,4},{1,5},{2,6},{3,7},{4,8},{5,9},{6,10},{7,11},{8,12},{9,13},{1... | collective-permute-start | bytes 786440 | tf_op jit(solution)/shard_map/ppermute | solution.py:44
  24.7 1.8 %collective-permute-start.8 = (bf16[4,64,512]{2,1,0:T(8,128)(2,1)S(1)}, bf16[4,64,512]{2,1,0:T(8,128)(2,1)S(1)}, u32[]{:S(2)}, u32[]{:S(2)}) collective-permute-start(bf16[4,64,512]{2,1,0:T(8,128)(2,1)S(1)} %get-tuple-element.70), channel_id=1, source_target_pairs={{0,12},{1,13},{2,14},{3,15},{4,0},{5,1},{6,2},{7,3},{8,4},{9,5},{1... | collective-permute-start | bytes 786440 | tf_op jit(solution)/shard_map/ppermute | solution.py:44
  26.5 1.3 %collective-permute-start.9 = (bf16[4,64,512]{2,1,0:T(8,128)(2,1)S(1)}, bf16[4,64,512]{2,1,0:T(8,128)(2,1)S(1)}, u32[]{:S(2)}, u32[]{:S(2)}) collective-permute-start(bf16[4,64,512]{2,1,0:T(8,128)(2,1)S(1)} %get-tuple-element.71), channel_id=1, source_target_pairs={{0,8},{1,9},{2,10},{3,11},{4,12},{5,13},{6,14},{7,15},{8,0},{9,1},... | collective-permute-start | bytes 786440 | tf_op jit(solution)/shard_map/ppermute | solution.py:44
  27.7 2.4 %collective-permute-done.7.b = bf16[4,64,512]{2,1,0:T(8,128)(2,1)S(1)} collective-permute-done((bf16[4,64,512]{2,1,0:T(8,128)(2,1)S(1)}, bf16[4,64,512]{2,1,0:T(8,128)(2,1)S(1)}, u32[]{:S(2)}, u32[]{:S(2)}) %collective-permute-start.7) | collective-permute-done | bytes 262176 | tf_op jit(solution)/shard_map/ppermute | solution.py:44
  30.1 2.4 %collective-permute-done.8.d = bf16[4,64,512]{2,1,0:T(8,128)(2,1)S(1)} collective-permute-done((bf16[4,64,512]{2,1,0:T(8,128)(2,1)S(1)}, bf16[4,64,512]{2,1,0:T(8,128)(2,1)S(1)}, u32[]{:S(2)}, u32[]{:S(2)}) %collective-permute-start.8) | collective-permute-done | bytes 262176 | tf_op jit(solution)/shard_map/ppermute | solution.py:44
  32.6 1.5 %collective-permute-done.9.c = bf16[4,64,512]{2,1,0:T(8,128)(2,1)S(1)} collective-permute-done((bf16[4,64,512]{2,1,0:T(8,128)(2,1)S(1)}, bf16[4,64,512]{2,1,0:T(8,128)(2,1)S(1)}, u32[]{:S(2)}, u32[]{:S(2)}) %collective-permute-start.9) | collective-permute-done | bytes 262176 | tf_op jit(solution)/shard_map/ppermute | solution.py:44
  34.1 0.1 here.1.refs_0_
  34.2 1.6 %collective-permute-start.10 = (bf16[4,64,512]{2,1,0:T(8,128)(2,1)S(1)}, bf16[4,64,512]{2,1,0:T(8,128)(2,1)S(1)}, u32[]{:S(2)}, u32[]{:S(2)}) collective-permute-start(bf16[4,64,512]{2,1,0:T(8,128)(2,1)S(1)} %here.1.refs_0_), channel_id=1, source_target_pairs={{0,64},{1,65},{2,66},{3,67},{4,68},{5,69},{6,70},{7,71},{8,72},{9,... | collective-permute-start | bytes 786440 | tf_op jit(solution)/shard_map/ppermute | solution.py:44
  35.8 1.3 %collective-permute-start.11 = (bf16[4,64,512]{2,1,0:T(8,128)(2,1)S(1)}, bf16[4,64,512]{2,1,0:T(8,128)(2,1)S(1)}, u32[]{:S(2)}, u32[]{:S(2)}) collective-permute-start(bf16[4,64,512]{2,1,0:T(8,128)(2,1)S(1)} %here.1.refs_0_), channel_id=1, source_target_pairs={{0,96},{1,97},{2,98},{3,99},{4,100},{5,101},{6,102},{7,103},{8,104... | collective-permute-start | bytes 786440 | tf_op jit(solution)/shard_map/ppermute | solution.py:44
  37.1 0.2 collective-permute-start.12
  37.3 3.8 %collective-permute-done.10.refs_1_ = bf16[4,64,512]{2,1,0:T(8,128)(2,1)S(1)} collective-permute-done((bf16[4,64,512]{2,1,0:T(8,128)(2,1)S(1)}, bf16[4,64,512]{2,1,0:T(8,128)(2,1)S(1)}, u32[]{:S(2)}, u32[]{:S(2)}) %collective-permute-start.10) | collective-permute-done | bytes 262176 | tf_op jit(solution)/shard_map/ppermute | solution.py:44
  41.0 4.2 %collective-permute-done.11.refs_2_ = bf16[4,64,512]{2,1,0:T(8,128)(2,1)S(1)} collective-permute-done((bf16[4,64,512]{2,1,0:T(8,128)(2,1)S(1)}, bf16[4,64,512]{2,1,0:T(8,128)(2,1)S(1)}, u32[]{:S(2)}, u32[]{:S(2)}) %collective-permute-start.11) | collective-permute-done | bytes 262176 | tf_op jit(solution)/shard_map/ppermute | solution.py:44
  45.3 0.0 collective-permute-done.12.refs_3_
  45.3 0.1 line.1
  45.3 4.9 %collective-permute-start.13 = (bf16[4,3,64,512]{3,2,1,0:T(8,128)(2,1)S(1)}, bf16[4,3,64,512]{3,2,1,0:T(8,128)(2,1)S(1)}, u32[]{:S(2)}, u32[]{:S(2)}) collective-permute-start(bf16[4,3,64,512]{3,2,1,0:T(8,128)(2,1)S(1)} %get-tuple-element.72.mine), channel_id=1, source_target_pairs={{0,16},{1,17},{2,18},{3,19},{4,20},{5,21},{6,22},{7,23},{8,24},{9,... | collective-permute-start | bytes 2359304 | tf_op jit(solution)/shard_map/ppermute | solution.py:44
  50.3 1.9 %collective-permute-done.13.other = bf16[4,3,64,512]{3,2,1,0:T(8,128)(2,1)S(1)} collective-permute-done((bf16[4,3,64,512]{3,2,1,0:T(8,128)(2,1)S(1)}, bf16[4,3,64,512]{3,2,1,0:T(8,128)(2,1)S(1)}, u32[]{:S(2)}, u32[]{:S(2)}) %collective-permute-start.13) | collective-permute-done | bytes 786464 | tf_op jit(solution)/shard_map/ppermute | solution.py:44
  52.2 1.2 %step.1.a = bf16[6,64,512]{2,1,0:T(8,128)(2,1)S(1)} custom-call(bf16[4,3,64,512]{3,2,1,0:T(8,128)(2,1)S(1)} %get-tuple-element.72.mine, bf16[4,64,512]{2,1,0:T(8,128)(2,1)S(1)} %get-tuple-element.73.moment, bf16[4,3,64,512]{3,2,1,0:T(8,128)(2,1)S(1)} %collective-permute-done.13.other), custom_call_target="tpu_custom_call" | custom-call | flops 805306368 | bytes 2228224 | tf_op jit(solution)/shard_map/step/pallas_call | solution.py:164
  53.4 0.3 collective-permute-start.14
  53.8 3.0 %collective-permute-start.15 = (bf16[6,64,512]{2,1,0:T(8,128)(2,1)S(1)}, bf16[6,64,512]{2,1,0:T(8,128)(2,1)S(1)}, u32[]{:S(2)}, u32[]{:S(2)}) collective-permute-start(bf16[6,64,512]{2,1,0:T(8,128)(2,1)S(1)} %step.1.a), channel_id=1, source_target_pairs={{0,3},{1,0},{2,1},{3,2},{4,7},{5,4},{6,5},{7,6},{8,11},{9,8},{10,9... | collective-permute-start | bytes 1179656 | tf_op jit(solution)/shard_map/ppermute | solution.py:44
  56.8 5.2 %collective-permute-done.14.c = bf16[6,64,512]{2,1,0:T(8,128)(2,1)S(1)} collective-permute-done((bf16[6,64,512]{2,1,0:T(8,128)(2,1)S(1)}, bf16[6,64,512]{2,1,0:T(8,128)(2,1)S(1)}, u32[]{:S(2)}, u32[]{:S(2)}) %collective-permute-start.14) | collective-permute-done | bytes 393248 | tf_op jit(solution)/shard_map/ppermute | solution.py:44
  61.9 3.7 %collective-permute-done.15.d = bf16[6,64,512]{2,1,0:T(8,128)(2,1)S(1)} collective-permute-done((bf16[6,64,512]{2,1,0:T(8,128)(2,1)S(1)}, bf16[6,64,512]{2,1,0:T(8,128)(2,1)S(1)}, u32[]{:S(2)}, u32[]{:S(2)}) %collective-permute-start.15) | collective-permute-done | bytes 393248 | tf_op jit(solution)/shard_map/ppermute | solution.py:44
  65.6 0.5 collective-permute-done.16.b
  66.1 0.3 near.1
  66.5 0.0 copy-start.8
  66.5 0.6 collective-permute-start.17
  67.1 2.1 %collective-permute-start.19 = (bf16[19,64,512]{2,1,0:T(8,128)(2,1)S(1)}, bf16[19,64,512]{2,1,0:T(8,128)(2,1)S(1)}, u32[]{:S(2)}, u32[]{:S(2)}) collective-permute-start(bf16[19,64,512]{2,1,0:T(8,128)(2,1)S(1)} %get-tuple-element.75), channel_id=1, source_target_pairs={{0,12},{1,13},{2,14},{3,15},{4,0},{5,1},{6,2},{7,3},{8,4},{9,5},{1... | collective-permute-start | bytes 3735560 | tf_op jit(solution)/shard_map/ppermute | solution.py:44
  69.2 14.6 %collective-permute-done.17.refs_1_.one = bf16[19,64,512]{2,1,0:T(8,128)(2,1)S(1)} collective-permute-done((bf16[19,64,512]{2,1,0:T(8,128)(2,1)S(1)}, bf16[19,64,512]{2,1,0:T(8,128)(2,1)S(1)}, u32[]{:S(2)}, u32[]{:S(2)}) %collective-permute-start.17) | collective-permute-done | bytes 1245216 | tf_op jit(solution)/shard_map/ppermute | solution.py:44
  83.8 2.1 %collective-permute-start.22 = (bf16[19,64,512]{2,1,0:T(8,128)(2,1)S(1)}, bf16[19,64,512]{2,1,0:T(8,128)(2,1)S(1)}, u32[]{:S(2)}, u32[]{:S(2)}) collective-permute-start(bf16[19,64,512]{2,1,0:T(8,128)(2,1)S(1)} %collective-permute-done.17.refs_1_.one), channel_id=1, source_target_pairs={{0,16},{1,17},{2,18},{3,19},{4,20},{5,21},{6,22},{7,23},{8,24},{9,... | collective-permute-start | bytes 3735560 | tf_op jit(solution)/shard_map/ppermute | solution.py:44
  85.9 0.0 collective-permute-start.23
  85.9 0.5 collective-permute-start.21
  86.4 1.0 collective-permute-start.18
  87.4 1.9 %collective-permute-start.20 = (bf16[9,64,512]{2,1,0:T(8,128)(2,1)S(1)}, bf16[9,64,512]{2,1,0:T(8,128)(2,1)S(1)}, u32[]{:S(2)}, u32[]{:S(2)}) collective-permute-start(bf16[9,64,512]{2,1,0:T(8,128)(2,1)S(1)} %slice.9), channel_id=1, source_target_pairs={{0,12},{1,13},{2,14},{3,15},{4,0},{5,1},{6,2},{7,3},{8,4},{9,5},{1... | collective-permute-start | bytes 1769480 | tf_op jit(solution)/shard_map/ppermute | solution.py:44
  89.3 2.6 %collective-permute-done.21.refs_1_ = bf16[18,64,512]{2,1,0:T(8,128)(2,1)S(1)} collective-permute-done((bf16[18,64,512]{2,1,0:T(8,128)(2,1)S(1)}, bf16[18,64,512]{2,1,0:T(8,128)(2,1)S(1)}, u32[]{:S(2)}, u32[]{:S(2)}) %collective-permute-start.21) | collective-permute-done | bytes 1179680 | tf_op jit(solution)/shard_map/ppermute | solution.py:44
  91.9 1.9 %place.3.refs_0_ = bf16[16,4,2,64,512]{4,3,2,1,0:T(8,128)(2,1)} custom-call(s32[62]{0:T(128)S(1)} %copy-done.8, bf16[18,64,512]{2,1,0:T(8,128)(2,1)S(1)} %get-tuple-element.76.refs_0_.near, bf16[18,64,512]{2,1,0:T(8,128)(2,1)S(1)} %collective-permute-done.21.refs_1_), custom_call_target="tpu_custom_call" | custom-call | bytes 4718592 | tf_op jit(solution)/shard_map/place/pallas_call | solution.py:320
  93.9 1.9 %place.4.refs_0_ = bf16[16,4,2,64,512]{4,3,2,1,0:T(8,128)(2,1)} custom-call(s32[62]{0:T(128)S(1)} %copy-done.8, bf16[16,4,2,64,512]{4,3,2,1,0:T(8,128)(2,1)} %place.3.refs_0_, bf16[19,64,512]{2,1,0:T(8,128)(2,1)S(1)} %collective-permute-done.17.refs_1_.one, bf16[19,64,512]{2,1,0:T(8,128)(2,1)S(1)} %collective-permute-done.22.refs_2_), custom_call_target="tpu_custom_call", output_to_operand_aliasing={{}: (1, {})} | custom-call | bytes 4980736 | tf_op jit(solution)/shard_map/place/pallas_call | solution.py:320
  95.8 0.0 copy-start.3
  95.8 0.0 copy-start.4
  95.8 1.9 %place.5.begun = bf16[16,4,2,64,512]{4,3,2,1,0:T(8,128)(2,1)} custom-call(s32[62]{0:T(128)S(1)} %copy-done.8, bf16[16,4,2,64,512]{4,3,2,1,0:T(8,128)(2,1)} %place.4.refs_0_, bf16[19,64,512]{2,1,0:T(8,128)(2,1)S(1)} %collective-permute-done.19.refs_1_.three, bf16[19,64,512]{2,1,0:T(8,128)(2,1)S(1)} %collective-permute-done.23.refs_2_), custom_call_target="tpu_custom_call", output_to_operand_aliasing={{}: (1, {})} | custom-call | bytes 4980736 | tf_op jit(solution)/shard_map/place/pallas_call | solution.py:320
  97.8 0.5 collective-permute-start.24
  98.2 0.1 collective-permute-start.25
  98.4 1.5 %stats.1 = (f32[3,64,512]{2,1,0:T(8,128)}, f32[3,64,512]{2,1,0:T(8,128)}) custom-call(s32[62]{0:T(128)S(1)} %copy-done.8, f32[3,64,512]{2,1,0:T(8,128)S(1)} %bitcast.14, f32[3,64,512]{2,1,0:T(8,128)S(1)} %bitcast.15, bf16[18,64,512]{2,1,0:T(8,128)(2,1)S(1)} %get-tuple-element.76.refs_0_.near, bf16[19,64,512]{2,1,0:T(8,128)(2,1)S(1)} %collective-permute-done.17.refs_1_.one, ...), custom_call_target="tpu_custom_call" | custom-call | bytes 6422776 | tf_op jit(solution)/shard_map/stats/pallas_call | solution.py:164
  99.9 0.8 collective-permute-done.25.high_other
  100.7 2.1 %finish.1 = (bf16[16,4,2,64,512]{4,3,2,1,0:T(8,128)(2,1)}, f32[3,64,512]{2,1,0:T(8,128)}) custom-call(s32[62]{0:T(128)S(1)} %copy-done.8, bf16[16,4,2,64,512]{4,3,2,1,0:T(8,128)(2,1)} %place.5.begun, f32[3,64,512]{2,1,0:T(8,128)S(1)} %bitcast.11, bf16[18,64,512]{2,1,0:T(8,128)(2,1)S(1)} %get-tuple-element.76.refs_0_.near, ...), custom_call_target="tpu_custom_call", output_to_operand_aliasing={{0}: (1, {})} | custom-call | bytes 6029312 | tf_op jit(solution)/shard_map/finish/pallas_call | solution.py:459
  (23 shorter events, 0.2 us)
Async XLA Ops:
  0.6 9.3 %copy-start.1 = (f32[1,3,64,512]{3,2,1,0:T(8,128)S(1)}, f32[1,3,64,512]{3,2,1,0:T(8,128)}, u32[]{:S(2)}) copy-start(f32[1,3,64,512]{3,2,1,0:T(8,128)} %param.15) | copy-start | bytes 1179652
  0.6 3.2 %collective-permute-start = (bf16[512,512]{1,0:T(8,128)(2,1)}, bf16[512,512]{1,0:T(8,128)(2,1)S(1)}, u32[]{:S(2)}, u32[]{:S(2)}) collective-permute-start(bf16[512,512]{1,0:T(8,128)(2,1)} %bitcast.12), channel_id=1, source_target_pairs={{0,16},{1,17},{2,18},{3,19},{4,20},{5,21},{6,22},{7,23},{8,24},{9,... | collective-permute-start | bytes 1572872 | tf_op jit(solution)/shard_map/ppermute | solution.py:44
  2.1 1.0 %copy-start.2 = (bf16[1,1,512,512]{3,2,1,0:T(8,128)(2,1)S(1)}, bf16[1,1,512,512]{3,2,1,0:T(8,128)(2,1)}, u32[]{:S(2)}) copy-start(bf16[1,1,512,512]{3,2,1,0:T(8,128)(2,1)} %param.8) | copy-start | bytes 1572868
  3.2 6.8 %copy-start.5 = (f32[1,3,64,512]{3,2,1,0:T(8,128)S(1)}, f32[1,3,64,512]{3,2,1,0:T(8,128)}, u32[]{:S(2)}) copy-start(f32[1,3,64,512]{3,2,1,0:T(8,128)} %param.13) | copy-start | bytes 1179652
  3.2 6.8 %copy-start.6 = (f32[1,3,64,512]{3,2,1,0:T(8,128)S(1)}, f32[1,3,64,512]{3,2,1,0:T(8,128)}, u32[]{:S(2)}) copy-start(f32[1,3,64,512]{3,2,1,0:T(8,128)} %param.14) | copy-start | bytes 1179652
  4.0 7.3 %collective-permute-start.1 = (bf16[64,512]{1,0:T(8,128)(2,1)S(1)}, bf16[64,512]{1,0:T(8,128)(2,1)S(1)}, u32[]{:S(2)}, u32[]{:S(2)}) collective-permute-start(bf16[64,512]{1,0:T(8,128)(2,1)S(1)} %get-tuple-element.54), channel_id=1, source_target_pairs={{0,32},{1,33},{2,34},{3,35},{4,36},{5,37},{6,38},{7,39},{8,40},{9,... | collective-permute-start | bytes 196616 | tf_op jit(solution)/shard_map/ppermute | solution.py:44
  5.3 5.9 %collective-permute-start.2 = (bf16[64,512]{1,0:T(8,128)(2,1)S(1)}, bf16[64,512]{1,0:T(8,128)(2,1)S(1)}, u32[]{:S(2)}, u32[]{:S(2)}) collective-permute-start(bf16[64,512]{1,0:T(8,128)(2,1)S(1)} %get-tuple-element.55), channel_id=1, source_target_pairs={{0,96},{1,97},{2,98},{3,99},{4,100},{5,101},{6,102},{7,103},{8,104... | collective-permute-start | bytes 196616 | tf_op jit(solution)/shard_map/ppermute | solution.py:44
  6.7 4.6 %collective-permute-start.3 = (bf16[64,512]{1,0:T(8,128)(2,1)S(1)}, bf16[64,512]{1,0:T(8,128)(2,1)S(1)}, u32[]{:S(2)}, u32[]{:S(2)}) collective-permute-start(bf16[64,512]{1,0:T(8,128)(2,1)S(1)} %get-tuple-element.56), channel_id=1, source_target_pairs={{0,64},{1,65},{2,66},{3,67},{4,68},{5,69},{6,70},{7,71},{8,72},{9,... | collective-permute-start | bytes 196616 | tf_op jit(solution)/shard_map/ppermute | solution.py:44
  10.0 0.7 copy-start.7
  10.6 12.7 %copy-start = (bf16[14,16,512]{2,1,0:T(8,128)(2,1)S(1)}, bf16[14,16,512]{2,1,0:T(8,128)(2,1)}, u32[]{:S(2)}) copy-start(bf16[14,16,512]{2,1,0:T(8,128)(2,1)} %get-tuple-element.52.tiles) | copy-start | bytes 688132
  11.4 8.0 %collective-permute-start.4 = (bf16[4,64,512]{2,1,0:T(8,128)(2,1)S(1)}, bf16[4,64,512]{2,1,0:T(8,128)(2,1)S(1)}, u32[]{:S(2)}, u32[]{:S(2)}) collective-permute-start(bf16[4,64,512]{2,1,0:T(8,128)(2,1)S(1)} %get-tuple-element.65), channel_id=1, source_target_pairs={{0,1},{1,2},{2,3},{3,0},{4,5},{5,6},{6,7},{7,4},{8,9},{9,10},{10,1... | collective-permute-start | bytes 786440 | tf_op jit(solution)/shard_map/ppermute | solution.py:44
  13.1 8.3 %collective-permute-start.5 = (bf16[4,64,512]{2,1,0:T(8,128)(2,1)S(1)}, bf16[4,64,512]{2,1,0:T(8,128)(2,1)S(1)}, u32[]{:S(2)}, u32[]{:S(2)}) collective-permute-start(bf16[4,64,512]{2,1,0:T(8,128)(2,1)S(1)} %get-tuple-element.66), channel_id=1, source_target_pairs={{0,3},{1,0},{2,1},{3,2},{4,7},{5,4},{6,5},{7,6},{8,11},{9,8},{10,9... | collective-permute-start | bytes 786440 | tf_op jit(solution)/shard_map/ppermute | solution.py:44
  15.3 8.0 %collective-permute-start.6 = (bf16[4,64,512]{2,1,0:T(8,128)(2,1)S(1)}, bf16[4,64,512]{2,1,0:T(8,128)(2,1)S(1)}, u32[]{:S(2)}, u32[]{:S(2)}) collective-permute-start(bf16[4,64,512]{2,1,0:T(8,128)(2,1)S(1)} %get-tuple-element.67), channel_id=1, source_target_pairs={{0,2},{1,3},{2,0},{3,1},{4,6},{5,7},{6,4},{7,5},{8,10},{9,11},{10,... | collective-permute-start | bytes 786440 | tf_op jit(solution)/shard_map/ppermute | solution.py:44
  23.6 6.6 %collective-permute-start.7 = (bf16[4,64,512]{2,1,0:T(8,128)(2,1)S(1)}, bf16[4,64,512]{2,1,0:T(8,128)(2,1)S(1)}, u32[]{:S(2)}, u32[]{:S(2)}) collective-permute-start(bf16[4,64,512]{2,1,0:T(8,128)(2,1)S(1)} %get-tuple-element.69), channel_id=1, source_target_pairs={{0,4},{1,5},{2,6},{3,7},{4,8},{5,9},{6,10},{7,11},{8,12},{9,13},{1... | collective-permute-start | bytes 786440 | tf_op jit(solution)/shard_map/ppermute | solution.py:44
  24.7 7.9 %collective-permute-start.8 = (bf16[4,64,512]{2,1,0:T(8,128)(2,1)S(1)}, bf16[4,64,512]{2,1,0:T(8,128)(2,1)S(1)}, u32[]{:S(2)}, u32[]{:S(2)}) collective-permute-start(bf16[4,64,512]{2,1,0:T(8,128)(2,1)S(1)} %get-tuple-element.70), channel_id=1, source_target_pairs={{0,12},{1,13},{2,14},{3,15},{4,0},{5,1},{6,2},{7,3},{8,4},{9,5},{1... | collective-permute-start | bytes 786440 | tf_op jit(solution)/shard_map/ppermute | solution.py:44
  26.5 7.7 %collective-permute-start.9 = (bf16[4,64,512]{2,1,0:T(8,128)(2,1)S(1)}, bf16[4,64,512]{2,1,0:T(8,128)(2,1)S(1)}, u32[]{:S(2)}, u32[]{:S(2)}) collective-permute-start(bf16[4,64,512]{2,1,0:T(8,128)(2,1)S(1)} %get-tuple-element.71), channel_id=1, source_target_pairs={{0,8},{1,9},{2,10},{3,11},{4,12},{5,13},{6,14},{7,15},{8,0},{9,1},... | collective-permute-start | bytes 786440 | tf_op jit(solution)/shard_map/ppermute | solution.py:44
  34.2 6.8 %collective-permute-start.10 = (bf16[4,64,512]{2,1,0:T(8,128)(2,1)S(1)}, bf16[4,64,512]{2,1,0:T(8,128)(2,1)S(1)}, u32[]{:S(2)}, u32[]{:S(2)}) collective-permute-start(bf16[4,64,512]{2,1,0:T(8,128)(2,1)S(1)} %here.1.refs_0_), channel_id=1, source_target_pairs={{0,64},{1,65},{2,66},{3,67},{4,68},{5,69},{6,70},{7,71},{8,72},{9,... | collective-permute-start | bytes 786440 | tf_op jit(solution)/shard_map/ppermute | solution.py:44
  35.8 9.4 %collective-permute-start.11 = (bf16[4,64,512]{2,1,0:T(8,128)(2,1)S(1)}, bf16[4,64,512]{2,1,0:T(8,128)(2,1)S(1)}, u32[]{:S(2)}, u32[]{:S(2)}) collective-permute-start(bf16[4,64,512]{2,1,0:T(8,128)(2,1)S(1)} %here.1.refs_0_), channel_id=1, source_target_pairs={{0,96},{1,97},{2,98},{3,99},{4,100},{5,101},{6,102},{7,103},{8,104... | collective-permute-start | bytes 786440 | tf_op jit(solution)/shard_map/ppermute | solution.py:44
  37.1 8.2 %collective-permute-start.12 = (bf16[4,64,512]{2,1,0:T(8,128)(2,1)S(1)}, bf16[4,64,512]{2,1,0:T(8,128)(2,1)S(1)}, u32[]{:S(2)}, u32[]{:S(2)}) collective-permute-start(bf16[4,64,512]{2,1,0:T(8,128)(2,1)S(1)} %here.1.refs_0_), channel_id=1, source_target_pairs={{0,32},{1,33},{2,34},{3,35},{4,36},{5,37},{6,38},{7,39},{8,40},{9,... | collective-permute-start | bytes 786440 | tf_op jit(solution)/shard_map/ppermute | solution.py:44
  45.3 6.9 %collective-permute-start.13 = (bf16[4,3,64,512]{3,2,1,0:T(8,128)(2,1)S(1)}, bf16[4,3,64,512]{3,2,1,0:T(8,128)(2,1)S(1)}, u32[]{:S(2)}, u32[]{:S(2)}) collective-permute-start(bf16[4,3,64,512]{3,2,1,0:T(8,128)(2,1)S(1)} %get-tuple-element.72.mine), channel_id=1, source_target_pairs={{0,16},{1,17},{2,18},{3,19},{4,20},{5,21},{6,22},{7,23},{8,24},{9,... | collective-permute-start | bytes 2359304 | tf_op jit(solution)/shard_map/ppermute | solution.py:44
  53.4 8.5 %collective-permute-start.14 = (bf16[6,64,512]{2,1,0:T(8,128)(2,1)S(1)}, bf16[6,64,512]{2,1,0:T(8,128)(2,1)S(1)}, u32[]{:S(2)}, u32[]{:S(2)}) collective-permute-start(bf16[6,64,512]{2,1,0:T(8,128)(2,1)S(1)} %step.1.a), channel_id=1, source_target_pairs={{0,2},{1,3},{2,0},{3,1},{4,6},{5,7},{6,4},{7,5},{8,10},{9,11},{10,... | collective-permute-start | bytes 1179656 | tf_op jit(solution)/shard_map/ppermute | solution.py:44
  53.8 11.9 %collective-permute-start.15 = (bf16[6,64,512]{2,1,0:T(8,128)(2,1)S(1)}, bf16[6,64,512]{2,1,0:T(8,128)(2,1)S(1)}, u32[]{:S(2)}, u32[]{:S(2)}) collective-permute-start(bf16[6,64,512]{2,1,0:T(8,128)(2,1)S(1)} %step.1.a), channel_id=1, source_target_pairs={{0,3},{1,0},{2,1},{3,2},{4,7},{5,4},{6,5},{7,6},{8,11},{9,8},{10,9... | collective-permute-start | bytes 1179656 | tf_op jit(solution)/shard_map/ppermute | solution.py:44
  56.7 9.4 %collective-permute-start.16 = (bf16[6,64,512]{2,1,0:T(8,128)(2,1)S(1)}, bf16[6,64,512]{2,1,0:T(8,128)(2,1)S(1)}, u32[]{:S(2)}, u32[]{:S(2)}) collective-permute-start(bf16[6,64,512]{2,1,0:T(8,128)(2,1)S(1)} %step.1.a), channel_id=1, source_target_pairs={{0,1},{1,2},{2,3},{3,0},{4,5},{5,6},{6,7},{7,4},{8,9},{9,10},{10,1... | collective-permute-start | bytes 1179656 | tf_op jit(solution)/shard_map/ppermute | solution.py:44
  66.5 25.4 %copy-start.8 = (s32[62]{0:T(128)S(1)}, s32[62]{0:T(128)}, u32[]{:S(2)}) copy-start(s32[62]{0:T(128)} %get-tuple-element.51.spot) | copy-start | bytes 748
  66.5 17.3 %collective-permute-start.17 = (bf16[19,64,512]{2,1,0:T(8,128)(2,1)S(1)}, bf16[19,64,512]{2,1,0:T(8,128)(2,1)S(1)}, u32[]{:S(2)}, u32[]{:S(2)}) collective-permute-start(bf16[19,64,512]{2,1,0:T(8,128)(2,1)S(1)} %get-tuple-element.74), channel_id=1, source_target_pairs={{0,4},{1,5},{2,6},{3,7},{4,8},{5,9},{6,10},{7,11},{8,12},{9,13},{1... | collective-permute-start | bytes 3735560 | tf_op jit(solution)/shard_map/ppermute | solution.py:44
  67.1 18.8 %collective-permute-start.19 = (bf16[19,64,512]{2,1,0:T(8,128)(2,1)S(1)}, bf16[19,64,512]{2,1,0:T(8,128)(2,1)S(1)}, u32[]{:S(2)}, u32[]{:S(2)}) collective-permute-start(bf16[19,64,512]{2,1,0:T(8,128)(2,1)S(1)} %get-tuple-element.75), channel_id=1, source_target_pairs={{0,12},{1,13},{2,14},{3,15},{4,0},{5,1},{6,2},{7,3},{8,4},{9,5},{1... | collective-permute-start | bytes 3735560 | tf_op jit(solution)/shard_map/ppermute | solution.py:44
  83.8 10.0 %collective-permute-start.22 = (bf16[19,64,512]{2,1,0:T(8,128)(2,1)S(1)}, bf16[19,64,512]{2,1,0:T(8,128)(2,1)S(1)}, u32[]{:S(2)}, u32[]{:S(2)}) collective-permute-start(bf16[19,64,512]{2,1,0:T(8,128)(2,1)S(1)} %collective-permute-done.17.refs_1_.one), channel_id=1, source_target_pairs={{0,16},{1,17},{2,18},{3,19},{4,20},{5,21},{6,22},{7,23},{8,24},{9,... | collective-permute-start | bytes 3735560 | tf_op jit(solution)/shard_map/ppermute | solution.py:44
  85.9 9.9 %collective-permute-start.23 = (bf16[19,64,512]{2,1,0:T(8,128)(2,1)S(1)}, bf16[19,64,512]{2,1,0:T(8,128)(2,1)S(1)}, u32[]{:S(2)}, u32[]{:S(2)}) collective-permute-start(bf16[19,64,512]{2,1,0:T(8,128)(2,1)S(1)} %collective-permute-done.19.refs_1_.three), channel_id=1, source_target_pairs={{0,16},{1,17},{2,18},{3,19},{4,20},{5,21},{6,22},{7,23},{8,24},{9,... | collective-permute-start | bytes 3735560 | tf_op jit(solution)/shard_map/ppermute | solution.py:44
  85.9 6.0 %collective-permute-start.21 = (bf16[18,64,512]{2,1,0:T(8,128)(2,1)S(1)}, bf16[18,64,512]{2,1,0:T(8,128)(2,1)S(1)}, u32[]{:S(2)}, u32[]{:S(2)}) collective-permute-start(bf16[18,64,512]{2,1,0:T(8,128)(2,1)S(1)} %get-tuple-element.76.refs_0_.near), channel_id=1, source_target_pairs={{0,16},{1,17},{2,18},{3,19},{4,20},{5,21},{6,22},{7,23},{8,24},{9,... | collective-permute-start | bytes 3538952 | tf_op jit(solution)/shard_map/ppermute | solution.py:44
  86.4 11.3 %collective-permute-start.18 = (bf16[9,64,512]{2,1,0:T(8,128)(2,1)S(1)}, bf16[9,64,512]{2,1,0:T(8,128)(2,1)S(1)}, u32[]{:S(2)}, u32[]{:S(2)}) collective-permute-start(bf16[9,64,512]{2,1,0:T(8,128)(2,1)S(1)} %slice.8), channel_id=1, source_target_pairs={{0,4},{1,5},{2,6},{3,7},{4,8},{5,9},{6,10},{7,11},{8,12},{9,13},{1... | collective-permute-start | bytes 1769480 | tf_op jit(solution)/shard_map/ppermute | solution.py:44
  87.4 10.4 %collective-permute-start.20 = (bf16[9,64,512]{2,1,0:T(8,128)(2,1)S(1)}, bf16[9,64,512]{2,1,0:T(8,128)(2,1)S(1)}, u32[]{:S(2)}, u32[]{:S(2)}) collective-permute-start(bf16[9,64,512]{2,1,0:T(8,128)(2,1)S(1)} %slice.9), channel_id=1, source_target_pairs={{0,12},{1,13},{2,14},{3,15},{4,0},{5,1},{6,2},{7,3},{8,4},{9,5},{1... | collective-permute-start | bytes 1769480 | tf_op jit(solution)/shard_map/ppermute | solution.py:44
  95.8 2.6 %copy-start.3 = (f32[1,3,64,512]{3,2,1,0:T(8,128)S(1)}, f32[1,3,64,512]{3,2,1,0:T(8,128)}, u32[]{:S(2)}) copy-start(f32[1,3,64,512]{3,2,1,0:T(8,128)} %param.11) | copy-start | bytes 1179652
  95.8 2.6 %copy-start.4 = (f32[1,3,64,512]{3,2,1,0:T(8,128)S(1)}, f32[1,3,64,512]{3,2,1,0:T(8,128)}, u32[]{:S(2)}) copy-start(f32[1,3,64,512]{3,2,1,0:T(8,128)} %param.12) | copy-start | bytes 1179652
  97.8 2.1 %collective-permute-start.24 = (bf16[9,64,512]{2,1,0:T(8,128)(2,1)S(1)}, bf16[9,64,512]{2,1,0:T(8,128)(2,1)S(1)}, u32[]{:S(2)}, u32[]{:S(2)}) collective-permute-start(bf16[9,64,512]{2,1,0:T(8,128)(2,1)S(1)} %collective-permute-done.18.low), channel_id=1, source_target_pairs={{0,16},{1,17},{2,18},{3,19},{4,20},{5,21},{6,22},{7,23},{8,24},{9,... | collective-permute-start | bytes 1769480 | tf_op jit(solution)/shard_map/ppermute | solution.py:44
  98.2 2.5 %collective-permute-start.25 = (bf16[9,64,512]{2,1,0:T(8,128)(2,1)S(1)}, bf16[9,64,512]{2,1,0:T(8,128)(2,1)S(1)}, u32[]{:S(2)}, u32[]{:S(2)}) collective-permute-start(bf16[9,64,512]{2,1,0:T(8,128)(2,1)S(1)} %collective-permute-done.20.high), channel_id=1, source_target_pairs={{0,16},{1,17},{2,18},{3,19},{4,20},{5,21},{6,22},{7,23},{8,24},{9,... | collective-permute-start | bytes 1769480 | tf_op jit(solution)/shard_map/ppermute | solution.py:44

commit v5 on v4

--- a/solution.py
+++ b/solution.py
@@ -217,7 +217,7 @@
         out[3] = total
 
 
-def turn_kernel(tiles, a, b, d, c, *outs):
+def turn_kernel(tiles, a, c, b, d, *outs):
     for n in range(4):
         options = [source[n] for source in (a, b, c, d)]
         base = GRAD_PICK if n == 3 else ROOT_PICK
@@ -225,7 +225,7 @@
             out[n] = blend(tiles[base + k], options)
 
 
-def here_kernel(tiles, a, b, d, c, out):
+def here_kernel(tiles, a, c, b, d, out):
     for n in range(4):
         options = [source[n] for source in (a, b, c, d)]
         out[n] = blend(tiles[GRAD_LAST if n == 3 else ROOT_LAST], options)
@@ -234,7 +234,7 @@
 def line_kernel(*refs):
     shared, moment = refs[4:]
     x = position()[0]
-    for i, k in enumerate((0, 2, 3, 1)):
+    for i, k in enumerate((0, 2, 1, 3)):
         n = (x - k) & 3
         shared[n, 0] = refs[i][0]
         shared[n, 1] = refs[i][1]
@@ -274,7 +274,7 @@
     out[5] = held[pl.ds(pl.multiple_of(c * ROWS, ROWS), ROWS), :].astype(half_type)
 
 
-def near_kernel(tiles, a, c, d, b, near, ahead, back):
+def near_kernel(tiles, a, c, b, d, near, ahead, back):
     sources = (a, b, c, d)
     for out, first in ((near, 0), (ahead, 1), (back, 0)):
         for j, source in enumerate(sources):
@@ -330,18 +330,20 @@
     )(spot, *given)
 
 
-def finish_kernel(spot, begun, moment, near, one, three, low, high, low_other, high_other, *refs):
+def owner_kernel(spot, begun, moment, left, right, near, one, three, low, high, *refs):
     del begun
-    out, out_moment, fresh, sems, more = refs
+    out, out_moment, out_left, out_right, fresh, new_left, new_right, sems, more = refs
     sources = ((2, 0, 2, 1, low), (2, 2, 2, 0, high))
-    sources += ((6, 0, 2, 1, low_other), (6, 2, 2, 0, high_other))
     copies = placed_copies(spot, sources, out, sems)
     for copy in copies:
         copy.start()
     x = position()[0]
-    parts = ((0, 0, 4, 0, near), (1, 0, 4, 1, one), (3, 0, 4, 0, three)) + sources[:2]
+    parts = ((0, 0, 4, 0, near), (1, 0, 4, 1, one), (3, 0, 4, 0, three)) + sources
+    terms = ((near, 16, near, 17), (one, 17, one, 18), (low, 0, high, 8), (three, 17, three, 18))
     for s in range(SLOTS):
         fresh[s] = moment[s]
+        new_left[s] = left[s]
+        new_right[s] = right[s]
         came, place = spot[SLOT_FROM + s], spot[SLOT_ROW + s]
         for which, first, count, skip, source in parts:
 
@@ -349,26 +351,33 @@
             def _():
                 fresh[s] = source[skip + (place - first) * 4 + x].astype(wide_type)
 
-        copy = pltpu.make_async_copy(fresh.at[s], out_moment.at[s], more.at[s])
-        copy.start()
-        copies.append(copy)
+        for n, (left_from, m, right_from, r) in enumerate(terms):
+
+            @pl.when((spot[SLOT_LIVE + s] == 1) & (spot[TERM_LAST + s] == n))
+            def _():
+                term = left_from[m].astype(wide_type)
+                new_left[s] = decay_stats * left[s] + (1.0 - decay_stats) * term
+                term = right_from[r].astype(wide_type)
+                new_right[s] = decay_stats * right[s] + (1.0 - decay_stats) * term
+
+        for n, (value, home) in enumerate(
+            ((fresh, out_moment), (new_left, out_left), (new_right, out_right))
+        ):
+            copy = pltpu.make_async_copy(value.at[s], home.at[s], more.at[n * SLOTS + s])
+            copy.start()
+            copies.append(copy)
     for copy in copies:
         copy.wait()
 
 
-def stats_kernel(spot, left, right, near, one, low, high, three, out_left, out_right):
-    terms = ((near, 16, near, 17), (one, 17, one, 18), (low, 0, high, 8), (three, 17, three, 18))
-    for s in range(SLOTS):
-        out_left[s] = left[s]
-        out_right[s] = right[s]
-        for n, (left_from, m, right_from, r) in enumerate(terms):
-
-            @pl.when((spot[SLOT_LIVE + s] == 1) & (spot[TERM_LAST + s] == n))
-            def _():
-                new = left_from[m].astype(wide_type)
-                out_left[s] = decay_stats * left[s] + (1.0 - decay_stats) * new
-                new = right_from[r].astype(wide_type)
-                out_right[s] = decay_stats * right[s] + (1.0 - decay_stats) * new
+def finish_kernel(spot, begun, low_other, high_other, out, sems):
+    del begun
+    sources = ((6, 0, 2, 1, low_other), (6, 2, 2, 0, high_other))
+    copies = placed_copies(spot, sources, out, sems)
+    for copy in copies:
+        copy.start()
+    for copy in copies:
+        copy.wait()
 
 
 def local(
@@ -400,8 +409,8 @@
     packs = small_call(
         total_kernel, [pack_type] * 4, "total", *got, *packs, aliases={4: 0, 5: 1, 6: 2, 7: 3}
     )
-    row = along(to_u, packs)
-    column = along(to_v, small_call(turn_kernel, [pack_type] * 4, "turn", tiles, *row))
+    row = along(to_u, packs, (2, 1, 3))
+    column = along(to_v, small_call(turn_kernel, [pack_type] * 4, "turn", tiles, *row), (2, 1, 3))
     pack = small_call(here_kernel, pack_type, "here", tiles, *column)
     shared, moment = small_call(
         line_kernel,
@@ -410,7 +419,7 @@
             jax.ShapeDtypeStruct((X, ROWS, BS), half_type),
         ],
         "line",
-        *along(to_x, [pack] * 4, (2, 3, 1)),
+        *along(to_x, [pack] * 4, (2, 1, 3)),
     )
     send = small_call(
         step_kernel,
@@ -427,7 +436,7 @@
         ],
     )
 
-    row = along(to_u, [send] * 4, (2, 3, 1))
+    row = along(to_u, [send] * 4, (2, 1, 3))
     near_type = jax.ShapeDtypeStruct((18, ROWS, BS), half_type)
     sent_type = jax.ShapeDtypeStruct((19, ROWS, BS), half_type)
     near, ahead, back = small_call(
@@ -442,35 +451,30 @@
     begun = place(1, spot, begun, one, one_other)
     begun = place(3, spot, begun, three, three_other)
     low, high, begun = hold((low, high, begun))
-    left_stats, right_stats = small_call(
-        stats_kernel,
-        [stat_type] * 2,
-        "stats",
-        spot,
-        stat_left[0],
-        stat_right[0],
-        near,
-        one,
-        low,
-        high,
-        three,
-    )
-    given = [near, one, three, low, high, to_core(low), to_core(high)]
-    update_blocks, new_momentum = pl.pallas_call(
+    low_other, high_other = to_core(low), to_core(high)
+    begun, new_momentum, left_stats, right_stats = pl.pallas_call(
+        owner_kernel,
+        out_shape=[jax.ShapeDtypeStruct(begun.shape, half_type)] + [stat_type] * 3,
+        in_specs=[SMEM, ANY] + [VMEM] * 8,
+        out_specs=[ANY] * 4,
+        scratch_shapes=[pltpu.VMEM((SLOTS, ROWS, BS), wide_type)] * 3
+        + [pltpu.SemaphoreType.DMA((4,)), pltpu.SemaphoreType.DMA((3 * SLOTS,))],
+        input_output_aliases={1: 0},
+        compiler_params=pltpu.CompilerParams(vmem_limit_bytes=8 << 20),
+        cost_estimate=cost(0, near, one, three, low, high),
+        name="owner",
+    )(spot, begun, momentum[0], stat_left[0], stat_right[0], near, one, three, low, high)
+    update_blocks = pl.pallas_call(
         finish_kernel,
-        out_shape=[jax.ShapeDtypeStruct(begun.shape, half_type), stat_type],
-        in_specs=[SMEM, ANY] + [VMEM] * (1 + len(given)),
-        out_specs=[ANY, ANY],
-        scratch_shapes=[
-            pltpu.VMEM((SLOTS, ROWS, BS), wide_type),
-            pltpu.SemaphoreType.DMA((8,)),
-            pltpu.SemaphoreType.DMA((SLOTS,)),
-        ],
+        out_shape=jax.ShapeDtypeStruct(begun.shape, half_type),
+        in_specs=[SMEM, ANY, VMEM, VMEM],
+        out_specs=ANY,
+        scratch_shapes=[pltpu.SemaphoreType.DMA((4,))],
         input_output_aliases={1: 0},
-        compiler_params=pltpu.CompilerParams(vmem_limit_bytes=16 << 20),
-        cost_estimate=cost(0, *given),
+        compiler_params=pltpu.CompilerParams(vmem_limit_bytes=4 << 20),
+        cost_estimate=cost(0, low_other, high_other),
         name="finish",
-    )(spot, begun, momentum[0], *given)
+    )(spot, begun, low_other, high_other)
     update_blocks = update_blocks.reshape(BLOCKS, BS, BS)
     return (update_blocks, left_stats[None], right_stats[None], new_momentum[None])
 

time: 103 us -> 102 us (level)
  waiting for transfers between devices: 51.1 us -> 46.8 us
  starting transfers between devices: 35.3 us -> 38.3 us
    ppermute x26, waiting for transfers between devices: 51.1 us -> 46.8 us  [permute(): return lax.ppermute(value, AXES, pairs)]
    ppermute x26, starting transfers between devices: 35.3 us -> 38.3 us  [permute(): return lax.ppermute(value, AXES, pairs)]
    pallas_call x10 -> x9, Pallas kernels: 4.22 us -> 2.67 us  [small_call(): pl.pallas_call(body, out_shape=outs, in_specs=[SMEM if a.dtype == jnp.int...]
    pallas_call x1 -> x2, Pallas kernels: 2.07 us -> 3.56 us  [the longest x1 2.01 us: local(): pl.pallas_call(owner_kernel, out_shape=[jax.ShapeDtypeStruct(begun.shape,...]
  transfers between devices with their start and end apart: 26 -> 26, of which waited for: 16 -> 15; matrix products, arithmetic and copies ran while one was open for 0% -> 0% of each run, Pallas kernels for 9% -> 10%
where the time goes in v5:
time: 102 us; the launch traced here: 101 us
  waiting for transfers between devices  46.8 us (46%)
  starting transfers between devices  38.3 us (38%)
  Pallas kernels  13.6 us (13%)
  local copies, waits for them, and re-layouts  1.8 us (2%)
    ppermute x26, waiting for transfers between devices, permute(): return lax.ppermute(value, AXES, pairs)  46.8 us
    ppermute x26, starting transfers between devices, permute(): return lax.ppermute(value, AXES, pairs)  38.3 us
    pallas_call x3, Pallas kernels, place(): pl.pallas_call(functools.partial(place_kernel, which), out_shape=jax.Shap...  5.78 us
    pallas_call x9, Pallas kernels, small_call(): pl.pallas_call(body, out_shape=outs, in_specs=[SMEM if a.dtype == jnp.int...  2.67 us
  transfers between devices with their start and end apart: 26, of which 15 were waited for; matrix products, arithmetic and copies ran while one was open for 0% of the time, Pallas kernels for 10%

profile of v5, /device:TPU:1, one launch (start us, length us, event | category | flops | bytes accessed | tf_op | source)
XLA Modules:
  0.0 101.4 jit_solution(5983768184206719879)
XLA Ops:
  0.6 1.5 %collective-permute-start = (bf16[512,512]{1,0:T(8,128)(2,1)}, bf16[512,512]{1,0:T(8,128)(2,1)S(1)}, u32[]{:S(2)}, u32[]{:S(2)}) collective-permute-start(bf16[512,512]{1,0:T(8,128)(2,1)} %bitcast.12), channel_id=1, source_target_pairs={{0,16},{1,17},{2,18},{3,19},{4,20},{5,21},{6,22},{7,23},{8,24},{9,... | collective-permute-start | bytes 1572872 | tf_op jit(solution)/shard_map/ppermute | solution.py:44
  2.1 1.0 %copy-done.2 = bf16[1,1,512,512]{3,2,1,0:T(8,128)(2,1)S(1)} copy-done((bf16[1,1,512,512]{3,2,1,0:T(8,128)(2,1)S(1)}, bf16[1,1,512,512]{3,2,1,0:T(8,128)(2,1)}, u32[]{:S(2)}) %copy-start.2) | copy-done | bytes 524312
  3.2 0.7 collective-permute-done.theirs
  3.9 0.1 pair.1
  4.0 1.4 %collective-permute-start.1 = (bf16[64,512]{1,0:T(8,128)(2,1)S(1)}, bf16[64,512]{1,0:T(8,128)(2,1)S(1)}, u32[]{:S(2)}, u32[]{:S(2)}) collective-permute-start(bf16[64,512]{1,0:T(8,128)(2,1)S(1)} %get-tuple-element.54), channel_id=1, source_target_pairs={{0,32},{1,33},{2,34},{3,35},{4,36},{5,37},{6,38},{7,39},{8,40},{9,... | collective-permute-start | bytes 196616 | tf_op jit(solution)/shard_map/ppermute | solution.py:44
  5.3 1.4 %collective-permute-start.2 = (bf16[64,512]{1,0:T(8,128)(2,1)S(1)}, bf16[64,512]{1,0:T(8,128)(2,1)S(1)}, u32[]{:S(2)}, u32[]{:S(2)}) collective-permute-start(bf16[64,512]{1,0:T(8,128)(2,1)S(1)} %get-tuple-element.55), channel_id=1, source_target_pairs={{0,96},{1,97},{2,98},{3,99},{4,100},{5,101},{6,102},{7,103},{8,104... | collective-permute-start | bytes 196616 | tf_op jit(solution)/shard_map/ppermute | solution.py:44
  6.7 1.6 %collective-permute-start.3 = (bf16[64,512]{1,0:T(8,128)(2,1)S(1)}, bf16[64,512]{1,0:T(8,128)(2,1)S(1)}, u32[]{:S(2)}, u32[]{:S(2)}) collective-permute-start(bf16[64,512]{1,0:T(8,128)(2,1)S(1)} %get-tuple-element.56), channel_id=1, source_target_pairs={{0,64},{1,65},{2,66},{3,67},{4,68},{5,69},{6,70},{7,71},{8,72},{9,... | collective-permute-start | bytes 196616 | tf_op jit(solution)/shard_map/ppermute | solution.py:44
  8.3 1.6 %choices.1 = (s32[62]{0:T(128)}, bf16[14,16,512]{2,1,0:T(8,128)(2,1)}) custom-call(s32[16]{0:T(128)} %order_ref, s32[16]{0:T(128)} %count_ref), custom_call_target="tpu_custom_call" | custom-call | bytes 4194304 | tf_op jit(solution)/shard_map/choices/pallas_call | solution.py:144
  10.0 0.0 copy-start.7
  10.0 0.6 copy-done.7
  10.6 0.6 packs.1
  11.3 0.0 collective-permute-done.2.c
  11.3 0.1 collective-permute-done.3.b
  11.4 3.8 %collective-permute-start.4 = (bf16[4,64,512]{2,1,0:T(8,128)(2,1)S(1)}, bf16[4,64,512]{2,1,0:T(8,128)(2,1)S(1)}, u32[]{:S(2)}, u32[]{:S(2)}) collective-permute-start(bf16[4,64,512]{2,1,0:T(8,128)(2,1)S(1)} %get-tuple-element.65), channel_id=1, source_target_pairs={{0,2},{1,3},{2,0},{3,1},{4,6},{5,7},{6,4},{7,5},{8,10},{9,11},{10,... | collective-permute-start | bytes 786440 | tf_op jit(solution)/shard_map/ppermute | solution.py:44
  15.1 0.7 collective-permute-start.5
  15.9 1.9 %collective-permute-start.6 = (bf16[4,64,512]{2,1,0:T(8,128)(2,1)S(1)}, bf16[4,64,512]{2,1,0:T(8,128)(2,1)S(1)}, u32[]{:S(2)}, u32[]{:S(2)}) collective-permute-start(bf16[4,64,512]{2,1,0:T(8,128)(2,1)S(1)} %get-tuple-element.67), channel_id=1, source_target_pairs={{0,3},{1,0},{2,1},{3,2},{4,7},{5,4},{6,5},{7,6},{8,11},{9,8},{10,9... | collective-permute-start | bytes 786440 | tf_op jit(solution)/shard_map/ppermute | solution.py:44
  17.8 1.4 %collective-permute-done.4.c = bf16[4,64,512]{2,1,0:T(8,128)(2,1)S(1)} collective-permute-done((bf16[4,64,512]{2,1,0:T(8,128)(2,1)S(1)}, bf16[4,64,512]{2,1,0:T(8,128)(2,1)S(1)}, u32[]{:S(2)}, u32[]{:S(2)}) %collective-permute-start.4) | collective-permute-done | bytes 262176 | tf_op jit(solution)/shard_map/ppermute | solution.py:44
  19.2 2.8 %collective-permute-done.5.b = bf16[4,64,512]{2,1,0:T(8,128)(2,1)S(1)} collective-permute-done((bf16[4,64,512]{2,1,0:T(8,128)(2,1)S(1)}, bf16[4,64,512]{2,1,0:T(8,128)(2,1)S(1)}, u32[]{:S(2)}, u32[]{:S(2)}) %collective-permute-start.5) | collective-permute-done | bytes 262176 | tf_op jit(solution)/shard_map/ppermute | solution.py:44
  22.0 0.7 collective-permute-done.6.d
  22.7 0.3 turn.1
  23.0 3.0 %collective-permute-start.7 = (bf16[4,64,512]{2,1,0:T(8,128)(2,1)S(1)}, bf16[4,64,512]{2,1,0:T(8,128)(2,1)S(1)}, u32[]{:S(2)}, u32[]{:S(2)}) collective-permute-start(bf16[4,64,512]{2,1,0:T(8,128)(2,1)S(1)} %get-tuple-element.69), channel_id=1, source_target_pairs={{0,8},{1,9},{2,10},{3,11},{4,12},{5,13},{6,14},{7,15},{8,0},{9,1},... | collective-permute-start | bytes 786440 | tf_op jit(solution)/shard_map/ppermute | solution.py:44
  26.0 0.4 collective-permute-start.8
  26.4 2.3 %collective-permute-start.9 = (bf16[4,64,512]{2,1,0:T(8,128)(2,1)S(1)}, bf16[4,64,512]{2,1,0:T(8,128)(2,1)S(1)}, u32[]{:S(2)}, u32[]{:S(2)}) collective-permute-start(bf16[4,64,512]{2,1,0:T(8,128)(2,1)S(1)} %get-tuple-element.71), channel_id=1, source_target_pairs={{0,12},{1,13},{2,14},{3,15},{4,0},{5,1},{6,2},{7,3},{8,4},{9,5},{1... | collective-permute-start | bytes 786440 | tf_op jit(solution)/shard_map/ppermute | solution.py:44
  28.7 1.4 %collective-permute-done.7.c = bf16[4,64,512]{2,1,0:T(8,128)(2,1)S(1)} collective-permute-done((bf16[4,64,512]{2,1,0:T(8,128)(2,1)S(1)}, bf16[4,64,512]{2,1,0:T(8,128)(2,1)S(1)}, u32[]{:S(2)}, u32[]{:S(2)}) %collective-permute-start.7) | collective-permute-done | bytes 262176 | tf_op jit(solution)/shard_map/ppermute | solution.py:44
  30.1 2.7 %collective-permute-done.8.b = bf16[4,64,512]{2,1,0:T(8,128)(2,1)S(1)} collective-permute-done((bf16[4,64,512]{2,1,0:T(8,128)(2,1)S(1)}, bf16[4,64,512]{2,1,0:T(8,128)(2,1)S(1)}, u32[]{:S(2)}, u32[]{:S(2)}) %collective-permute-start.8) | collective-permute-done | bytes 262176 | tf_op jit(solution)/shard_map/ppermute | solution.py:44
  32.8 0.4 collective-permute-done.9.d
  33.2 0.1 here.1.refs_0_
  33.3 1.6 %collective-permute-start.10 = (bf16[4,64,512]{2,1,0:T(8,128)(2,1)S(1)}, bf16[4,64,512]{2,1,0:T(8,128)(2,1)S(1)}, u32[]{:S(2)}, u32[]{:S(2)}) collective-permute-start(bf16[4,64,512]{2,1,0:T(8,128)(2,1)S(1)} %here.1.refs_0_), channel_id=1, source_target_pairs={{0,64},{1,65},{2,66},{3,67},{4,68},{5,69},{6,70},{7,71},{8,72},{9,... | collective-permute-start | bytes 786440 | tf_op jit(solution)/shard_map/ppermute | solution.py:44
  34.9 0.4 collective-permute-start.11
  35.3 2.3 %collective-permute-start.12 = (bf16[4,64,512]{2,1,0:T(8,128)(2,1)S(1)}, bf16[4,64,512]{2,1,0:T(8,128)(2,1)S(1)}, u32[]{:S(2)}, u32[]{:S(2)}) collective-permute-start(bf16[4,64,512]{2,1,0:T(8,128)(2,1)S(1)} %here.1.refs_0_), channel_id=1, source_target_pairs={{0,96},{1,97},{2,98},{3,99},{4,100},{5,101},{6,102},{7,103},{8,104... | collective-permute-start | bytes 786440 | tf_op jit(solution)/shard_map/ppermute | solution.py:44
  37.6 2.6 %collective-permute-done.10.refs_1_ = bf16[4,64,512]{2,1,0:T(8,128)(2,1)S(1)} collective-permute-done((bf16[4,64,512]{2,1,0:T(8,128)(2,1)S(1)}, bf16[4,64,512]{2,1,0:T(8,128)(2,1)S(1)}, u32[]{:S(2)}, u32[]{:S(2)}) %collective-permute-start.10) | collective-permute-done | bytes 262176 | tf_op jit(solution)/shard_map/ppermute | solution.py:44
  40.2 6.3 %collective-permute-done.11.refs_2_ = bf16[4,64,512]{2,1,0:T(8,128)(2,1)S(1)} collective-permute-done((bf16[4,64,512]{2,1,0:T(8,128)(2,1)S(1)}, bf16[4,64,512]{2,1,0:T(8,128)(2,1)S(1)}, u32[]{:S(2)}, u32[]{:S(2)}) %collective-permute-start.11) | collective-permute-done | bytes 262176 | tf_op jit(solution)/shard_map/ppermute | solution.py:44
  46.5 0.0 collective-permute-done.12.refs_3_
  46.5 0.1 line.1
  46.6 2.8 %collective-permute-start.13 = (bf16[4,3,64,512]{3,2,1,0:T(8,128)(2,1)S(1)}, bf16[4,3,64,512]{3,2,1,0:T(8,128)(2,1)S(1)}, u32[]{:S(2)}, u32[]{:S(2)}) collective-permute-start(bf16[4,3,64,512]{3,2,1,0:T(8,128)(2,1)S(1)} %get-tuple-element.72.mine), channel_id=1, source_target_pairs={{0,16},{1,17},{2,18},{3,19},{4,20},{5,21},{6,22},{7,23},{8,24},{9,... | collective-permute-start | bytes 2359304 | tf_op jit(solution)/shard_map/ppermute | solution.py:44
  49.4 1.9 %collective-permute-done.13.other = bf16[4,3,64,512]{3,2,1,0:T(8,128)(2,1)S(1)} collective-permute-done((bf16[4,3,64,512]{3,2,1,0:T(8,128)(2,1)S(1)}, bf16[4,3,64,512]{3,2,1,0:T(8,128)(2,1)S(1)}, u32[]{:S(2)}, u32[]{:S(2)}) %collective-permute-start.13) | collective-permute-done | bytes 786464 | tf_op jit(solution)/shard_map/ppermute | solution.py:44
  51.3 1.2 %step.1.a = bf16[6,64,512]{2,1,0:T(8,128)(2,1)S(1)} custom-call(bf16[4,3,64,512]{3,2,1,0:T(8,128)(2,1)S(1)} %get-tuple-element.72.mine, bf16[4,64,512]{2,1,0:T(8,128)(2,1)S(1)} %get-tuple-element.73.moment, bf16[4,3,64,512]{3,2,1,0:T(8,128)(2,1)S(1)} %collective-permute-done.13.other), custom_call_target="tpu_custom_call" | custom-call | flops 805306368 | bytes 2228224 | tf_op jit(solution)/shard_map/step/pallas_call | solution.py:164
  52.5 1.9 %collective-permute-start.14 = (bf16[6,64,512]{2,1,0:T(8,128)(2,1)S(1)}, bf16[6,64,512]{2,1,0:T(8,128)(2,1)S(1)}, u32[]{:S(2)}, u32[]{:S(2)}) collective-permute-start(bf16[6,64,512]{2,1,0:T(8,128)(2,1)S(1)} %step.1.a), channel_id=1, source_target_pairs={{0,2},{1,3},{2,0},{3,1},{4,6},{5,7},{6,4},{7,5},{8,10},{9,11},{10,... | collective-permute-start | bytes 1179656 | tf_op jit(solution)/shard_map/ppermute | solution.py:44
  54.4 0.9 collective-permute-start.15
  55.3 1.8 %collective-permute-start.16 = (bf16[6,64,512]{2,1,0:T(8,128)(2,1)S(1)}, bf16[6,64,512]{2,1,0:T(8,128)(2,1)S(1)}, u32[]{:S(2)}, u32[]{:S(2)}) collective-permute-start(bf16[6,64,512]{2,1,0:T(8,128)(2,1)S(1)} %step.1.a), channel_id=1, source_target_pairs={{0,3},{1,0},{2,1},{3,2},{4,7},{5,4},{6,5},{7,6},{8,11},{9,8},{10,9... | collective-permute-start | bytes 1179656 | tf_op jit(solution)/shard_map/ppermute | solution.py:44
  57.1 4.0 %collective-permute-done.14.c = bf16[6,64,512]{2,1,0:T(8,128)(2,1)S(1)} collective-permute-done((bf16[6,64,512]{2,1,0:T(8,128)(2,1)S(1)}, bf16[6,64,512]{2,1,0:T(8,128)(2,1)S(1)}, u32[]{:S(2)}, u32[]{:S(2)}) %collective-permute-start.14) | collective-permute-done | bytes 393248 | tf_op jit(solution)/shard_map/ppermute | solution.py:44
  61.1 4.2 %collective-permute-done.15.b = bf16[6,64,512]{2,1,0:T(8,128)(2,1)S(1)} collective-permute-done((bf16[6,64,512]{2,1,0:T(8,128)(2,1)S(1)}, bf16[6,64,512]{2,1,0:T(8,128)(2,1)S(1)}, u32[]{:S(2)}, u32[]{:S(2)}) %collective-permute-start.15) | collective-permute-done | bytes 393248 | tf_op jit(solution)/shard_map/ppermute | solution.py:44
  65.2 0.0 collective-permute-done.16.d
  65.2 0.3 near.1
  65.6 0.0 copy-start.8
  65.6 1.0 collective-permute-start.17
  66.6 1.7 %collective-permute-start.19 = (bf16[19,64,512]{2,1,0:T(8,128)(2,1)S(1)}, bf16[19,64,512]{2,1,0:T(8,128)(2,1)S(1)}, u32[]{:S(2)}, u32[]{:S(2)}) collective-permute-start(bf16[19,64,512]{2,1,0:T(8,128)(2,1)S(1)} %get-tuple-element.75), channel_id=1, source_target_pairs={{0,12},{1,13},{2,14},{3,15},{4,0},{5,1},{6,2},{7,3},{8,4},{9,5},{1... | collective-permute-start | bytes 3735560 | tf_op jit(solution)/shard_map/ppermute | solution.py:44
  68.3 14.6 %collective-permute-done.17.refs_1_.one = bf16[19,64,512]{2,1,0:T(8,128)(2,1)S(1)} collective-permute-done((bf16[19,64,512]{2,1,0:T(8,128)(2,1)S(1)}, bf16[19,64,512]{2,1,0:T(8,128)(2,1)S(1)}, u32[]{:S(2)}, u32[]{:S(2)}) %collective-permute-start.17) | collective-permute-done | bytes 1245216 | tf_op jit(solution)/shard_map/ppermute | solution.py:44
  82.9 2.1 %collective-permute-start.22 = (bf16[19,64,512]{2,1,0:T(8,128)(2,1)S(1)}, bf16[19,64,512]{2,1,0:T(8,128)(2,1)S(1)}, u32[]{:S(2)}, u32[]{:S(2)}) collective-permute-start(bf16[19,64,512]{2,1,0:T(8,128)(2,1)S(1)} %collective-permute-done.17.refs_1_.one), channel_id=1, source_target_pairs={{0,16},{1,17},{2,18},{3,19},{4,20},{5,21},{6,22},{7,23},{8,24},{9,... | collective-permute-start | bytes 3735560 | tf_op jit(solution)/shard_map/ppermute | solution.py:44
  85.0 0.0 collective-permute-start.23
  85.0 0.5 collective-permute-start.21
  85.6 0.9 collective-permute-start.18
  86.5 1.9 %collective-permute-start.20 = (bf16[9,64,512]{2,1,0:T(8,128)(2,1)S(1)}, bf16[9,64,512]{2,1,0:T(8,128)(2,1)S(1)}, u32[]{:S(2)}, u32[]{:S(2)}) collective-permute-start(bf16[9,64,512]{2,1,0:T(8,128)(2,1)S(1)} %slice.9), channel_id=1, source_target_pairs={{0,12},{1,13},{2,14},{3,15},{4,0},{5,1},{6,2},{7,3},{8,4},{9,5},{1... | collective-permute-start | bytes 1769480 | tf_op jit(solution)/shard_map/ppermute | solution.py:44
  88.4 2.6 %collective-permute-done.21.refs_1_ = bf16[18,64,512]{2,1,0:T(8,128)(2,1)S(1)} collective-permute-done((bf16[18,64,512]{2,1,0:T(8,128)(2,1)S(1)}, bf16[18,64,512]{2,1,0:T(8,128)(2,1)S(1)}, u32[]{:S(2)}, u32[]{:S(2)}) %collective-permute-start.21) | collective-permute-done | bytes 1179680 | tf_op jit(solution)/shard_map/ppermute | solution.py:44
  91.1 1.9 %place.3.refs_0_ = bf16[16,4,2,64,512]{4,3,2,1,0:T(8,128)(2,1)} custom-call(s32[62]{0:T(128)S(1)} %copy-done.8, bf16[18,64,512]{2,1,0:T(8,128)(2,1)S(1)} %get-tuple-element.76.refs_0_.near, bf16[18,64,512]{2,1,0:T(8,128)(2,1)S(1)} %collective-permute-done.21.refs_1_), custom_call_target="tpu_custom_call" | custom-call | bytes 4718592 | tf_op jit(solution)/shard_map/place/pallas_call | solution.py:320
  93.0 1.9 %place.4.refs_0_ = bf16[16,4,2,64,512]{4,3,2,1,0:T(8,128)(2,1)} custom-call(s32[62]{0:T(128)S(1)} %copy-done.8, bf16[16,4,2,64,512]{4,3,2,1,0:T(8,128)(2,1)} %place.3.refs_0_, bf16[19,64,512]{2,1,0:T(8,128)(2,1)S(1)} %collective-permute-done.17.refs_1_.one, bf16[19,64,512]{2,1,0:T(8,128)(2,1)S(1)} %collective-permute-done.22.refs_2_), custom_call_target="tpu_custom_call", output_to_operand_aliasing={{}: (1, {})} | custom-call | bytes 4980736 | tf_op jit(solution)/shard_map/place/pallas_call | solution.py:320
  94.9 0.0 copy-start.5
  94.9 0.0 copy-start.6
  95.0 1.9 %place.5.begun = bf16[16,4,2,64,512]{4,3,2,1,0:T(8,128)(2,1)} custom-call(s32[62]{0:T(128)S(1)} %copy-done.8, bf16[16,4,2,64,512]{4,3,2,1,0:T(8,128)(2,1)} %place.4.refs_0_, bf16[19,64,512]{2,1,0:T(8,128)(2,1)S(1)} %collective-permute-done.19.refs_1_.three, bf16[19,64,512]{2,1,0:T(8,128)(2,1)S(1)} %collective-permute-done.23.refs_2_), custom_call_target="tpu_custom_call", output_to_operand_aliasing={{}: (1, {})} | custom-call | bytes 4980736 | tf_op jit(solution)/shard_map/place/pallas_call | solution.py:320
  96.9 0.5 collective-permute-start.24
  97.4 0.1 collective-permute-start.25
  97.5 2.0 %owner.1 = (bf16[16,4,2,64,512]{4,3,2,1,0:T(8,128)(2,1)}, f32[3,64,512]{2,1,0:T(8,128)}, f32[3,64,512]{2,1,0:T(8,128)}, f32[3,64,512]{2,1,0:T(8,128)}) custom-call(s32[62]{0:T(128)S(1)} %copy-done.8, bf16[16,4,2,64,512]{4,3,2,1,0:T(8,128)(2,1)} %place.5.begun, f32[3,64,512]{2,1,0:T(8,128)S(1)} %bitcast.11, ...), custom_call_target="tpu_custom_call", output_to_operand_aliasing={{0}: (1, {})} | custom-call | bytes 4849664 | tf_op jit(solution)/shard_map/owner/pallas_call | solution.py:455
  99.6 0.3 collective-permute-done.25.high_other
  99.9 1.5 %finish.1 = bf16[16,4,2,64,512]{4,3,2,1,0:T(8,128)(2,1)} custom-call(s32[62]{0:T(128)S(1)} %copy-done.8, bf16[16,4,2,64,512]{4,3,2,1,0:T(8,128)(2,1)} %get-tuple-element.80.begun, bf16[9,64,512]{2,1,0:T(8,128)(2,1)S(1)} %collective-permute-done.24.low_other, bf16[9,64,512]{2,1,0:T(8,128)(2,1)S(1)} %collective-permute-done.25.high_other), custom_call_target="tpu_custom_call", output_to_operand_aliasing={{}: (1, {})} | custom-call | bytes 1179648 | tf_op jit(solution)/shard_map/finish/pallas_call | solution.py:467
  (23 shorter events, 0.2 us)
Async XLA Ops:
  0.6 9.3 %copy-start.1 = (f32[1,3,64,512]{3,2,1,0:T(8,128)S(1)}, f32[1,3,64,512]{3,2,1,0:T(8,128)}, u32[]{:S(2)}) copy-start(f32[1,3,64,512]{3,2,1,0:T(8,128)} %param.15) | copy-start | bytes 1179652
  0.6 3.2 %collective-permute-start = (bf16[512,512]{1,0:T(8,128)(2,1)}, bf16[512,512]{1,0:T(8,128)(2,1)S(1)}, u32[]{:S(2)}, u32[]{:S(2)}) collective-permute-start(bf16[512,512]{1,0:T(8,128)(2,1)} %bitcast.12), channel_id=1, source_target_pairs={{0,16},{1,17},{2,18},{3,19},{4,20},{5,21},{6,22},{7,23},{8,24},{9,... | collective-permute-start | bytes 1572872 | tf_op jit(solution)/shard_map/ppermute | solution.py:44
  2.1 1.0 %copy-start.2 = (bf16[1,1,512,512]{3,2,1,0:T(8,128)(2,1)S(1)}, bf16[1,1,512,512]{3,2,1,0:T(8,128)(2,1)}, u32[]{:S(2)}) copy-start(bf16[1,1,512,512]{3,2,1,0:T(8,128)(2,1)} %param.8) | copy-start | bytes 1572868
  3.2 6.8 %copy-start.3 = (f32[1,3,64,512]{3,2,1,0:T(8,128)S(1)}, f32[1,3,64,512]{3,2,1,0:T(8,128)}, u32[]{:S(2)}) copy-start(f32[1,3,64,512]{3,2,1,0:T(8,128)} %param.13) | copy-start | bytes 1179652
  3.2 6.8 %copy-start.4 = (f32[1,3,64,512]{3,2,1,0:T(8,128)S(1)}, f32[1,3,64,512]{3,2,1,0:T(8,128)}, u32[]{:S(2)}) copy-start(f32[1,3,64,512]{3,2,1,0:T(8,128)} %param.14) | copy-start | bytes 1179652
  4.0 7.3 %collective-permute-start.1 = (bf16[64,512]{1,0:T(8,128)(2,1)S(1)}, bf16[64,512]{1,0:T(8,128)(2,1)S(1)}, u32[]{:S(2)}, u32[]{:S(2)}) collective-permute-start(bf16[64,512]{1,0:T(8,128)(2,1)S(1)} %get-tuple-element.54), channel_id=1, source_target_pairs={{0,32},{1,33},{2,34},{3,35},{4,36},{5,37},{6,38},{7,39},{8,40},{9,... | collective-permute-start | bytes 196616 | tf_op jit(solution)/shard_map/ppermute | solution.py:44
  5.3 5.9 %collective-permute-start.2 = (bf16[64,512]{1,0:T(8,128)(2,1)S(1)}, bf16[64,512]{1,0:T(8,128)(2,1)S(1)}, u32[]{:S(2)}, u32[]{:S(2)}) collective-permute-start(bf16[64,512]{1,0:T(8,128)(2,1)S(1)} %get-tuple-element.55), channel_id=1, source_target_pairs={{0,96},{1,97},{2,98},{3,99},{4,100},{5,101},{6,102},{7,103},{8,104... | collective-permute-start | bytes 196616 | tf_op jit(solution)/shard_map/ppermute | solution.py:44
  6.7 4.6 %collective-permute-start.3 = (bf16[64,512]{1,0:T(8,128)(2,1)S(1)}, bf16[64,512]{1,0:T(8,128)(2,1)S(1)}, u32[]{:S(2)}, u32[]{:S(2)}) collective-permute-start(bf16[64,512]{1,0:T(8,128)(2,1)S(1)} %get-tuple-element.56), channel_id=1, source_target_pairs={{0,64},{1,65},{2,66},{3,67},{4,68},{5,69},{6,70},{7,71},{8,72},{9,... | collective-permute-start | bytes 196616 | tf_op jit(solution)/shard_map/ppermute | solution.py:44
  10.0 0.7 copy-start.7
  10.6 12.1 %copy-start = (bf16[14,16,512]{2,1,0:T(8,128)(2,1)S(1)}, bf16[14,16,512]{2,1,0:T(8,128)(2,1)}, u32[]{:S(2)}) copy-start(bf16[14,16,512]{2,1,0:T(8,128)(2,1)} %get-tuple-element.52.tiles) | copy-start | bytes 688132
  11.4 7.8 %collective-permute-start.4 = (bf16[4,64,512]{2,1,0:T(8,128)(2,1)S(1)}, bf16[4,64,512]{2,1,0:T(8,128)(2,1)S(1)}, u32[]{:S(2)}, u32[]{:S(2)}) collective-permute-start(bf16[4,64,512]{2,1,0:T(8,128)(2,1)S(1)} %get-tuple-element.65), channel_id=1, source_target_pairs={{0,2},{1,3},{2,0},{3,1},{4,6},{5,7},{6,4},{7,5},{8,10},{9,11},{10,... | collective-permute-start | bytes 786440 | tf_op jit(solution)/shard_map/ppermute | solution.py:44
  15.1 6.9 %collective-permute-start.5 = (bf16[4,64,512]{2,1,0:T(8,128)(2,1)S(1)}, bf16[4,64,512]{2,1,0:T(8,128)(2,1)S(1)}, u32[]{:S(2)}, u32[]{:S(2)}) collective-permute-start(bf16[4,64,512]{2,1,0:T(8,128)(2,1)S(1)} %get-tuple-element.66), channel_id=1, source_target_pairs={{0,1},{1,2},{2,3},{3,0},{4,5},{5,6},{6,7},{7,4},{8,9},{9,10},{10,1... | collective-permute-start | bytes 786440 | tf_op jit(solution)/shard_map/ppermute | solution.py:44
  15.9 6.9 %collective-permute-start.6 = (bf16[4,64,512]{2,1,0:T(8,128)(2,1)S(1)}, bf16[4,64,512]{2,1,0:T(8,128)(2,1)S(1)}, u32[]{:S(2)}, u32[]{:S(2)}) collective-permute-start(bf16[4,64,512]{2,1,0:T(8,128)(2,1)S(1)} %get-tuple-element.67), channel_id=1, source_target_pairs={{0,3},{1,0},{2,1},{3,2},{4,7},{5,4},{6,5},{7,6},{8,11},{9,8},{10,9... | collective-permute-start | bytes 786440 | tf_op jit(solution)/shard_map/ppermute | solution.py:44
  23.0 7.1 %collective-permute-start.7 = (bf16[4,64,512]{2,1,0:T(8,128)(2,1)S(1)}, bf16[4,64,512]{2,1,0:T(8,128)(2,1)S(1)}, u32[]{:S(2)}, u32[]{:S(2)}) collective-permute-start(bf16[4,64,512]{2,1,0:T(8,128)(2,1)S(1)} %get-tuple-element.69), channel_id=1, source_target_pairs={{0,8},{1,9},{2,10},{3,11},{4,12},{5,13},{6,14},{7,15},{8,0},{9,1},... | collective-permute-start | bytes 786440 | tf_op jit(solution)/shard_map/ppermute | solution.py:44
  26.0 6.8 %collective-permute-start.8 = (bf16[4,64,512]{2,1,0:T(8,128)(2,1)S(1)}, bf16[4,64,512]{2,1,0:T(8,128)(2,1)S(1)}, u32[]{:S(2)}, u32[]{:S(2)}) collective-permute-start(bf16[4,64,512]{2,1,0:T(8,128)(2,1)S(1)} %get-tuple-element.70), channel_id=1, source_target_pairs={{0,4},{1,5},{2,6},{3,7},{4,8},{5,9},{6,10},{7,11},{8,12},{9,13},{1... | collective-permute-start | bytes 786440 | tf_op jit(solution)/shard_map/ppermute | solution.py:44
  26.4 6.9 %collective-permute-start.9 = (bf16[4,64,512]{2,1,0:T(8,128)(2,1)S(1)}, bf16[4,64,512]{2,1,0:T(8,128)(2,1)S(1)}, u32[]{:S(2)}, u32[]{:S(2)}) collective-permute-start(bf16[4,64,512]{2,1,0:T(8,128)(2,1)S(1)} %get-tuple-element.71), channel_id=1, source_target_pairs={{0,12},{1,13},{2,14},{3,15},{4,0},{5,1},{6,2},{7,3},{8,4},{9,5},{1... | collective-permute-start | bytes 786440 | tf_op jit(solution)/shard_map/ppermute | solution.py:44
  33.3 6.9 %collective-permute-start.10 = (bf16[4,64,512]{2,1,0:T(8,128)(2,1)S(1)}, bf16[4,64,512]{2,1,0:T(8,128)(2,1)S(1)}, u32[]{:S(2)}, u32[]{:S(2)}) collective-permute-start(bf16[4,64,512]{2,1,0:T(8,128)(2,1)S(1)} %here.1.refs_0_), channel_id=1, source_target_pairs={{0,64},{1,65},{2,66},{3,67},{4,68},{5,69},{6,70},{7,71},{8,72},{9,... | collective-permute-start | bytes 786440 | tf_op jit(solution)/shard_map/ppermute | solution.py:44
  34.9 11.6 %collective-permute-start.11 = (bf16[4,64,512]{2,1,0:T(8,128)(2,1)S(1)}, bf16[4,64,512]{2,1,0:T(8,128)(2,1)S(1)}, u32[]{:S(2)}, u32[]{:S(2)}) collective-permute-start(bf16[4,64,512]{2,1,0:T(8,128)(2,1)S(1)} %here.1.refs_0_), channel_id=1, source_target_pairs={{0,32},{1,33},{2,34},{3,35},{4,36},{5,37},{6,38},{7,39},{8,40},{9,... | collective-permute-start | bytes 786440 | tf_op jit(solution)/shard_map/ppermute | solution.py:44
  35.3 11.2 %collective-permute-start.12 = (bf16[4,64,512]{2,1,0:T(8,128)(2,1)S(1)}, bf16[4,64,512]{2,1,0:T(8,128)(2,1)S(1)}, u32[]{:S(2)}, u32[]{:S(2)}) collective-permute-start(bf16[4,64,512]{2,1,0:T(8,128)(2,1)S(1)} %here.1.refs_0_), channel_id=1, source_target_pairs={{0,96},{1,97},{2,98},{3,99},{4,100},{5,101},{6,102},{7,103},{8,104... | collective-permute-start | bytes 786440 | tf_op jit(solution)/shard_map/ppermute | solution.py:44
  46.6 4.7 %collective-permute-start.13 = (bf16[4,3,64,512]{3,2,1,0:T(8,128)(2,1)S(1)}, bf16[4,3,64,512]{3,2,1,0:T(8,128)(2,1)S(1)}, u32[]{:S(2)}, u32[]{:S(2)}) collective-permute-start(bf16[4,3,64,512]{3,2,1,0:T(8,128)(2,1)S(1)} %get-tuple-element.72.mine), channel_id=1, source_target_pairs={{0,16},{1,17},{2,18},{3,19},{4,20},{5,21},{6,22},{7,23},{8,24},{9,... | collective-permute-start | bytes 2359304 | tf_op jit(solution)/shard_map/ppermute | solution.py:44
  52.5 8.5 %collective-permute-start.14 = (bf16[6,64,512]{2,1,0:T(8,128)(2,1)S(1)}, bf16[6,64,512]{2,1,0:T(8,128)(2,1)S(1)}, u32[]{:S(2)}, u32[]{:S(2)}) collective-permute-start(bf16[6,64,512]{2,1,0:T(8,128)(2,1)S(1)} %step.1.a), channel_id=1, source_target_pairs={{0,2},{1,3},{2,0},{3,1},{4,6},{5,7},{6,4},{7,5},{8,10},{9,11},{10,... | collective-permute-start | bytes 1179656 | tf_op jit(solution)/shard_map/ppermute | solution.py:44
  54.4 10.9 %collective-permute-start.15 = (bf16[6,64,512]{2,1,0:T(8,128)(2,1)S(1)}, bf16[6,64,512]{2,1,0:T(8,128)(2,1)S(1)}, u32[]{:S(2)}, u32[]{:S(2)}) collective-permute-start(bf16[6,64,512]{2,1,0:T(8,128)(2,1)S(1)} %step.1.a), channel_id=1, source_target_pairs={{0,1},{1,2},{2,3},{3,0},{4,5},{5,6},{6,7},{7,4},{8,9},{9,10},{10,1... | collective-permute-start | bytes 1179656 | tf_op jit(solution)/shard_map/ppermute | solution.py:44
  55.3 9.9 %collective-permute-start.16 = (bf16[6,64,512]{2,1,0:T(8,128)(2,1)S(1)}, bf16[6,64,512]{2,1,0:T(8,128)(2,1)S(1)}, u32[]{:S(2)}, u32[]{:S(2)}) collective-permute-start(bf16[6,64,512]{2,1,0:T(8,128)(2,1)S(1)} %step.1.a), channel_id=1, source_target_pairs={{0,3},{1,0},{2,1},{3,2},{4,7},{5,4},{6,5},{7,6},{8,11},{9,8},{10,9... | collective-permute-start | bytes 1179656 | tf_op jit(solution)/shard_map/ppermute | solution.py:44
  65.6 25.5 %copy-start.8 = (s32[62]{0:T(128)S(1)}, s32[62]{0:T(128)}, u32[]{:S(2)}) copy-start(s32[62]{0:T(128)} %get-tuple-element.51.spot) | copy-start | bytes 748
  65.6 17.3 %collective-permute-start.17 = (bf16[19,64,512]{2,1,0:T(8,128)(2,1)S(1)}, bf16[19,64,512]{2,1,0:T(8,128)(2,1)S(1)}, u32[]{:S(2)}, u32[]{:S(2)}) collective-permute-start(bf16[19,64,512]{2,1,0:T(8,128)(2,1)S(1)} %get-tuple-element.74), channel_id=1, source_target_pairs={{0,4},{1,5},{2,6},{3,7},{4,8},{5,9},{6,10},{7,11},{8,12},{9,13},{1... | collective-permute-start | bytes 3735560 | tf_op jit(solution)/shard_map/ppermute | solution.py:44
  66.6 18.4 %collective-permute-start.19 = (bf16[19,64,512]{2,1,0:T(8,128)(2,1)S(1)}, bf16[19,64,512]{2,1,0:T(8,128)(2,1)S(1)}, u32[]{:S(2)}, u32[]{:S(2)}) collective-permute-start(bf16[19,64,512]{2,1,0:T(8,128)(2,1)S(1)} %get-tuple-element.75), channel_id=1, source_target_pairs={{0,12},{1,13},{2,14},{3,15},{4,0},{5,1},{6,2},{7,3},{8,4},{9,5},{1... | collective-permute-start | bytes 3735560 | tf_op jit(solution)/shard_map/ppermute | solution.py:44
  82.9 10.1 %collective-permute-start.22 = (bf16[19,64,512]{2,1,0:T(8,128)(2,1)S(1)}, bf16[19,64,512]{2,1,0:T(8,128)(2,1)S(1)}, u32[]{:S(2)}, u32[]{:S(2)}) collective-permute-start(bf16[19,64,512]{2,1,0:T(8,128)(2,1)S(1)} %collective-permute-done.17.refs_1_.one), channel_id=1, source_target_pairs={{0,16},{1,17},{2,18},{3,19},{4,20},{5,21},{6,22},{7,23},{8,24},{9,... | collective-permute-start | bytes 3735560 | tf_op jit(solution)/shard_map/ppermute | solution.py:44
  85.0 9.9 %collective-permute-start.23 = (bf16[19,64,512]{2,1,0:T(8,128)(2,1)S(1)}, bf16[19,64,512]{2,1,0:T(8,128)(2,1)S(1)}, u32[]{:S(2)}, u32[]{:S(2)}) collective-permute-start(bf16[19,64,512]{2,1,0:T(8,128)(2,1)S(1)} %collective-permute-done.19.refs_1_.three), channel_id=1, source_target_pairs={{0,16},{1,17},{2,18},{3,19},{4,20},{5,21},{6,22},{7,23},{8,24},{9,... | collective-permute-start | bytes 3735560 | tf_op jit(solution)/shard_map/ppermute | solution.py:44
  85.0 6.0 %collective-permute-start.21 = (bf16[18,64,512]{2,1,0:T(8,128)(2,1)S(1)}, bf16[18,64,512]{2,1,0:T(8,128)(2,1)S(1)}, u32[]{:S(2)}, u32[]{:S(2)}) collective-permute-start(bf16[18,64,512]{2,1,0:T(8,128)(2,1)S(1)} %get-tuple-element.76.refs_0_.near), channel_id=1, source_target_pairs={{0,16},{1,17},{2,18},{3,19},{4,20},{5,21},{6,22},{7,23},{8,24},{9,... | collective-permute-start | bytes 3538952 | tf_op jit(solution)/shard_map/ppermute | solution.py:44
  85.6 11.3 %collective-permute-start.18 = (bf16[9,64,512]{2,1,0:T(8,128)(2,1)S(1)}, bf16[9,64,512]{2,1,0:T(8,128)(2,1)S(1)}, u32[]{:S(2)}, u32[]{:S(2)}) collective-permute-start(bf16[9,64,512]{2,1,0:T(8,128)(2,1)S(1)} %slice.8), channel_id=1, source_target_pairs={{0,4},{1,5},{2,6},{3,7},{4,8},{5,9},{6,10},{7,11},{8,12},{9,13},{1... | collective-permute-start | bytes 1769480 | tf_op jit(solution)/shard_map/ppermute | solution.py:44
  86.5 10.4 %collective-permute-start.20 = (bf16[9,64,512]{2,1,0:T(8,128)(2,1)S(1)}, bf16[9,64,512]{2,1,0:T(8,128)(2,1)S(1)}, u32[]{:S(2)}, u32[]{:S(2)}) collective-permute-start(bf16[9,64,512]{2,1,0:T(8,128)(2,1)S(1)} %slice.9), channel_id=1, source_target_pairs={{0,12},{1,13},{2,14},{3,15},{4,0},{5,1},{6,2},{7,3},{8,4},{9,5},{1... | collective-permute-start | bytes 1769480 | tf_op jit(solution)/shard_map/ppermute | solution.py:44
  94.9 2.6 %copy-start.5 = (f32[1,3,64,512]{3,2,1,0:T(8,128)S(1)}, f32[1,3,64,512]{3,2,1,0:T(8,128)}, u32[]{:S(2)}) copy-start(f32[1,3,64,512]{3,2,1,0:T(8,128)} %param.11) | copy-start | bytes 1179652
  94.9 2.6 %copy-start.6 = (f32[1,3,64,512]{3,2,1,0:T(8,128)S(1)}, f32[1,3,64,512]{3,2,1,0:T(8,128)}, u32[]{:S(2)}) copy-start(f32[1,3,64,512]{3,2,1,0:T(8,128)} %param.12) | copy-start | bytes 1179652
  96.9 2.6 %collective-permute-start.24 = (bf16[9,64,512]{2,1,0:T(8,128)(2,1)S(1)}, bf16[9,64,512]{2,1,0:T(8,128)(2,1)S(1)}, u32[]{:S(2)}, u32[]{:S(2)}) collective-permute-start(bf16[9,64,512]{2,1,0:T(8,128)(2,1)S(1)} %collective-permute-done.18.low), channel_id=1, source_target_pairs={{0,16},{1,17},{2,18},{3,19},{4,20},{5,21},{6,22},{7,23},{8,24},{9,... | collective-permute-start | bytes 1769480 | tf_op jit(solution)/shard_map/ppermute | solution.py:44
  97.4 2.5 %collective-permute-start.25 = (bf16[9,64,512]{2,1,0:T(8,128)(2,1)S(1)}, bf16[9,64,512]{2,1,0:T(8,128)(2,1)S(1)}, u32[]{:S(2)}, u32[]{:S(2)}) collective-permute-start(bf16[9,64,512]{2,1,0:T(8,128)(2,1)S(1)} %collective-permute-done.20.high), channel_id=1, source_target_pairs={{0,16},{1,17},{2,18},{3,19},{4,20},{5,21},{6,22},{7,23},{8,24},{9,... | collective-permute-start | bytes 1769480 | tf_op jit(solution)/shard_map/ppermute | solution.py:44

commit v6 on v5

--- a/solution.py
+++ b/solution.py
@@ -206,7 +206,7 @@
         slot = spot[SLOT_PICK + k]
         out[0] = left[slot].astype(half_type)
         out[1] = right[slot].astype(half_type)
-        out[2] = moment[slot].astype(half_type)
+        out[3] = moment[slot].astype(half_type)
 
 
 def total_kernel(own, a, c, b, *packs):
@@ -214,13 +214,13 @@
     total = total + b[...].astype(wide_type)
     total = (total + c[...].astype(wide_type)).astype(half_type)
     for out in packs[4:]:
-        out[3] = total
+        out[2] = total
 
 
 def turn_kernel(tiles, a, c, b, d, *outs):
     for n in range(4):
         options = [source[n] for source in (a, b, c, d)]
-        base = GRAD_PICK if n == 3 else ROOT_PICK
+        base = GRAD_PICK if n == 2 else ROOT_PICK
         for k, out in enumerate(outs):
             out[n] = blend(tiles[base + k], options)
 
@@ -228,28 +228,24 @@
 def here_kernel(tiles, a, c, b, d, out):
     for n in range(4):
         options = [source[n] for source in (a, b, c, d)]
-        out[n] = blend(tiles[GRAD_LAST if n == 3 else ROOT_LAST], options)
-
-
-def line_kernel(*refs):
-    shared, moment = refs[4:]
-    x = position()[0]
-    for i, k in enumerate((0, 2, 1, 3)):
+        out[n] = blend(tiles[GRAD_LAST if n == 2 else ROOT_LAST], options)
+
+
+def both_kernel(one, three, out):
+    out[0] = one[:3]
+    out[1] = three[:3]
+
+
+def step_kernel(own, two, one, three, own_other, two_other, rest_other, out, grad, full, held):
+    x, c, _, _ = position()
+    others = (own_other, rest_other.at[0], two_other, rest_other.at[1])
+    for k, mine in enumerate((own, one, two, three)):
         n = (x - k) & 3
-        shared[n, 0] = refs[i][0]
-        shared[n, 1] = refs[i][1]
-        shared[n, 2] = refs[i][3]
-        moment[n] = refs[i][2]
-
-
-def step_kernel(mine, moment, other, out, grad, full, held):
-    x, c, _, _ = position()
-    for n in range(X):
-        for core, source in ((c, mine), (1 - c, other)):
+        for core, source in ((c, mine), (1 - c, others[k])):
             rows = pl.ds(pl.multiple_of((2 * n + core) * ROWS, ROWS), ROWS)
             for which in range(2):
-                full[which, rows, :] = source[n, which]
-            grad[pl.ds(pl.multiple_of(core * HALF + n * ROWS, ROWS), ROWS), :] = source[n, 2]
+                full[which, rows, :] = source[which]
+            grad[pl.ds(pl.multiple_of(core * HALF + n * ROWS, ROWS), ROWS), :] = source[2]
     g = grad[...]
     wide = g.astype(wide_type)
     grad_square = jnp.sum(wide * wide)
@@ -259,9 +255,10 @@
     entries = float(BS * BS)
     top = jnp.sqrt(jnp.full((1, BS), grad_square / entries, wide_type))
     graft = top / jnp.sqrt(jnp.full((1, BS), dir_square / entries + epsilon, wide_type))
-    for n in range(X):
+    for k, mine in enumerate((own, one, two, three)):
+        n = (x - k) & 3
         rows = pl.ds(pl.multiple_of((2 * n + c) * ROWS, ROWS), ROWS)
-        fresh = decay_moment * moment[n].astype(wide_type) + graft * held[rows, :]
+        fresh = decay_moment * mine[3].astype(wide_type) + graft * held[rows, :]
         out[n] = fresh.astype(half_type)
     rows = grad[pl.ds(pl.multiple_of((2 * x + c) * ROWS, ROWS), ROWS), :]
     out[4] = lax.dot_general(
@@ -372,7 +369,7 @@
 
 def finish_kernel(spot, begun, low_other, high_other, out, sems):
     del begun
-    sources = ((6, 0, 2, 1, low_other), (6, 2, 2, 0, high_other))
+    sources = ((6, 0, 2, 0, low_other), (6, 2, 2, 0, high_other))
     copies = placed_copies(spot, sources, out, sems)
     for copy in copies:
         copy.start()
@@ -412,22 +409,23 @@
     row = along(to_u, packs, (2, 1, 3))
     column = along(to_v, small_call(turn_kernel, [pack_type] * 4, "turn", tiles, *row), (2, 1, 3))
     pack = small_call(here_kernel, pack_type, "here", tiles, *column)
-    shared, moment = small_call(
-        line_kernel,
-        [
-            jax.ShapeDtypeStruct((X, 3, ROWS, BS), half_type),
-            jax.ShapeDtypeStruct((X, ROWS, BS), half_type),
-        ],
-        "line",
-        *along(to_x, [pack] * 4, (2, 1, 3)),
+    own, two, one, three = along(to_x, [pack] * 4, (2, 1, 3))
+    own_other, two_other = to_core(own[:3]), to_core(two[:3])
+    one, three, own_other, two_other = hold((one, three, own_other, two_other))
+    rest = small_call(
+        both_kernel, jax.ShapeDtypeStruct((2, 3, ROWS, BS), half_type), "both", one, three
     )
     send = small_call(
         step_kernel,
         jax.ShapeDtypeStruct((6, ROWS, BS), half_type),
         "step",
-        shared,
-        moment,
-        to_core(shared),
+        own,
+        two,
+        one,
+        three,
+        own_other,
+        two_other,
+        to_core(rest),
         flops=6 * BS**3,
         scratch=[
             pltpu.VMEM((BS, BS), half_type),
@@ -446,12 +444,13 @@
     near_other = to_core(near)
     low = to_v(one[:9], 1)
     high = to_v(three[8:17], 3)
-    one_other, three_other = to_core(one), to_core(three)
     begun = place(0, spot, None, near, near_other)
+    (far_one, far_three), _ = hold(((one, three), begun))
+    one_other, three_other = to_core(far_one), to_core(far_three)
     begun = place(1, spot, begun, one, one_other)
     begun = place(3, spot, begun, three, three_other)
     low, high, begun = hold((low, high, begun))
-    low_other, high_other = to_core(low), to_core(high)
+    low_other, high_other = to_core(low[1:]), to_core(high[:8])
     begun, new_momentum, left_stats, right_stats = pl.pallas_call(
         owner_kernel,
         out_shape=[jax.ShapeDtypeStruct(begun.shape, half_type)] + [stat_type] * 3,

time: 102 us -> 100 us (0.980)
  waiting for transfers between devices: 46.8 us -> 35.3 us
  starting transfers between devices: 38.3 us -> 48.4 us
    ppermute x26 -> x28, waiting for transfers between devices: 46.8 us -> 35.3 us  [permute(): return lax.ppermute(value, AXES, pairs)]
    ppermute x26 -> x28, starting transfers between devices: 38.3 us -> 48.4 us  [permute(): return lax.ppermute(value, AXES, pairs)]
  transfers between devices with their start and end apart: 26 -> 28, of which waited for: 15 -> 15; matrix products, arithmetic and copies ran while one was open for 0% -> 0% of each run, Pallas kernels for 10% -> 10%
where the time goes in v6:
time: 100 us
  starting transfers between devices  48.4 us (48%)
  waiting for transfers between devices  35.3 us (35%)
  Pallas kernels  13.6 us (14%)
  local copies, waits for them, and re-layouts  1.9 us (2%)
    ppermute x28, starting transfers between devices, permute(): return lax.ppermute(value, AXES, pairs)  48.4 us
    ppermute x28, waiting for transfers between devices, permute(): return lax.ppermute(value, AXES, pairs)  35.3 us
    pallas_call x3, Pallas kernels, place(): pl.pallas_call(functools.partial(place_kernel, which), out_shape=jax.Shap...  5.78 us
    pallas_call x9, Pallas kernels, small_call(): pl.pallas_call(body, out_shape=outs, in_specs=[SMEM if a.dtype == jnp.int...  2.65 us
    pallas_call x1, Pallas kernels, local(): pl.pallas_call(owner_kernel, out_shape=[jax.ShapeDtypeStruct(begun.shape,...  2.02 us
  transfers between devices with their start and end apart: 28, of which 15 were waited for; matrix products, arithmetic and copies ran while one was open for 0% of the time, Pallas kernels for 10%

profile of v6, /device:TPU:1, one launch (start us, length us, event | category | flops | bytes accessed | tf_op | source)
XLA Modules:
  0.0 100.1 jit_solution(13376117996593457980)
XLA Ops:
  0.6 1.5 %collective-permute-start = (bf16[512,512]{1,0:T(8,128)(2,1)}, bf16[512,512]{1,0:T(8,128)(2,1)S(1)}, u32[]{:S(2)}, u32[]{:S(2)}) collective-permute-start(bf16[512,512]{1,0:T(8,128)(2,1)} %bitcast.12), channel_id=1, source_target_pairs={{0,16},{1,17},{2,18},{3,19},{4,20},{5,21},{6,22},{7,23},{8,24},{9,... | collective-permute-start | bytes 1572872 | tf_op jit(solution)/shard_map/ppermute | solution.py:44
  2.1 1.0 %copy-done.2 = bf16[1,1,512,512]{3,2,1,0:T(8,128)(2,1)S(1)} copy-done((bf16[1,1,512,512]{3,2,1,0:T(8,128)(2,1)S(1)}, bf16[1,1,512,512]{3,2,1,0:T(8,128)(2,1)}, u32[]{:S(2)}) %copy-start.2) | copy-done | bytes 524312
  3.2 0.7 collective-permute-done.theirs
  3.9 0.1 pair.1
  4.0 1.4 %collective-permute-start.1 = (bf16[64,512]{1,0:T(8,128)(2,1)S(1)}, bf16[64,512]{1,0:T(8,128)(2,1)S(1)}, u32[]{:S(2)}, u32[]{:S(2)}) collective-permute-start(bf16[64,512]{1,0:T(8,128)(2,1)S(1)} %get-tuple-element.58), channel_id=1, source_target_pairs={{0,32},{1,33},{2,34},{3,35},{4,36},{5,37},{6,38},{7,39},{8,40},{9,... | collective-permute-start | bytes 196616 | tf_op jit(solution)/shard_map/ppermute | solution.py:44
  5.3 1.4 %collective-permute-start.2 = (bf16[64,512]{1,0:T(8,128)(2,1)S(1)}, bf16[64,512]{1,0:T(8,128)(2,1)S(1)}, u32[]{:S(2)}, u32[]{:S(2)}) collective-permute-start(bf16[64,512]{1,0:T(8,128)(2,1)S(1)} %get-tuple-element.59), channel_id=1, source_target_pairs={{0,96},{1,97},{2,98},{3,99},{4,100},{5,101},{6,102},{7,103},{8,104... | collective-permute-start | bytes 196616 | tf_op jit(solution)/shard_map/ppermute | solution.py:44
  6.7 1.6 %collective-permute-start.3 = (bf16[64,512]{1,0:T(8,128)(2,1)S(1)}, bf16[64,512]{1,0:T(8,128)(2,1)S(1)}, u32[]{:S(2)}, u32[]{:S(2)}) collective-permute-start(bf16[64,512]{1,0:T(8,128)(2,1)S(1)} %get-tuple-element.60), channel_id=1, source_target_pairs={{0,64},{1,65},{2,66},{3,67},{4,68},{5,69},{6,70},{7,71},{8,72},{9,... | collective-permute-start | bytes 196616 | tf_op jit(solution)/shard_map/ppermute | solution.py:44
  8.3 1.6 %choices.1 = (s32[62]{0:T(128)}, bf16[14,16,512]{2,1,0:T(8,128)(2,1)}) custom-call(s32[16]{0:T(128)} %order_ref, s32[16]{0:T(128)} %count_ref), custom_call_target="tpu_custom_call" | custom-call | bytes 4194304 | tf_op jit(solution)/shard_map/choices/pallas_call | solution.py:144
  10.0 0.0 copy-start.7
  10.0 0.6 copy-done.7
  10.6 0.6 packs.1
  11.3 0.0 collective-permute-done.2.c
  11.3 0.1 collective-permute-done.3.b
  11.4 3.8 %collective-permute-start.4 = (bf16[4,64,512]{2,1,0:T(8,128)(2,1)S(1)}, bf16[4,64,512]{2,1,0:T(8,128)(2,1)S(1)}, u32[]{:S(2)}, u32[]{:S(2)}) collective-permute-start(bf16[4,64,512]{2,1,0:T(8,128)(2,1)S(1)} %get-tuple-element.69), channel_id=1, source_target_pairs={{0,2},{1,3},{2,0},{3,1},{4,6},{5,7},{6,4},{7,5},{8,10},{9,11},{10,... | collective-permute-start | bytes 786440 | tf_op jit(solution)/shard_map/ppermute | solution.py:44
  15.1 0.7 collective-permute-start.5
  15.9 1.9 %collective-permute-start.6 = (bf16[4,64,512]{2,1,0:T(8,128)(2,1)S(1)}, bf16[4,64,512]{2,1,0:T(8,128)(2,1)S(1)}, u32[]{:S(2)}, u32[]{:S(2)}) collective-permute-start(bf16[4,64,512]{2,1,0:T(8,128)(2,1)S(1)} %get-tuple-element.71), channel_id=1, source_target_pairs={{0,3},{1,0},{2,1},{3,2},{4,7},{5,4},{6,5},{7,6},{8,11},{9,8},{10,9... | collective-permute-start | bytes 786440 | tf_op jit(solution)/shard_map/ppermute | solution.py:44
  17.8 1.4 %collective-permute-done.4.c = bf16[4,64,512]{2,1,0:T(8,128)(2,1)S(1)} collective-permute-done((bf16[4,64,512]{2,1,0:T(8,128)(2,1)S(1)}, bf16[4,64,512]{2,1,0:T(8,128)(2,1)S(1)}, u32[]{:S(2)}, u32[]{:S(2)}) %collective-permute-start.4) | collective-permute-done | bytes 262176 | tf_op jit(solution)/shard_map/ppermute | solution.py:44
  19.2 2.8 %collective-permute-done.5.b = bf16[4,64,512]{2,1,0:T(8,128)(2,1)S(1)} collective-permute-done((bf16[4,64,512]{2,1,0:T(8,128)(2,1)S(1)}, bf16[4,64,512]{2,1,0:T(8,128)(2,1)S(1)}, u32[]{:S(2)}, u32[]{:S(2)}) %collective-permute-start.5) | collective-permute-done | bytes 262176 | tf_op jit(solution)/shard_map/ppermute | solution.py:44
  22.0 0.7 collective-permute-done.6.d
  22.7 0.3 turn.1
  23.0 3.0 %collective-permute-start.7 = (bf16[4,64,512]{2,1,0:T(8,128)(2,1)S(1)}, bf16[4,64,512]{2,1,0:T(8,128)(2,1)S(1)}, u32[]{:S(2)}, u32[]{:S(2)}) collective-permute-start(bf16[4,64,512]{2,1,0:T(8,128)(2,1)S(1)} %get-tuple-element.73), channel_id=1, source_target_pairs={{0,8},{1,9},{2,10},{3,11},{4,12},{5,13},{6,14},{7,15},{8,0},{9,1},... | collective-permute-start | bytes 786440 | tf_op jit(solution)/shard_map/ppermute | solution.py:44
  26.0 0.4 collective-permute-start.8
  26.4 2.3 %collective-permute-start.9 = (bf16[4,64,512]{2,1,0:T(8,128)(2,1)S(1)}, bf16[4,64,512]{2,1,0:T(8,128)(2,1)S(1)}, u32[]{:S(2)}, u32[]{:S(2)}) collective-permute-start(bf16[4,64,512]{2,1,0:T(8,128)(2,1)S(1)} %get-tuple-element.75), channel_id=1, source_target_pairs={{0,12},{1,13},{2,14},{3,15},{4,0},{5,1},{6,2},{7,3},{8,4},{9,5},{1... | collective-permute-start | bytes 786440 | tf_op jit(solution)/shard_map/ppermute | solution.py:44
  28.7 1.4 %collective-permute-done.7.c = bf16[4,64,512]{2,1,0:T(8,128)(2,1)S(1)} collective-permute-done((bf16[4,64,512]{2,1,0:T(8,128)(2,1)S(1)}, bf16[4,64,512]{2,1,0:T(8,128)(2,1)S(1)}, u32[]{:S(2)}, u32[]{:S(2)}) %collective-permute-start.7) | collective-permute-done | bytes 262176 | tf_op jit(solution)/shard_map/ppermute | solution.py:44
  30.1 2.7 %collective-permute-done.8.b = bf16[4,64,512]{2,1,0:T(8,128)(2,1)S(1)} collective-permute-done((bf16[4,64,512]{2,1,0:T(8,128)(2,1)S(1)}, bf16[4,64,512]{2,1,0:T(8,128)(2,1)S(1)}, u32[]{:S(2)}, u32[]{:S(2)}) %collective-permute-start.8) | collective-permute-done | bytes 262176 | tf_op jit(solution)/shard_map/ppermute | solution.py:44
  32.8 0.4 collective-permute-done.9.d
  33.2 0.1 here.1.own
  33.3 1.6 %collective-permute-start.10 = (bf16[4,64,512]{2,1,0:T(8,128)(2,1)S(1)}, bf16[4,64,512]{2,1,0:T(8,128)(2,1)S(1)}, u32[]{:S(2)}, u32[]{:S(2)}) collective-permute-start(bf16[4,64,512]{2,1,0:T(8,128)(2,1)S(1)} %here.1.own), channel_id=1, source_target_pairs={{0,64},{1,65},{2,66},{3,67},{4,68},{5,69},{6,70},{7,71},{8,72},{9,... | collective-permute-start | bytes 786440 | tf_op jit(solution)/shard_map/ppermute | solution.py:44
  34.9 0.4 collective-permute-start.11
  35.3 2.3 %collective-permute-start.12 = (bf16[4,64,512]{2,1,0:T(8,128)(2,1)S(1)}, bf16[4,64,512]{2,1,0:T(8,128)(2,1)S(1)}, u32[]{:S(2)}, u32[]{:S(2)}) collective-permute-start(bf16[4,64,512]{2,1,0:T(8,128)(2,1)S(1)} %here.1.own), channel_id=1, source_target_pairs={{0,96},{1,97},{2,98},{3,99},{4,100},{5,101},{6,102},{7,103},{8,104... | collective-permute-start | bytes 786440 | tf_op jit(solution)/shard_map/ppermute | solution.py:44
  37.6 4.7 %collective-permute-start.13 = (bf16[3,64,512]{2,1,0:T(8,128)(2,1)S(1)}, bf16[3,64,512]{2,1,0:T(8,128)(2,1)S(1)}, u32[]{:S(2)}, u32[]{:S(2)}) collective-permute-start(bf16[3,64,512]{2,1,0:T(8,128)(2,1)S(1)} %slice.24), channel_id=1, source_target_pairs={{0,16},{1,17},{2,18},{3,19},{4,20},{5,21},{6,22},{7,23},{8,24},{9,... | collective-permute-start | bytes 589832 | tf_op jit(solution)/shard_map/ppermute | solution.py:44
  42.3 0.0 collective-permute-done.10.two
  42.3 4.3 %collective-permute-start.14 = (bf16[3,64,512]{2,1,0:T(8,128)(2,1)S(1)}, bf16[3,64,512]{2,1,0:T(8,128)(2,1)S(1)}, u32[]{:S(2)}, u32[]{:S(2)}) collective-permute-start(bf16[3,64,512]{2,1,0:T(8,128)(2,1)S(1)} %slice.25), channel_id=1, source_target_pairs={{0,16},{1,17},{2,18},{3,19},{4,20},{5,21},{6,22},{7,23},{8,24},{9,... | collective-permute-start | bytes 589832 | tf_op jit(solution)/shard_map/ppermute | solution.py:44
  46.6 1.1 %collective-permute-done.14.two_other = bf16[3,64,512]{2,1,0:T(8,128)(2,1)S(1)} collective-permute-done((bf16[3,64,512]{2,1,0:T(8,128)(2,1)S(1)}, bf16[3,64,512]{2,1,0:T(8,128)(2,1)S(1)}, u32[]{:S(2)}, u32[]{:S(2)}) %collective-permute-start.14) | collective-permute-done | bytes 196640 | tf_op jit(solution)/shard_map/ppermute | solution.py:44
  47.7 1.6 %collective-permute-start.15 = (bf16[2,3,64,512]{3,2,1,0:T(8,128)(2,1)S(1)}, bf16[2,3,64,512]{3,2,1,0:T(8,128)(2,1)S(1)}, u32[]{:S(2)}, u32[]{:S(2)}) collective-permute-start(bf16[2,3,64,512]{3,2,1,0:T(8,128)(2,1)S(1)} %both.1), channel_id=1, source_target_pairs={{0,16},{1,17},{2,18},{3,19},{4,20},{5,21},{6,22},{7,23},{8,24},{9,... | collective-permute-start | bytes 1179656 | tf_op jit(solution)/shard_map/ppermute | solution.py:44
  49.3 1.3 %collective-permute-done.15.rest_other = bf16[2,3,64,512]{3,2,1,0:T(8,128)(2,1)S(1)} collective-permute-done((bf16[2,3,64,512]{3,2,1,0:T(8,128)(2,1)S(1)}, bf16[2,3,64,512]{3,2,1,0:T(8,128)(2,1)S(1)}, u32[]{:S(2)}, u32[]{:S(2)}) %collective-permute-start.15) | collective-permute-done | bytes 393248 | tf_op jit(solution)/shard_map/ppermute | solution.py:44
  50.7 1.2 %step.1.a = bf16[6,64,512]{2,1,0:T(8,128)(2,1)S(1)} custom-call(bf16[4,64,512]{2,1,0:T(8,128)(2,1)S(1)} %here.1.own, bf16[4,64,512]{2,1,0:T(8,128)(2,1)S(1)} %collective-permute-done.10.two, bf16[4,64,512]{2,1,0:T(8,128)(2,1)S(1)} %collective-permute-done.11.one, bf16[4,64,512]{2,1,0:T(8,128)(2,1)S(1)} %collective-permute-done.12.three, ...), custom_call_target="tpu_custom_call" | custom-call | flops 805306368 | bytes 2228224 | tf_op jit(solution)/shard_map/step/pallas_call | solution.py:164
  51.9 0.0 copy-start.8
  52.0 1.9 %collective-permute-start.16 = (bf16[6,64,512]{2,1,0:T(8,128)(2,1)S(1)}, bf16[6,64,512]{2,1,0:T(8,128)(2,1)S(1)}, u32[]{:S(2)}, u32[]{:S(2)}) collective-permute-start(bf16[6,64,512]{2,1,0:T(8,128)(2,1)S(1)} %step.1.a), channel_id=1, source_target_pairs={{0,2},{1,3},{2,0},{3,1},{4,6},{5,7},{6,4},{7,5},{8,10},{9,11},{10,... | collective-permute-start | bytes 1179656 | tf_op jit(solution)/shard_map/ppermute | solution.py:44
  53.8 0.9 collective-permute-start.17
  54.7 1.8 %collective-permute-start.18 = (bf16[6,64,512]{2,1,0:T(8,128)(2,1)S(1)}, bf16[6,64,512]{2,1,0:T(8,128)(2,1)S(1)}, u32[]{:S(2)}, u32[]{:S(2)}) collective-permute-start(bf16[6,64,512]{2,1,0:T(8,128)(2,1)S(1)} %step.1.a), channel_id=1, source_target_pairs={{0,3},{1,0},{2,1},{3,2},{4,7},{5,4},{6,5},{7,6},{8,11},{9,8},{10,9... | collective-permute-start | bytes 1179656 | tf_op jit(solution)/shard_map/ppermute | solution.py:44
  56.5 4.0 %collective-permute-done.16.c = bf16[6,64,512]{2,1,0:T(8,128)(2,1)S(1)} collective-permute-done((bf16[6,64,512]{2,1,0:T(8,128)(2,1)S(1)}, bf16[6,64,512]{2,1,0:T(8,128)(2,1)S(1)}, u32[]{:S(2)}, u32[]{:S(2)}) %collective-permute-start.16) | collective-permute-done | bytes 393248 | tf_op jit(solution)/shard_map/ppermute | solution.py:44
  60.5 4.2 %collective-permute-done.17.b = bf16[6,64,512]{2,1,0:T(8,128)(2,1)S(1)} collective-permute-done((bf16[6,64,512]{2,1,0:T(8,128)(2,1)S(1)}, bf16[6,64,512]{2,1,0:T(8,128)(2,1)S(1)}, u32[]{:S(2)}, u32[]{:S(2)}) %collective-permute-start.17) | collective-permute-done | bytes 393248 | tf_op jit(solution)/shard_map/ppermute | solution.py:44
  64.7 0.3 near.1
  65.0 1.0 %collective-permute-start.19 = (bf16[19,64,512]{2,1,0:T(8,128)(2,1)S(1)}, bf16[19,64,512]{2,1,0:T(8,128)(2,1)S(1)}, u32[]{:S(2)}, u32[]{:S(2)}) collective-permute-start(bf16[19,64,512]{2,1,0:T(8,128)(2,1)S(1)} %get-tuple-element.80), channel_id=1, source_target_pairs={{0,4},{1,5},{2,6},{3,7},{4,8},{5,9},{6,10},{7,11},{8,12},{9,13},{1... | collective-permute-start | bytes 3735560 | tf_op jit(solution)/shard_map/ppermute | solution.py:44
  66.0 1.7 %collective-permute-start.21 = (bf16[19,64,512]{2,1,0:T(8,128)(2,1)S(1)}, bf16[19,64,512]{2,1,0:T(8,128)(2,1)S(1)}, u32[]{:S(2)}, u32[]{:S(2)}) collective-permute-start(bf16[19,64,512]{2,1,0:T(8,128)(2,1)S(1)} %get-tuple-element.81), channel_id=1, source_target_pairs={{0,12},{1,13},{2,14},{3,15},{4,0},{5,1},{6,2},{7,3},{8,4},{9,5},{1... | collective-permute-start | bytes 3735560 | tf_op jit(solution)/shard_map/ppermute | solution.py:44
  67.8 1.8 %collective-permute-start.23 = (bf16[18,64,512]{2,1,0:T(8,128)(2,1)S(1)}, bf16[18,64,512]{2,1,0:T(8,128)(2,1)S(1)}, u32[]{:S(2)}, u32[]{:S(2)}) collective-permute-start(bf16[18,64,512]{2,1,0:T(8,128)(2,1)S(1)} %get-tuple-element.82.refs_0_.near), channel_id=1, source_target_pairs={{0,16},{1,17},{2,18},{3,19},{4,20},{5,21},{6,22},{7,23},{8,24},{9,... | collective-permute-start | bytes 3538952 | tf_op jit(solution)/shard_map/ppermute | solution.py:44
  69.5 2.5 %collective-permute-done.23.refs_1_ = bf16[18,64,512]{2,1,0:T(8,128)(2,1)S(1)} collective-permute-done((bf16[18,64,512]{2,1,0:T(8,128)(2,1)S(1)}, bf16[18,64,512]{2,1,0:T(8,128)(2,1)S(1)}, u32[]{:S(2)}, u32[]{:S(2)}) %collective-permute-start.23) | collective-permute-done | bytes 1179680 | tf_op jit(solution)/shard_map/ppermute | solution.py:44
  72.0 1.9 %place.3.refs_0_ = bf16[16,4,2,64,512]{4,3,2,1,0:T(8,128)(2,1)} custom-call(s32[62]{0:T(128)S(1)} %copy-done.8, bf16[18,64,512]{2,1,0:T(8,128)(2,1)S(1)} %get-tuple-element.82.refs_0_.near, bf16[18,64,512]{2,1,0:T(8,128)(2,1)S(1)} %collective-permute-done.23.refs_1_), custom_call_target="tpu_custom_call" | custom-call | bytes 4718592 | tf_op jit(solution)/shard_map/place/pallas_call | solution.py:317
  74.0 8.4 %collective-permute-done.19.refs_1_.one = bf16[19,64,512]{2,1,0:T(8,128)(2,1)S(1)} collective-permute-done((bf16[19,64,512]{2,1,0:T(8,128)(2,1)S(1)}, bf16[19,64,512]{2,1,0:T(8,128)(2,1)S(1)}, u32[]{:S(2)}, u32[]{:S(2)}) %collective-permute-start.19) | collective-permute-done | bytes 1245216 | tf_op jit(solution)/shard_map/ppermute | solution.py:44
  82.3 2.1 %collective-permute-start.24 = (bf16[19,64,512]{2,1,0:T(8,128)(2,1)S(1)}, bf16[19,64,512]{2,1,0:T(8,128)(2,1)S(1)}, u32[]{:S(2)}, u32[]{:S(2)}) collective-permute-start(bf16[19,64,512]{2,1,0:T(8,128)(2,1)S(1)} %collective-permute-done.19.refs_1_.one), channel_id=1, source_target_pairs={{0,16},{1,17},{2,18},{3,19},{4,20},{5,21},{6,22},{7,23},{8,24},{9,... | collective-permute-start | bytes 3735560 | tf_op jit(solution)/shard_map/ppermute | solution.py:44
  84.4 0.0 collective-permute-start.25
  84.5 1.0 %collective-permute-start.20 = (bf16[9,64,512]{2,1,0:T(8,128)(2,1)S(1)}, bf16[9,64,512]{2,1,0:T(8,128)(2,1)S(1)}, u32[]{:S(2)}, u32[]{:S(2)}) collective-permute-start(bf16[9,64,512]{2,1,0:T(8,128)(2,1)S(1)} %slice.26), channel_id=1, source_target_pairs={{0,4},{1,5},{2,6},{3,7},{4,8},{5,9},{6,10},{7,11},{8,12},{9,13},{1... | collective-permute-start | bytes 1769480 | tf_op jit(solution)/shard_map/ppermute | solution.py:44
  85.5 1.8 %collective-permute-start.22 = (bf16[9,64,512]{2,1,0:T(8,128)(2,1)S(1)}, bf16[9,64,512]{2,1,0:T(8,128)(2,1)S(1)}, u32[]{:S(2)}, u32[]{:S(2)}) collective-permute-start(bf16[9,64,512]{2,1,0:T(8,128)(2,1)S(1)} %slice.27), channel_id=1, source_target_pairs={{0,12},{1,13},{2,14},{3,15},{4,0},{5,1},{6,2},{7,3},{8,4},{9,5},{1... | collective-permute-start | bytes 1769480 | tf_op jit(solution)/shard_map/ppermute | solution.py:44
  87.3 1.9 %place.4.refs_0_ = bf16[16,4,2,64,512]{4,3,2,1,0:T(8,128)(2,1)} custom-call(s32[62]{0:T(128)S(1)} %copy-done.8, bf16[16,4,2,64,512]{4,3,2,1,0:T(8,128)(2,1)} %place.3.refs_0_, bf16[19,64,512]{2,1,0:T(8,128)(2,1)S(1)} %collective-permute-done.19.refs_1_.one, bf16[19,64,512]{2,1,0:T(8,128)(2,1)S(1)} %collective-permute-done.24.refs_2_), custom_call_target="tpu_custom_call", output_to_operand_aliasing={{}: (1, {})} | custom-call | bytes 4980736 | tf_op jit(solution)/shard_map/place/pallas_call | solution.py:317
  89.3 1.9 %place.5.begun = bf16[16,4,2,64,512]{4,3,2,1,0:T(8,128)(2,1)} custom-call(s32[62]{0:T(128)S(1)} %copy-done.8, bf16[16,4,2,64,512]{4,3,2,1,0:T(8,128)(2,1)} %place.4.refs_0_, bf16[19,64,512]{2,1,0:T(8,128)(2,1)S(1)} %collective-permute-done.21.refs_1_.three, bf16[19,64,512]{2,1,0:T(8,128)(2,1)S(1)} %collective-permute-done.25.refs_2_), custom_call_target="tpu_custom_call", output_to_operand_aliasing={{}: (1, {})} | custom-call | bytes 4980736 | tf_op jit(solution)/shard_map/place/pallas_call | solution.py:317
  91.2 0.0 copy-start.5
  91.2 0.0 copy-start.6
  91.2 3.5 %collective-permute-done.20.low = bf16[9,64,512]{2,1,0:T(8,128)(2,1)S(1)} collective-permute-done((bf16[9,64,512]{2,1,0:T(8,128)(2,1)S(1)}, bf16[9,64,512]{2,1,0:T(8,128)(2,1)S(1)}, u32[]{:S(2)}, u32[]{:S(2)}) %collective-permute-start.20) | collective-permute-done | bytes 589856 | tf_op jit(solution)/shard_map/ppermute | solution.py:44
  94.8 1.4 %collective-permute-start.26 = (bf16[8,64,512]{2,1,0:T(8,128)(2,1)S(1)}, bf16[8,64,512]{2,1,0:T(8,128)(2,1)S(1)}, u32[]{:S(2)}, u32[]{:S(2)}) collective-permute-start(bf16[8,64,512]{2,1,0:T(8,128)(2,1)S(1)} %slice.22), channel_id=1, source_target_pairs={{0,16},{1,17},{2,18},{3,19},{4,20},{5,21},{6,22},{7,23},{8,24},{9,... | collective-permute-start | bytes 1572872 | tf_op jit(solution)/shard_map/ppermute | solution.py:44
  96.3 0.1 collective-permute-start.27
  96.4 2.0 %owner.1 = (bf16[16,4,2,64,512]{4,3,2,1,0:T(8,128)(2,1)}, f32[3,64,512]{2,1,0:T(8,128)}, f32[3,64,512]{2,1,0:T(8,128)}, f32[3,64,512]{2,1,0:T(8,128)}) custom-call(s32[62]{0:T(128)S(1)} %copy-done.8, bf16[16,4,2,64,512]{4,3,2,1,0:T(8,128)(2,1)} %place.5.begun, f32[3,64,512]{2,1,0:T(8,128)S(1)} %bitcast.11, ...), custom_call_target="tpu_custom_call", output_to_operand_aliasing={{0}: (1, {})} | custom-call | bytes 4849664 | tf_op jit(solution)/shard_map/owner/pallas_call | solution.py:454
  98.5 0.1 collective-permute-done.27.high_other
  98.6 1.5 %finish.1 = bf16[16,4,2,64,512]{4,3,2,1,0:T(8,128)(2,1)} custom-call(s32[62]{0:T(128)S(1)} %copy-done.8, bf16[16,4,2,64,512]{4,3,2,1,0:T(8,128)(2,1)} %get-tuple-element.88.begun, bf16[8,64,512]{2,1,0:T(8,128)(2,1)S(1)} %collective-permute-done.26.low_other, bf16[8,64,512]{2,1,0:T(8,128)(2,1)S(1)} %collective-permute-done.27.high_other), custom_call_target="tpu_custom_call", output_to_operand_aliasing={{}: (1, {})} | custom-call | bytes 1048576 | tf_op jit(solution)/shard_map/finish/pallas_call | solution.py:466
  (31 shorter events, 0.3 us)
Async XLA Ops:
  0.6 9.3 %copy-start.1 = (f32[1,3,64,512]{3,2,1,0:T(8,128)S(1)}, f32[1,3,64,512]{3,2,1,0:T(8,128)}, u32[]{:S(2)}) copy-start(f32[1,3,64,512]{3,2,1,0:T(8,128)} %param.15) | copy-start | bytes 1179652
  0.6 3.2 %collective-permute-start = (bf16[512,512]{1,0:T(8,128)(2,1)}, bf16[512,512]{1,0:T(8,128)(2,1)S(1)}, u32[]{:S(2)}, u32[]{:S(2)}) collective-permute-start(bf16[512,512]{1,0:T(8,128)(2,1)} %bitcast.12), channel_id=1, source_target_pairs={{0,16},{1,17},{2,18},{3,19},{4,20},{5,21},{6,22},{7,23},{8,24},{9,... | collective-permute-start | bytes 1572872 | tf_op jit(solution)/shard_map/ppermute | solution.py:44
  2.1 1.0 %copy-start.2 = (bf16[1,1,512,512]{3,2,1,0:T(8,128)(2,1)S(1)}, bf16[1,1,512,512]{3,2,1,0:T(8,128)(2,1)}, u32[]{:S(2)}) copy-start(bf16[1,1,512,512]{3,2,1,0:T(8,128)(2,1)} %param.8) | copy-start | bytes 1572868
  3.2 6.8 %copy-start.3 = (f32[1,3,64,512]{3,2,1,0:T(8,128)S(1)}, f32[1,3,64,512]{3,2,1,0:T(8,128)}, u32[]{:S(2)}) copy-start(f32[1,3,64,512]{3,2,1,0:T(8,128)} %param.13) | copy-start | bytes 1179652
  3.2 6.8 %copy-start.4 = (f32[1,3,64,512]{3,2,1,0:T(8,128)S(1)}, f32[1,3,64,512]{3,2,1,0:T(8,128)}, u32[]{:S(2)}) copy-start(f32[1,3,64,512]{3,2,1,0:T(8,128)} %param.14) | copy-start | bytes 1179652
  4.0 7.3 %collective-permute-start.1 = (bf16[64,512]{1,0:T(8,128)(2,1)S(1)}, bf16[64,512]{1,0:T(8,128)(2,1)S(1)}, u32[]{:S(2)}, u32[]{:S(2)}) collective-permute-start(bf16[64,512]{1,0:T(8,128)(2,1)S(1)} %get-tuple-element.58), channel_id=1, source_target_pairs={{0,32},{1,33},{2,34},{3,35},{4,36},{5,37},{6,38},{7,39},{8,40},{9,... | collective-permute-start | bytes 196616 | tf_op jit(solution)/shard_map/ppermute | solution.py:44
  5.3 5.9 %collective-permute-start.2 = (bf16[64,512]{1,0:T(8,128)(2,1)S(1)}, bf16[64,512]{1,0:T(8,128)(2,1)S(1)}, u32[]{:S(2)}, u32[]{:S(2)}) collective-permute-start(bf16[64,512]{1,0:T(8,128)(2,1)S(1)} %get-tuple-element.59), channel_id=1, source_target_pairs={{0,96},{1,97},{2,98},{3,99},{4,100},{5,101},{6,102},{7,103},{8,104... | collective-permute-start | bytes 196616 | tf_op jit(solution)/shard_map/ppermute | solution.py:44
  6.7 4.6 %collective-permute-start.3 = (bf16[64,512]{1,0:T(8,128)(2,1)S(1)}, bf16[64,512]{1,0:T(8,128)(2,1)S(1)}, u32[]{:S(2)}, u32[]{:S(2)}) collective-permute-start(bf16[64,512]{1,0:T(8,128)(2,1)S(1)} %get-tuple-element.60), channel_id=1, source_target_pairs={{0,64},{1,65},{2,66},{3,67},{4,68},{5,69},{6,70},{7,71},{8,72},{9,... | collective-permute-start | bytes 196616 | tf_op jit(solution)/shard_map/ppermute | solution.py:44
  10.0 0.7 copy-start.7
  10.6 12.1 %copy-start = (bf16[14,16,512]{2,1,0:T(8,128)(2,1)S(1)}, bf16[14,16,512]{2,1,0:T(8,128)(2,1)}, u32[]{:S(2)}) copy-start(bf16[14,16,512]{2,1,0:T(8,128)(2,1)} %get-tuple-element.56.tiles) | copy-start | bytes 688132
  11.4 7.8 %collective-permute-start.4 = (bf16[4,64,512]{2,1,0:T(8,128)(2,1)S(1)}, bf16[4,64,512]{2,1,0:T(8,128)(2,1)S(1)}, u32[]{:S(2)}, u32[]{:S(2)}) collective-permute-start(bf16[4,64,512]{2,1,0:T(8,128)(2,1)S(1)} %get-tuple-element.69), channel_id=1, source_target_pairs={{0,2},{1,3},{2,0},{3,1},{4,6},{5,7},{6,4},{7,5},{8,10},{9,11},{10,... | collective-permute-start | bytes 786440 | tf_op jit(solution)/shard_map/ppermute | solution.py:44
  15.1 6.9 %collective-permute-start.5 = (bf16[4,64,512]{2,1,0:T(8,128)(2,1)S(1)}, bf16[4,64,512]{2,1,0:T(8,128)(2,1)S(1)}, u32[]{:S(2)}, u32[]{:S(2)}) collective-permute-start(bf16[4,64,512]{2,1,0:T(8,128)(2,1)S(1)} %get-tuple-element.70), channel_id=1, source_target_pairs={{0,1},{1,2},{2,3},{3,0},{4,5},{5,6},{6,7},{7,4},{8,9},{9,10},{10,1... | collective-permute-start | bytes 786440 | tf_op jit(solution)/shard_map/ppermute | solution.py:44
  15.9 6.9 %collective-permute-start.6 = (bf16[4,64,512]{2,1,0:T(8,128)(2,1)S(1)}, bf16[4,64,512]{2,1,0:T(8,128)(2,1)S(1)}, u32[]{:S(2)}, u32[]{:S(2)}) collective-permute-start(bf16[4,64,512]{2,1,0:T(8,128)(2,1)S(1)} %get-tuple-element.71), channel_id=1, source_target_pairs={{0,3},{1,0},{2,1},{3,2},{4,7},{5,4},{6,5},{7,6},{8,11},{9,8},{10,9... | collective-permute-start | bytes 786440 | tf_op jit(solution)/shard_map/ppermute | solution.py:44
  23.0 7.1 %collective-permute-start.7 = (bf16[4,64,512]{2,1,0:T(8,128)(2,1)S(1)}, bf16[4,64,512]{2,1,0:T(8,128)(2,1)S(1)}, u32[]{:S(2)}, u32[]{:S(2)}) collective-permute-start(bf16[4,64,512]{2,1,0:T(8,128)(2,1)S(1)} %get-tuple-element.73), channel_id=1, source_target_pairs={{0,8},{1,9},{2,10},{3,11},{4,12},{5,13},{6,14},{7,15},{8,0},{9,1},... | collective-permute-start | bytes 786440 | tf_op jit(solution)/shard_map/ppermute | solution.py:44
  26.0 6.8 %collective-permute-start.8 = (bf16[4,64,512]{2,1,0:T(8,128)(2,1)S(1)}, bf16[4,64,512]{2,1,0:T(8,128)(2,1)S(1)}, u32[]{:S(2)}, u32[]{:S(2)}) collective-permute-start(bf16[4,64,512]{2,1,0:T(8,128)(2,1)S(1)} %get-tuple-element.74), channel_id=1, source_target_pairs={{0,4},{1,5},{2,6},{3,7},{4,8},{5,9},{6,10},{7,11},{8,12},{9,13},{1... | collective-permute-start | bytes 786440 | tf_op jit(solution)/shard_map/ppermute | solution.py:44
  26.4 6.9 %collective-permute-start.9 = (bf16[4,64,512]{2,1,0:T(8,128)(2,1)S(1)}, bf16[4,64,512]{2,1,0:T(8,128)(2,1)S(1)}, u32[]{:S(2)}, u32[]{:S(2)}) collective-permute-start(bf16[4,64,512]{2,1,0:T(8,128)(2,1)S(1)} %get-tuple-element.75), channel_id=1, source_target_pairs={{0,12},{1,13},{2,14},{3,15},{4,0},{5,1},{6,2},{7,3},{8,4},{9,5},{1... | collective-permute-start | bytes 786440 | tf_op jit(solution)/shard_map/ppermute | solution.py:44
  33.3 9.0 %collective-permute-start.10 = (bf16[4,64,512]{2,1,0:T(8,128)(2,1)S(1)}, bf16[4,64,512]{2,1,0:T(8,128)(2,1)S(1)}, u32[]{:S(2)}, u32[]{:S(2)}) collective-permute-start(bf16[4,64,512]{2,1,0:T(8,128)(2,1)S(1)} %here.1.own), channel_id=1, source_target_pairs={{0,64},{1,65},{2,66},{3,67},{4,68},{5,69},{6,70},{7,71},{8,72},{9,... | collective-permute-start | bytes 786440 | tf_op jit(solution)/shard_map/ppermute | solution.py:44
  34.9 11.7 %collective-permute-start.11 = (bf16[4,64,512]{2,1,0:T(8,128)(2,1)S(1)}, bf16[4,64,512]{2,1,0:T(8,128)(2,1)S(1)}, u32[]{:S(2)}, u32[]{:S(2)}) collective-permute-start(bf16[4,64,512]{2,1,0:T(8,128)(2,1)S(1)} %here.1.own), channel_id=1, source_target_pairs={{0,32},{1,33},{2,34},{3,35},{4,36},{5,37},{6,38},{7,39},{8,40},{9,... | collective-permute-start | bytes 786440 | tf_op jit(solution)/shard_map/ppermute | solution.py:44
  35.3 11.3 %collective-permute-start.12 = (bf16[4,64,512]{2,1,0:T(8,128)(2,1)S(1)}, bf16[4,64,512]{2,1,0:T(8,128)(2,1)S(1)}, u32[]{:S(2)}, u32[]{:S(2)}) collective-permute-start(bf16[4,64,512]{2,1,0:T(8,128)(2,1)S(1)} %here.1.own), channel_id=1, source_target_pairs={{0,96},{1,97},{2,98},{3,99},{4,100},{5,101},{6,102},{7,103},{8,104... | collective-permute-start | bytes 786440 | tf_op jit(solution)/shard_map/ppermute | solution.py:44
  37.6 9.0 %collective-permute-start.13 = (bf16[3,64,512]{2,1,0:T(8,128)(2,1)S(1)}, bf16[3,64,512]{2,1,0:T(8,128)(2,1)S(1)}, u32[]{:S(2)}, u32[]{:S(2)}) collective-permute-start(bf16[3,64,512]{2,1,0:T(8,128)(2,1)S(1)} %slice.24), channel_id=1, source_target_pairs={{0,16},{1,17},{2,18},{3,19},{4,20},{5,21},{6,22},{7,23},{8,24},{9,... | collective-permute-start | bytes 589832 | tf_op jit(solution)/shard_map/ppermute | solution.py:44
  42.3 5.4 %collective-permute-start.14 = (bf16[3,64,512]{2,1,0:T(8,128)(2,1)S(1)}, bf16[3,64,512]{2,1,0:T(8,128)(2,1)S(1)}, u32[]{:S(2)}, u32[]{:S(2)}) collective-permute-start(bf16[3,64,512]{2,1,0:T(8,128)(2,1)S(1)} %slice.25), channel_id=1, source_target_pairs={{0,16},{1,17},{2,18},{3,19},{4,20},{5,21},{6,22},{7,23},{8,24},{9,... | collective-permute-start | bytes 589832 | tf_op jit(solution)/shard_map/ppermute | solution.py:44
  47.7 3.0 %collective-permute-start.15 = (bf16[2,3,64,512]{3,2,1,0:T(8,128)(2,1)S(1)}, bf16[2,3,64,512]{3,2,1,0:T(8,128)(2,1)S(1)}, u32[]{:S(2)}, u32[]{:S(2)}) collective-permute-start(bf16[2,3,64,512]{3,2,1,0:T(8,128)(2,1)S(1)} %both.1), channel_id=1, source_target_pairs={{0,16},{1,17},{2,18},{3,19},{4,20},{5,21},{6,22},{7,23},{8,24},{9,... | collective-permute-start | bytes 1179656 | tf_op jit(solution)/shard_map/ppermute | solution.py:44
  51.9 20.1 %copy-start.8 = (s32[62]{0:T(128)S(1)}, s32[62]{0:T(128)}, u32[]{:S(2)}) copy-start(s32[62]{0:T(128)} %get-tuple-element.55.spot) | copy-start | bytes 748
  52.0 8.5 %collective-permute-start.16 = (bf16[6,64,512]{2,1,0:T(8,128)(2,1)S(1)}, bf16[6,64,512]{2,1,0:T(8,128)(2,1)S(1)}, u32[]{:S(2)}, u32[]{:S(2)}) collective-permute-start(bf16[6,64,512]{2,1,0:T(8,128)(2,1)S(1)} %step.1.a), channel_id=1, source_target_pairs={{0,2},{1,3},{2,0},{3,1},{4,6},{5,7},{6,4},{7,5},{8,10},{9,11},{10,... | collective-permute-start | bytes 1179656 | tf_op jit(solution)/shard_map/ppermute | solution.py:44
  53.8 10.8 %collective-permute-start.17 = (bf16[6,64,512]{2,1,0:T(8,128)(2,1)S(1)}, bf16[6,64,512]{2,1,0:T(8,128)(2,1)S(1)}, u32[]{:S(2)}, u32[]{:S(2)}) collective-permute-start(bf16[6,64,512]{2,1,0:T(8,128)(2,1)S(1)} %step.1.a), channel_id=1, source_target_pairs={{0,1},{1,2},{2,3},{3,0},{4,5},{5,6},{6,7},{7,4},{8,9},{9,10},{10,1... | collective-permute-start | bytes 1179656 | tf_op jit(solution)/shard_map/ppermute | solution.py:44
  54.7 9.9 %collective-permute-start.18 = (bf16[6,64,512]{2,1,0:T(8,128)(2,1)S(1)}, bf16[6,64,512]{2,1,0:T(8,128)(2,1)S(1)}, u32[]{:S(2)}, u32[]{:S(2)}) collective-permute-start(bf16[6,64,512]{2,1,0:T(8,128)(2,1)S(1)} %step.1.a), channel_id=1, source_target_pairs={{0,3},{1,0},{2,1},{3,2},{4,7},{5,4},{6,5},{7,6},{8,11},{9,8},{10,9... | collective-permute-start | bytes 1179656 | tf_op jit(solution)/shard_map/ppermute | solution.py:44
  65.0 17.3 %collective-permute-start.19 = (bf16[19,64,512]{2,1,0:T(8,128)(2,1)S(1)}, bf16[19,64,512]{2,1,0:T(8,128)(2,1)S(1)}, u32[]{:S(2)}, u32[]{:S(2)}) collective-permute-start(bf16[19,64,512]{2,1,0:T(8,128)(2,1)S(1)} %get-tuple-element.80), channel_id=1, source_target_pairs={{0,4},{1,5},{2,6},{3,7},{4,8},{5,9},{6,10},{7,11},{8,12},{9,13},{1... | collective-permute-start | bytes 3735560 | tf_op jit(solution)/shard_map/ppermute | solution.py:44
  66.0 16.3 %collective-permute-start.21 = (bf16[19,64,512]{2,1,0:T(8,128)(2,1)S(1)}, bf16[19,64,512]{2,1,0:T(8,128)(2,1)S(1)}, u32[]{:S(2)}, u32[]{:S(2)}) collective-permute-start(bf16[19,64,512]{2,1,0:T(8,128)(2,1)S(1)} %get-tuple-element.81), channel_id=1, source_target_pairs={{0,12},{1,13},{2,14},{3,15},{4,0},{5,1},{6,2},{7,3},{8,4},{9,5},{1... | collective-permute-start | bytes 3735560 | tf_op jit(solution)/shard_map/ppermute | solution.py:44
  67.8 4.3 %collective-permute-start.23 = (bf16[18,64,512]{2,1,0:T(8,128)(2,1)S(1)}, bf16[18,64,512]{2,1,0:T(8,128)(2,1)S(1)}, u32[]{:S(2)}, u32[]{:S(2)}) collective-permute-start(bf16[18,64,512]{2,1,0:T(8,128)(2,1)S(1)} %get-tuple-element.82.refs_0_.near), channel_id=1, source_target_pairs={{0,16},{1,17},{2,18},{3,19},{4,20},{5,21},{6,22},{7,23},{8,24},{9,... | collective-permute-start | bytes 3538952 | tf_op jit(solution)/shard_map/ppermute | solution.py:44
  82.3 5.0 %collective-permute-start.24 = (bf16[19,64,512]{2,1,0:T(8,128)(2,1)S(1)}, bf16[19,64,512]{2,1,0:T(8,128)(2,1)S(1)}, u32[]{:S(2)}, u32[]{:S(2)}) collective-permute-start(bf16[19,64,512]{2,1,0:T(8,128)(2,1)S(1)} %collective-permute-done.19.refs_1_.one), channel_id=1, source_target_pairs={{0,16},{1,17},{2,18},{3,19},{4,20},{5,21},{6,22},{7,23},{8,24},{9,... | collective-permute-start | bytes 3735560 | tf_op jit(solution)/shard_map/ppermute | solution.py:44
  84.4 4.8 %collective-permute-start.25 = (bf16[19,64,512]{2,1,0:T(8,128)(2,1)S(1)}, bf16[19,64,512]{2,1,0:T(8,128)(2,1)S(1)}, u32[]{:S(2)}, u32[]{:S(2)}) collective-permute-start(bf16[19,64,512]{2,1,0:T(8,128)(2,1)S(1)} %collective-permute-done.21.refs_1_.three), channel_id=1, source_target_pairs={{0,16},{1,17},{2,18},{3,19},{4,20},{5,21},{6,22},{7,23},{8,24},{9,... | collective-permute-start | bytes 3735560 | tf_op jit(solution)/shard_map/ppermute | solution.py:44
  84.5 10.3 %collective-permute-start.20 = (bf16[9,64,512]{2,1,0:T(8,128)(2,1)S(1)}, bf16[9,64,512]{2,1,0:T(8,128)(2,1)S(1)}, u32[]{:S(2)}, u32[]{:S(2)}) collective-permute-start(bf16[9,64,512]{2,1,0:T(8,128)(2,1)S(1)} %slice.26), channel_id=1, source_target_pairs={{0,4},{1,5},{2,6},{3,7},{4,8},{5,9},{6,10},{7,11},{8,12},{9,13},{1... | collective-permute-start | bytes 1769480 | tf_op jit(solution)/shard_map/ppermute | solution.py:44
  85.5 9.2 %collective-permute-start.22 = (bf16[9,64,512]{2,1,0:T(8,128)(2,1)S(1)}, bf16[9,64,512]{2,1,0:T(8,128)(2,1)S(1)}, u32[]{:S(2)}, u32[]{:S(2)}) collective-permute-start(bf16[9,64,512]{2,1,0:T(8,128)(2,1)S(1)} %slice.27), channel_id=1, source_target_pairs={{0,12},{1,13},{2,14},{3,15},{4,0},{5,1},{6,2},{7,3},{8,4},{9,5},{1... | collective-permute-start | bytes 1769480 | tf_op jit(solution)/shard_map/ppermute | solution.py:44
  91.2 5.2 %copy-start.5 = (f32[1,3,64,512]{3,2,1,0:T(8,128)S(1)}, f32[1,3,64,512]{3,2,1,0:T(8,128)}, u32[]{:S(2)}) copy-start(f32[1,3,64,512]{3,2,1,0:T(8,128)} %param.11) | copy-start | bytes 1179652
  91.2 5.2 %copy-start.6 = (f32[1,3,64,512]{3,2,1,0:T(8,128)S(1)}, f32[1,3,64,512]{3,2,1,0:T(8,128)}, u32[]{:S(2)}) copy-start(f32[1,3,64,512]{3,2,1,0:T(8,128)} %param.12) | copy-start | bytes 1179652
  94.8 3.6 %collective-permute-start.26 = (bf16[8,64,512]{2,1,0:T(8,128)(2,1)S(1)}, bf16[8,64,512]{2,1,0:T(8,128)(2,1)S(1)}, u32[]{:S(2)}, u32[]{:S(2)}) collective-permute-start(bf16[8,64,512]{2,1,0:T(8,128)(2,1)S(1)} %slice.22), channel_id=1, source_target_pairs={{0,16},{1,17},{2,18},{3,19},{4,20},{5,21},{6,22},{7,23},{8,24},{9,... | collective-permute-start | bytes 1572872 | tf_op jit(solution)/shard_map/ppermute | solution.py:44
  96.3 2.2 %collective-permute-start.27 = (bf16[8,64,512]{2,1,0:T(8,128)(2,1)S(1)}, bf16[8,64,512]{2,1,0:T(8,128)(2,1)S(1)}, u32[]{:S(2)}, u32[]{:S(2)}) collective-permute-start(bf16[8,64,512]{2,1,0:T(8,128)(2,1)S(1)} %slice.23), channel_id=1, source_target_pairs={{0,16},{1,17},{2,18},{3,19},{4,20},{5,21},{6,22},{7,23},{8,24},{9,... | collective-permute-start | bytes 1572872 | tf_op jit(solution)/shard_map/ppermute | solution.py:44

commit v7 on v6

--- a/solution.py
+++ b/solution.py
@@ -250,8 +250,9 @@
     wide = g.astype(wide_type)
     grad_square = jnp.sum(wide * wide)
     precond = jnp.dot(full[0], g, preferred_element_type=wide_type).astype(half_type)
-    held[...] = jnp.dot(precond, full[1], preferred_element_type=wide_type)
-    dir_square = jnp.sum(held[...] * held[...])
+    direction = jnp.dot(precond, full[1], preferred_element_type=wide_type)
+    dir_square = jnp.sum(direction * direction)
+    held[...] = direction
     entries = float(BS * BS)
     top = jnp.sqrt(jnp.full((1, BS), grad_square / entries, wide_type))
     graft = top / jnp.sqrt(jnp.full((1, BS), dir_square / entries + epsilon, wide_type))
@@ -271,14 +272,14 @@
     out[5] = held[pl.ds(pl.multiple_of(c * ROWS, ROWS), ROWS), :].astype(half_type)
 
 
-def near_kernel(tiles, a, c, b, d, near, ahead, back):
+def near_kernel(tiles, a, c, b, d, terms, ahead, back):
     sources = (a, b, c, d)
-    for out, first in ((near, 0), (ahead, 1), (back, 0)):
+    for out, first in ((ahead, 1), (back, 0)):
         for j, source in enumerate(sources):
             out[first + j * 4 : first + j * 4 + 4] = source[:4]
     left = [source[4] for source in sources]
     right = [source[5] for source in sources]
-    for k, out, first in ((0, near, 16), (1, ahead, 17), (3, back, 17)):
+    for k, out, first in ((0, terms, 0), (1, ahead, 17), (3, back, 17)):
         out[first] = blend(tiles[TERM_PICK + k], left)
         out[first + 1] = blend(tiles[TERM_PICK + k], right)
     ahead[0] = blend(tiles[TERM_PICK + 2], left)
@@ -303,7 +304,7 @@
 
 def place_kernel(which, spot, *refs):
     mine, other, out, sems = refs[-4:]
-    skip = 1 if which == 1 else 0
+    skip = 1 if which < 3 else 0
     sources = ((which, 0, 4, skip, mine), (which + 4, 0, 4, skip, other))
     copies = placed_copies(spot, sources, out, sems)
     for copy in copies:
@@ -327,7 +328,7 @@
     )(spot, *given)
 
 
-def owner_kernel(spot, begun, moment, left, right, near, one, three, low, high, *refs):
+def owner_kernel(spot, begun, moment, left, right, near, own, one, three, low, high, *refs):
     del begun
     out, out_moment, out_left, out_right, fresh, new_left, new_right, sems, more = refs
     sources = ((2, 0, 2, 1, low), (2, 2, 2, 0, high))
@@ -335,8 +336,8 @@
     for copy in copies:
         copy.start()
     x = position()[0]
-    parts = ((0, 0, 4, 0, near), (1, 0, 4, 1, one), (3, 0, 4, 0, three)) + sources
-    terms = ((near, 16, near, 17), (one, 17, one, 18), (low, 0, high, 8), (three, 17, three, 18))
+    parts = ((0, 0, 4, 1, near), (1, 0, 4, 1, one), (3, 0, 4, 0, three)) + sources
+    terms = ((own, 0, own, 1), (one, 17, one, 18), (low, 0, high, 8), (three, 17, three, 18))
     for s in range(SLOTS):
         fresh[s] = moment[s]
         new_left[s] = left[s]
@@ -435,12 +436,12 @@
     )
 
     row = along(to_u, [send] * 4, (2, 1, 3))
-    near_type = jax.ShapeDtypeStruct((18, ROWS, BS), half_type)
+    terms_type = jax.ShapeDtypeStruct((2, ROWS, BS), half_type)
     sent_type = jax.ShapeDtypeStruct((19, ROWS, BS), half_type)
-    near, ahead, back = small_call(
-        near_kernel, [near_type, sent_type, sent_type], "near", tiles, *row
-    )
-    one, three = to_v(ahead, 1), to_v(back, 3)
+    terms, near, back = small_call(
+        near_kernel, [terms_type, sent_type, sent_type], "near", tiles, *row
+    )
+    one, three = to_v(near, 1), to_v(back, 3)
     near_other = to_core(near)
     low = to_v(one[:9], 1)
     high = to_v(three[8:17], 3)
@@ -454,7 +455,7 @@
     begun, new_momentum, left_stats, right_stats = pl.pallas_call(
         owner_kernel,
         out_shape=[jax.ShapeDtypeStruct(begun.shape, half_type)] + [stat_type] * 3,
-        in_specs=[SMEM, ANY] + [VMEM] * 8,
+        in_specs=[SMEM, ANY] + [VMEM] * 9,
         out_specs=[ANY] * 4,
         scratch_shapes=[pltpu.VMEM((SLOTS, ROWS, BS), wide_type)] * 3
         + [pltpu.SemaphoreType.DMA((4,)), pltpu.SemaphoreType.DMA((3 * SLOTS,))],
@@ -462,7 +463,7 @@
         compiler_params=pltpu.CompilerParams(vmem_limit_bytes=8 << 20),
         cost_estimate=cost(0, near, one, three, low, high),
         name="owner",
-    )(spot, begun, momentum[0], stat_left[0], stat_right[0], near, one, three, low, high)
+    )(spot, begun, momentum[0], stat_left[0], stat_right[0], near, terms, one, three, low, high)
     update_blocks = pl.pallas_call(
         finish_kernel,
         out_shape=jax.ShapeDtypeStruct(begun.shape, half_type),

time: 100 us -> 100 us (level)
  waiting for transfers between devices: 35.3 us -> 37.1 us
  starting transfers between devices: 48.4 us -> 46.7 us
    ppermute x28, waiting for transfers between devices: 35.3 us -> 37.1 us  [permute(): return lax.ppermute(value, AXES, pairs)]
    ppermute x28, starting transfers between devices: 48.4 us -> 46.7 us  [permute(): return lax.ppermute(value, AXES, pairs)]
  transfers between devices with their start and end apart: 28 -> 28, of which waited for: 15 -> 14; matrix products, arithmetic and copies ran while one was open for 0% -> 0% of each run, Pallas kernels for 10% -> 10%
where the time goes in v7:
time: 100 us
  starting transfers between devices  46.7 us (47%)
  waiting for transfers between devices  37.1 us (37%)
  Pallas kernels  13.5 us (14%)
  local copies, waits for them, and re-layouts  1.9 us (2%)
    ppermute x28, starting transfers between devices, permute(): return lax.ppermute(value, AXES, pairs)  46.7 us
    ppermute x28, waiting for transfers between devices, permute(): return lax.ppermute(value, AXES, pairs)  37.1 us
    pallas_call x3, Pallas kernels, place(): pl.pallas_call(functools.partial(place_kernel, which), out_shape=jax.Shap...  5.78 us
    pallas_call x9, Pallas kernels, small_call(): pl.pallas_call(body, out_shape=outs, in_specs=[SMEM if a.dtype == jnp.int...  2.59 us
    pallas_call x1, Pallas kernels, local(): pl.pallas_call(owner_kernel, out_shape=[jax.ShapeDtypeStruct(begun.shape,...  2.02 us
  transfers between devices with their start and end apart: 28, of which 14 were waited for; matrix products, arithmetic and copies ran while one was open for 0% of the time, Pallas kernels for 10%

profile of v7, /device:TPU:1, one launch (start us, length us, event | category | flops | bytes accessed | tf_op | source)
XLA Modules:
  0.0 100.1 jit_solution(6197542614014086661)
XLA Ops:
  0.6 1.5 %collective-permute-start = (bf16[512,512]{1,0:T(8,128)(2,1)}, bf16[512,512]{1,0:T(8,128)(2,1)S(1)}, u32[]{:S(2)}, u32[]{:S(2)}) collective-permute-start(bf16[512,512]{1,0:T(8,128)(2,1)} %bitcast.12), channel_id=1, source_target_pairs={{0,16},{1,17},{2,18},{3,19},{4,20},{5,21},{6,22},{7,23},{8,24},{9,... | collective-permute-start | bytes 1572872 | tf_op jit(solution)/shard_map/ppermute | solution.py:44
  2.1 1.0 %copy-done.2 = bf16[1,1,512,512]{3,2,1,0:T(8,128)(2,1)S(1)} copy-done((bf16[1,1,512,512]{3,2,1,0:T(8,128)(2,1)S(1)}, bf16[1,1,512,512]{3,2,1,0:T(8,128)(2,1)}, u32[]{:S(2)}) %copy-start.2) | copy-done | bytes 524312
  3.2 0.7 collective-permute-done.theirs
  3.9 0.1 pair.1
  4.0 1.4 %collective-permute-start.1 = (bf16[64,512]{1,0:T(8,128)(2,1)S(1)}, bf16[64,512]{1,0:T(8,128)(2,1)S(1)}, u32[]{:S(2)}, u32[]{:S(2)}) collective-permute-start(bf16[64,512]{1,0:T(8,128)(2,1)S(1)} %get-tuple-element.58), channel_id=1, source_target_pairs={{0,32},{1,33},{2,34},{3,35},{4,36},{5,37},{6,38},{7,39},{8,40},{9,... | collective-permute-start | bytes 196616 | tf_op jit(solution)/shard_map/ppermute | solution.py:44
  5.3 1.4 %collective-permute-start.2 = (bf16[64,512]{1,0:T(8,128)(2,1)S(1)}, bf16[64,512]{1,0:T(8,128)(2,1)S(1)}, u32[]{:S(2)}, u32[]{:S(2)}) collective-permute-start(bf16[64,512]{1,0:T(8,128)(2,1)S(1)} %get-tuple-element.59), channel_id=1, source_target_pairs={{0,96},{1,97},{2,98},{3,99},{4,100},{5,101},{6,102},{7,103},{8,104... | collective-permute-start | bytes 196616 | tf_op jit(solution)/shard_map/ppermute | solution.py:44
  6.7 1.6 %collective-permute-start.3 = (bf16[64,512]{1,0:T(8,128)(2,1)S(1)}, bf16[64,512]{1,0:T(8,128)(2,1)S(1)}, u32[]{:S(2)}, u32[]{:S(2)}) collective-permute-start(bf16[64,512]{1,0:T(8,128)(2,1)S(1)} %get-tuple-element.60), channel_id=1, source_target_pairs={{0,64},{1,65},{2,66},{3,67},{4,68},{5,69},{6,70},{7,71},{8,72},{9,... | collective-permute-start | bytes 196616 | tf_op jit(solution)/shard_map/ppermute | solution.py:44
  8.3 1.6 %choices.1 = (s32[62]{0:T(128)}, bf16[14,16,512]{2,1,0:T(8,128)(2,1)}) custom-call(s32[16]{0:T(128)} %order_ref, s32[16]{0:T(128)} %count_ref), custom_call_target="tpu_custom_call" | custom-call | bytes 4194304 | tf_op jit(solution)/shard_map/choices/pallas_call | solution.py:144
  10.0 0.0 copy-start.7
  10.0 0.6 copy-done.7
  10.6 0.6 packs.1
  11.3 0.1 collective-permute-done.3.b
  11.4 3.8 %collective-permute-start.4 = (bf16[4,64,512]{2,1,0:T(8,128)(2,1)S(1)}, bf16[4,64,512]{2,1,0:T(8,128)(2,1)S(1)}, u32[]{:S(2)}, u32[]{:S(2)}) collective-permute-start(bf16[4,64,512]{2,1,0:T(8,128)(2,1)S(1)} %get-tuple-element.69), channel_id=1, source_target_pairs={{0,2},{1,3},{2,0},{3,1},{4,6},{5,7},{6,4},{7,5},{8,10},{9,11},{10,... | collective-permute-start | bytes 786440 | tf_op jit(solution)/shard_map/ppermute | solution.py:44
  15.1 0.7 collective-permute-start.5
  15.9 1.9 %collective-permute-start.6 = (bf16[4,64,512]{2,1,0:T(8,128)(2,1)S(1)}, bf16[4,64,512]{2,1,0:T(8,128)(2,1)S(1)}, u32[]{:S(2)}, u32[]{:S(2)}) collective-permute-start(bf16[4,64,512]{2,1,0:T(8,128)(2,1)S(1)} %get-tuple-element.71), channel_id=1, source_target_pairs={{0,3},{1,0},{2,1},{3,2},{4,7},{5,4},{6,5},{7,6},{8,11},{9,8},{10,9... | collective-permute-start | bytes 786440 | tf_op jit(solution)/shard_map/ppermute | solution.py:44
  17.8 1.4 %collective-permute-done.4.c = bf16[4,64,512]{2,1,0:T(8,128)(2,1)S(1)} collective-permute-done((bf16[4,64,512]{2,1,0:T(8,128)(2,1)S(1)}, bf16[4,64,512]{2,1,0:T(8,128)(2,1)S(1)}, u32[]{:S(2)}, u32[]{:S(2)}) %collective-permute-start.4) | collective-permute-done | bytes 262176 | tf_op jit(solution)/shard_map/ppermute | solution.py:44
  19.2 2.8 %collective-permute-done.5.b = bf16[4,64,512]{2,1,0:T(8,128)(2,1)S(1)} collective-permute-done((bf16[4,64,512]{2,1,0:T(8,128)(2,1)S(1)}, bf16[4,64,512]{2,1,0:T(8,128)(2,1)S(1)}, u32[]{:S(2)}, u32[]{:S(2)}) %collective-permute-start.5) | collective-permute-done | bytes 262176 | tf_op jit(solution)/shard_map/ppermute | solution.py:44
  22.0 0.7 collective-permute-done.6.d
  22.7 0.3 turn.1
  23.0 3.0 %collective-permute-start.7 = (bf16[4,64,512]{2,1,0:T(8,128)(2,1)S(1)}, bf16[4,64,512]{2,1,0:T(8,128)(2,1)S(1)}, u32[]{:S(2)}, u32[]{:S(2)}) collective-permute-start(bf16[4,64,512]{2,1,0:T(8,128)(2,1)S(1)} %get-tuple-element.73), channel_id=1, source_target_pairs={{0,8},{1,9},{2,10},{3,11},{4,12},{5,13},{6,14},{7,15},{8,0},{9,1},... | collective-permute-start | bytes 786440 | tf_op jit(solution)/shard_map/ppermute | solution.py:44
  26.0 0.4 collective-permute-start.8
  26.4 2.3 %collective-permute-start.9 = (bf16[4,64,512]{2,1,0:T(8,128)(2,1)S(1)}, bf16[4,64,512]{2,1,0:T(8,128)(2,1)S(1)}, u32[]{:S(2)}, u32[]{:S(2)}) collective-permute-start(bf16[4,64,512]{2,1,0:T(8,128)(2,1)S(1)} %get-tuple-element.75), channel_id=1, source_target_pairs={{0,12},{1,13},{2,14},{3,15},{4,0},{5,1},{6,2},{7,3},{8,4},{9,5},{1... | collective-permute-start | bytes 786440 | tf_op jit(solution)/shard_map/ppermute | solution.py:44
  28.7 1.4 %collective-permute-done.7.c = bf16[4,64,512]{2,1,0:T(8,128)(2,1)S(1)} collective-permute-done((bf16[4,64,512]{2,1,0:T(8,128)(2,1)S(1)}, bf16[4,64,512]{2,1,0:T(8,128)(2,1)S(1)}, u32[]{:S(2)}, u32[]{:S(2)}) %collective-permute-start.7) | collective-permute-done | bytes 262176 | tf_op jit(solution)/shard_map/ppermute | solution.py:44
  30.1 2.7 %collective-permute-done.8.b = bf16[4,64,512]{2,1,0:T(8,128)(2,1)S(1)} collective-permute-done((bf16[4,64,512]{2,1,0:T(8,128)(2,1)S(1)}, bf16[4,64,512]{2,1,0:T(8,128)(2,1)S(1)}, u32[]{:S(2)}, u32[]{:S(2)}) %collective-permute-start.8) | collective-permute-done | bytes 262176 | tf_op jit(solution)/shard_map/ppermute | solution.py:44
  32.8 0.4 collective-permute-done.9.d
  33.2 0.1 here.1.own
  33.3 1.6 %collective-permute-start.10 = (bf16[4,64,512]{2,1,0:T(8,128)(2,1)S(1)}, bf16[4,64,512]{2,1,0:T(8,128)(2,1)S(1)}, u32[]{:S(2)}, u32[]{:S(2)}) collective-permute-start(bf16[4,64,512]{2,1,0:T(8,128)(2,1)S(1)} %here.1.own), channel_id=1, source_target_pairs={{0,64},{1,65},{2,66},{3,67},{4,68},{5,69},{6,70},{7,71},{8,72},{9,... | collective-permute-start | bytes 786440 | tf_op jit(solution)/shard_map/ppermute | solution.py:44
  34.9 0.4 collective-permute-start.11
  35.3 2.3 %collective-permute-start.12 = (bf16[4,64,512]{2,1,0:T(8,128)(2,1)S(1)}, bf16[4,64,512]{2,1,0:T(8,128)(2,1)S(1)}, u32[]{:S(2)}, u32[]{:S(2)}) collective-permute-start(bf16[4,64,512]{2,1,0:T(8,128)(2,1)S(1)} %here.1.own), channel_id=1, source_target_pairs={{0,96},{1,97},{2,98},{3,99},{4,100},{5,101},{6,102},{7,103},{8,104... | collective-permute-start | bytes 786440 | tf_op jit(solution)/shard_map/ppermute | solution.py:44
  37.6 4.7 %collective-permute-start.13 = (bf16[3,64,512]{2,1,0:T(8,128)(2,1)S(1)}, bf16[3,64,512]{2,1,0:T(8,128)(2,1)S(1)}, u32[]{:S(2)}, u32[]{:S(2)}) collective-permute-start(bf16[3,64,512]{2,1,0:T(8,128)(2,1)S(1)} %slice.24), channel_id=1, source_target_pairs={{0,16},{1,17},{2,18},{3,19},{4,20},{5,21},{6,22},{7,23},{8,24},{9,... | collective-permute-start | bytes 589832 | tf_op jit(solution)/shard_map/ppermute | solution.py:44
  42.3 0.0 collective-permute-done.10.two
  42.3 4.3 %collective-permute-start.14 = (bf16[3,64,512]{2,1,0:T(8,128)(2,1)S(1)}, bf16[3,64,512]{2,1,0:T(8,128)(2,1)S(1)}, u32[]{:S(2)}, u32[]{:S(2)}) collective-permute-start(bf16[3,64,512]{2,1,0:T(8,128)(2,1)S(1)} %slice.25), channel_id=1, source_target_pairs={{0,16},{1,17},{2,18},{3,19},{4,20},{5,21},{6,22},{7,23},{8,24},{9,... | collective-permute-start | bytes 589832 | tf_op jit(solution)/shard_map/ppermute | solution.py:44
  46.6 0.0 collective-permute-done.13.own_other
  46.6 0.0 collective-permute-done.11.one
  46.6 1.1 %collective-permute-done.14.two_other = bf16[3,64,512]{2,1,0:T(8,128)(2,1)S(1)} collective-permute-done((bf16[3,64,512]{2,1,0:T(8,128)(2,1)S(1)}, bf16[3,64,512]{2,1,0:T(8,128)(2,1)S(1)}, u32[]{:S(2)}, u32[]{:S(2)}) %collective-permute-start.14) | collective-permute-done | bytes 196640 | tf_op jit(solution)/shard_map/ppermute | solution.py:44
  47.7 1.6 %collective-permute-start.15 = (bf16[2,3,64,512]{3,2,1,0:T(8,128)(2,1)S(1)}, bf16[2,3,64,512]{3,2,1,0:T(8,128)(2,1)S(1)}, u32[]{:S(2)}, u32[]{:S(2)}) collective-permute-start(bf16[2,3,64,512]{3,2,1,0:T(8,128)(2,1)S(1)} %both.1), channel_id=1, source_target_pairs={{0,16},{1,17},{2,18},{3,19},{4,20},{5,21},{6,22},{7,23},{8,24},{9,... | collective-permute-start | bytes 1179656 | tf_op jit(solution)/shard_map/ppermute | solution.py:44
  49.3 1.3 %collective-permute-done.15.rest_other = bf16[2,3,64,512]{3,2,1,0:T(8,128)(2,1)S(1)} collective-permute-done((bf16[2,3,64,512]{3,2,1,0:T(8,128)(2,1)S(1)}, bf16[2,3,64,512]{3,2,1,0:T(8,128)(2,1)S(1)}, u32[]{:S(2)}, u32[]{:S(2)}) %collective-permute-start.15) | collective-permute-done | bytes 393248 | tf_op jit(solution)/shard_map/ppermute | solution.py:44
  50.7 1.2 %step.1.a = bf16[6,64,512]{2,1,0:T(8,128)(2,1)S(1)} custom-call(bf16[4,64,512]{2,1,0:T(8,128)(2,1)S(1)} %here.1.own, bf16[4,64,512]{2,1,0:T(8,128)(2,1)S(1)} %collective-permute-done.10.two, bf16[4,64,512]{2,1,0:T(8,128)(2,1)S(1)} %collective-permute-done.11.one, bf16[4,64,512]{2,1,0:T(8,128)(2,1)S(1)} %collective-permute-done.12.three, ...), custom_call_target="tpu_custom_call" | custom-call | flops 805306368 | bytes 2228224 | tf_op jit(solution)/shard_map/step/pallas_call | solution.py:164
  51.9 0.0 copy-start.8
  52.0 1.9 %collective-permute-start.16 = (bf16[6,64,512]{2,1,0:T(8,128)(2,1)S(1)}, bf16[6,64,512]{2,1,0:T(8,128)(2,1)S(1)}, u32[]{:S(2)}, u32[]{:S(2)}) collective-permute-start(bf16[6,64,512]{2,1,0:T(8,128)(2,1)S(1)} %step.1.a), channel_id=1, source_target_pairs={{0,2},{1,3},{2,0},{3,1},{4,6},{5,7},{6,4},{7,5},{8,10},{9,11},{10,... | collective-permute-start | bytes 1179656 | tf_op jit(solution)/shard_map/ppermute | solution.py:44
  53.8 0.9 collective-permute-start.17
  54.7 1.8 %collective-permute-start.18 = (bf16[6,64,512]{2,1,0:T(8,128)(2,1)S(1)}, bf16[6,64,512]{2,1,0:T(8,128)(2,1)S(1)}, u32[]{:S(2)}, u32[]{:S(2)}) collective-permute-start(bf16[6,64,512]{2,1,0:T(8,128)(2,1)S(1)} %step.1.a), channel_id=1, source_target_pairs={{0,3},{1,0},{2,1},{3,2},{4,7},{5,4},{6,5},{7,6},{8,11},{9,8},{10,9... | collective-permute-start | bytes 1179656 | tf_op jit(solution)/shard_map/ppermute | solution.py:44
  56.5 4.0 %collective-permute-done.16.c = bf16[6,64,512]{2,1,0:T(8,128)(2,1)S(1)} collective-permute-done((bf16[6,64,512]{2,1,0:T(8,128)(2,1)S(1)}, bf16[6,64,512]{2,1,0:T(8,128)(2,1)S(1)}, u32[]{:S(2)}, u32[]{:S(2)}) %collective-permute-start.16) | collective-permute-done | bytes 393248 | tf_op jit(solution)/shard_map/ppermute | solution.py:44
  60.5 4.2 %collective-permute-done.17.b = bf16[6,64,512]{2,1,0:T(8,128)(2,1)S(1)} collective-permute-done((bf16[6,64,512]{2,1,0:T(8,128)(2,1)S(1)}, bf16[6,64,512]{2,1,0:T(8,128)(2,1)S(1)}, u32[]{:S(2)}, u32[]{:S(2)}) %collective-permute-start.17) | collective-permute-done | bytes 393248 | tf_op jit(solution)/shard_map/ppermute | solution.py:44
  64.7 0.3 near.1
  64.9 1.3 %collective-permute-start.23 = (bf16[19,64,512]{2,1,0:T(8,128)(2,1)S(1)}, bf16[19,64,512]{2,1,0:T(8,128)(2,1)S(1)}, u32[]{:S(2)}, u32[]{:S(2)}) collective-permute-start(bf16[19,64,512]{2,1,0:T(8,128)(2,1)S(1)} %get-tuple-element.80.refs_0_.near), channel_id=1, source_target_pairs={{0,16},{1,17},{2,18},{3,19},{4,20},{5,21},{6,22},{7,23},{8,24},{9,... | collective-permute-start | bytes 3735560 | tf_op jit(solution)/shard_map/ppermute | solution.py:44
  66.3 0.8 collective-permute-start.19
  67.1 1.9 %collective-permute-start.21 = (bf16[19,64,512]{2,1,0:T(8,128)(2,1)S(1)}, bf16[19,64,512]{2,1,0:T(8,128)(2,1)S(1)}, u32[]{:S(2)}, u32[]{:S(2)}) collective-permute-start(bf16[19,64,512]{2,1,0:T(8,128)(2,1)S(1)} %get-tuple-element.81), channel_id=1, source_target_pairs={{0,12},{1,13},{2,14},{3,15},{4,0},{5,1},{6,2},{7,3},{8,4},{9,5},{1... | collective-permute-start | bytes 3735560 | tf_op jit(solution)/shard_map/ppermute | solution.py:44
  68.9 1.9 %place.3.refs_0_ = bf16[16,4,2,64,512]{4,3,2,1,0:T(8,128)(2,1)} custom-call(s32[62]{0:T(128)S(1)} %copy-done.8, bf16[19,64,512]{2,1,0:T(8,128)(2,1)S(1)} %get-tuple-element.80.refs_0_.near, bf16[19,64,512]{2,1,0:T(8,128)(2,1)S(1)} %collective-permute-done.23.refs_1_), custom_call_target="tpu_custom_call" | custom-call | bytes 4980736 | tf_op jit(solution)/shard_map/place/pallas_call | solution.py:318
  70.9 12.6 %collective-permute-done.19.refs_1_.one = bf16[19,64,512]{2,1,0:T(8,128)(2,1)S(1)} collective-permute-done((bf16[19,64,512]{2,1,0:T(8,128)(2,1)S(1)}, bf16[19,64,512]{2,1,0:T(8,128)(2,1)S(1)}, u32[]{:S(2)}, u32[]{:S(2)}) %collective-permute-start.19) | collective-permute-done | bytes 1245216 | tf_op jit(solution)/shard_map/ppermute | solution.py:44
  83.5 0.9 collective-permute-start.24
  84.5 0.0 collective-permute-start.25
  84.5 1.0 %collective-permute-start.20 = (bf16[9,64,512]{2,1,0:T(8,128)(2,1)S(1)}, bf16[9,64,512]{2,1,0:T(8,128)(2,1)S(1)}, u32[]{:S(2)}, u32[]{:S(2)}) collective-permute-start(bf16[9,64,512]{2,1,0:T(8,128)(2,1)S(1)} %slice.26), channel_id=1, source_target_pairs={{0,4},{1,5},{2,6},{3,7},{4,8},{5,9},{6,10},{7,11},{8,12},{9,13},{1... | collective-permute-start | bytes 1769480 | tf_op jit(solution)/shard_map/ppermute | solution.py:44
  85.6 1.8 %collective-permute-start.22 = (bf16[9,64,512]{2,1,0:T(8,128)(2,1)S(1)}, bf16[9,64,512]{2,1,0:T(8,128)(2,1)S(1)}, u32[]{:S(2)}, u32[]{:S(2)}) collective-permute-start(bf16[9,64,512]{2,1,0:T(8,128)(2,1)S(1)} %slice.27), channel_id=1, source_target_pairs={{0,12},{1,13},{2,14},{3,15},{4,0},{5,1},{6,2},{7,3},{8,4},{9,5},{1... | collective-permute-start | bytes 1769480 | tf_op jit(solution)/shard_map/ppermute | solution.py:44
  87.4 1.9 %place.4.refs_0_ = bf16[16,4,2,64,512]{4,3,2,1,0:T(8,128)(2,1)} custom-call(s32[62]{0:T(128)S(1)} %copy-done.8, bf16[16,4,2,64,512]{4,3,2,1,0:T(8,128)(2,1)} %place.3.refs_0_, bf16[19,64,512]{2,1,0:T(8,128)(2,1)S(1)} %collective-permute-done.19.refs_1_.one, bf16[19,64,512]{2,1,0:T(8,128)(2,1)S(1)} %collective-permute-done.24.refs_2_), custom_call_target="tpu_custom_call", output_to_operand_aliasing={{}: (1, {})} | custom-call | bytes 4980736 | tf_op jit(solution)/shard_map/place/pallas_call | solution.py:318
  89.3 1.9 %place.5.begun = bf16[16,4,2,64,512]{4,3,2,1,0:T(8,128)(2,1)} custom-call(s32[62]{0:T(128)S(1)} %copy-done.8, bf16[16,4,2,64,512]{4,3,2,1,0:T(8,128)(2,1)} %place.4.refs_0_, bf16[19,64,512]{2,1,0:T(8,128)(2,1)S(1)} %collective-permute-done.21.refs_1_.three, bf16[19,64,512]{2,1,0:T(8,128)(2,1)S(1)} %collective-permute-done.25.refs_2_), custom_call_target="tpu_custom_call", output_to_operand_aliasing={{}: (1, {})} | custom-call | bytes 4980736 | tf_op jit(solution)/shard_map/place/pallas_call | solution.py:318
  91.2 0.0 copy-start.5
  91.3 0.0 copy-start.6
  91.3 3.5 %collective-permute-done.20.low = bf16[9,64,512]{2,1,0:T(8,128)(2,1)S(1)} collective-permute-done((bf16[9,64,512]{2,1,0:T(8,128)(2,1)S(1)}, bf16[9,64,512]{2,1,0:T(8,128)(2,1)S(1)}, u32[]{:S(2)}, u32[]{:S(2)}) %collective-permute-start.20) | collective-permute-done | bytes 589856 | tf_op jit(solution)/shard_map/ppermute | solution.py:44
  94.9 1.4 %collective-permute-start.26 = (bf16[8,64,512]{2,1,0:T(8,128)(2,1)S(1)}, bf16[8,64,512]{2,1,0:T(8,128)(2,1)S(1)}, u32[]{:S(2)}, u32[]{:S(2)}) collective-permute-start(bf16[8,64,512]{2,1,0:T(8,128)(2,1)S(1)} %slice.22), channel_id=1, source_target_pairs={{0,16},{1,17},{2,18},{3,19},{4,20},{5,21},{6,22},{7,23},{8,24},{9,... | collective-permute-start | bytes 1572872 | tf_op jit(solution)/shard_map/ppermute | solution.py:44
  96.3 0.1 collective-permute-start.27
  96.4 2.0 %owner.1 = (bf16[16,4,2,64,512]{4,3,2,1,0:T(8,128)(2,1)}, f32[3,64,512]{2,1,0:T(8,128)}, f32[3,64,512]{2,1,0:T(8,128)}, f32[3,64,512]{2,1,0:T(8,128)}) custom-call(s32[62]{0:T(128)S(1)} %copy-done.8, bf16[16,4,2,64,512]{4,3,2,1,0:T(8,128)(2,1)} %place.5.begun, f32[3,64,512]{2,1,0:T(8,128)S(1)} %bitcast.11, ...), custom_call_target="tpu_custom_call", output_to_operand_aliasing={{0}: (1, {})} | custom-call | bytes 4915200 | tf_op jit(solution)/shard_map/owner/pallas_call | solution.py:455
  98.5 0.1 collective-permute-done.27.high_other
  98.6 1.5 %finish.1 = bf16[16,4,2,64,512]{4,3,2,1,0:T(8,128)(2,1)} custom-call(s32[62]{0:T(128)S(1)} %copy-done.8, bf16[16,4,2,64,512]{4,3,2,1,0:T(8,128)(2,1)} %get-tuple-element.88.begun, bf16[8,64,512]{2,1,0:T(8,128)(2,1)S(1)} %collective-permute-done.26.low_other, bf16[8,64,512]{2,1,0:T(8,128)(2,1)S(1)} %collective-permute-done.27.high_other), custom_call_target="tpu_custom_call", output_to_operand_aliasing={{}: (1, {})} | custom-call | bytes 1048576 | tf_op jit(solution)/shard_map/finish/pallas_call | solution.py:467
  (31 shorter events, 0.3 us)
Async XLA Ops:
  0.6 9.3 %copy-start.1 = (f32[1,3,64,512]{3,2,1,0:T(8,128)S(1)}, f32[1,3,64,512]{3,2,1,0:T(8,128)}, u32[]{:S(2)}) copy-start(f32[1,3,64,512]{3,2,1,0:T(8,128)} %param.15) | copy-start | bytes 1179652
  0.6 3.2 %collective-permute-start = (bf16[512,512]{1,0:T(8,128)(2,1)}, bf16[512,512]{1,0:T(8,128)(2,1)S(1)}, u32[]{:S(2)}, u32[]{:S(2)}) collective-permute-start(bf16[512,512]{1,0:T(8,128)(2,1)} %bitcast.12), channel_id=1, source_target_pairs={{0,16},{1,17},{2,18},{3,19},{4,20},{5,21},{6,22},{7,23},{8,24},{9,... | collective-permute-start | bytes 1572872 | tf_op jit(solution)/shard_map/ppermute | solution.py:44
  2.1 1.0 %copy-start.2 = (bf16[1,1,512,512]{3,2,1,0:T(8,128)(2,1)S(1)}, bf16[1,1,512,512]{3,2,1,0:T(8,128)(2,1)}, u32[]{:S(2)}) copy-start(bf16[1,1,512,512]{3,2,1,0:T(8,128)(2,1)} %param.8) | copy-start | bytes 1572868
  3.2 6.8 %copy-start.3 = (f32[1,3,64,512]{3,2,1,0:T(8,128)S(1)}, f32[1,3,64,512]{3,2,1,0:T(8,128)}, u32[]{:S(2)}) copy-start(f32[1,3,64,512]{3,2,1,0:T(8,128)} %param.13) | copy-start | bytes 1179652
  3.2 6.8 %copy-start.4 = (f32[1,3,64,512]{3,2,1,0:T(8,128)S(1)}, f32[1,3,64,512]{3,2,1,0:T(8,128)}, u32[]{:S(2)}) copy-start(f32[1,3,64,512]{3,2,1,0:T(8,128)} %param.14) | copy-start | bytes 1179652
  4.0 7.3 %collective-permute-start.1 = (bf16[64,512]{1,0:T(8,128)(2,1)S(1)}, bf16[64,512]{1,0:T(8,128)(2,1)S(1)}, u32[]{:S(2)}, u32[]{:S(2)}) collective-permute-start(bf16[64,512]{1,0:T(8,128)(2,1)S(1)} %get-tuple-element.58), channel_id=1, source_target_pairs={{0,32},{1,33},{2,34},{3,35},{4,36},{5,37},{6,38},{7,39},{8,40},{9,... | collective-permute-start | bytes 196616 | tf_op jit(solution)/shard_map/ppermute | solution.py:44
  5.3 5.9 %collective-permute-start.2 = (bf16[64,512]{1,0:T(8,128)(2,1)S(1)}, bf16[64,512]{1,0:T(8,128)(2,1)S(1)}, u32[]{:S(2)}, u32[]{:S(2)}) collective-permute-start(bf16[64,512]{1,0:T(8,128)(2,1)S(1)} %get-tuple-element.59), channel_id=1, source_target_pairs={{0,96},{1,97},{2,98},{3,99},{4,100},{5,101},{6,102},{7,103},{8,104... | collective-permute-start | bytes 196616 | tf_op jit(solution)/shard_map/ppermute | solution.py:44
  6.7 4.6 %collective-permute-start.3 = (bf16[64,512]{1,0:T(8,128)(2,1)S(1)}, bf16[64,512]{1,0:T(8,128)(2,1)S(1)}, u32[]{:S(2)}, u32[]{:S(2)}) collective-permute-start(bf16[64,512]{1,0:T(8,128)(2,1)S(1)} %get-tuple-element.60), channel_id=1, source_target_pairs={{0,64},{1,65},{2,66},{3,67},{4,68},{5,69},{6,70},{7,71},{8,72},{9,... | collective-permute-start | bytes 196616 | tf_op jit(solution)/shard_map/ppermute | solution.py:44
  10.0 0.7 copy-start.7
  10.6 12.1 %copy-start = (bf16[14,16,512]{2,1,0:T(8,128)(2,1)S(1)}, bf16[14,16,512]{2,1,0:T(8,128)(2,1)}, u32[]{:S(2)}) copy-start(bf16[14,16,512]{2,1,0:T(8,128)(2,1)} %get-tuple-element.56.tiles) | copy-start | bytes 688132
  11.4 7.8 %collective-permute-start.4 = (bf16[4,64,512]{2,1,0:T(8,128)(2,1)S(1)}, bf16[4,64,512]{2,1,0:T(8,128)(2,1)S(1)}, u32[]{:S(2)}, u32[]{:S(2)}) collective-permute-start(bf16[4,64,512]{2,1,0:T(8,128)(2,1)S(1)} %get-tuple-element.69), channel_id=1, source_target_pairs={{0,2},{1,3},{2,0},{3,1},{4,6},{5,7},{6,4},{7,5},{8,10},{9,11},{10,... | collective-permute-start | bytes 786440 | tf_op jit(solution)/shard_map/ppermute | solution.py:44
  15.1 6.9 %collective-permute-start.5 = (bf16[4,64,512]{2,1,0:T(8,128)(2,1)S(1)}, bf16[4,64,512]{2,1,0:T(8,128)(2,1)S(1)}, u32[]{:S(2)}, u32[]{:S(2)}) collective-permute-start(bf16[4,64,512]{2,1,0:T(8,128)(2,1)S(1)} %get-tuple-element.70), channel_id=1, source_target_pairs={{0,1},{1,2},{2,3},{3,0},{4,5},{5,6},{6,7},{7,4},{8,9},{9,10},{10,1... | collective-permute-start | bytes 786440 | tf_op jit(solution)/shard_map/ppermute | solution.py:44
  15.9 6.9 %collective-permute-start.6 = (bf16[4,64,512]{2,1,0:T(8,128)(2,1)S(1)}, bf16[4,64,512]{2,1,0:T(8,128)(2,1)S(1)}, u32[]{:S(2)}, u32[]{:S(2)}) collective-permute-start(bf16[4,64,512]{2,1,0:T(8,128)(2,1)S(1)} %get-tuple-element.71), channel_id=1, source_target_pairs={{0,3},{1,0},{2,1},{3,2},{4,7},{5,4},{6,5},{7,6},{8,11},{9,8},{10,9... | collective-permute-start | bytes 786440 | tf_op jit(solution)/shard_map/ppermute | solution.py:44
  23.0 7.1 %collective-permute-start.7 = (bf16[4,64,512]{2,1,0:T(8,128)(2,1)S(1)}, bf16[4,64,512]{2,1,0:T(8,128)(2,1)S(1)}, u32[]{:S(2)}, u32[]{:S(2)}) collective-permute-start(bf16[4,64,512]{2,1,0:T(8,128)(2,1)S(1)} %get-tuple-element.73), channel_id=1, source_target_pairs={{0,8},{1,9},{2,10},{3,11},{4,12},{5,13},{6,14},{7,15},{8,0},{9,1},... | collective-permute-start | bytes 786440 | tf_op jit(solution)/shard_map/ppermute | solution.py:44
  26.0 6.8 %collective-permute-start.8 = (bf16[4,64,512]{2,1,0:T(8,128)(2,1)S(1)}, bf16[4,64,512]{2,1,0:T(8,128)(2,1)S(1)}, u32[]{:S(2)}, u32[]{:S(2)}) collective-permute-start(bf16[4,64,512]{2,1,0:T(8,128)(2,1)S(1)} %get-tuple-element.74), channel_id=1, source_target_pairs={{0,4},{1,5},{2,6},{3,7},{4,8},{5,9},{6,10},{7,11},{8,12},{9,13},{1... | collective-permute-start | bytes 786440 | tf_op jit(solution)/shard_map/ppermute | solution.py:44
  26.4 6.9 %collective-permute-start.9 = (bf16[4,64,512]{2,1,0:T(8,128)(2,1)S(1)}, bf16[4,64,512]{2,1,0:T(8,128)(2,1)S(1)}, u32[]{:S(2)}, u32[]{:S(2)}) collective-permute-start(bf16[4,64,512]{2,1,0:T(8,128)(2,1)S(1)} %get-tuple-element.75), channel_id=1, source_target_pairs={{0,12},{1,13},{2,14},{3,15},{4,0},{5,1},{6,2},{7,3},{8,4},{9,5},{1... | collective-permute-start | bytes 786440 | tf_op jit(solution)/shard_map/ppermute | solution.py:44
  33.3 9.0 %collective-permute-start.10 = (bf16[4,64,512]{2,1,0:T(8,128)(2,1)S(1)}, bf16[4,64,512]{2,1,0:T(8,128)(2,1)S(1)}, u32[]{:S(2)}, u32[]{:S(2)}) collective-permute-start(bf16[4,64,512]{2,1,0:T(8,128)(2,1)S(1)} %here.1.own), channel_id=1, source_target_pairs={{0,64},{1,65},{2,66},{3,67},{4,68},{5,69},{6,70},{7,71},{8,72},{9,... | collective-permute-start | bytes 786440 | tf_op jit(solution)/shard_map/ppermute | solution.py:44
  34.9 11.7 %collective-permute-start.11 = (bf16[4,64,512]{2,1,0:T(8,128)(2,1)S(1)}, bf16[4,64,512]{2,1,0:T(8,128)(2,1)S(1)}, u32[]{:S(2)}, u32[]{:S(2)}) collective-permute-start(bf16[4,64,512]{2,1,0:T(8,128)(2,1)S(1)} %here.1.own), channel_id=1, source_target_pairs={{0,32},{1,33},{2,34},{3,35},{4,36},{5,37},{6,38},{7,39},{8,40},{9,... | collective-permute-start | bytes 786440 | tf_op jit(solution)/shard_map/ppermute | solution.py:44
  35.3 11.3 %collective-permute-start.12 = (bf16[4,64,512]{2,1,0:T(8,128)(2,1)S(1)}, bf16[4,64,512]{2,1,0:T(8,128)(2,1)S(1)}, u32[]{:S(2)}, u32[]{:S(2)}) collective-permute-start(bf16[4,64,512]{2,1,0:T(8,128)(2,1)S(1)} %here.1.own), channel_id=1, source_target_pairs={{0,96},{1,97},{2,98},{3,99},{4,100},{5,101},{6,102},{7,103},{8,104... | collective-permute-start | bytes 786440 | tf_op jit(solution)/shard_map/ppermute | solution.py:44
  37.6 9.0 %collective-permute-start.13 = (bf16[3,64,512]{2,1,0:T(8,128)(2,1)S(1)}, bf16[3,64,512]{2,1,0:T(8,128)(2,1)S(1)}, u32[]{:S(2)}, u32[]{:S(2)}) collective-permute-start(bf16[3,64,512]{2,1,0:T(8,128)(2,1)S(1)} %slice.24), channel_id=1, source_target_pairs={{0,16},{1,17},{2,18},{3,19},{4,20},{5,21},{6,22},{7,23},{8,24},{9,... | collective-permute-start | bytes 589832 | tf_op jit(solution)/shard_map/ppermute | solution.py:44
  42.3 5.4 %collective-permute-start.14 = (bf16[3,64,512]{2,1,0:T(8,128)(2,1)S(1)}, bf16[3,64,512]{2,1,0:T(8,128)(2,1)S(1)}, u32[]{:S(2)}, u32[]{:S(2)}) collective-permute-start(bf16[3,64,512]{2,1,0:T(8,128)(2,1)S(1)} %slice.25), channel_id=1, source_target_pairs={{0,16},{1,17},{2,18},{3,19},{4,20},{5,21},{6,22},{7,23},{8,24},{9,... | collective-permute-start | bytes 589832 | tf_op jit(solution)/shard_map/ppermute | solution.py:44
  47.7 3.0 %collective-permute-start.15 = (bf16[2,3,64,512]{3,2,1,0:T(8,128)(2,1)S(1)}, bf16[2,3,64,512]{3,2,1,0:T(8,128)(2,1)S(1)}, u32[]{:S(2)}, u32[]{:S(2)}) collective-permute-start(bf16[2,3,64,512]{3,2,1,0:T(8,128)(2,1)S(1)} %both.1), channel_id=1, source_target_pairs={{0,16},{1,17},{2,18},{3,19},{4,20},{5,21},{6,22},{7,23},{8,24},{9,... | collective-permute-start | bytes 1179656 | tf_op jit(solution)/shard_map/ppermute | solution.py:44
  51.9 17.0 %copy-start.8 = (s32[62]{0:T(128)S(1)}, s32[62]{0:T(128)}, u32[]{:S(2)}) copy-start(s32[62]{0:T(128)} %get-tuple-element.55.spot) | copy-start | bytes 748
  52.0 8.5 %collective-permute-start.16 = (bf16[6,64,512]{2,1,0:T(8,128)(2,1)S(1)}, bf16[6,64,512]{2,1,0:T(8,128)(2,1)S(1)}, u32[]{:S(2)}, u32[]{:S(2)}) collective-permute-start(bf16[6,64,512]{2,1,0:T(8,128)(2,1)S(1)} %step.1.a), channel_id=1, source_target_pairs={{0,2},{1,3},{2,0},{3,1},{4,6},{5,7},{6,4},{7,5},{8,10},{9,11},{10,... | collective-permute-start | bytes 1179656 | tf_op jit(solution)/shard_map/ppermute | solution.py:44
  53.8 10.8 %collective-permute-start.17 = (bf16[6,64,512]{2,1,0:T(8,128)(2,1)S(1)}, bf16[6,64,512]{2,1,0:T(8,128)(2,1)S(1)}, u32[]{:S(2)}, u32[]{:S(2)}) collective-permute-start(bf16[6,64,512]{2,1,0:T(8,128)(2,1)S(1)} %step.1.a), channel_id=1, source_target_pairs={{0,1},{1,2},{2,3},{3,0},{4,5},{5,6},{6,7},{7,4},{8,9},{9,10},{10,1... | collective-permute-start | bytes 1179656 | tf_op jit(solution)/shard_map/ppermute | solution.py:44
  54.7 9.9 %collective-permute-start.18 = (bf16[6,64,512]{2,1,0:T(8,128)(2,1)S(1)}, bf16[6,64,512]{2,1,0:T(8,128)(2,1)S(1)}, u32[]{:S(2)}, u32[]{:S(2)}) collective-permute-start(bf16[6,64,512]{2,1,0:T(8,128)(2,1)S(1)} %step.1.a), channel_id=1, source_target_pairs={{0,3},{1,0},{2,1},{3,2},{4,7},{5,4},{6,5},{7,6},{8,11},{9,8},{10,9... | collective-permute-start | bytes 1179656 | tf_op jit(solution)/shard_map/ppermute | solution.py:44
  64.9 4.0 %collective-permute-start.23 = (bf16[19,64,512]{2,1,0:T(8,128)(2,1)S(1)}, bf16[19,64,512]{2,1,0:T(8,128)(2,1)S(1)}, u32[]{:S(2)}, u32[]{:S(2)}) collective-permute-start(bf16[19,64,512]{2,1,0:T(8,128)(2,1)S(1)} %get-tuple-element.80.refs_0_.near), channel_id=1, source_target_pairs={{0,16},{1,17},{2,18},{3,19},{4,20},{5,21},{6,22},{7,23},{8,24},{9,... | collective-permute-start | bytes 3735560 | tf_op jit(solution)/shard_map/ppermute | solution.py:44
  66.3 17.3 %collective-permute-start.19 = (bf16[19,64,512]{2,1,0:T(8,128)(2,1)S(1)}, bf16[19,64,512]{2,1,0:T(8,128)(2,1)S(1)}, u32[]{:S(2)}, u32[]{:S(2)}) collective-permute-start(bf16[19,64,512]{2,1,0:T(8,128)(2,1)S(1)} %get-tuple-element.80.refs_0_.near), channel_id=1, source_target_pairs={{0,4},{1,5},{2,6},{3,7},{4,8},{5,9},{6,10},{7,11},{8,12},{9,13},{1... | collective-permute-start | bytes 3735560 | tf_op jit(solution)/shard_map/ppermute | solution.py:44
  67.1 16.4 %collective-permute-start.21 = (bf16[19,64,512]{2,1,0:T(8,128)(2,1)S(1)}, bf16[19,64,512]{2,1,0:T(8,128)(2,1)S(1)}, u32[]{:S(2)}, u32[]{:S(2)}) collective-permute-start(bf16[19,64,512]{2,1,0:T(8,128)(2,1)S(1)} %get-tuple-element.81), channel_id=1, source_target_pairs={{0,12},{1,13},{2,14},{3,15},{4,0},{5,1},{6,2},{7,3},{8,4},{9,5},{1... | collective-permute-start | bytes 3735560 | tf_op jit(solution)/shard_map/ppermute | solution.py:44
  83.5 3.8 %collective-permute-start.24 = (bf16[19,64,512]{2,1,0:T(8,128)(2,1)S(1)}, bf16[19,64,512]{2,1,0:T(8,128)(2,1)S(1)}, u32[]{:S(2)}, u32[]{:S(2)}) collective-permute-start(bf16[19,64,512]{2,1,0:T(8,128)(2,1)S(1)} %collective-permute-done.19.refs_1_.one), channel_id=1, source_target_pairs={{0,16},{1,17},{2,18},{3,19},{4,20},{5,21},{6,22},{7,23},{8,24},{9,... | collective-permute-start | bytes 3735560 | tf_op jit(solution)/shard_map/ppermute | solution.py:44
  84.5 4.8 %collective-permute-start.25 = (bf16[19,64,512]{2,1,0:T(8,128)(2,1)S(1)}, bf16[19,64,512]{2,1,0:T(8,128)(2,1)S(1)}, u32[]{:S(2)}, u32[]{:S(2)}) collective-permute-start(bf16[19,64,512]{2,1,0:T(8,128)(2,1)S(1)} %collective-permute-done.21.refs_1_.three), channel_id=1, source_target_pairs={{0,16},{1,17},{2,18},{3,19},{4,20},{5,21},{6,22},{7,23},{8,24},{9,... | collective-permute-start | bytes 3735560 | tf_op jit(solution)/shard_map/ppermute | solution.py:44
  84.5 10.3 %collective-permute-start.20 = (bf16[9,64,512]{2,1,0:T(8,128)(2,1)S(1)}, bf16[9,64,512]{2,1,0:T(8,128)(2,1)S(1)}, u32[]{:S(2)}, u32[]{:S(2)}) collective-permute-start(bf16[9,64,512]{2,1,0:T(8,128)(2,1)S(1)} %slice.26), channel_id=1, source_target_pairs={{0,4},{1,5},{2,6},{3,7},{4,8},{5,9},{6,10},{7,11},{8,12},{9,13},{1... | collective-permute-start | bytes 1769480 | tf_op jit(solution)/shard_map/ppermute | solution.py:44
  85.6 9.2 %collective-permute-start.22 = (bf16[9,64,512]{2,1,0:T(8,128)(2,1)S(1)}, bf16[9,64,512]{2,1,0:T(8,128)(2,1)S(1)}, u32[]{:S(2)}, u32[]{:S(2)}) collective-permute-start(bf16[9,64,512]{2,1,0:T(8,128)(2,1)S(1)} %slice.27), channel_id=1, source_target_pairs={{0,12},{1,13},{2,14},{3,15},{4,0},{5,1},{6,2},{7,3},{8,4},{9,5},{1... | collective-permute-start | bytes 1769480 | tf_op jit(solution)/shard_map/ppermute | solution.py:44
  91.2 5.2 %copy-start.5 = (f32[1,3,64,512]{3,2,1,0:T(8,128)S(1)}, f32[1,3,64,512]{3,2,1,0:T(8,128)}, u32[]{:S(2)}) copy-start(f32[1,3,64,512]{3,2,1,0:T(8,128)} %param.11) | copy-start | bytes 1179652
  91.3 5.2 %copy-start.6 = (f32[1,3,64,512]{3,2,1,0:T(8,128)S(1)}, f32[1,3,64,512]{3,2,1,0:T(8,128)}, u32[]{:S(2)}) copy-start(f32[1,3,64,512]{3,2,1,0:T(8,128)} %param.12) | copy-start | bytes 1179652
  94.9 3.6 %collective-permute-start.26 = (bf16[8,64,512]{2,1,0:T(8,128)(2,1)S(1)}, bf16[8,64,512]{2,1,0:T(8,128)(2,1)S(1)}, u32[]{:S(2)}, u32[]{:S(2)}) collective-permute-start(bf16[8,64,512]{2,1,0:T(8,128)(2,1)S(1)} %slice.22), channel_id=1, source_target_pairs={{0,16},{1,17},{2,18},{3,19},{4,20},{5,21},{6,22},{7,23},{8,24},{9,... | collective-permute-start | bytes 1572872 | tf_op jit(solution)/shard_map/ppermute | solution.py:44
  96.3 2.2 %collective-permute-start.27 = (bf16[8,64,512]{2,1,0:T(8,128)(2,1)S(1)}, bf16[8,64,512]{2,1,0:T(8,128)(2,1)S(1)}, u32[]{:S(2)}, u32[]{:S(2)}) collective-permute-start(bf16[8,64,512]{2,1,0:T(8,128)(2,1)S(1)} %slice.23), channel_id=1, source_target_pairs={{0,16},{1,17},{2,18},{3,19},{4,20},{5,21},{6,22},{7,23},{8,24},{9,... | collective-permute-start | bytes 1572872 | tf_op jit(solution)/shard_map/ppermute | solution.py:44

commit v8 on v6

--- a/solution.py
+++ b/solution.py
@@ -53,11 +53,11 @@
 
 
 def to_u(value, k):
-    return permute(value, lambda x, c, z, y: (x, c, z, y + k) if c == 0 else (x, c, z + k, y))
+    return permute(value, lambda x, c, z, y: (x, c, z, y + k) if c == 1 else (x, c, z + k, y))
 
 
 def to_v(value, k):
-    return permute(value, lambda x, c, z, y: (x, c, z + k, y) if c == 0 else (x, c, z, y + k))
+    return permute(value, lambda x, c, z, y: (x, c, z + k, y) if c == 1 else (x, c, z, y + k))
 
 
 def along(send, values, shifts=(1, 3, 2)):
@@ -72,7 +72,7 @@
 def choice_kernel(order_ref, count_ref, out, tiles, start_ref, owner_ref):
     x, c, z, y = position()
     me = z * 4 + y
-    first = c == 0
+    first = c == 1
     u, v = jnp.where(first, y, z), jnp.where(first, z, y)
 
     def place_at(uu, vv):

time: 100 us -> 100 us (level)
  no operation moved by 1% of the time
where the time goes in v8:
time: 100 us
  starting transfers between devices  48.8 us (49%)
  waiting for transfers between devices  35.1 us (35%)
  Pallas kernels  13.6 us (14%)
  local copies, waits for them, and re-layouts  1.9 us (2%)
    ppermute x28, starting transfers between devices, permute(): return lax.ppermute(value, AXES, pairs)  48.8 us
    ppermute x28, waiting for transfers between devices, permute(): return lax.ppermute(value, AXES, pairs)  35.1 us
    pallas_call x3, Pallas kernels, place(): pl.pallas_call(functools.partial(place_kernel, which), out_shape=jax.Shap...  5.78 us
    pallas_call x9, Pallas kernels, small_call(): pl.pallas_call(body, out_shape=outs, in_specs=[SMEM if a.dtype == jnp.int...  2.65 us
    pallas_call x1, Pallas kernels, local(): pl.pallas_call(owner_kernel, out_shape=[jax.ShapeDtypeStruct(begun.shape,...  2.02 us
  transfers between devices with their start and end apart: 28, of which 15 were waited for; matrix products, arithmetic and copies ran while one was open for 0% of the time, Pallas kernels for 10%

profile of v8, /device:TPU:1, one launch (start us, length us, event | category | flops | bytes accessed | tf_op | source)
XLA Modules:
  0.0 100.3 jit_solution(11279055398329342319)
XLA Ops:
  0.6 1.5 %collective-permute-start = (bf16[512,512]{1,0:T(8,128)(2,1)}, bf16[512,512]{1,0:T(8,128)(2,1)S(1)}, u32[]{:S(2)}, u32[]{:S(2)}) collective-permute-start(bf16[512,512]{1,0:T(8,128)(2,1)} %bitcast.12), channel_id=1, source_target_pairs={{0,16},{1,17},{2,18},{3,19},{4,20},{5,21},{6,22},{7,23},{8,24},{9,... | collective-permute-start | bytes 1572872 | tf_op jit(solution)/shard_map/ppermute | solution.py:44
  2.1 1.0 %copy-done.2 = bf16[1,1,512,512]{3,2,1,0:T(8,128)(2,1)S(1)} copy-done((bf16[1,1,512,512]{3,2,1,0:T(8,128)(2,1)S(1)}, bf16[1,1,512,512]{3,2,1,0:T(8,128)(2,1)}, u32[]{:S(2)}) %copy-start.2) | copy-done | bytes 524312
  3.2 0.7 collective-permute-done.theirs
  3.9 0.1 pair.1
  4.0 1.4 %collective-permute-start.1 = (bf16[64,512]{1,0:T(8,128)(2,1)S(1)}, bf16[64,512]{1,0:T(8,128)(2,1)S(1)}, u32[]{:S(2)}, u32[]{:S(2)}) collective-permute-start(bf16[64,512]{1,0:T(8,128)(2,1)S(1)} %get-tuple-element.58), channel_id=1, source_target_pairs={{0,32},{1,33},{2,34},{3,35},{4,36},{5,37},{6,38},{7,39},{8,40},{9,... | collective-permute-start | bytes 196616 | tf_op jit(solution)/shard_map/ppermute | solution.py:44
  5.3 1.4 %collective-permute-start.2 = (bf16[64,512]{1,0:T(8,128)(2,1)S(1)}, bf16[64,512]{1,0:T(8,128)(2,1)S(1)}, u32[]{:S(2)}, u32[]{:S(2)}) collective-permute-start(bf16[64,512]{1,0:T(8,128)(2,1)S(1)} %get-tuple-element.59), channel_id=1, source_target_pairs={{0,96},{1,97},{2,98},{3,99},{4,100},{5,101},{6,102},{7,103},{8,104... | collective-permute-start | bytes 196616 | tf_op jit(solution)/shard_map/ppermute | solution.py:44
  6.7 1.6 %collective-permute-start.3 = (bf16[64,512]{1,0:T(8,128)(2,1)S(1)}, bf16[64,512]{1,0:T(8,128)(2,1)S(1)}, u32[]{:S(2)}, u32[]{:S(2)}) collective-permute-start(bf16[64,512]{1,0:T(8,128)(2,1)S(1)} %get-tuple-element.60), channel_id=1, source_target_pairs={{0,64},{1,65},{2,66},{3,67},{4,68},{5,69},{6,70},{7,71},{8,72},{9,... | collective-permute-start | bytes 196616 | tf_op jit(solution)/shard_map/ppermute | solution.py:44
  8.3 1.6 %choices.1 = (s32[62]{0:T(128)}, bf16[14,16,512]{2,1,0:T(8,128)(2,1)}) custom-call(s32[16]{0:T(128)} %order_ref, s32[16]{0:T(128)} %count_ref), custom_call_target="tpu_custom_call" | custom-call | bytes 4194304 | tf_op jit(solution)/shard_map/choices/pallas_call | solution.py:144
  10.0 0.0 copy-start.7
  10.0 0.6 copy-done.7
  10.6 0.6 packs.1
  11.2 0.0 collective-permute-done.1.a
  11.3 0.1 collective-permute-done.3.b
  11.4 3.1 %collective-permute-start.4 = (bf16[4,64,512]{2,1,0:T(8,128)(2,1)S(1)}, bf16[4,64,512]{2,1,0:T(8,128)(2,1)S(1)}, u32[]{:S(2)}, u32[]{:S(2)}) collective-permute-start(bf16[4,64,512]{2,1,0:T(8,128)(2,1)S(1)} %get-tuple-element.69), channel_id=1, source_target_pairs={{0,8},{1,9},{2,10},{3,11},{4,12},{5,13},{6,14},{7,15},{8,0},{9,1},... | collective-permute-start | bytes 786440 | tf_op jit(solution)/shard_map/ppermute | solution.py:44
  14.4 0.4 collective-permute-start.5
  14.8 2.3 %collective-permute-start.6 = (bf16[4,64,512]{2,1,0:T(8,128)(2,1)S(1)}, bf16[4,64,512]{2,1,0:T(8,128)(2,1)S(1)}, u32[]{:S(2)}, u32[]{:S(2)}) collective-permute-start(bf16[4,64,512]{2,1,0:T(8,128)(2,1)S(1)} %get-tuple-element.71), channel_id=1, source_target_pairs={{0,12},{1,13},{2,14},{3,15},{4,0},{5,1},{6,2},{7,3},{8,4},{9,5},{1... | collective-permute-start | bytes 786440 | tf_op jit(solution)/shard_map/ppermute | solution.py:44
  17.1 1.1 %collective-permute-done.4.c = bf16[4,64,512]{2,1,0:T(8,128)(2,1)S(1)} collective-permute-done((bf16[4,64,512]{2,1,0:T(8,128)(2,1)S(1)}, bf16[4,64,512]{2,1,0:T(8,128)(2,1)S(1)}, u32[]{:S(2)}, u32[]{:S(2)}) %collective-permute-start.4) | collective-permute-done | bytes 262176 | tf_op jit(solution)/shard_map/ppermute | solution.py:44
  18.2 3.1 %collective-permute-done.5.b = bf16[4,64,512]{2,1,0:T(8,128)(2,1)S(1)} collective-permute-done((bf16[4,64,512]{2,1,0:T(8,128)(2,1)S(1)}, bf16[4,64,512]{2,1,0:T(8,128)(2,1)S(1)}, u32[]{:S(2)}, u32[]{:S(2)}) %collective-permute-start.5) | collective-permute-done | bytes 262176 | tf_op jit(solution)/shard_map/ppermute | solution.py:44
  21.3 0.1 collective-permute-done.6.d
  21.4 0.3 turn.1
  21.7 3.9 %collective-permute-start.7 = (bf16[4,64,512]{2,1,0:T(8,128)(2,1)S(1)}, bf16[4,64,512]{2,1,0:T(8,128)(2,1)S(1)}, u32[]{:S(2)}, u32[]{:S(2)}) collective-permute-start(bf16[4,64,512]{2,1,0:T(8,128)(2,1)S(1)} %get-tuple-element.73), channel_id=1, source_target_pairs={{0,2},{1,3},{2,0},{3,1},{4,6},{5,7},{6,4},{7,5},{8,10},{9,11},{10,... | collective-permute-start | bytes 786440 | tf_op jit(solution)/shard_map/ppermute | solution.py:44
  25.6 0.7 collective-permute-start.8
  26.4 1.9 %collective-permute-start.9 = (bf16[4,64,512]{2,1,0:T(8,128)(2,1)S(1)}, bf16[4,64,512]{2,1,0:T(8,128)(2,1)S(1)}, u32[]{:S(2)}, u32[]{:S(2)}) collective-permute-start(bf16[4,64,512]{2,1,0:T(8,128)(2,1)S(1)} %get-tuple-element.75), channel_id=1, source_target_pairs={{0,3},{1,0},{2,1},{3,2},{4,7},{5,4},{6,5},{7,6},{8,11},{9,8},{10,9... | collective-permute-start | bytes 786440 | tf_op jit(solution)/shard_map/ppermute | solution.py:44
  28.3 1.1 %collective-permute-done.7.c = bf16[4,64,512]{2,1,0:T(8,128)(2,1)S(1)} collective-permute-done((bf16[4,64,512]{2,1,0:T(8,128)(2,1)S(1)}, bf16[4,64,512]{2,1,0:T(8,128)(2,1)S(1)}, u32[]{:S(2)}, u32[]{:S(2)}) %collective-permute-start.7) | collective-permute-done | bytes 262176 | tf_op jit(solution)/shard_map/ppermute | solution.py:44
  29.4 3.1 %collective-permute-done.8.b = bf16[4,64,512]{2,1,0:T(8,128)(2,1)S(1)} collective-permute-done((bf16[4,64,512]{2,1,0:T(8,128)(2,1)S(1)}, bf16[4,64,512]{2,1,0:T(8,128)(2,1)S(1)}, u32[]{:S(2)}, u32[]{:S(2)}) %collective-permute-start.8) | collective-permute-done | bytes 262176 | tf_op jit(solution)/shard_map/ppermute | solution.py:44
  32.5 0.7 collective-permute-done.9.d
  33.2 0.1 here.1.own
  33.3 1.6 %collective-permute-start.10 = (bf16[4,64,512]{2,1,0:T(8,128)(2,1)S(1)}, bf16[4,64,512]{2,1,0:T(8,128)(2,1)S(1)}, u32[]{:S(2)}, u32[]{:S(2)}) collective-permute-start(bf16[4,64,512]{2,1,0:T(8,128)(2,1)S(1)} %here.1.own), channel_id=1, source_target_pairs={{0,64},{1,65},{2,66},{3,67},{4,68},{5,69},{6,70},{7,71},{8,72},{9,... | collective-permute-start | bytes 786440 | tf_op jit(solution)/shard_map/ppermute | solution.py:44
  34.9 0.4 collective-permute-start.11
  35.3 2.3 %collective-permute-start.12 = (bf16[4,64,512]{2,1,0:T(8,128)(2,1)S(1)}, bf16[4,64,512]{2,1,0:T(8,128)(2,1)S(1)}, u32[]{:S(2)}, u32[]{:S(2)}) collective-permute-start(bf16[4,64,512]{2,1,0:T(8,128)(2,1)S(1)} %here.1.own), channel_id=1, source_target_pairs={{0,96},{1,97},{2,98},{3,99},{4,100},{5,101},{6,102},{7,103},{8,104... | collective-permute-start | bytes 786440 | tf_op jit(solution)/shard_map/ppermute | solution.py:44
  37.6 4.7 %collective-permute-start.13 = (bf16[3,64,512]{2,1,0:T(8,128)(2,1)S(1)}, bf16[3,64,512]{2,1,0:T(8,128)(2,1)S(1)}, u32[]{:S(2)}, u32[]{:S(2)}) collective-permute-start(bf16[3,64,512]{2,1,0:T(8,128)(2,1)S(1)} %slice.24), channel_id=1, source_target_pairs={{0,16},{1,17},{2,18},{3,19},{4,20},{5,21},{6,22},{7,23},{8,24},{9,... | collective-permute-start | bytes 589832 | tf_op jit(solution)/shard_map/ppermute | solution.py:44
  42.3 4.3 %collective-permute-start.14 = (bf16[3,64,512]{2,1,0:T(8,128)(2,1)S(1)}, bf16[3,64,512]{2,1,0:T(8,128)(2,1)S(1)}, u32[]{:S(2)}, u32[]{:S(2)}) collective-permute-start(bf16[3,64,512]{2,1,0:T(8,128)(2,1)S(1)} %slice.25), channel_id=1, source_target_pairs={{0,16},{1,17},{2,18},{3,19},{4,20},{5,21},{6,22},{7,23},{8,24},{9,... | collective-permute-start | bytes 589832 | tf_op jit(solution)/shard_map/ppermute | solution.py:44
  46.6 1.1 %collective-permute-done.14.two_other = bf16[3,64,512]{2,1,0:T(8,128)(2,1)S(1)} collective-permute-done((bf16[3,64,512]{2,1,0:T(8,128)(2,1)S(1)}, bf16[3,64,512]{2,1,0:T(8,128)(2,1)S(1)}, u32[]{:S(2)}, u32[]{:S(2)}) %collective-permute-start.14) | collective-permute-done | bytes 196640 | tf_op jit(solution)/shard_map/ppermute | solution.py:44
  47.7 1.6 %collective-permute-start.15 = (bf16[2,3,64,512]{3,2,1,0:T(8,128)(2,1)S(1)}, bf16[2,3,64,512]{3,2,1,0:T(8,128)(2,1)S(1)}, u32[]{:S(2)}, u32[]{:S(2)}) collective-permute-start(bf16[2,3,64,512]{3,2,1,0:T(8,128)(2,1)S(1)} %both.1), channel_id=1, source_target_pairs={{0,16},{1,17},{2,18},{3,19},{4,20},{5,21},{6,22},{7,23},{8,24},{9,... | collective-permute-start | bytes 1179656 | tf_op jit(solution)/shard_map/ppermute | solution.py:44
  49.3 1.3 %collective-permute-done.15.rest_other = bf16[2,3,64,512]{3,2,1,0:T(8,128)(2,1)S(1)} collective-permute-done((bf16[2,3,64,512]{3,2,1,0:T(8,128)(2,1)S(1)}, bf16[2,3,64,512]{3,2,1,0:T(8,128)(2,1)S(1)}, u32[]{:S(2)}, u32[]{:S(2)}) %collective-permute-start.15) | collective-permute-done | bytes 393248 | tf_op jit(solution)/shard_map/ppermute | solution.py:44
  50.7 1.2 %step.1.a = bf16[6,64,512]{2,1,0:T(8,128)(2,1)S(1)} custom-call(bf16[4,64,512]{2,1,0:T(8,128)(2,1)S(1)} %here.1.own, bf16[4,64,512]{2,1,0:T(8,128)(2,1)S(1)} %collective-permute-done.10.two, bf16[4,64,512]{2,1,0:T(8,128)(2,1)S(1)} %collective-permute-done.11.one, bf16[4,64,512]{2,1,0:T(8,128)(2,1)S(1)} %collective-permute-done.12.three, ...), custom_call_target="tpu_custom_call" | custom-call | flops 805306368 | bytes 2228224 | tf_op jit(solution)/shard_map/step/pallas_call | solution.py:164
  51.9 0.0 copy-start.8
  52.0 1.9 %collective-permute-start.16 = (bf16[6,64,512]{2,1,0:T(8,128)(2,1)S(1)}, bf16[6,64,512]{2,1,0:T(8,128)(2,1)S(1)}, u32[]{:S(2)}, u32[]{:S(2)}) collective-permute-start(bf16[6,64,512]{2,1,0:T(8,128)(2,1)S(1)} %step.1.a), channel_id=1, source_target_pairs={{0,8},{1,9},{2,10},{3,11},{4,12},{5,13},{6,14},{7,15},{8,0},{9,1},... | collective-permute-start | bytes 1179656 | tf_op jit(solution)/shard_map/ppermute | solution.py:44
  53.8 1.2 %collective-permute-start.17 = (bf16[6,64,512]{2,1,0:T(8,128)(2,1)S(1)}, bf16[6,64,512]{2,1,0:T(8,128)(2,1)S(1)}, u32[]{:S(2)}, u32[]{:S(2)}) collective-permute-start(bf16[6,64,512]{2,1,0:T(8,128)(2,1)S(1)} %step.1.a), channel_id=1, source_target_pairs={{0,4},{1,5},{2,6},{3,7},{4,8},{5,9},{6,10},{7,11},{8,12},{9,13},{1... | collective-permute-start | bytes 1179656 | tf_op jit(solution)/shard_map/ppermute | solution.py:44
  55.0 1.5 %collective-permute-start.18 = (bf16[6,64,512]{2,1,0:T(8,128)(2,1)S(1)}, bf16[6,64,512]{2,1,0:T(8,128)(2,1)S(1)}, u32[]{:S(2)}, u32[]{:S(2)}) collective-permute-start(bf16[6,64,512]{2,1,0:T(8,128)(2,1)S(1)} %step.1.a), channel_id=1, source_target_pairs={{0,12},{1,13},{2,14},{3,15},{4,0},{5,1},{6,2},{7,3},{8,4},{9,5},{1... | collective-permute-start | bytes 1179656 | tf_op jit(solution)/shard_map/ppermute | solution.py:44
  56.5 4.0 %collective-permute-done.16.c = bf16[6,64,512]{2,1,0:T(8,128)(2,1)S(1)} collective-permute-done((bf16[6,64,512]{2,1,0:T(8,128)(2,1)S(1)}, bf16[6,64,512]{2,1,0:T(8,128)(2,1)S(1)}, u32[]{:S(2)}, u32[]{:S(2)}) %collective-permute-start.16) | collective-permute-done | bytes 393248 | tf_op jit(solution)/shard_map/ppermute | solution.py:44
  60.5 4.2 %collective-permute-done.17.b = bf16[6,64,512]{2,1,0:T(8,128)(2,1)S(1)} collective-permute-done((bf16[6,64,512]{2,1,0:T(8,128)(2,1)S(1)}, bf16[6,64,512]{2,1,0:T(8,128)(2,1)S(1)}, u32[]{:S(2)}, u32[]{:S(2)}) %collective-permute-start.17) | collective-permute-done | bytes 393248 | tf_op jit(solution)/shard_map/ppermute | solution.py:44
  64.7 0.0 collective-permute-done.18.d
  64.7 0.3 near.1
  65.0 0.6 collective-permute-start.19
  65.7 2.1 %collective-permute-start.21 = (bf16[19,64,512]{2,1,0:T(8,128)(2,1)S(1)}, bf16[19,64,512]{2,1,0:T(8,128)(2,1)S(1)}, u32[]{:S(2)}, u32[]{:S(2)}) collective-permute-start(bf16[19,64,512]{2,1,0:T(8,128)(2,1)S(1)} %get-tuple-element.81), channel_id=1, source_target_pairs={{0,3},{1,0},{2,1},{3,2},{4,7},{5,4},{6,5},{7,6},{8,11},{9,8},{10,9... | collective-permute-start | bytes 3735560 | tf_op jit(solution)/shard_map/ppermute | solution.py:44
  67.8 1.8 %collective-permute-start.23 = (bf16[18,64,512]{2,1,0:T(8,128)(2,1)S(1)}, bf16[18,64,512]{2,1,0:T(8,128)(2,1)S(1)}, u32[]{:S(2)}, u32[]{:S(2)}) collective-permute-start(bf16[18,64,512]{2,1,0:T(8,128)(2,1)S(1)} %get-tuple-element.82.refs_0_.near), channel_id=1, source_target_pairs={{0,16},{1,17},{2,18},{3,19},{4,20},{5,21},{6,22},{7,23},{8,24},{9,... | collective-permute-start | bytes 3538952 | tf_op jit(solution)/shard_map/ppermute | solution.py:44
  69.6 2.5 %collective-permute-done.23.refs_1_ = bf16[18,64,512]{2,1,0:T(8,128)(2,1)S(1)} collective-permute-done((bf16[18,64,512]{2,1,0:T(8,128)(2,1)S(1)}, bf16[18,64,512]{2,1,0:T(8,128)(2,1)S(1)}, u32[]{:S(2)}, u32[]{:S(2)}) %collective-permute-start.23) | collective-permute-done | bytes 1179680 | tf_op jit(solution)/shard_map/ppermute | solution.py:44
  72.1 1.9 %place.3.refs_0_ = bf16[16,4,2,64,512]{4,3,2,1,0:T(8,128)(2,1)} custom-call(s32[62]{0:T(128)S(1)} %copy-done.8, bf16[18,64,512]{2,1,0:T(8,128)(2,1)S(1)} %get-tuple-element.82.refs_0_.near, bf16[18,64,512]{2,1,0:T(8,128)(2,1)S(1)} %collective-permute-done.23.refs_1_), custom_call_target="tpu_custom_call" | custom-call | bytes 4718592 | tf_op jit(solution)/shard_map/place/pallas_call | solution.py:317
  74.0 8.4 %collective-permute-done.19.refs_1_.one = bf16[19,64,512]{2,1,0:T(8,128)(2,1)S(1)} collective-permute-done((bf16[19,64,512]{2,1,0:T(8,128)(2,1)S(1)}, bf16[19,64,512]{2,1,0:T(8,128)(2,1)S(1)}, u32[]{:S(2)}, u32[]{:S(2)}) %collective-permute-start.19) | collective-permute-done | bytes 1245216 | tf_op jit(solution)/shard_map/ppermute | solution.py:44
  82.4 2.2 %collective-permute-start.24 = (bf16[19,64,512]{2,1,0:T(8,128)(2,1)S(1)}, bf16[19,64,512]{2,1,0:T(8,128)(2,1)S(1)}, u32[]{:S(2)}, u32[]{:S(2)}) collective-permute-start(bf16[19,64,512]{2,1,0:T(8,128)(2,1)S(1)} %collective-permute-done.19.refs_1_.one), channel_id=1, source_target_pairs={{0,16},{1,17},{2,18},{3,19},{4,20},{5,21},{6,22},{7,23},{8,24},{9,... | collective-permute-start | bytes 3735560 | tf_op jit(solution)/shard_map/ppermute | solution.py:44
  84.6 0.0 collective-permute-start.25
  84.7 0.8 collective-permute-start.20
  85.5 2.0 %collective-permute-start.22 = (bf16[9,64,512]{2,1,0:T(8,128)(2,1)S(1)}, bf16[9,64,512]{2,1,0:T(8,128)(2,1)S(1)}, u32[]{:S(2)}, u32[]{:S(2)}) collective-permute-start(bf16[9,64,512]{2,1,0:T(8,128)(2,1)S(1)} %slice.27), channel_id=1, source_target_pairs={{0,3},{1,0},{2,1},{3,2},{4,7},{5,4},{6,5},{7,6},{8,11},{9,8},{10,9... | collective-permute-start | bytes 1769480 | tf_op jit(solution)/shard_map/ppermute | solution.py:44
  87.5 1.9 %place.4.refs_0_ = bf16[16,4,2,64,512]{4,3,2,1,0:T(8,128)(2,1)} custom-call(s32[62]{0:T(128)S(1)} %copy-done.8, bf16[16,4,2,64,512]{4,3,2,1,0:T(8,128)(2,1)} %place.3.refs_0_, bf16[19,64,512]{2,1,0:T(8,128)(2,1)S(1)} %collective-permute-done.19.refs_1_.one, bf16[19,64,512]{2,1,0:T(8,128)(2,1)S(1)} %collective-permute-done.24.refs_2_), custom_call_target="tpu_custom_call", output_to_operand_aliasing={{}: (1, {})} | custom-call | bytes 4980736 | tf_op jit(solution)/shard_map/place/pallas_call | solution.py:317
  89.5 1.9 %place.5.begun = bf16[16,4,2,64,512]{4,3,2,1,0:T(8,128)(2,1)} custom-call(s32[62]{0:T(128)S(1)} %copy-done.8, bf16[16,4,2,64,512]{4,3,2,1,0:T(8,128)(2,1)} %place.4.refs_0_, bf16[19,64,512]{2,1,0:T(8,128)(2,1)S(1)} %collective-permute-done.21.refs_1_.three, bf16[19,64,512]{2,1,0:T(8,128)(2,1)S(1)} %collective-permute-done.25.refs_2_), custom_call_target="tpu_custom_call", output_to_operand_aliasing={{}: (1, {})} | custom-call | bytes 4980736 | tf_op jit(solution)/shard_map/place/pallas_call | solution.py:317
  91.4 0.0 copy-start.5
  91.4 0.0 copy-start.6
  91.4 3.5 %collective-permute-done.20.low = bf16[9,64,512]{2,1,0:T(8,128)(2,1)S(1)} collective-permute-done((bf16[9,64,512]{2,1,0:T(8,128)(2,1)S(1)}, bf16[9,64,512]{2,1,0:T(8,128)(2,1)S(1)}, u32[]{:S(2)}, u32[]{:S(2)}) %collective-permute-start.20) | collective-permute-done | bytes 589856 | tf_op jit(solution)/shard_map/ppermute | solution.py:44
  95.0 1.4 %collective-permute-start.26 = (bf16[8,64,512]{2,1,0:T(8,128)(2,1)S(1)}, bf16[8,64,512]{2,1,0:T(8,128)(2,1)S(1)}, u32[]{:S(2)}, u32[]{:S(2)}) collective-permute-start(bf16[8,64,512]{2,1,0:T(8,128)(2,1)S(1)} %slice.22), channel_id=1, source_target_pairs={{0,16},{1,17},{2,18},{3,19},{4,20},{5,21},{6,22},{7,23},{8,24},{9,... | collective-permute-start | bytes 1572872 | tf_op jit(solution)/shard_map/ppermute | solution.py:44
  96.5 0.1 collective-permute-start.27
  96.6 2.0 %owner.1 = (bf16[16,4,2,64,512]{4,3,2,1,0:T(8,128)(2,1)}, f32[3,64,512]{2,1,0:T(8,128)}, f32[3,64,512]{2,1,0:T(8,128)}, f32[3,64,512]{2,1,0:T(8,128)}) custom-call(s32[62]{0:T(128)S(1)} %copy-done.8, bf16[16,4,2,64,512]{4,3,2,1,0:T(8,128)(2,1)} %place.5.begun, f32[3,64,512]{2,1,0:T(8,128)S(1)} %bitcast.11, ...), custom_call_target="tpu_custom_call", output_to_operand_aliasing={{0}: (1, {})} | custom-call | bytes 4849664 | tf_op jit(solution)/shard_map/owner/pallas_call | solution.py:454
  98.6 0.1 collective-permute-done.27.high_other
  98.7 1.5 %finish.1 = bf16[16,4,2,64,512]{4,3,2,1,0:T(8,128)(2,1)} custom-call(s32[62]{0:T(128)S(1)} %copy-done.8, bf16[16,4,2,64,512]{4,3,2,1,0:T(8,128)(2,1)} %get-tuple-element.88.begun, bf16[8,64,512]{2,1,0:T(8,128)(2,1)S(1)} %collective-permute-done.26.low_other, bf16[8,64,512]{2,1,0:T(8,128)(2,1)S(1)} %collective-permute-done.27.high_other), custom_call_target="tpu_custom_call", output_to_operand_aliasing={{}: (1, {})} | custom-call | bytes 1048576 | tf_op jit(solution)/shard_map/finish/pallas_call | solution.py:466
  (31 shorter events, 0.3 us)
Async XLA Ops:
  0.6 9.3 %copy-start.1 = (f32[1,3,64,512]{3,2,1,0:T(8,128)S(1)}, f32[1,3,64,512]{3,2,1,0:T(8,128)}, u32[]{:S(2)}) copy-start(f32[1,3,64,512]{3,2,1,0:T(8,128)} %param.15) | copy-start | bytes 1179652
  0.6 3.2 %collective-permute-start = (bf16[512,512]{1,0:T(8,128)(2,1)}, bf16[512,512]{1,0:T(8,128)(2,1)S(1)}, u32[]{:S(2)}, u32[]{:S(2)}) collective-permute-start(bf16[512,512]{1,0:T(8,128)(2,1)} %bitcast.12), channel_id=1, source_target_pairs={{0,16},{1,17},{2,18},{3,19},{4,20},{5,21},{6,22},{7,23},{8,24},{9,... | collective-permute-start | bytes 1572872 | tf_op jit(solution)/shard_map/ppermute | solution.py:44
  2.1 1.0 %copy-start.2 = (bf16[1,1,512,512]{3,2,1,0:T(8,128)(2,1)S(1)}, bf16[1,1,512,512]{3,2,1,0:T(8,128)(2,1)}, u32[]{:S(2)}) copy-start(bf16[1,1,512,512]{3,2,1,0:T(8,128)(2,1)} %param.8) | copy-start | bytes 1572868
  3.2 6.8 %copy-start.3 = (f32[1,3,64,512]{3,2,1,0:T(8,128)S(1)}, f32[1,3,64,512]{3,2,1,0:T(8,128)}, u32[]{:S(2)}) copy-start(f32[1,3,64,512]{3,2,1,0:T(8,128)} %param.13) | copy-start | bytes 1179652
  3.2 6.8 %copy-start.4 = (f32[1,3,64,512]{3,2,1,0:T(8,128)S(1)}, f32[1,3,64,512]{3,2,1,0:T(8,128)}, u32[]{:S(2)}) copy-start(f32[1,3,64,512]{3,2,1,0:T(8,128)} %param.14) | copy-start | bytes 1179652
  4.0 7.3 %collective-permute-start.1 = (bf16[64,512]{1,0:T(8,128)(2,1)S(1)}, bf16[64,512]{1,0:T(8,128)(2,1)S(1)}, u32[]{:S(2)}, u32[]{:S(2)}) collective-permute-start(bf16[64,512]{1,0:T(8,128)(2,1)S(1)} %get-tuple-element.58), channel_id=1, source_target_pairs={{0,32},{1,33},{2,34},{3,35},{4,36},{5,37},{6,38},{7,39},{8,40},{9,... | collective-permute-start | bytes 196616 | tf_op jit(solution)/shard_map/ppermute | solution.py:44
  5.3 5.9 %collective-permute-start.2 = (bf16[64,512]{1,0:T(8,128)(2,1)S(1)}, bf16[64,512]{1,0:T(8,128)(2,1)S(1)}, u32[]{:S(2)}, u32[]{:S(2)}) collective-permute-start(bf16[64,512]{1,0:T(8,128)(2,1)S(1)} %get-tuple-element.59), channel_id=1, source_target_pairs={{0,96},{1,97},{2,98},{3,99},{4,100},{5,101},{6,102},{7,103},{8,104... | collective-permute-start | bytes 196616 | tf_op jit(solution)/shard_map/ppermute | solution.py:44
  6.7 4.6 %collective-permute-start.3 = (bf16[64,512]{1,0:T(8,128)(2,1)S(1)}, bf16[64,512]{1,0:T(8,128)(2,1)S(1)}, u32[]{:S(2)}, u32[]{:S(2)}) collective-permute-start(bf16[64,512]{1,0:T(8,128)(2,1)S(1)} %get-tuple-element.60), channel_id=1, source_target_pairs={{0,64},{1,65},{2,66},{3,67},{4,68},{5,69},{6,70},{7,71},{8,72},{9,... | collective-permute-start | bytes 196616 | tf_op jit(solution)/shard_map/ppermute | solution.py:44
  10.0 0.7 copy-start.7
  10.6 10.8 %copy-start = (bf16[14,16,512]{2,1,0:T(8,128)(2,1)S(1)}, bf16[14,16,512]{2,1,0:T(8,128)(2,1)}, u32[]{:S(2)}) copy-start(bf16[14,16,512]{2,1,0:T(8,128)(2,1)} %get-tuple-element.56.tiles) | copy-start | bytes 688132
  11.4 6.9 %collective-permute-start.4 = (bf16[4,64,512]{2,1,0:T(8,128)(2,1)S(1)}, bf16[4,64,512]{2,1,0:T(8,128)(2,1)S(1)}, u32[]{:S(2)}, u32[]{:S(2)}) collective-permute-start(bf16[4,64,512]{2,1,0:T(8,128)(2,1)S(1)} %get-tuple-element.69), channel_id=1, source_target_pairs={{0,8},{1,9},{2,10},{3,11},{4,12},{5,13},{6,14},{7,15},{8,0},{9,1},... | collective-permute-start | bytes 786440 | tf_op jit(solution)/shard_map/ppermute | solution.py:44
  14.4 6.9 %collective-permute-start.5 = (bf16[4,64,512]{2,1,0:T(8,128)(2,1)S(1)}, bf16[4,64,512]{2,1,0:T(8,128)(2,1)S(1)}, u32[]{:S(2)}, u32[]{:S(2)}) collective-permute-start(bf16[4,64,512]{2,1,0:T(8,128)(2,1)S(1)} %get-tuple-element.70), channel_id=1, source_target_pairs={{0,4},{1,5},{2,6},{3,7},{4,8},{5,9},{6,10},{7,11},{8,12},{9,13},{1... | collective-permute-start | bytes 786440 | tf_op jit(solution)/shard_map/ppermute | solution.py:44
  14.8 6.6 %collective-permute-start.6 = (bf16[4,64,512]{2,1,0:T(8,128)(2,1)S(1)}, bf16[4,64,512]{2,1,0:T(8,128)(2,1)S(1)}, u32[]{:S(2)}, u32[]{:S(2)}) collective-permute-start(bf16[4,64,512]{2,1,0:T(8,128)(2,1)S(1)} %get-tuple-element.71), channel_id=1, source_target_pairs={{0,12},{1,13},{2,14},{3,15},{4,0},{5,1},{6,2},{7,3},{8,4},{9,5},{1... | collective-permute-start | bytes 786440 | tf_op jit(solution)/shard_map/ppermute | solution.py:44
  21.7 7.7 %collective-permute-start.7 = (bf16[4,64,512]{2,1,0:T(8,128)(2,1)S(1)}, bf16[4,64,512]{2,1,0:T(8,128)(2,1)S(1)}, u32[]{:S(2)}, u32[]{:S(2)}) collective-permute-start(bf16[4,64,512]{2,1,0:T(8,128)(2,1)S(1)} %get-tuple-element.73), channel_id=1, source_target_pairs={{0,2},{1,3},{2,0},{3,1},{4,6},{5,7},{6,4},{7,5},{8,10},{9,11},{10,... | collective-permute-start | bytes 786440 | tf_op jit(solution)/shard_map/ppermute | solution.py:44
  25.6 6.9 %collective-permute-start.8 = (bf16[4,64,512]{2,1,0:T(8,128)(2,1)S(1)}, bf16[4,64,512]{2,1,0:T(8,128)(2,1)S(1)}, u32[]{:S(2)}, u32[]{:S(2)}) collective-permute-start(bf16[4,64,512]{2,1,0:T(8,128)(2,1)S(1)} %get-tuple-element.74), channel_id=1, source_target_pairs={{0,1},{1,2},{2,3},{3,0},{4,5},{5,6},{6,7},{7,4},{8,9},{9,10},{10,1... | collective-permute-start | bytes 786440 | tf_op jit(solution)/shard_map/ppermute | solution.py:44
  26.4 6.9 %collective-permute-start.9 = (bf16[4,64,512]{2,1,0:T(8,128)(2,1)S(1)}, bf16[4,64,512]{2,1,0:T(8,128)(2,1)S(1)}, u32[]{:S(2)}, u32[]{:S(2)}) collective-permute-start(bf16[4,64,512]{2,1,0:T(8,128)(2,1)S(1)} %get-tuple-element.75), channel_id=1, source_target_pairs={{0,3},{1,0},{2,1},{3,2},{4,7},{5,4},{6,5},{7,6},{8,11},{9,8},{10,9... | collective-permute-start | bytes 786440 | tf_op jit(solution)/shard_map/ppermute | solution.py:44
  33.3 9.0 %collective-permute-start.10 = (bf16[4,64,512]{2,1,0:T(8,128)(2,1)S(1)}, bf16[4,64,512]{2,1,0:T(8,128)(2,1)S(1)}, u32[]{:S(2)}, u32[]{:S(2)}) collective-permute-start(bf16[4,64,512]{2,1,0:T(8,128)(2,1)S(1)} %here.1.own), channel_id=1, source_target_pairs={{0,64},{1,65},{2,66},{3,67},{4,68},{5,69},{6,70},{7,71},{8,72},{9,... | collective-permute-start | bytes 786440 | tf_op jit(solution)/shard_map/ppermute | solution.py:44
  34.9 11.7 %collective-permute-start.11 = (bf16[4,64,512]{2,1,0:T(8,128)(2,1)S(1)}, bf16[4,64,512]{2,1,0:T(8,128)(2,1)S(1)}, u32[]{:S(2)}, u32[]{:S(2)}) collective-permute-start(bf16[4,64,512]{2,1,0:T(8,128)(2,1)S(1)} %here.1.own), channel_id=1, source_target_pairs={{0,32},{1,33},{2,34},{3,35},{4,36},{5,37},{6,38},{7,39},{8,40},{9,... | collective-permute-start | bytes 786440 | tf_op jit(solution)/shard_map/ppermute | solution.py:44
  35.3 11.3 %collective-permute-start.12 = (bf16[4,64,512]{2,1,0:T(8,128)(2,1)S(1)}, bf16[4,64,512]{2,1,0:T(8,128)(2,1)S(1)}, u32[]{:S(2)}, u32[]{:S(2)}) collective-permute-start(bf16[4,64,512]{2,1,0:T(8,128)(2,1)S(1)} %here.1.own), channel_id=1, source_target_pairs={{0,96},{1,97},{2,98},{3,99},{4,100},{5,101},{6,102},{7,103},{8,104... | collective-permute-start | bytes 786440 | tf_op jit(solution)/shard_map/ppermute | solution.py:44
  37.6 9.0 %collective-permute-start.13 = (bf16[3,64,512]{2,1,0:T(8,128)(2,1)S(1)}, bf16[3,64,512]{2,1,0:T(8,128)(2,1)S(1)}, u32[]{:S(2)}, u32[]{:S(2)}) collective-permute-start(bf16[3,64,512]{2,1,0:T(8,128)(2,1)S(1)} %slice.24), channel_id=1, source_target_pairs={{0,16},{1,17},{2,18},{3,19},{4,20},{5,21},{6,22},{7,23},{8,24},{9,... | collective-permute-start | bytes 589832 | tf_op jit(solution)/shard_map/ppermute | solution.py:44
  42.3 5.4 %collective-permute-start.14 = (bf16[3,64,512]{2,1,0:T(8,128)(2,1)S(1)}, bf16[3,64,512]{2,1,0:T(8,128)(2,1)S(1)}, u32[]{:S(2)}, u32[]{:S(2)}) collective-permute-start(bf16[3,64,512]{2,1,0:T(8,128)(2,1)S(1)} %slice.25), channel_id=1, source_target_pairs={{0,16},{1,17},{2,18},{3,19},{4,20},{5,21},{6,22},{7,23},{8,24},{9,... | collective-permute-start | bytes 589832 | tf_op jit(solution)/shard_map/ppermute | solution.py:44
  47.7 3.0 %collective-permute-start.15 = (bf16[2,3,64,512]{3,2,1,0:T(8,128)(2,1)S(1)}, bf16[2,3,64,512]{3,2,1,0:T(8,128)(2,1)S(1)}, u32[]{:S(2)}, u32[]{:S(2)}) collective-permute-start(bf16[2,3,64,512]{3,2,1,0:T(8,128)(2,1)S(1)} %both.1), channel_id=1, source_target_pairs={{0,16},{1,17},{2,18},{3,19},{4,20},{5,21},{6,22},{7,23},{8,24},{9,... | collective-permute-start | bytes 1179656 | tf_op jit(solution)/shard_map/ppermute | solution.py:44
  51.9 20.1 %copy-start.8 = (s32[62]{0:T(128)S(1)}, s32[62]{0:T(128)}, u32[]{:S(2)}) copy-start(s32[62]{0:T(128)} %get-tuple-element.55.spot) | copy-start | bytes 748
  52.0 8.5 %collective-permute-start.16 = (bf16[6,64,512]{2,1,0:T(8,128)(2,1)S(1)}, bf16[6,64,512]{2,1,0:T(8,128)(2,1)S(1)}, u32[]{:S(2)}, u32[]{:S(2)}) collective-permute-start(bf16[6,64,512]{2,1,0:T(8,128)(2,1)S(1)} %step.1.a), channel_id=1, source_target_pairs={{0,8},{1,9},{2,10},{3,11},{4,12},{5,13},{6,14},{7,15},{8,0},{9,1},... | collective-permute-start | bytes 1179656 | tf_op jit(solution)/shard_map/ppermute | solution.py:44
  53.8 10.8 %collective-permute-start.17 = (bf16[6,64,512]{2,1,0:T(8,128)(2,1)S(1)}, bf16[6,64,512]{2,1,0:T(8,128)(2,1)S(1)}, u32[]{:S(2)}, u32[]{:S(2)}) collective-permute-start(bf16[6,64,512]{2,1,0:T(8,128)(2,1)S(1)} %step.1.a), channel_id=1, source_target_pairs={{0,4},{1,5},{2,6},{3,7},{4,8},{5,9},{6,10},{7,11},{8,12},{9,13},{1... | collective-permute-start | bytes 1179656 | tf_op jit(solution)/shard_map/ppermute | solution.py:44
  55.0 9.7 %collective-permute-start.18 = (bf16[6,64,512]{2,1,0:T(8,128)(2,1)S(1)}, bf16[6,64,512]{2,1,0:T(8,128)(2,1)S(1)}, u32[]{:S(2)}, u32[]{:S(2)}) collective-permute-start(bf16[6,64,512]{2,1,0:T(8,128)(2,1)S(1)} %step.1.a), channel_id=1, source_target_pairs={{0,12},{1,13},{2,14},{3,15},{4,0},{5,1},{6,2},{7,3},{8,4},{9,5},{1... | collective-permute-start | bytes 1179656 | tf_op jit(solution)/shard_map/ppermute | solution.py:44
  65.0 17.3 %collective-permute-start.19 = (bf16[19,64,512]{2,1,0:T(8,128)(2,1)S(1)}, bf16[19,64,512]{2,1,0:T(8,128)(2,1)S(1)}, u32[]{:S(2)}, u32[]{:S(2)}) collective-permute-start(bf16[19,64,512]{2,1,0:T(8,128)(2,1)S(1)} %get-tuple-element.80), channel_id=1, source_target_pairs={{0,1},{1,2},{2,3},{3,0},{4,5},{5,6},{6,7},{7,4},{8,9},{9,10},{10,1... | collective-permute-start | bytes 3735560 | tf_op jit(solution)/shard_map/ppermute | solution.py:44
  65.7 16.7 %collective-permute-start.21 = (bf16[19,64,512]{2,1,0:T(8,128)(2,1)S(1)}, bf16[19,64,512]{2,1,0:T(8,128)(2,1)S(1)}, u32[]{:S(2)}, u32[]{:S(2)}) collective-permute-start(bf16[19,64,512]{2,1,0:T(8,128)(2,1)S(1)} %get-tuple-element.81), channel_id=1, source_target_pairs={{0,3},{1,0},{2,1},{3,2},{4,7},{5,4},{6,5},{7,6},{8,11},{9,8},{10,9... | collective-permute-start | bytes 3735560 | tf_op jit(solution)/shard_map/ppermute | solution.py:44
  67.8 4.3 %collective-permute-start.23 = (bf16[18,64,512]{2,1,0:T(8,128)(2,1)S(1)}, bf16[18,64,512]{2,1,0:T(8,128)(2,1)S(1)}, u32[]{:S(2)}, u32[]{:S(2)}) collective-permute-start(bf16[18,64,512]{2,1,0:T(8,128)(2,1)S(1)} %get-tuple-element.82.refs_0_.near), channel_id=1, source_target_pairs={{0,16},{1,17},{2,18},{3,19},{4,20},{5,21},{6,22},{7,23},{8,24},{9,... | collective-permute-start | bytes 3538952 | tf_op jit(solution)/shard_map/ppermute | solution.py:44
  82.4 5.1 %collective-permute-start.24 = (bf16[19,64,512]{2,1,0:T(8,128)(2,1)S(1)}, bf16[19,64,512]{2,1,0:T(8,128)(2,1)S(1)}, u32[]{:S(2)}, u32[]{:S(2)}) collective-permute-start(bf16[19,64,512]{2,1,0:T(8,128)(2,1)S(1)} %collective-permute-done.19.refs_1_.one), channel_id=1, source_target_pairs={{0,16},{1,17},{2,18},{3,19},{4,20},{5,21},{6,22},{7,23},{8,24},{9,... | collective-permute-start | bytes 3735560 | tf_op jit(solution)/shard_map/ppermute | solution.py:44
  84.6 4.8 %collective-permute-start.25 = (bf16[19,64,512]{2,1,0:T(8,128)(2,1)S(1)}, bf16[19,64,512]{2,1,0:T(8,128)(2,1)S(1)}, u32[]{:S(2)}, u32[]{:S(2)}) collective-permute-start(bf16[19,64,512]{2,1,0:T(8,128)(2,1)S(1)} %collective-permute-done.21.refs_1_.three), channel_id=1, source_target_pairs={{0,16},{1,17},{2,18},{3,19},{4,20},{5,21},{6,22},{7,23},{8,24},{9,... | collective-permute-start | bytes 3735560 | tf_op jit(solution)/shard_map/ppermute | solution.py:44
  84.7 10.3 %collective-permute-start.20 = (bf16[9,64,512]{2,1,0:T(8,128)(2,1)S(1)}, bf16[9,64,512]{2,1,0:T(8,128)(2,1)S(1)}, u32[]{:S(2)}, u32[]{:S(2)}) collective-permute-start(bf16[9,64,512]{2,1,0:T(8,128)(2,1)S(1)} %slice.26), channel_id=1, source_target_pairs={{0,1},{1,2},{2,3},{3,0},{4,5},{5,6},{6,7},{7,4},{8,9},{9,10},{10,1... | collective-permute-start | bytes 1769480 | tf_op jit(solution)/shard_map/ppermute | solution.py:44
  85.5 9.4 %collective-permute-start.22 = (bf16[9,64,512]{2,1,0:T(8,128)(2,1)S(1)}, bf16[9,64,512]{2,1,0:T(8,128)(2,1)S(1)}, u32[]{:S(2)}, u32[]{:S(2)}) collective-permute-start(bf16[9,64,512]{2,1,0:T(8,128)(2,1)S(1)} %slice.27), channel_id=1, source_target_pairs={{0,3},{1,0},{2,1},{3,2},{4,7},{5,4},{6,5},{7,6},{8,11},{9,8},{10,9... | collective-permute-start | bytes 1769480 | tf_op jit(solution)/shard_map/ppermute | solution.py:44
  91.4 5.2 %copy-start.5 = (f32[1,3,64,512]{3,2,1,0:T(8,128)S(1)}, f32[1,3,64,512]{3,2,1,0:T(8,128)}, u32[]{:S(2)}) copy-start(f32[1,3,64,512]{3,2,1,0:T(8,128)} %param.11) | copy-start | bytes 1179652
  91.4 5.2 %copy-start.6 = (f32[1,3,64,512]{3,2,1,0:T(8,128)S(1)}, f32[1,3,64,512]{3,2,1,0:T(8,128)}, u32[]{:S(2)}) copy-start(f32[1,3,64,512]{3,2,1,0:T(8,128)} %param.12) | copy-start | bytes 1179652
  95.0 3.6 %collective-permute-start.26 = (bf16[8,64,512]{2,1,0:T(8,128)(2,1)S(1)}, bf16[8,64,512]{2,1,0:T(8,128)(2,1)S(1)}, u32[]{:S(2)}, u32[]{:S(2)}) collective-permute-start(bf16[8,64,512]{2,1,0:T(8,128)(2,1)S(1)} %slice.22), channel_id=1, source_target_pairs={{0,16},{1,17},{2,18},{3,19},{4,20},{5,21},{6,22},{7,23},{8,24},{9,... | collective-permute-start | bytes 1572872 | tf_op jit(solution)/shard_map/ppermute | solution.py:44
  96.5 2.2 %collective-permute-start.27 = (bf16[8,64,512]{2,1,0:T(8,128)(2,1)S(1)}, bf16[8,64,512]{2,1,0:T(8,128)(2,1)S(1)}, u32[]{:S(2)}, u32[]{:S(2)}) collective-permute-start(bf16[8,64,512]{2,1,0:T(8,128)(2,1)S(1)} %slice.23), channel_id=1, source_target_pairs={{0,16},{1,17},{2,18},{3,19},{4,20},{5,21},{6,22},{7,23},{8,24},{9,... | collective-permute-start | bytes 1572872 | tf_op jit(solution)/shard_map/ppermute | solution.py:44
